TPU v7x, 32 devices: a whole 2x2x4 slice. The times are simulated.
32 devices in a mesh: gx: 8 (over z, y), yz: 4 (over x, core).
Axes of the slice: x: 2, y: 2, z: 4, core: 2. Of those that a mesh axis runs over, the one named last changes fastest.
Arguments:
- cell_matrix: bfloat16 [16, 128, 256, 256], P('gx', 'yz'), as said below
- x_coupling: bfloat16 [16, 128, 128], P('gx', 'yz'), may hold values from 0.5 to 2
- y_coupling: bfloat16 [16, 128, 128], P('gx', 'yz'), may hold values from 0.5 to 2
- cell_interp: bfloat16 [16, 128, 256, 128], P('gx', 'yz'), may hold values from -0.375 to 0.375
- cell_skel: int32 [16, 128, 128], P('gx', 'yz'), may hold values from 0 to 255, as said below
- cell_rank: int32 [16, 128], P('gx', 'yz'), may hold values from 64 to 128, as said below
- x_face_interp: bfloat16 [16, 128, 256, 128], P('gx', 'yz'), may hold values from -0.375 to 0.375
- x_face_skel: int32 [16, 128, 128], P('gx', 'yz'), may hold values from 0 to 255, as said below
- x_face_rank: int32 [16, 128], P('gx', 'yz'), may hold values from 64 to 128, as said below
- y_face_interp: bfloat16 [16, 128, 256, 128], P('gx', 'yz'), may hold values from -0.375 to 0.375
- y_face_skel: int32 [16, 128, 128], P('gx', 'yz'), may hold values from 0 to 255, as said below
- y_face_rank: int32 [16, 128], P('gx', 'yz'), may hold values from 64 to 128, as said below
Outputs:
- x_face_block: bfloat16 [16, 128, 128, 128], P('gx', 'yz')
- y_face_block: bfloat16 [16, 128, 128, 128], P('gx', 'yz')
Inputs may be any that keep to these rules, and one draw needn't show every extreme that they name: `cell_skel`: each row names 128 distinct unknowns of a cell block. `cell_rank`: the slots of cell_skel below a cell's rank are its live skeleton. `x_face_skel`: each row names 128 distinct unknowns of the face's two cells. `x_face_rank`: the slots of x_face_skel below a face's rank are its live skeleton. `y_face_skel`: each row names 128 distinct unknowns of the face's two cells. `y_face_rank`: the slots of y_face_skel below a face's rank are its live skeleton. `cell_matrix`: symmetric.
All inputs are finite; a program needn't handle non-finite values.
Results may differ from a plain program's by a relative error of at most 0.0053.
Values may be sent and summed in bfloat16 or wider, within the bound.
No kernel may reach another device: no remote copies, remote signals or barrier semaphores. Data moves between devices by JAX's collectives and lax.ppermute only.
A program may use at most 128 MiB of HBM per device.

v0:
```python
import jax
import jax.numpy as jnp
from jax import lax
from jax.sharding import PartitionSpec as P


def passed_along(x, axis, by):
    devices = lax.axis_size(axis)
    pairs = [(i, i + by) for i in range(devices) if 0 <= i + by < devices]
    return lax.ppermute(x, axis, pairs)


def make_basis(skel_list, rank_list, interp):
    row_count = interp.shape[-2]
    slot_count = skel_list.shape[-1]
    slot_index = lax.broadcasted_iota(jnp.int32, skel_list.shape, skel_list.ndim - 1)
    live_slots = slot_index < rank_list[..., None]
    row_index = lax.broadcasted_iota(
        jnp.int32, skel_list.shape[:-1] + (row_count, slot_count), skel_list.ndim - 1
    )
    picked_rows = (row_index == skel_list[..., None, :]) & live_slots[..., None, :]
    kept_rows = jnp.any(picked_rows, axis=-1, keepdims=True)
    interp_part = jnp.where(live_slots[..., None, :], interp.astype(jnp.float32), jnp.float32(0.0))
    return jnp.where(
        picked_rows, jnp.float32(1.0), jnp.where(kept_rows, jnp.float32(0.0), interp_part)
    ).astype(jnp.bfloat16)


def project(matrix, left_basis, right_basis):
    inner_prod = jnp.einsum(
        "...ij,...jk->...ik", matrix, right_basis, preferred_element_type=jnp.float32
    ).astype(jnp.bfloat16)
    return jnp.einsum(
        "...ji,...jk->...ik", left_basis, inner_prod, preferred_element_type=jnp.float32
    )


def coupling_link(conduct, own_basis, right_basis):
    half_rows = own_basis.shape[-2] // 2
    scaled = (
        -conduct.astype(jnp.float32)[..., None]
        * right_basis[..., :half_rows, :].astype(jnp.float32)
    ).astype(jnp.bfloat16)
    return jnp.einsum(
        "...ji,...jk->...ik",
        own_basis[..., half_rows:, :],
        scaled,
        preferred_element_type=jnp.float32,
    )


def face_matrix(left_block, link_block, right_block):
    upper_half = jnp.concatenate([left_block, link_block], axis=-1)
    lower_half = jnp.concatenate([jnp.swapaxes(link_block, -1, -2), right_block], axis=-1)
    return jnp.concatenate([upper_half, lower_half], axis=-2)


def body(
    cell_matrix,
    x_coupling,
    y_coupling,
    cell_interp,
    cell_skel,
    cell_rank,
    x_face_interp,
    x_face_skel,
    x_face_rank,
    y_face_interp,
    y_face_skel,
    y_face_rank,
):
    cell_basis = make_basis(cell_skel, cell_rank, cell_interp)
    schur_block = project(cell_matrix, cell_basis, cell_basis).astype(jnp.bfloat16)
    x_basis = make_basis(x_face_skel, x_face_rank, x_face_interp)
    y_basis = make_basis(y_face_skel, y_face_rank, y_face_interp)
    y_basis_in, y_schur_in = passed_along((cell_basis[:, :1], schur_block[:, :1]), "yz", -1)
    right_y_basis = jnp.concatenate([cell_basis[:, 1:], y_basis_in], axis=1)
    right_y_schur = jnp.concatenate([schur_block[:, 1:], y_schur_in], axis=1)
    y_link = coupling_link(y_coupling, cell_basis, right_y_basis).astype(jnp.bfloat16)
    y_face_block = project(
        face_matrix(schur_block, y_link, right_y_schur), y_basis, y_basis
    ).astype(jnp.bfloat16)
    x_basis_in, x_schur_in = passed_along((cell_basis[:1], schur_block[:1]), "gx", -1)
    right_x_basis = jnp.concatenate([cell_basis[1:], x_basis_in], axis=0)
    x_link = coupling_link(x_coupling, cell_basis, right_x_basis).astype(jnp.bfloat16)
    right_x_schur = jnp.concatenate([schur_block[1:], x_schur_in], axis=0)
    x_face_block = project(
        face_matrix(schur_block, x_link, right_x_schur), x_basis, x_basis
    ).astype(jnp.bfloat16)
    return (x_face_block, y_face_block)


def solution(mesh):
    return jax.shard_map(
        body,
        mesh=mesh,
        in_specs=(
            P("gx", "yz", None, None),
            P("gx", "yz", None),
            P("gx", "yz", None),
            P("gx", "yz", None, None),
            P("gx", "yz", None),
            P("gx", "yz"),
            P("gx", "yz", None, None),
            P("gx", "yz", None),
            P("gx", "yz"),
            P("gx", "yz", None, None),
            P("gx", "yz", None),
            P("gx", "yz"),
        ),
        out_specs=(P("gx", "yz", None, None), P("gx", "yz", None, None)),
        check_vma=False,
    )
```

profile of v0, /device:TPU:22, one launch (start us, length us, event | category | flops | bytes accessed | tf_op | source)
XLA Modules:
  0.0 123.5 jit_solution(10828127851869492120)
XLA Ops:
  1.4 6.4 %copy.15 = bf16[2,32,256,128]{2,3,1,0:T(8,128)(2,1)} copy(bf16[2,32,256,128]{3,2,1,0:T(8,128)(2,1)} %param.15) | data formatting | bytes 8388608 | tf_op args[3]
  7.8 2.8 %fusion.21 = pred[2,32,256]{2,1,0:T(8,128)(4,1)S(1)} fusion(s32[2,32,128]{2,1,0:T(8,128)S(1)} %copy-done.8, pred[2,32,128]{2,1,0:T(8,128)(4,1)S(1)} %iota_compare_fusion.4), kind=kLoop, calls=%fused_computation.27 | loop fusion | flops 6275072 | bytes 57344 | tf_op jit(solution)/shard_map/reduce_or | solution.py:22
  10.6 6.4 %select_convert_fusion.1 = bf16[2,32,256,128]{2,3,1,0:T(8,128)(2,1)S(1)} fusion(bf16[2,32,256,128]{2,3,1,0:T(8,128)(2,1)} %copy.15, s32[2,32,128]{2,1,0:T(8,128)S(1)} %copy-done.8, pred[2,32,256]{2,1,0:T(8,128)(4,1)S(1)} %fusion.21, pred[2,32,128]{2,1,0:T(8,128)(4,1)S(1)} %iota_compare_fusion.4), kind=kLoop, calls=%fused_computation.20 | loop fusion | flops 14680064 | bytes 8445952 | tf_op jit(solution)/shard_map/convert_element_type | solution.py:26
  17.0 2.0 %copy-done = bf16[2,32,256,128]{2,3,1,0:T(8,128)(2,1)} copy-done((bf16[2,32,256,128]{2,3,1,0:T(8,128)(2,1)}, bf16[2,32,256,128]{2,3,1,0:T(8,128)(2,1)S(1)}, u32[]{:S(2)}) %copy-start) | copy-done | bytes 4194328
  19.0 1.9 %collective-permute-start.2 = (bf16[2,1,256,128]{2,3,1,0:T(8,128)(2,1)S(1)}, bf16[2,1,256,128]{2,3,1,0:T(8,128)(2,1)S(1)}, u32[]{:S(2)}, u32[]{:S(2)}) collective-permute-start(bf16[2,1,256,128]{2,3,1,0:T(8,128)(2,1)S(1)} %slice.51), channel_id=1, source_target_pairs={{1,0},{2,1},{3,2},{5,4},{6,5},{7,6},{9,8},{10,9},{11,10},{13,12},{... | collective-permute-start | bytes 393224 | tf_op jit(solution)/shard_map/ppermute | solution.py:10
  20.9 7.9 %fusion.58 = bf16[2,32,128,128]{2,3,1,0:T(8,128)(2,1)S(1)} fusion(bf16[2,32,256,128]{2,3,1,0:T(8,128)(2,1)} %copy-done, bf16[2,32,256,256]{3,2,1,0:T(8,128)(2,1)} %param.12), kind=kOutput, calls=%fused_computation.51 | convolution fusion | flops 1613758464 | bytes 14680064 | tf_op jit(solution)/shard_map/...ji,...jk->...ik/dot_general | solution.py:33
  28.9 2.5 %collective-permute-start.3 = (bf16[2,1,128,128]{2,3,1,0:T(8,128)(2,1)S(1)}, bf16[2,1,128,128]{2,3,1,0:T(8,128)(2,1)}, u32[]{:S(2)}, u32[]{:S(2)}) collective-permute-start(bf16[2,1,128,128]{2,3,1,0:T(8,128)(2,1)S(1)} %slice.53), channel_id=1, source_target_pairs={{1,0},{2,1},{3,2},{5,4},{6,5},{7,6},{9,8},{10,9},{11,10},{13,12},{... | collective-permute-start | bytes 196616 | tf_op jit(solution)/shard_map/ppermute | solution.py:10
  31.4 4.8 %fusion.77 = (bf16[1,32,256,128]{2,3,1,0:T(8,128)(2,1)}, bf16[1,32,256,128]{2,3,1,0:T(8,128)(2,1)}) fusion(bf16[2,32,256,128]{2,3,1,0:T(8,128)(2,1)} %copy-done), kind=kLoop, calls=%fused_computation.67 | loop fusion | bytes 8388608 | tf_op jit(solution)/shard_map/slice | solution.py:84
  36.2 2.7 %collective-permute-start = (bf16[1,32,256,128]{2,3,1,0:T(8,128)(2,1)}, bf16[1,32,256,128]{2,3,1,0:T(8,128)(2,1)}, u32[]{:S(2)}, u32[]{:S(2)}) collective-permute-start(bf16[1,32,256,128]{2,3,1,0:T(8,128)(2,1)} %get-tuple-element.3), channel_id=1, source_target_pairs={{4,0},{8,4},{12,8},{16,12},{20,16},{24,20},{28,24},{5,1},{9,5},{13... | collective-permute-start | bytes 6291464 | tf_op jit(solution)/shard_map/ppermute | solution.py:10
  40.1 3.6 %collective-permute-start.1 = (bf16[1,32,128,128]{2,3,1,0:T(8,128)(2,1)}, bf16[1,32,128,128]{2,3,1,0:T(8,128)(2,1)}, u32[]{:S(2)}, u32[]{:S(2)}) collective-permute-start(bf16[1,32,128,128]{2,3,1,0:T(8,128)(2,1)} %get-tuple-element.5), channel_id=1, source_target_pairs={{4,0},{8,4},{12,8},{16,12},{20,16},{24,20},{28,24},{5,1},{9,5},{13... | collective-permute-start | bytes 3145736 | tf_op jit(solution)/shard_map/ppermute | solution.py:10
  43.7 2.2 %slice.50 = bf16[2,31,256,128]{2,3,1,0:T(8,128)(2,1)} slice(bf16[2,32,256,128]{2,3,1,0:T(8,128)(2,1)S(1)} %copy-done.1), slice={[0:2], [1:32], [0:256], [0:128]} | slice | bytes 8126464 | tf_op jit(solution)/shard_map/slice | solution.py:77
  46.0 6.4 %copy.20 = bf16[2,32,256,128]{2,3,1,0:T(8,128)(2,1)} copy(bf16[2,32,256,128]{3,2,1,0:T(8,128)(2,1)} %param.21) | data formatting | bytes 8388608 | tf_op args[9]
  52.5 6.4 %copy.14 = bf16[2,32,256,128]{2,3,1,0:T(8,128)(2,1)} copy(bf16[2,32,256,128]{3,2,1,0:T(8,128)(2,1)} %param.18) | data formatting | bytes 8388608 | tf_op args[6]
  58.8 3.4 %fusion.23 = pred[2,32,256]{2,1,0:T(8,128)(4,1)} fusion(s32[2,32,128]{2,1,0:T(8,128)S(1)} %copy-done.9, pred[2,32,128]{2,1,0:T(8,128)(4,1)S(1)} %iota_compare_fusion.3), kind=kLoop, calls=%fused_computation.29 | loop fusion | flops 6275072 | bytes 57344 | tf_op jit(solution)/shard_map/reduce_or | solution.py:22
  62.2 3.4 %fusion.19 = pred[2,32,256]{2,1,0:T(8,128)(4,1)} fusion(s32[2,32,128]{2,1,0:T(8,128)S(1)} %copy-done.10, pred[2,32,128]{2,1,0:T(8,128)(4,1)S(1)} %iota_compare_fusion.5), kind=kLoop, calls=%fused_computation.25 | loop fusion | flops 6275072 | bytes 57344 | tf_op jit(solution)/shard_map/reduce_or | solution.py:22
  65.7 5.1 %fusion.56 = bf16[2,32,128,128]{2,3,1,0:T(8,128)(2,1)} fusion(bf16[2,1,256,128]{2,3,1,0:T(8,128)(2,1)S(1)} %collective-permute-done.2, bf16[2,31,256,128]{2,3,1,0:T(8,128)(2,1)} %slice.50, f32[2,32,128]{2,1,0:T(8,128)S(1)} %convert_negate_fusion, bf16[2,32,256,128]{2,3,1,0:T(8,128)(2,1)} %copy-done), kind=kOutput, calls=%fused_computation.49 | convolution fusion | flops 275775488 | bytes 8421376 | tf_op jit(solution)/shard_map/...ji,...jk->...ik/dot_general | solution.py:44
  70.8 4.3 %copy.23 = bf16[2,32,128,128]{2,3,1,0:T(8,128)(2,1)} copy(bf16[2,32,128,128]{3,2,1,0:T(8,128)(2,1)} %bitcast.8) | data formatting | bytes 4194304 | tf_op jit(solution)/shard_map/convert_element_type | solution.py:79
  75.0 8.7 %fusion.98 = bf16[2,32,256,128]{3,2,1,0:T(8,128)(2,1)S(1)} fusion(bf16[2,32,128,128]{2,3,1,0:T(8,128)(2,1)} %copy-done.3, bf16[2,1,128,128]{2,3,1,0:T(8,128)(2,1)} %collective-permute-done.3, bf16[2,31,128,128]{2,3,1,0:T(8,128)(2,1)S(1)} %slice-done, bf16[2,32,128,128]{2,3,1,0:T(8,128)(2,1)} %copy.23, ...), kind=kOutput, calls=%fused_computation.31.clone.clone.clone.2 | convolution fusion | flops 1132462080 | bytes 16834560 | tf_op jit(solution)/shard_map/...ij,...jk->...ik/dot_general | solution.py:30
  83.8 5.5 %fusion.51 = bf16[2,32,128,128]{3,2,1,0:T(8,128)(2,1)} fusion(bf16[2,32,256,128]{2,3,1,0:T(8,128)(2,1)S(1)} %copy-done.7, s32[2,32,128]{2,1,0:T(8,128)S(1)} %copy-done.9, pred[2,32,256]{2,1,0:T(8,128)(4,1)S(1)} %copy-done.14, pred[2,32,128]{2,1,0:T(8,128)(4,1)S(1)} %iota_compare_fusion.3, bf16[2,32,256,128]{3,2,1,0:T(8,128)(2,1)S(1)} %fusion.98), kind=kOutput, calls=%fused_computation.48 | convolution fusion | flops 552599552 | bytes 10543104 | tf_op jit(solution)/shard_map/...ji,...jk->...ik/dot_general | solution.py:33
  89.3 4.2 %fusion.57 = bf16[2,32,128,128]{2,3,1,0:T(8,128)(2,1)} fusion(bf16[1,32,256,128]{2,3,1,0:T(8,128)(2,1)} %collective-permute-done, bf16[1,32,256,128]{2,3,1,0:T(8,128)(2,1)S(1)} %copy-done.5, f32[2,32,128]{2,1,0:T(8,128)S(1)} %convert_negate_fusion.1, bf16[2,32,256,128]{2,3,1,0:T(8,128)(2,1)S(1)} %copy-done.2), kind=kOutput, calls=%fused_computation.50 | convolution fusion | flops 275775488 | bytes 8421376 | tf_op jit(solution)/shard_map/...ji,...jk->...ik/dot_general | solution.py:44
  93.5 4.3 %copy.19 = bf16[2,32,128,128]{2,3,1,0:T(8,128)(2,1)} copy(bf16[2,32,128,128]{3,2,1,0:T(8,128)(2,1)} %bitcast.7) | data formatting | bytes 4194304 | tf_op jit(solution)/shard_map/convert_element_type | solution.py:85
  97.8 12.3 %collective-permute-done.1 = bf16[1,32,128,128]{2,3,1,0:T(8,128)(2,1)} collective-permute-done((bf16[1,32,128,128]{2,3,1,0:T(8,128)(2,1)}, bf16[1,32,128,128]{2,3,1,0:T(8,128)(2,1)}, u32[]{:S(2)}, u32[]{:S(2)}) %collective-permute-start.1) | collective-permute-done | bytes 1048608 | tf_op jit(solution)/shard_map/ppermute | solution.py:10
  110.0 8.0 %fusion.95 = bf16[2,32,256,128]{3,2,1,0:T(8,128)(2,1)S(1)} fusion(bf16[2,32,128,128]{2,3,1,0:T(8,128)(2,1)S(1)} %copy-done.4, bf16[1,32,128,128]{2,3,1,0:T(8,128)(2,1)} %collective-permute-done.1, bf16[1,32,128,128]{2,3,1,0:T(8,128)(2,1)S(1)} %get-tuple-element.4, bf16[2,32,128,128]{2,3,1,0:T(8,128)(2,1)} %copy.19, ...), kind=kOutput, calls=%fused_computation.34.clone.clone.clone.2 | convolution fusion | flops 1132462080 | bytes 16834560 | tf_op jit(solution)/shard_map/...ij,...jk->...ik/dot_general | solution.py:30
  118.0 5.5 %fusion.46 = bf16[2,32,128,128]{3,2,1,0:T(8,128)(2,1)} fusion(bf16[2,32,256,128]{2,3,1,0:T(8,128)(2,1)S(1)} %copy-done.6, s32[2,32,128]{2,1,0:T(8,128)S(1)} %copy-done.10, pred[2,32,256]{2,1,0:T(8,128)(4,1)S(1)} %copy-done.13, pred[2,32,128]{2,1,0:T(8,128)(4,1)S(1)} %iota_compare_fusion.5, bf16[2,32,256,128]{3,2,1,0:T(8,128)(2,1)S(1)} %fusion.95), kind=kOutput, calls=%fused_computation.47 | convolution fusion | flops 552599552 | bytes 10543104 | tf_op jit(solution)/shard_map/...ji,...jk->...ik/dot_general | solution.py:33
  (46 shorter events, 2.2 us)
Async XLA Ops:
  1.4 6.4 %copy-start.8 = (s32[2,32,128]{2,1,0:T(8,128)S(1)}, s32[2,32,128]{2,1,0:T(8,128)}, u32[]{:S(2)}) copy-start(s32[2,32,128]{2,1,0:T(8,128)} %param.16) | copy-start | bytes 98308
  17.0 2.0 %copy-start = (bf16[2,32,256,128]{2,3,1,0:T(8,128)(2,1)}, bf16[2,32,256,128]{2,3,1,0:T(8,128)(2,1)S(1)}, u32[]{:S(2)}) copy-start(bf16[2,32,256,128]{2,3,1,0:T(8,128)(2,1)S(1)} %select_convert_fusion.1) | copy-start | bytes 12582916
  19.0 46.7 %collective-permute-start.2 = (bf16[2,1,256,128]{2,3,1,0:T(8,128)(2,1)S(1)}, bf16[2,1,256,128]{2,3,1,0:T(8,128)(2,1)S(1)}, u32[]{:S(2)}, u32[]{:S(2)}) collective-permute-start(bf16[2,1,256,128]{2,3,1,0:T(8,128)(2,1)S(1)} %slice.51), channel_id=1, source_target_pairs={{1,0},{2,1},{3,2},{5,4},{6,5},{7,6},{9,8},{10,9},{11,10},{13,12},{... | collective-permute-start | bytes 393224 | tf_op jit(solution)/shard_map/ppermute | solution.py:10
  28.8 17.0 %copy-start.3 = (bf16[2,32,128,128]{2,3,1,0:T(8,128)(2,1)}, bf16[2,32,128,128]{2,3,1,0:T(8,128)(2,1)S(1)}, u32[]{:S(2)}) copy-start(bf16[2,32,128,128]{2,3,1,0:T(8,128)(2,1)S(1)} %fusion.58) | copy-start | bytes 6291460
  28.9 46.2 %collective-permute-start.3 = (bf16[2,1,128,128]{2,3,1,0:T(8,128)(2,1)S(1)}, bf16[2,1,128,128]{2,3,1,0:T(8,128)(2,1)}, u32[]{:S(2)}, u32[]{:S(2)}) collective-permute-start(bf16[2,1,128,128]{2,3,1,0:T(8,128)(2,1)S(1)} %slice.53), channel_id=1, source_target_pairs={{1,0},{2,1},{3,2},{5,4},{6,5},{7,6},{9,8},{10,9},{11,10},{13,12},{... | collective-permute-start | bytes 196616 | tf_op jit(solution)/shard_map/ppermute | solution.py:10
  36.2 7.5 %copy-start.1 = (bf16[2,32,256,128]{2,3,1,0:T(8,128)(2,1)S(1)}, bf16[2,32,256,128]{2,3,1,0:T(8,128)(2,1)}, u32[]{:S(2)}) copy-start(bf16[2,32,256,128]{2,3,1,0:T(8,128)(2,1)} %copy-done) | copy-start | bytes 12582916
  36.2 53.1 %collective-permute-start = (bf16[1,32,256,128]{2,3,1,0:T(8,128)(2,1)}, bf16[1,32,256,128]{2,3,1,0:T(8,128)(2,1)}, u32[]{:S(2)}, u32[]{:S(2)}) collective-permute-start(bf16[1,32,256,128]{2,3,1,0:T(8,128)(2,1)} %get-tuple-element.3), channel_id=1, source_target_pairs={{4,0},{8,4},{12,8},{16,12},{20,16},{24,20},{28,24},{5,1},{9,5},{13... | collective-permute-start | bytes 6291464 | tf_op jit(solution)/shard_map/ppermute | solution.py:10
  40.1 5.8 %copy-start.11 = (bf16[2,32,128]{2,1,0:T(8,128)(2,1)S(1)}, bf16[2,32,128]{2,1,0:T(8,128)(2,1)}, u32[]{:S(2)}) copy-start(bf16[2,32,128]{2,1,0:T(8,128)(2,1)} %param.14) | copy-start | bytes 49156
  40.1 5.8 %copy-start.15 = (s32[2,32]{1,0:T(2,128)S(1)}, s32[2,32]{1,0:T(2,128)}, u32[]{:S(2)}) copy-start(s32[2,32]{1,0:T(2,128)} %param.23) | copy-start | bytes 772
  40.1 70.0 %collective-permute-start.1 = (bf16[1,32,128,128]{2,3,1,0:T(8,128)(2,1)}, bf16[1,32,128,128]{2,3,1,0:T(8,128)(2,1)}, u32[]{:S(2)}, u32[]{:S(2)}) collective-permute-start(bf16[1,32,128,128]{2,3,1,0:T(8,128)(2,1)} %get-tuple-element.5), channel_id=1, source_target_pairs={{4,0},{8,4},{12,8},{16,12},{20,16},{24,20},{28,24},{5,1},{9,5},{13... | collective-permute-start | bytes 3145736 | tf_op jit(solution)/shard_map/ppermute | solution.py:10
  46.0 6.4 %copy-start.16 = (s32[2,32]{1,0:T(2,128)S(1)}, s32[2,32]{1,0:T(2,128)}, u32[]{:S(2)}) copy-start(s32[2,32]{1,0:T(2,128)} %param.20) | copy-start | bytes 772
  52.4 6.4 %copy-start.9 = (s32[2,32,128]{2,1,0:T(8,128)S(1)}, s32[2,32,128]{2,1,0:T(8,128)}, u32[]{:S(2)}) copy-start(s32[2,32,128]{2,1,0:T(8,128)} %param.22) | copy-start | bytes 98308
  52.4 9.8 %copy-start.10 = (s32[2,32,128]{2,1,0:T(8,128)S(1)}, s32[2,32,128]{2,1,0:T(8,128)}, u32[]{:S(2)}) copy-start(s32[2,32,128]{2,1,0:T(8,128)} %param.19) | copy-start | bytes 98308
  52.4 13.2 %copy-start.12 = (bf16[2,32,128]{2,1,0:T(8,128)(2,1)S(1)}, bf16[2,32,128]{2,1,0:T(8,128)(2,1)}, u32[]{:S(2)}) copy-start(bf16[2,32,128]{2,1,0:T(8,128)(2,1)} %param.13) | copy-start | bytes 49156
  70.8 4.3 %slice-start = ((bf16[2,32,128,128]{2,3,1,0:T(8,128)(2,1)}), bf16[2,31,128,128]{2,3,1,0:T(8,128)(2,1)S(1)}, s32[]{:S(2)}) async-start(bf16[2,32,128,128]{2,3,1,0:T(8,128)(2,1)} %copy-done.3), calls=%async_computation | async-start | bytes 4063232 | tf_op jit(solution)/shard_map/slice | solution.py:78
  70.8 4.3 %copy-start.14 = (pred[2,32,256]{2,1,0:T(8,128)(4,1)S(1)}, pred[2,32,256]{2,1,0:T(8,128)(4,1)}, u32[]{:S(2)}) copy-start(pred[2,32,256]{2,1,0:T(8,128)(4,1)} %fusion.23) | copy-start | bytes 49156
  75.0 8.8 %copy-start.7 = (bf16[2,32,256,128]{2,3,1,0:T(8,128)(2,1)S(1)}, bf16[2,32,256,128]{2,3,1,0:T(8,128)(2,1)}, u32[]{:S(2)}) copy-start(bf16[2,32,256,128]{2,3,1,0:T(8,128)(2,1)} %copy.20) | copy-start | bytes 12582916
  83.8 5.5 %copy-start.2 = (bf16[2,32,256,128]{2,3,1,0:T(8,128)(2,1)S(1)}, bf16[2,32,256,128]{2,3,1,0:T(8,128)(2,1)}, u32[]{:S(2)}) copy-start(bf16[2,32,256,128]{2,3,1,0:T(8,128)(2,1)} %copy-done) | copy-start | bytes 12582916
  83.8 5.5 %copy-start.5 = (bf16[1,32,256,128]{2,3,1,0:T(8,128)(2,1)S(1)}, bf16[1,32,256,128]{2,3,1,0:T(8,128)(2,1)}, u32[]{:S(2)}) copy-start(bf16[1,32,256,128]{2,3,1,0:T(8,128)(2,1)} %get-tuple-element.2) | copy-start | bytes 6291460
  93.5 16.6 %copy-start.4 = (bf16[2,32,128,128]{2,3,1,0:T(8,128)(2,1)S(1)}, bf16[2,32,128,128]{2,3,1,0:T(8,128)(2,1)}, u32[]{:S(2)}) copy-start(bf16[2,32,128,128]{2,3,1,0:T(8,128)(2,1)} %copy-done.3) | copy-start | bytes 6291460
  93.5 16.6 %copy-start.13 = (pred[2,32,256]{2,1,0:T(8,128)(4,1)S(1)}, pred[2,32,256]{2,1,0:T(8,128)(4,1)}, u32[]{:S(2)}) copy-start(pred[2,32,256]{2,1,0:T(8,128)(4,1)} %fusion.19) | copy-start | bytes 49156
  110.0 8.0 %copy-start.6 = (bf16[2,32,256,128]{2,3,1,0:T(8,128)(2,1)S(1)}, bf16[2,32,256,128]{2,3,1,0:T(8,128)(2,1)}, u32[]{:S(2)}) copy-start(bf16[2,32,256,128]{2,3,1,0:T(8,128)(2,1)} %copy.14) | copy-start | bytes 12582916
where the time goes:
time: 124 us
  matrix products  44.9 us (36%)
  local copies, waits for them, and re-layouts  37.8 us (30%)
  other arithmetic  17 us (14%)
  waiting for transfers between devices  12.3 us (10%)
  starting transfers between devices  10.8 us (9%)
    unnamed x37, local copies, waits for them, and re-layouts  21.1 us
    dot_general x3, matrix products, project(): jnp.einsum('...ji,...jk->...ik', left_basis, inner_prod, preferred_elemen...  18.9 us
    dot_general x2, matrix products, project(): jnp.einsum('...ij,...jk->...ik', matrix, right_basis, preferred_element_t...  16.7 us
    ppermute x4, waiting for transfers between devices, passed_along(): return lax.ppermute(x, axis, pairs)  12.3 us
    ppermute x4, starting transfers between devices, passed_along(): return lax.ppermute(x, axis, pairs)  10.8 us
    reduce_or x3, other arithmetic, make_basis(): kept_rows = jnp.any(picked_rows, axis=-1, keepdims=True)  9.64 us
    dot_general x2, matrix products, coupling_link(): jnp.einsum('...ji,...jk->...ik', own_basis[..., half_rows:, :], scaled, p...  9.25 us
    convert_element_type x1, other arithmetic, make_basis(): return jnp.where(picked_rows, jnp.float32(1.0), jnp.where(kept_rows, jnp....  6.4 us
  transfers between devices with their start and end apart: 4, of which 1 were waited for; matrix products, arithmetic and copies ran while one was open for 55% of the time, Pallas kernels for 0%

commit v1 on v0

v1 whole, which is shorter than its diff:
```python
import functools

import jax
import jax.numpy as jnp
from jax import lax
from jax.experimental import pallas as pl
from jax.experimental.pallas import tpu as pltpu
from jax.sharding import PartitionSpec as P

BF = jnp.bfloat16
F32 = jnp.float32
VMEM_LIMIT = 56 * 1024 * 1024


def passed_along(x, axis, by):
    devices = lax.axis_size(axis)
    pairs = [(i, i + by) for i in range(devices) if 0 <= i + by < devices]
    return lax.ppermute(x, axis, pairs)


def dot(a, b):
    return lax.dot_general(a, b, (((1,), (0,)), ((), ())), preferred_element_type=F32)


def dot_nt(a, b):
    return lax.dot_general(a, b, (((1,), (1,)), ((), ())), preferred_element_type=F32)


def basis_t(skel_row, rank, interp):
    rows, slots = interp.shape
    live = lax.broadcasted_iota(jnp.int32, (1, slots), 1) < rank
    picked_row = jnp.where(live, skel_row, -1)
    row = lax.broadcasted_iota(jnp.int32, (rows, slots), 0)
    marked = jnp.where(
        row == picked_row, F32(1.0), jnp.where(live, interp.astype(F32), F32(0.0))
    ).astype(BF)
    turned = jnp.transpose(marked).astype(F32)
    most = jnp.max(turned, axis=0, keepdims=True)
    least = jnp.where(most == 1.0, F32(1.0), F32(-2.0))
    return jnp.where(turned >= least, turned, F32(0.0)).astype(BF)


def project_t(basis, matrix):
    return dot_nt(dot(basis, matrix).astype(BF), basis)


def links(own, conduct, right_top):
    half = own.shape[-1] // 2
    scaled = (right_top.astype(F32) * -conduct.astype(F32)).astype(BF)
    lower = own[:, half:]
    return dot_nt(lower, scaled).astype(BF), dot_nt(scaled, lower).astype(BF)


def face_t(basis, left, link, link_t, right):
    upper = jnp.concatenate([left, link], axis=1)
    lower = jnp.concatenate([link_t, right], axis=1)
    return project_t(basis, jnp.concatenate([upper, lower], axis=0))


def top_kernel(cells, rank_ref, skel_ref, interp_ref, out_ref):
    first = pl.program_id(0) * cells
    for k in range(cells):
        out_ref[k] = basis_t(skel_ref[0, k : k + 1], rank_ref[0, first + k], interp_ref[0, k])


def pack_masks(size):
    half = size // 2
    row = lax.broadcasted_iota(jnp.int32, (half, size), 0)
    lane = lax.broadcasted_iota(jnp.int32, (half, size), 1)
    ahead = lane - row
    upper = (ahead >= 0) & (ahead < half)
    return upper, ahead == 0, ahead == half


def cells_kernel(cells, rank_ref, skel_ref, interp_ref, matrix_ref, basis_ref, schur_ref, edge_ref, packed_ref):
    layer, chunk = pl.program_id(0), pl.program_id(1)
    first = chunk * cells
    slots = skel_ref.shape[-1]
    half = slots // 2
    upper, _, opposite = pack_masks(slots)
    packs, extras = [], []
    for k in range(cells):
        basis = basis_t(skel_ref[0, k : k + 1], rank_ref[layer, first + k], interp_ref[0, k])
        schur = project_t(basis, matrix_ref[0, k]).astype(BF)
        basis_ref[0, k] = basis
        schur_ref[0, k] = schur
        wide = schur.astype(F32)
        packs.append(jnp.where(upper, wide[:half], wide[half:]).astype(BF))
        extras.append(
            jnp.sum(jnp.where(opposite, wide[:half], F32(0.0)), axis=0, keepdims=True)
        )

    @pl.when(layer == 0)
    def _():
        pad = packed_ref.shape[1] - cells * half - cells
        for k in range(cells):
            packed_ref[chunk, k * half : (k + 1) * half] = packs[k]
        rows = extras + [jnp.zeros((pad, slots), F32)]
        packed_ref[chunk, cells * half :] = jnp.concatenate(rows, axis=0).astype(BF)

    @pl.when(chunk == 0)
    def _():
        edge_ref[layer, 0] = basis_ref[0, 0, :, : basis_ref.shape[-1] // 2]
        edge_ref[layer, 1] = schur_ref[0, 0]


def y_faces_kernel(cells, rank_ref, skel_ref, interp_ref, coup_ref, basis_ref, schur_ref, nbasis_ref, nschur_ref, out_ref):
    layer, chunk = pl.program_id(0), pl.program_id(1)
    first = chunk * cells
    half = nbasis_ref.shape[-1]
    for k in range(cells):
        face = basis_t(skel_ref[0, k : k + 1], rank_ref[layer, first + k], interp_ref[0, k])
        if k + 1 < cells:
            right_top, right = basis_ref[0, k + 1, :, :half], schur_ref[0, k + 1]
        else:
            right_top, right = nbasis_ref[0, 0], nschur_ref[0, 0]
        link, link_t = links(basis_ref[0, k], coup_ref[0, k : k + 1], right_top)
        out_ref[0, k] = face_t(face, schur_ref[0, k], link, link_t, right).astype(BF)


def y_edge_kernel(place, rank_ref, skel_ref, interp_ref, coup_ref, basis_ref, schur_ref, edge_ref, _, out_ref):
    layer = pl.program_id(0)
    row = place % skel_ref.shape[1]
    face = basis_t(skel_ref[0, row : row + 1], rank_ref[layer, place], interp_ref[0, 0])
    link, link_t = links(basis_ref[0, 0], coup_ref[0, row : row + 1], edge_ref[0, 0])
    out_ref[0, 0] = face_t(face, schur_ref[0, 0], link, link_t, edge_ref[0, 1]).astype(BF)


def x_faces_kernel(cells, rank_ref, skel_ref, interp_ref, coup_ref, basis_ref, schur_ref, nbasis_ref, nschur_ref, out_ref):
    layer, chunk = pl.program_id(0), pl.program_id(1)
    first = chunk * cells
    for k in range(cells):
        face = basis_t(skel_ref[0, k : k + 1], rank_ref[layer, first + k], interp_ref[0, k])
        link, link_t = links(basis_ref[0, k], coup_ref[0, k : k + 1], nbasis_ref[0, k])
        out_ref[0, k] = face_t(face, schur_ref[0, k], link, link_t, nschur_ref[0, k]).astype(BF)


def x_part_kernel(cells, layer, rank_ref, skel_ref, interp_ref, coup_ref, basis_ref, schur_ref, top_ref, part_ref, lower_ref):
    first = pl.program_id(0) * cells
    half = top_ref.shape[-1]
    for k in range(cells):
        face = basis_t(skel_ref[0, k : k + 1], rank_ref[layer, first + k], interp_ref[0, k])
        link, link_t = links(basis_ref[0, k], coup_ref[0, k : k + 1], top_ref[k])
        part_ref[k] = face_t(face, schur_ref[0, k], link, link_t, jnp.zeros_like(link))
        lower_ref[k] = face[:, half:]


def x_last_kernel(cells, part_ref, lower_ref, packed_ref, _, out_ref):
    slots = part_ref.shape[-1]
    half = slots // 2
    upper, same, opposite = pack_masks(slots)
    one, zero, mid = F32(1.0), F32(0.0), F32(0.5)
    top_scale = jnp.where(same, mid, jnp.where(upper, one, zero))
    low_scale = jnp.where(opposite, mid, jnp.where(upper, zero, one))
    opp_scale = jnp.where(opposite, one, zero)
    extras = packed_ref[0, cells * half :].astype(F32)
    for k in range(cells):
        packed = packed_ref[0, k * half : (k + 1) * half].astype(F32)
        top = packed * top_scale + extras[k : k + 1] * opp_scale
        low = packed * low_scale
        tri = jnp.concatenate([top, low], axis=0).astype(BF)
        lower = lower_ref[k]
        inner = (dot(lower, tri) + dot_nt(lower, tri)).astype(BF)
        out_ref[0, k] = (part_ref[k] + dot_nt(inner, lower)).astype(BF)


def call(kernel, grid, in_specs, out_specs, out_shape, flops, moved, aliases=None):
    return pl.pallas_call(
        kernel,
        grid=grid,
        in_specs=in_specs,
        out_specs=out_specs,
        out_shape=out_shape,
        input_output_aliases=aliases or {},
        compiler_params=pltpu.CompilerParams(vmem_limit_bytes=VMEM_LIMIT),
        cost_estimate=pl.CostEstimate(flops=flops, bytes_accessed=moved, transcendentals=0),
    )


def body(
    cell_matrix,
    x_coupling,
    y_coupling,
    cell_interp,
    cell_skel,
    cell_rank,
    x_face_interp,
    x_face_skel,
    x_face_rank,
    y_face_interp,
    y_face_skel,
    y_face_rank,
):
    nx, nj, rows, slots = cell_interp.shape
    half = rows // 2
    fslots = x_face_interp.shape[-1]
    cells = 8 if nj % 8 == 0 else nj
    chunks = nj // cells
    unit = 2 * nx * nj * slots * slots * slots
    smem = pl.BlockSpec(memory_space=pltpu.SMEM)
    shape = jax.ShapeDtypeStruct

    def block(*dims):
        return pl.BlockSpec((1, cells) + dims, lambda i, c: (i, c) + (0,) * len(dims))

    top = call(
        functools.partial(top_kernel, cells),
        (chunks,),
        [
            smem,
            pl.BlockSpec((1, cells, slots), lambda c: (0, c, 0)),
            pl.BlockSpec((1, cells, half, slots), lambda c: (0, c, 0, 0)),
        ],
        pl.BlockSpec((cells, slots, half), lambda c: (c, 0, 0)),
        shape((nj, slots, half), BF),
        0,
        4 * nj * half * slots,
    )(cell_rank, cell_skel, cell_interp)
    top_in = passed_along(top, "gx", -1)

    pack_rows = cells * slots // 2 + -(-cells // 16) * 16
    basis, schur, edge, packed = call(
        functools.partial(cells_kernel, cells),
        (nx, chunks),
        [smem, block(slots), block(rows, slots), block(rows, rows)],
        [
            block(slots, rows),
            block(slots, slots),
            pl.BlockSpec((nx, 2, slots, slots), lambda i, c: (0, 0, 0, 0)),
            pl.BlockSpec((chunks, pack_rows, slots), lambda i, c: (0, 0, 0)),
        ],
        [
            shape((nx, nj, slots, rows), BF),
            shape((nx, nj, slots, slots), BF),
            shape((nx, 2, slots, slots), BF),
            shape((chunks, pack_rows, slots), BF),
        ],
        6 * unit,
        nx * nj * (rows * rows + 2 * rows * slots + slots * slots) * 2,
    )(cell_rank, cell_skel, cell_interp, cell_matrix)
    edge_in = passed_along(edge, "yz", -1)
    packed_in = passed_along(packed, "gx", -1)

    face_bytes = nj * (2 * rows * slots + 4 * slots * slots) * 2
    y_out = call(
        functools.partial(y_faces_kernel, cells),
        (nx, chunks),
        [
            smem,
            block(fslots),
            block(rows, fslots),
            block(half),
            block(slots, rows),
            block(slots, slots),
            pl.BlockSpec((1, 1, slots, half), lambda i, c: (i, jnp.minimum((c + 1) * cells, nj - 1), 0, 0)),
            pl.BlockSpec((1, 1, slots, slots), lambda i, c: (i, jnp.minimum((c + 1) * cells, nj - 1), 0, 0)),
        ],
        block(fslots, fslots),
        shape((nx, nj, fslots, fslots), BF),
        8 * unit,
        nx * face_bytes,
    )(y_face_rank, y_face_skel, y_face_interp, y_coupling, basis, schur, basis, schur)

    if nx > 1:
        x_out = call(
            functools.partial(x_faces_kernel, cells),
            (nx - 1, chunks),
            [
                smem,
                block(fslots),
                block(rows, fslots),
                block(half),
                block(slots, rows),
                block(slots, slots),
                pl.BlockSpec((1, cells, slots, half), lambda i, c: (i + 1, c, 0, 0)),
                pl.BlockSpec((1, cells, slots, slots), lambda i, c: (i + 1, c, 0, 0)),
            ],
            block(fslots, fslots),
            shape((nx, nj, fslots, fslots), BF),
            8 * unit // nx * (nx - 1),
            (nx - 1) * face_bytes,
        )(x_face_rank, x_face_skel, x_face_interp, x_coupling, basis, schur, basis, schur)
    else:
        x_out = jnp.zeros((nx, nj, fslots, fslots), BF)

    last = nx - 1
    tail = nj - 1
    group = tail // cells

    def last_block(*dims):
        return pl.BlockSpec((1, cells) + dims, lambda c: (last, c) + (0,) * len(dims))

    def plain(*dims):
        return pl.BlockSpec((cells,) + dims, lambda c: (c,) + (0,) * len(dims))

    part, lower = call(
        functools.partial(x_part_kernel, cells, last),
        (chunks,),
        [
            smem,
            last_block(fslots),
            last_block(rows, fslots),
            last_block(half),
            last_block(slots, rows),
            last_block(slots, slots),
            plain(slots, half),
        ],
        [plain(fslots, fslots), plain(fslots, slots)],
        [shape((nj, fslots, fslots), F32), shape((nj, fslots, slots), BF)],
        8 * unit // nx,
        face_bytes,
    )(x_face_rank, x_face_skel, x_face_interp, x_coupling, basis, schur, top_in)

    y_out = call(
        functools.partial(y_edge_kernel, tail),
        (nx,),
        [
            smem,
            pl.BlockSpec((1, cells, fslots), lambda i: (i, group, 0)),
            pl.BlockSpec((1, 1, rows, fslots), lambda i: (i, tail, 0, 0)),
            pl.BlockSpec((1, cells, half), lambda i: (i, group, 0)),
            pl.BlockSpec((1, 1, slots, rows), lambda i: (i, tail, 0, 0)),
            pl.BlockSpec((1, 1, slots, slots), lambda i: (i, tail, 0, 0)),
            pl.BlockSpec((1, 2, slots, slots), lambda i: (i, 0, 0, 0)),
            pl.BlockSpec(memory_space=pl.ANY),
        ],
        pl.BlockSpec((1, 1, fslots, fslots), lambda i: (i, tail, 0, 0)),
        shape((nx, nj, fslots, fslots), BF),
        8 * unit // nj,
        nx * face_bytes // nj,
        {7: 0},
    )(y_face_rank, y_face_skel, y_face_interp, y_coupling, basis, schur, edge_in, y_out)

    x_out = call(
        functools.partial(x_last_kernel, cells),
        (chunks,),
        [
            plain(fslots, fslots),
            plain(fslots, slots),
            pl.BlockSpec((1, pack_rows, slots), lambda c: (c, 0, 0)),
            pl.BlockSpec(memory_space=pl.ANY),
        ],
        last_block(fslots, fslots),
        shape((nx, nj, fslots, fslots), BF),
        3 * unit // nx,
        nj * slots * slots * 9,
        {3: 0},
    )(part, lower, packed_in, x_out)
    return (x_out, y_out)


def solution(mesh):
    return jax.shard_map(
        body,
        mesh=mesh,
        in_specs=(
            P("gx", "yz", None, None),
            P("gx", "yz", None),
            P("gx", "yz", None),
            P("gx", "yz", None, None),
            P("gx", "yz", None),
            P("gx", "yz"),
            P("gx", "yz", None, None),
            P("gx", "yz", None),
            P("gx", "yz"),
            P("gx", "yz", None, None),
            P("gx", "yz", None),
            P("gx", "yz"),
        ),
        out_specs=(P("gx", "yz", None, None), P("gx", "yz", None, None)),
        check_vma=False,
    )
```

time: 124 us -> 84.4 us (0.68)
  the two profiles are of different devices: /device:TPU:22 before, /device:TPU:29 now
where the time goes in v1:
time: 84.4 us; the launch traced here: 83.9 us
  Pallas kernels  72.5 us (86%)
  starting transfers between devices  8.33 us (10%)
  local copies, waits for them, and re-layouts  2.39 us (3%)
    pallas_call x1, Pallas kernels, body(): call(functools.partial(y_faces_kernel, cells), (nx, chunks), [smem, block...  22.3 us
    pallas_call x1, Pallas kernels, body(): call(functools.partial(x_part_kernel, cells, last), (chunks,), [smem, las...  12.2 us
    pallas_call x1, Pallas kernels, body(): call(functools.partial(x_faces_kernel, cells), (nx - 1, chunks), [smem, b...  12.2 us
    pallas_call x1, Pallas kernels, body(): call(functools.partial(cells_kernel, cells), (nx, chunks), [smem, block(s...  11.6 us
    ppermute x3, starting transfers between devices, passed_along(): return lax.ppermute(x, axis, pairs)  8.33 us
    pallas_call x1, Pallas kernels, body(): call(functools.partial(x_last_kernel, cells), (chunks,), [plain(fslots, f...  7.91 us
    pallas_call x1, Pallas kernels, body(): call(functools.partial(top_kernel, cells), (chunks,), [smem, pl.BlockSpec...  3.74 us
    pallas_call x1, Pallas kernels, body(): call(functools.partial(y_edge_kernel, tail), (nx,), [smem, pl.BlockSpec((...  2.53 us
  transfers between devices with their start and end apart: 3, of which 0 were waited for; matrix products, arithmetic and copies ran while one was open for 0% of the time, Pallas kernels for 73%

profile of v1, /device:TPU:29, one launch (start us, length us, event | category | flops | bytes accessed | tf_op | source)
XLA Modules:
  0.0 83.9 jit_solution(10035023460225554468)
XLA Ops:
  0.6 3.7 %shard_map.132 = bf16[32,128,128]{2,1,0:T(8,128)(2,1)} custom-call(s32[2,32]{1,0:T(2,128)} %rank_ref.7, s32[2,32,128]{2,1,0:T(8,128)} %skel_ref.7, bf16[2,32,256,128]{3,2,1,0:T(8,128)(2,1)} %interp_ref.7), custom_call_target="tpu_custom_call" | custom-call | bytes 2097152 | tf_op jit(solution)/shard_map/pallas_call | solution.py:206
  4.4 2.2 %collective-permute-start = (bf16[32,128,128]{2,1,0:T(8,128)(2,1)}, bf16[32,128,128]{2,1,0:T(8,128)(2,1)S(1)}, u32[]{:S(2)}, u32[]{:S(2)}) collective-permute-start(bf16[32,128,128]{2,1,0:T(8,128)(2,1)} %shard_map.132), channel_id=1, source_target_pairs={{4,0},{8,4},{12,8},{16,12},{20,16},{24,20},{28,24},{5,1},{9,5},{13... | collective-permute-start | bytes 3145736 | tf_op jit(solution)/shard_map/ppermute | solution.py:18
  6.6 11.6 %shard_map.131 = (bf16[2,32,128,256]{3,2,1,0:T(8,128)(2,1)}, bf16[2,32,128,128]{3,2,1,0:T(8,128)(2,1)}, bf16[2,2,128,128]{3,2,1,0:T(8,128)(2,1)}, bf16[4,528,128]{2,1,0:T(8,128)(2,1)}) custom-call(s32[2,32]{1,0:T(2,128)} %rank_ref.7, s32[2,32,128]{2,1,0:T(8,128)} %skel_ref.7, bf16[2,32,256,128]{3,2,1,0:T(8,128)(2,1)} %interp_ref.7, ...), custom_call_target="tpu_custom_call" | custom-call | flops 1610612736 | bytes 18874368 | tf_op jit(solution)/shard_map/pallas_call | solution.py:222
  18.2 3.0 %collective-permute-start.1 = (bf16[4,528,128]{2,1,0:T(8,128)(2,1)}, bf16[4,528,128]{2,1,0:T(8,128)(2,1)S(1)}, u32[]{:S(2)}, u32[]{:S(2)}) collective-permute-start(bf16[4,528,128]{2,1,0:T(8,128)(2,1)} %get-tuple-element.12), channel_id=1, source_target_pairs={{4,0},{8,4},{12,8},{16,12},{20,16},{24,20},{28,24},{5,1},{9,5},{13... | collective-permute-start | bytes 1622024 | tf_op jit(solution)/shard_map/ppermute | solution.py:18
  21.2 3.1 %collective-permute-start.2 = (bf16[2,2,128,128]{3,2,1,0:T(8,128)(2,1)}, bf16[2,2,128,128]{3,2,1,0:T(8,128)(2,1)S(1)}, u32[]{:S(2)}, u32[]{:S(2)}) collective-permute-start(bf16[2,2,128,128]{3,2,1,0:T(8,128)(2,1)} %get-tuple-element.13), channel_id=1, source_target_pairs={{1,0},{2,1},{3,2},{5,4},{6,5},{7,6},{9,8},{10,9},{11,10},{13,12},{... | collective-permute-start | bytes 393224 | tf_op jit(solution)/shard_map/ppermute | solution.py:18
  24.3 22.3 %shard_map.136._ = bf16[2,32,128,128]{3,2,1,0:T(8,128)(2,1)} custom-call(s32[2,32]{1,0:T(2,128)} %rank_ref.11, s32[2,32,128]{2,1,0:T(8,128)} %skel_ref.11, bf16[2,32,256,128]{3,2,1,0:T(8,128)(2,1)} %interp_ref.11, bf16[2,32,128]{2,1,0:T(8,128)(2,1)} %coup_ref.7, bf16[2,32,128,256]{3,2,1,0:T(8,128)(2,1)} %get-tuple-element.8.basis_ref.nbasis_ref, ...), custom_call_target="tpu_custom_call" | custom-call | flops 2147483648 | bytes 16777216 | tf_op jit(solution)/shard_map/pallas_call | solution.py:245
  46.6 12.2 %shard_map.134._ = bf16[2,32,128,128]{3,2,1,0:T(8,128)(2,1)} custom-call(s32[2,32]{1,0:T(2,128)} %rank_ref.9, s32[2,32,128]{2,1,0:T(8,128)} %skel_ref.9, bf16[2,32,256,128]{3,2,1,0:T(8,128)(2,1)} %interp_ref.9, bf16[2,32,128]{2,1,0:T(8,128)(2,1)} %coup_ref.5, bf16[2,32,128,256]{3,2,1,0:T(8,128)(2,1)} %get-tuple-element.8.basis_ref.nbasis_ref, ...), custom_call_target="tpu_custom_call" | custom-call | flops 1073741824 | bytes 8388608 | tf_op jit(solution)/shard_map/pallas_call | solution.py:265
  58.8 0.0 collective-permute-done.2.edge_ref
  58.8 0.0 copy-start.2
  58.8 0.6 copy-done.2
  59.4 2.5 %shard_map.137 = bf16[2,32,128,128]{3,2,1,0:T(8,128)(2,1)} custom-call(s32[2,32]{1,0:T(2,128)} %rank_ref.11, s32[2,32,128]{2,1,0:T(8,128)} %skel_ref.11, bf16[2,32,256,128]{3,2,1,0:T(8,128)(2,1)} %interp_ref.11, bf16[2,32,128]{2,1,0:T(8,128)(2,1)} %coup_ref.7, ...), custom_call_target="tpu_custom_call", output_to_operand_aliasing={{}: (7, {})} | custom-call | flops 67108864 | bytes 524288 | tf_op jit(solution)/shard_map/pallas_call | solution.py:314
  62.0 0.0 collective-permute-done.top_ref
  62.0 0.0 copy-start
  62.0 1.0 %copy-done = bf16[32,128,128]{2,1,0:T(8,128)(2,1)} copy-done((bf16[32,128,128]{2,1,0:T(8,128)(2,1)}, bf16[32,128,128]{2,1,0:T(8,128)(2,1)S(1)}, u32[]{:S(2)}) %copy-start) | copy-done | bytes 1048600
  62.9 12.2 %shard_map.133 = (f32[32,128,128]{2,1,0:T(8,128)}, bf16[32,128,128]{2,1,0:T(8,128)(2,1)}) custom-call(s32[2,32]{1,0:T(2,128)} %rank_ref.9, s32[2,32,128]{2,1,0:T(8,128)} %skel_ref.9, bf16[2,32,256,128]{3,2,1,0:T(8,128)(2,1)} %interp_ref.9, bf16[2,32,128]{2,1,0:T(8,128)(2,1)} %coup_ref.5, bf16[2,32,128,256]{3,2,1,0:T(8,128)(2,1)} %get-tuple-element.8.basis_ref.nbasis_ref, ...), custom_call_target="tpu_custom_call" | custom-call | flops 1073741824 | bytes 8388608 | tf_op jit(solution)/shard_map/pallas_call | solution.py:296
  75.2 0.0 collective-permute-done.1.packed_ref
  75.2 0.0 copy-start.1
  75.2 0.8 copy-done.1
  76.0 7.9 %shard_map.135 = bf16[2,32,128,128]{3,2,1,0:T(8,128)(2,1)} custom-call(f32[32,128,128]{2,1,0:T(8,128)} %get-tuple-element.10.part_ref, bf16[32,128,128]{2,1,0:T(8,128)(2,1)} %get-tuple-element.11.lower_ref, bf16[4,528,128]{2,1,0:T(8,128)(2,1)} %copy-done.1, bf16[2,32,128,128]{3,2,1,0:T(8,128)(2,1)} %shard_map.134._), custom_call_target="tpu_custom_call", output_to_operand_aliasing={{}: (3, {})} | custom-call | flops 402653184 | bytes 4718592 | tf_op jit(solution)/shard_map/pallas_call | solution.py:334
Async XLA Ops:
  4.4 57.6 %collective-permute-start = (bf16[32,128,128]{2,1,0:T(8,128)(2,1)}, bf16[32,128,128]{2,1,0:T(8,128)(2,1)S(1)}, u32[]{:S(2)}, u32[]{:S(2)}) collective-permute-start(bf16[32,128,128]{2,1,0:T(8,128)(2,1)} %shard_map.132), channel_id=1, source_target_pairs={{4,0},{8,4},{12,8},{16,12},{20,16},{24,20},{28,24},{5,1},{9,5},{13... | collective-permute-start | bytes 3145736 | tf_op jit(solution)/shard_map/ppermute | solution.py:18
  18.2 57.0 %collective-permute-start.1 = (bf16[4,528,128]{2,1,0:T(8,128)(2,1)}, bf16[4,528,128]{2,1,0:T(8,128)(2,1)S(1)}, u32[]{:S(2)}, u32[]{:S(2)}) collective-permute-start(bf16[4,528,128]{2,1,0:T(8,128)(2,1)} %get-tuple-element.12), channel_id=1, source_target_pairs={{4,0},{8,4},{12,8},{16,12},{20,16},{24,20},{28,24},{5,1},{9,5},{13... | collective-permute-start | bytes 1622024 | tf_op jit(solution)/shard_map/ppermute | solution.py:18
  21.2 37.6 %collective-permute-start.2 = (bf16[2,2,128,128]{3,2,1,0:T(8,128)(2,1)}, bf16[2,2,128,128]{3,2,1,0:T(8,128)(2,1)S(1)}, u32[]{:S(2)}, u32[]{:S(2)}) collective-permute-start(bf16[2,2,128,128]{3,2,1,0:T(8,128)(2,1)} %get-tuple-element.13), channel_id=1, source_target_pairs={{1,0},{2,1},{3,2},{5,4},{6,5},{7,6},{9,8},{10,9},{11,10},{13,12},{... | collective-permute-start | bytes 393224 | tf_op jit(solution)/shard_map/ppermute | solution.py:18
  58.8 0.6 copy-start.2
  62.0 1.0 %copy-start = (bf16[32,128,128]{2,1,0:T(8,128)(2,1)}, bf16[32,128,128]{2,1,0:T(8,128)(2,1)S(1)}, u32[]{:S(2)}) copy-start(bf16[32,128,128]{2,1,0:T(8,128)(2,1)S(1)} %collective-permute-done.top_ref) | copy-start | bytes 3145732
  75.2 0.8 copy-start.1

commit v2 on v1

v2 whole, which is shorter than its diff:
```python
import functools

import jax
import jax.numpy as jnp
from jax import lax
from jax.experimental import pallas as pl
from jax.experimental.pallas import tpu as pltpu
from jax.sharding import PartitionSpec as P

BF = jnp.bfloat16
F32 = jnp.float32
MIB = 1024 * 1024


def passed_along(x, axis, by):
    devices = lax.axis_size(axis)
    pairs = [(i, i + by) for i in range(devices) if 0 <= i + by < devices]
    return lax.ppermute(x, axis, pairs)


def dot(a, b):
    return lax.dot_general(a, b, (((1,), (0,)), ((), ())), preferred_element_type=F32)


def basis_of(skel_row, rank, interp):
    rows, slots = interp.shape
    live = lax.broadcasted_iota(jnp.int32, (1, slots), 1) < rank
    picked_row = jnp.where(live, skel_row, -1)
    row = lax.broadcasted_iota(jnp.int32, (rows, slots), 0)
    hit = jnp.where(row == picked_row, F32(1.0), F32(0.0))
    free = F32(1.0) - jnp.max(hit, axis=1, keepdims=True)
    live_row = jnp.where(live, F32(1.0), F32(0.0))
    return (hit + interp.astype(F32) * (free * live_row)).astype(BF)


def scaled(turned, conduct):
    return (turned.astype(F32) * -conduct.astype(F32)).astype(BF)


def face_of(left, link, link_t, right):
    upper = jnp.concatenate([left, link], axis=1)
    lower = jnp.concatenate([link_t, right], axis=1)
    return jnp.concatenate([upper, lower], axis=0)


def project(turned, matrices, bases):
    inner = [dot(t, m).astype(BF) for t, m in zip(turned, matrices)]
    return [dot(i, b) for i, b in zip(inner, bases)]


def bases_of(cells, layer, first, rank_ref, skel_ref, interp_ref):
    return [
        basis_of(skel_ref[0, k : k + 1], rank_ref[layer, first + k], interp_ref[0, k])
        for k in range(cells)
    ]


def top_kernel(cells, rank_ref, skel_ref, interp_ref, out_ref):
    first = pl.program_id(0) * cells
    for k in range(cells):
        out_ref[k] = basis_of(skel_ref[0, k : k + 1], rank_ref[0, first + k], interp_ref[0, k])


def pack_masks(size):
    half = size // 2
    row = lax.broadcasted_iota(jnp.int32, (half, size), 0)
    lane = lax.broadcasted_iota(jnp.int32, (half, size), 1)
    ahead = lane - row
    upper = (ahead >= 0) & (ahead < half)
    return upper, ahead == 0, ahead == half


def cells_kernel(cells, rank_ref, skel_ref, interp_ref, matrix_ref, basis_ref, turned_ref, schur_ref, edge_ref, packed_ref):
    layer, chunk = pl.program_id(0), pl.program_id(1)
    slots = skel_ref.shape[-1]
    half = slots // 2
    top = basis_ref.shape[2] // 2
    bases = bases_of(cells, layer, chunk * cells, rank_ref, skel_ref, interp_ref)
    turned = [jnp.transpose(b) for b in bases]
    for k in range(cells):
        basis_ref[0, k] = bases[k]
        turned_ref[0, k] = turned[k]
    schurs = project(turned, [matrix_ref[0, k] for k in range(cells)], bases)
    for k in range(cells):
        schur_ref[0, k] = schurs[k].astype(BF)

    @pl.when(layer == 0)
    def _():
        upper, _, opposite = pack_masks(slots)
        pad = packed_ref.shape[1] - cells * half - cells
        extras = []
        for k in range(cells):
            above = schur_ref[0, k, :half].astype(F32)
            below = schur_ref[0, k, half:].astype(F32)
            packed_ref[chunk, k * half : (k + 1) * half] = jnp.where(upper, above, below).astype(BF)
            extras.append(jnp.sum(jnp.where(opposite, above, F32(0.0)), axis=0, keepdims=True))
        rows = extras + [jnp.zeros((pad, slots), F32)]
        packed_ref[chunk, cells * half :] = jnp.concatenate(rows, axis=0).astype(BF)

    @pl.when(chunk == 0)
    def _():
        edge_ref[layer, 0] = basis_ref[0, 0, :top]
        edge_ref[layer, 1] = schur_ref[0, 0]


def y_faces_kernel(
    cells, rank_ref, skel_ref, interp_ref, coup_ref, basis_ref, turned_ref, schur_ref,
    next_basis_ref, next_turned_ref, next_schur_ref, out_ref,
):
    layer, chunk = pl.program_id(0), pl.program_id(1)
    half = next_turned_ref.shape[-1]
    faces = bases_of(cells, layer, chunk * cells, rank_ref, skel_ref, interp_ref)
    turned = [jnp.transpose(f) for f in faces]
    matrices = []
    for k in range(cells):
        if k + 1 < cells:
            right_top, right_turned = basis_ref[0, k + 1, :half], turned_ref[0, k + 1, :, :half]
            right = schur_ref[0, k + 1]
        else:
            right_top, right_turned = next_basis_ref[0, 0], next_turned_ref[0, 0]
            right = next_schur_ref[0, 0]
        conduct = coup_ref[0, k : k + 1]
        link = dot(scaled(turned_ref[0, k, :, half:], conduct), right_top).astype(BF)
        link_t = dot(scaled(right_turned, conduct), basis_ref[0, k, half:]).astype(BF)
        matrices.append(face_of(schur_ref[0, k], link, link_t, right))
    results = project(turned, matrices, faces)
    for k in range(cells):
        out_ref[0, k] = results[k].astype(BF)


def y_edge_kernel(place, rank_ref, skel_ref, interp_ref, coup_ref, turned_ref, schur_ref, edge_ref, _, out_ref):
    layer = pl.program_id(0)
    row = place % skel_ref.shape[1]
    face = basis_of(skel_ref[0, row : row + 1], rank_ref[layer, place], interp_ref[0, 0])
    link = dot(scaled(turned_ref[0, 0], coup_ref[0, row : row + 1]), edge_ref[0, 0]).astype(BF)
    matrix = face_of(schur_ref[0, 0], link, jnp.transpose(link), edge_ref[0, 1])
    out_ref[0, 0] = project([jnp.transpose(face)], [matrix], [face])[0].astype(BF)


def x_faces_kernel(
    cells, rank_ref, skel_ref, interp_ref, coup_ref, basis_ref, turned_ref, schur_ref,
    next_basis_ref, next_turned_ref, next_schur_ref, out_ref,
):
    layer, chunk = pl.program_id(0), pl.program_id(1)
    faces = bases_of(cells, layer, chunk * cells, rank_ref, skel_ref, interp_ref)
    turned = [jnp.transpose(f) for f in faces]
    matrices = []
    for k in range(cells):
        conduct = coup_ref[0, k : k + 1]
        link = dot(scaled(turned_ref[0, k], conduct), next_basis_ref[0, k]).astype(BF)
        link_t = dot(scaled(next_turned_ref[0, k], conduct), basis_ref[0, k]).astype(BF)
        matrices.append(face_of(schur_ref[0, k], link, link_t, next_schur_ref[0, k]))
    results = project(turned, matrices, faces)
    for k in range(cells):
        out_ref[0, k] = results[k].astype(BF)


def x_part_kernel(
    cells, layer, rank_ref, skel_ref, interp_ref, coup_ref, turned_ref, schur_ref, top_ref,
    part_ref, lower_ref, lower_turned_ref,
):
    half = top_ref.shape[-2]
    faces = bases_of(cells, layer, pl.program_id(0) * cells, rank_ref, skel_ref, interp_ref)
    turned = [jnp.transpose(f) for f in faces]
    for k in range(cells):
        lower_ref[k] = faces[k][half:]
        lower_turned_ref[k] = turned[k][:, half:]
    found = [
        dot(scaled(turned_ref[0, k], coup_ref[0, k : k + 1]), top_ref[k]).astype(BF)
        for k in range(cells)
    ]
    matrices = [
        face_of(schur_ref[0, k], found[k], jnp.transpose(found[k]), jnp.zeros_like(found[k]))
        for k in range(cells)
    ]
    results = project(turned, matrices, faces)
    for k in range(cells):
        part_ref[k] = results[k]


def x_last_kernel(cells, part_ref, lower_ref, lower_turned_ref, packed_ref, _, out_ref):
    slots = part_ref.shape[-1]
    half = slots // 2
    upper, same, opposite = pack_masks(slots)
    one, zero, mid = F32(1.0), F32(0.0), F32(0.5)
    top_scale = jnp.where(same, mid, jnp.where(upper, one, zero))
    low_scale = jnp.where(opposite, mid, jnp.where(upper, zero, one))
    opp_scale = jnp.where(opposite, one, zero)
    extras = packed_ref[0, cells * half :].astype(F32)
    schurs = []
    for k in range(cells):
        packed = packed_ref[0, k * half : (k + 1) * half].astype(F32)
        top = packed * top_scale + extras[k : k + 1] * opp_scale
        low = packed * low_scale
        tri = jnp.concatenate([top, low], axis=0).astype(BF)
        schurs.append(tri + jnp.transpose(tri))
    results = project(
        [lower_turned_ref[k] for k in range(cells)], schurs, [lower_ref[k] for k in range(cells)]
    )
    for k in range(cells):
        out_ref[0, k] = (part_ref[k] + results[k]).astype(BF)


def call(kernel, grid, in_specs, out_specs, out_shape, flops, moved, aliases=None, vmem=24):
    return pl.pallas_call(
        kernel,
        grid=grid,
        in_specs=in_specs,
        out_specs=out_specs,
        out_shape=out_shape,
        input_output_aliases=aliases or {},
        compiler_params=pltpu.CompilerParams(vmem_limit_bytes=vmem * MIB),
        cost_estimate=pl.CostEstimate(flops=flops, bytes_accessed=moved, transcendentals=0),
    )


def body(
    cell_matrix,
    x_coupling,
    y_coupling,
    cell_interp,
    cell_skel,
    cell_rank,
    x_face_interp,
    x_face_skel,
    x_face_rank,
    y_face_interp,
    y_face_skel,
    y_face_rank,
):
    nx, nj, rows, slots = cell_interp.shape
    half = rows // 2
    fslots = x_face_interp.shape[-1]
    cells = 8 if nj % 8 == 0 else nj
    chunks = nj // cells
    unit = 2 * nx * nj * slots * slots * slots
    smem = pl.BlockSpec(memory_space=pltpu.SMEM)
    shape = jax.ShapeDtypeStruct

    def block(*dims):
        return pl.BlockSpec((1, cells) + dims, lambda i, c: (i, c) + (0,) * len(dims))

    top = call(
        functools.partial(top_kernel, cells),
        (chunks,),
        [
            smem,
            pl.BlockSpec((1, cells, slots), lambda c: (0, c, 0)),
            pl.BlockSpec((1, cells, half, slots), lambda c: (0, c, 0, 0)),
        ],
        pl.BlockSpec((cells, half, slots), lambda c: (c, 0, 0)),
        shape((nj, half, slots), BF),
        0,
        4 * nj * half * slots,
        vmem=56,
    )(cell_rank, cell_skel, cell_interp)
    top_in = passed_along(top, "gx", -1)

    pack_rows = cells * slots // 2 + -(-cells // 16) * 16
    basis, turned, schur, edge, packed = call(
        functools.partial(cells_kernel, cells),
        (nx, chunks),
        [smem, block(slots), block(rows, slots), block(rows, rows)],
        [
            block(rows, slots),
            block(slots, rows),
            block(slots, slots),
            pl.BlockSpec((nx, 2, half, slots), lambda i, c: (0, 0, 0, 0)),
            pl.BlockSpec((chunks, pack_rows, slots), lambda i, c: (0, 0, 0)),
        ],
        [
            shape((nx, nj, rows, slots), BF),
            shape((nx, nj, slots, rows), BF),
            shape((nx, nj, slots, slots), BF),
            shape((nx, 2, half, slots), BF),
            shape((chunks, pack_rows, slots), BF),
        ],
        6 * unit,
        nx * nj * (rows * rows + 3 * rows * slots + slots * slots) * 2,
        vmem=56,
    )(cell_rank, cell_skel, cell_interp, cell_matrix)
    edge_in = passed_along(edge, "yz", -1)
    packed_in = passed_along(packed, "gx", -1)

    face_bytes = nj * (4 * rows * slots + 4 * slots * slots) * 2

    def after(c):
        return jnp.minimum((c + 1) * cells, nj - 1)

    y_out = call(
        functools.partial(y_faces_kernel, cells),
        (nx, chunks),
        [
            smem,
            block(fslots),
            block(rows, fslots),
            block(half),
            block(rows, slots),
            block(slots, rows),
            block(slots, slots),
            pl.BlockSpec((1, 1, half, slots), lambda i, c: (i, after(c), 0, 0)),
            pl.BlockSpec((1, 1, slots, half), lambda i, c: (i, after(c), 0, 0)),
            pl.BlockSpec((1, 1, slots, slots), lambda i, c: (i, after(c), 0, 0)),
        ],
        block(fslots, fslots),
        shape((nx, nj, fslots, fslots), BF),
        8 * unit,
        nx * face_bytes,
    )(y_face_rank, y_face_skel, y_face_interp, y_coupling, basis, turned, schur, basis, turned, schur)

    if nx > 1:
        x_out = call(
            functools.partial(x_faces_kernel, cells),
            (nx - 1, chunks),
            [
                smem,
                block(fslots),
                block(rows, fslots),
                block(half),
                pl.BlockSpec((1, cells, half, slots), lambda i, c: (i, c, 1, 0)),
                pl.BlockSpec((1, cells, slots, half), lambda i, c: (i, c, 0, 1)),
                block(slots, slots),
                pl.BlockSpec((1, cells, half, slots), lambda i, c: (i + 1, c, 0, 0)),
                pl.BlockSpec((1, cells, slots, half), lambda i, c: (i + 1, c, 0, 0)),
                pl.BlockSpec((1, cells, slots, slots), lambda i, c: (i + 1, c, 0, 0)),
            ],
            block(fslots, fslots),
            shape((nx, nj, fslots, fslots), BF),
            8 * unit // nx * (nx - 1),
            (nx - 1) * face_bytes,
        )(x_face_rank, x_face_skel, x_face_interp, x_coupling, basis, turned, schur, basis, turned, schur)
    else:
        x_out = jnp.zeros((nx, nj, fslots, fslots), BF)

    last = nx - 1
    tail = nj - 1
    group = tail // cells

    def last_block(*dims):
        return pl.BlockSpec((1, cells) + dims, lambda c: (last, c) + (0,) * len(dims))

    def plain(*dims):
        return pl.BlockSpec((cells,) + dims, lambda c: (c,) + (0,) * len(dims))

    part, lower, lower_turned = call(
        functools.partial(x_part_kernel, cells, last),
        (chunks,),
        [
            smem,
            last_block(fslots),
            last_block(rows, fslots),
            last_block(half),
            pl.BlockSpec((1, cells, slots, half), lambda c: (last, c, 0, 1)),
            last_block(slots, slots),
            plain(half, slots),
        ],
        [plain(fslots, fslots), plain(slots, fslots), plain(fslots, slots)],
        [
            shape((nj, fslots, fslots), F32),
            shape((nj, slots, fslots), BF),
            shape((nj, fslots, slots), BF),
        ],
        8 * unit // nx,
        face_bytes,
    )(x_face_rank, x_face_skel, x_face_interp, x_coupling, turned, schur, top_in)

    y_out = call(
        functools.partial(y_edge_kernel, tail),
        (nx,),
        [
            smem,
            pl.BlockSpec((1, cells, fslots), lambda i: (i, group, 0)),
            pl.BlockSpec((1, 1, rows, fslots), lambda i: (i, tail, 0, 0)),
            pl.BlockSpec((1, cells, half), lambda i: (i, group, 0)),
            pl.BlockSpec((1, 1, slots, half), lambda i: (i, tail, 0, 1)),
            pl.BlockSpec((1, 1, slots, slots), lambda i: (i, tail, 0, 0)),
            pl.BlockSpec((1, 2, half, slots), lambda i: (i, 0, 0, 0)),
            pl.BlockSpec(memory_space=pl.ANY),
        ],
        pl.BlockSpec((1, 1, fslots, fslots), lambda i: (i, tail, 0, 0)),
        shape((nx, nj, fslots, fslots), BF),
        8 * unit // nj,
        nx * face_bytes // nj,
        {7: 0},
    )(y_face_rank, y_face_skel, y_face_interp, y_coupling, turned, schur, edge_in, y_out)

    x_out = call(
        functools.partial(x_last_kernel, cells),
        (chunks,),
        [
            plain(fslots, fslots),
            plain(slots, fslots),
            plain(fslots, slots),
            pl.BlockSpec((1, pack_rows, slots), lambda c: (c, 0, 0)),
            pl.BlockSpec(memory_space=pl.ANY),
        ],
        last_block(fslots, fslots),
        shape((nx, nj, fslots, fslots), BF),
        3 * unit // nx,
        nj * slots * slots * 11,
        {4: 0},
    )(part, lower, lower_turned, packed_in, x_out)
    return (x_out, y_out)


def solution(mesh):
    return jax.shard_map(
        body,
        mesh=mesh,
        in_specs=(
            P("gx", "yz", None, None),
            P("gx", "yz", None),
            P("gx", "yz", None),
            P("gx", "yz", None, None),
            P("gx", "yz", None),
            P("gx", "yz"),
            P("gx", "yz", None, None),
            P("gx", "yz", None),
            P("gx", "yz"),
            P("gx", "yz", None, None),
            P("gx", "yz", None),
            P("gx", "yz"),
        ),
        out_specs=(P("gx", "yz", None, None), P("gx", "yz", None, None)),
        check_vma=False,
    )
```

time: 84.4 us -> 56.5 us (0.67)
  the two profiles are of different devices: /device:TPU:29 before, /device:TPU:31 now
where the time goes in v2:
time: 56.5 us; the launch traced here: 56 us
  Pallas kernels  40.6 us (72%)
  starting transfers between devices  8.61 us (15%)
  local copies, waits for them, and re-layouts  6 us (11%)
  between operations  0.77 us (1%)
    pallas_call x1, Pallas kernels, body(): call(functools.partial(cells_kernel, cells), (nx, chunks), [smem, block(s...  13.1 us
    pallas_call x1, Pallas kernels, body(): call(functools.partial(y_faces_kernel, cells), (nx, chunks), [smem, block...  8.78 us
    ppermute x3, starting transfers between devices, passed_along(): return lax.ppermute(x, axis, pairs)  8.61 us
    unnamed x26, local copies, waits for them, and re-layouts  6 us
    pallas_call x1, Pallas kernels, body(): call(functools.partial(x_faces_kernel, cells), (nx - 1, chunks), [smem, b...  5.34 us
    pallas_call x1, Pallas kernels, body(): call(functools.partial(x_part_kernel, cells, last), (chunks,), [smem, las...  4.73 us
    pallas_call x1, Pallas kernels, body(): call(functools.partial(top_kernel, cells), (chunks,), [smem, pl.BlockSpec...  3.84 us
    pallas_call x1, Pallas kernels, body(): call(functools.partial(x_last_kernel, cells), (chunks,), [plain(fslots, f...  2.69 us
  transfers between devices with their start and end apart: 3, of which 0 were waited for; matrix products, arithmetic and copies ran while one was open for 0% of the time, Pallas kernels for 61%

profile of v2, /device:TPU:31, one launch (start us, length us, event | category | flops | bytes accessed | tf_op | source)
XLA Modules:
  0.0 56.0 jit_solution(6635079556830784171)
XLA Ops:
  0.6 3.8 %shard_map.132 = bf16[32,128,128]{2,1,0:T(8,128)(2,1)} custom-call(s32[2,32]{1,0:T(2,128)} %rank_ref.7, s32[2,32,128]{2,1,0:T(8,128)} %skel_ref.7, bf16[2,32,256,128]{3,2,1,0:T(8,128)(2,1)} %interp_ref.7), custom_call_target="tpu_custom_call" | custom-call | bytes 2097152 | tf_op jit(solution)/shard_map/pallas_call | solution.py:243
  4.5 0.0 copy-start.11
  4.5 2.5 %collective-permute-start = (bf16[32,128,128]{2,1,0:T(8,128)(2,1)}, bf16[32,128,128]{2,1,0:T(8,128)(2,1)S(1)}, u32[]{:S(2)}, u32[]{:S(2)}) collective-permute-start(bf16[32,128,128]{2,1,0:T(8,128)(2,1)} %shard_map.132), channel_id=1, source_target_pairs={{4,0},{8,4},{12,8},{16,12},{20,16},{24,20},{28,24},{5,1},{9,5},{13... | collective-permute-start | bytes 3145736 | tf_op jit(solution)/shard_map/ppermute | solution.py:18
  7.0 13.1 %shard_map.131 = (bf16[2,32,256,128]{3,2,1,0:T(8,128)(2,1)}, bf16[2,32,128,256]{3,2,1,0:T(8,128)(2,1)}, bf16[2,32,128,128]{3,2,1,0:T(8,128)(2,1)}, bf16[2,2,128,128]{3,2,1,0:T(8,128)(2,1)}, bf16[4,528,128]{2,1,0:T(8,128)(2,1)}) custom-call(s32[2,32]{1,0:T(2,128)} %rank_ref.7, s32[2,32,128]{2,1,0:T(8,128)} %skel_ref.7, bf16[2,32,256,128]{3,2,1,0:T(8,128)(2,1)} %interp_ref.7, ...), custom_call_target="tpu_custom_call" | custom-call | flops 1610612736 | bytes 23068672 | tf_op jit(solution)/shard_map/pallas_call | solution.py:260
  20.0 3.0 %collective-permute-start.1 = (bf16[4,528,128]{2,1,0:T(8,128)(2,1)}, bf16[4,528,128]{2,1,0:T(8,128)(2,1)S(1)}, u32[]{:S(2)}, u32[]{:S(2)}) collective-permute-start(bf16[4,528,128]{2,1,0:T(8,128)(2,1)} %get-tuple-element.15), channel_id=1, source_target_pairs={{4,0},{8,4},{12,8},{16,12},{20,16},{24,20},{28,24},{5,1},{9,5},{13... | collective-permute-start | bytes 1622024 | tf_op jit(solution)/shard_map/ppermute | solution.py:18
  23.0 3.2 %collective-permute-start.2 = (bf16[2,2,128,128]{3,2,1,0:T(8,128)(2,1)}, bf16[2,2,128,128]{3,2,1,0:T(8,128)(2,1)S(1)}, u32[]{:S(2)}, u32[]{:S(2)}) collective-permute-start(bf16[2,2,128,128]{3,2,1,0:T(8,128)(2,1)} %get-tuple-element.17), channel_id=1, source_target_pairs={{1,0},{2,1},{3,2},{5,4},{6,5},{7,6},{9,8},{10,9},{11,10},{13,12},{... | collective-permute-start | bytes 393224 | tf_op jit(solution)/shard_map/ppermute | solution.py:18
  26.2 0.0 copy-done.5
  26.2 0.0 copy-done.7
  26.2 0.0 copy-done.9
  26.2 0.0 copy-done.11
  26.2 0.0 copy-start
  26.2 2.2 %copy-done = bf16[2,32,128,256]{3,2,1,0:T(8,128)(2,1)S(1)} copy-done((bf16[2,32,128,256]{3,2,1,0:T(8,128)(2,1)S(1)}, bf16[2,32,128,256]{3,2,1,0:T(8,128)(2,1)}, u32[]{:S(2)}) %copy-start) | copy-done | bytes 4194328
  28.4 1.6 %copy-done.2 = bf16[2,32,128,128]{3,2,1,0:T(8,128)(2,1)S(1)} copy-done((bf16[2,32,128,128]{3,2,1,0:T(8,128)(2,1)S(1)}, bf16[2,32,128,128]{3,2,1,0:T(8,128)(2,1)}, u32[]{:S(2)}) %copy-start.2) | copy-done | bytes 2097176
  30.0 2.2 %copy-done.4 = bf16[2,32,256,128]{3,2,1,0:T(8,128)(2,1)S(1)} copy-done((bf16[2,32,256,128]{3,2,1,0:T(8,128)(2,1)S(1)}, bf16[2,32,256,128]{3,2,1,0:T(8,128)(2,1)}, u32[]{:S(2)}) %copy-start.4) | copy-done | bytes 4194328
  32.2 8.8 %shard_map.136._ = bf16[2,32,128,128]{3,2,1,0:T(8,128)(2,1)} custom-call(s32[2,32]{1,0:T(2,128)S(1)} %copy-done.11, s32[2,32,128]{2,1,0:T(8,128)S(1)} %copy-done.7, bf16[2,32,256,128]{3,2,1,0:T(8,128)(2,1)S(1)} %copy-done.5, bf16[2,32,128]{2,1,0:T(8,128)(2,1)S(1)} %copy-done.9, bf16[2,32,256,128]{3,2,1,0:T(8,128)(2,1)S(1)} %copy-done.4, ...), custom_call_target="tpu_custom_call" | custom-call | flops 2147483648 | bytes 25165824 | tf_op jit(solution)/shard_map/pallas_call | solution.py:290
  41.0 0.0 copy-done.8
  41.0 5.3 %shard_map.134._ = bf16[2,32,128,128]{3,2,1,0:T(8,128)(2,1)} custom-call(s32[2,32]{1,0:T(2,128)S(1)} %copy-done.12, s32[2,32,128]{2,1,0:T(8,128)S(1)} %copy-done.8, bf16[2,32,256,128]{3,2,1,0:T(8,128)(2,1)S(1)} %copy-done.6, bf16[2,32,128]{2,1,0:T(8,128)(2,1)S(1)} %copy-done.10, bf16[2,32,256,128]{3,2,1,0:T(8,128)(2,1)S(1)} %copy-done.4, ...), custom_call_target="tpu_custom_call" | custom-call | flops 1073741824 | bytes 12582912 | tf_op jit(solution)/shard_map/pallas_call | solution.py:312
  46.4 0.0 collective-permute-done.2.edge_ref
  46.4 0.0 copy-done.1
  46.4 2.2 %shard_map.137 = bf16[2,32,128,128]{3,2,1,0:T(8,128)(2,1)} custom-call(s32[2,32]{1,0:T(2,128)S(1)} %copy-done.11, s32[2,32,128]{2,1,0:T(8,128)S(1)} %copy-done.7, bf16[2,32,256,128]{3,2,1,0:T(8,128)(2,1)S(1)} %copy-done.5, bf16[2,32,128]{2,1,0:T(8,128)(2,1)S(1)} %copy-done.9, ...), custom_call_target="tpu_custom_call", output_to_operand_aliasing={{}: (7, {})} | custom-call | flops 67108864 | bytes 786432 | tf_op jit(solution)/shard_map/pallas_call | solution.py:367
  48.6 0.0 collective-permute-done.top_ref
  48.6 4.7 %shard_map.133 = (f32[32,128,128]{2,1,0:T(8,128)S(1)}, bf16[32,128,128]{2,1,0:T(8,128)(2,1)S(1)}, bf16[32,128,128]{2,1,0:T(8,128)(2,1)S(1)}) custom-call(s32[2,32]{1,0:T(2,128)S(1)} %copy-done.12, s32[2,32,128]{2,1,0:T(8,128)S(1)} %copy-done.8, bf16[2,32,256,128]{3,2,1,0:T(8,128)(2,1)S(1)} %copy-done.6, bf16[2,32,128]{2,1,0:T(8,128)(2,1)S(1)} %copy-done.10, ...), custom_call_target="tpu_custom_call" | custom-call | flops 1073741824 | bytes 12582912 | tf_op jit(solution)/shard_map/pallas_call | solution.py:345
  53.3 0.0 collective-permute-done.1.packed_ref
  53.3 2.7 %shard_map.135 = bf16[2,32,128,128]{3,2,1,0:T(8,128)(2,1)} custom-call(f32[32,128,128]{2,1,0:T(8,128)S(1)} %get-tuple-element.12.part_ref, bf16[32,128,128]{2,1,0:T(8,128)(2,1)S(1)} %get-tuple-element.13.lower_ref, bf16[32,128,128]{2,1,0:T(8,128)(2,1)S(1)} %get-tuple-element.14.lower_turned_ref, ...), custom_call_target="tpu_custom_call", output_to_operand_aliasing={{}: (4, {})} | custom-call | flops 402653184 | bytes 5767168 | tf_op jit(solution)/shard_map/pallas_call | solution.py:387
  (15 shorter events, 0.0 us)
Async XLA Ops:
  4.5 21.7 %copy-start.5 = (bf16[2,32,256,128]{3,2,1,0:T(8,128)(2,1)S(1)}, bf16[2,32,256,128]{3,2,1,0:T(8,128)(2,1)}, u32[]{:S(2)}) copy-start(bf16[2,32,256,128]{3,2,1,0:T(8,128)(2,1)} %interp_ref.11) | copy-start | bytes 12582916
  4.5 21.7 %copy-start.7 = (s32[2,32,128]{2,1,0:T(8,128)S(1)}, s32[2,32,128]{2,1,0:T(8,128)}, u32[]{:S(2)}) copy-start(s32[2,32,128]{2,1,0:T(8,128)} %skel_ref.11) | copy-start | bytes 98308
  4.5 21.7 %copy-start.9 = (bf16[2,32,128]{2,1,0:T(8,128)(2,1)S(1)}, bf16[2,32,128]{2,1,0:T(8,128)(2,1)}, u32[]{:S(2)}) copy-start(bf16[2,32,128]{2,1,0:T(8,128)(2,1)} %coup_ref.7) | copy-start | bytes 49156
  4.5 21.7 %copy-start.11 = (s32[2,32]{1,0:T(2,128)S(1)}, s32[2,32]{1,0:T(2,128)}, u32[]{:S(2)}) copy-start(s32[2,32]{1,0:T(2,128)} %rank_ref.11) | copy-start | bytes 772
  4.5 44.1 %collective-permute-start = (bf16[32,128,128]{2,1,0:T(8,128)(2,1)}, bf16[32,128,128]{2,1,0:T(8,128)(2,1)S(1)}, u32[]{:S(2)}, u32[]{:S(2)}) collective-permute-start(bf16[32,128,128]{2,1,0:T(8,128)(2,1)} %shard_map.132), channel_id=1, source_target_pairs={{4,0},{8,4},{12,8},{16,12},{20,16},{24,20},{28,24},{5,1},{9,5},{13... | collective-permute-start | bytes 3145736 | tf_op jit(solution)/shard_map/ppermute | solution.py:18
  20.0 33.3 %collective-permute-start.1 = (bf16[4,528,128]{2,1,0:T(8,128)(2,1)}, bf16[4,528,128]{2,1,0:T(8,128)(2,1)S(1)}, u32[]{:S(2)}, u32[]{:S(2)}) collective-permute-start(bf16[4,528,128]{2,1,0:T(8,128)(2,1)} %get-tuple-element.15), channel_id=1, source_target_pairs={{4,0},{8,4},{12,8},{16,12},{20,16},{24,20},{28,24},{5,1},{9,5},{13... | collective-permute-start | bytes 1622024 | tf_op jit(solution)/shard_map/ppermute | solution.py:18
  23.0 23.3 %collective-permute-start.2 = (bf16[2,2,128,128]{3,2,1,0:T(8,128)(2,1)}, bf16[2,2,128,128]{3,2,1,0:T(8,128)(2,1)S(1)}, u32[]{:S(2)}, u32[]{:S(2)}) collective-permute-start(bf16[2,2,128,128]{3,2,1,0:T(8,128)(2,1)} %get-tuple-element.17), channel_id=1, source_target_pairs={{1,0},{2,1},{3,2},{5,4},{6,5},{7,6},{9,8},{10,9},{11,10},{13,12},{... | collective-permute-start | bytes 393224 | tf_op jit(solution)/shard_map/ppermute | solution.py:18
  26.2 2.2 %copy-start = (bf16[2,32,128,256]{3,2,1,0:T(8,128)(2,1)S(1)}, bf16[2,32,128,256]{3,2,1,0:T(8,128)(2,1)}, u32[]{:S(2)}) copy-start(bf16[2,32,128,256]{3,2,1,0:T(8,128)(2,1)} %get-tuple-element.10.turned_ref.next_turned_ref) | copy-start | bytes 12582916
  28.4 1.6 %copy-start.2 = (bf16[2,32,128,128]{3,2,1,0:T(8,128)(2,1)S(1)}, bf16[2,32,128,128]{3,2,1,0:T(8,128)(2,1)}, u32[]{:S(2)}) copy-start(bf16[2,32,128,128]{3,2,1,0:T(8,128)(2,1)} %get-tuple-element.11.schur_ref.next_schur_ref) | copy-start | bytes 6291460
  30.0 2.2 %copy-start.4 = (bf16[2,32,256,128]{3,2,1,0:T(8,128)(2,1)S(1)}, bf16[2,32,256,128]{3,2,1,0:T(8,128)(2,1)}, u32[]{:S(2)}) copy-start(bf16[2,32,256,128]{3,2,1,0:T(8,128)(2,1)} %get-tuple-element.16.basis_ref.next_basis_ref) | copy-start | bytes 12582916
  32.2 8.8 %copy-start.6 = (bf16[2,32,256,128]{3,2,1,0:T(8,128)(2,1)S(1)}, bf16[2,32,256,128]{3,2,1,0:T(8,128)(2,1)}, u32[]{:S(2)}) copy-start(bf16[2,32,256,128]{3,2,1,0:T(8,128)(2,1)} %interp_ref.9) | copy-start | bytes 12582916
  32.2 8.8 %copy-start.8 = (s32[2,32,128]{2,1,0:T(8,128)S(1)}, s32[2,32,128]{2,1,0:T(8,128)}, u32[]{:S(2)}) copy-start(s32[2,32,128]{2,1,0:T(8,128)} %skel_ref.9) | copy-start | bytes 98308
  32.2 8.8 %copy-start.10 = (bf16[2,32,128]{2,1,0:T(8,128)(2,1)S(1)}, bf16[2,32,128]{2,1,0:T(8,128)(2,1)}, u32[]{:S(2)}) copy-start(bf16[2,32,128]{2,1,0:T(8,128)(2,1)} %coup_ref.5) | copy-start | bytes 49156
  32.2 8.8 %copy-start.12 = (s32[2,32]{1,0:T(2,128)S(1)}, s32[2,32]{1,0:T(2,128)}, u32[]{:S(2)}) copy-start(s32[2,32]{1,0:T(2,128)} %rank_ref.9) | copy-start | bytes 772
  41.0 5.4 %copy-start.1 = (bf16[2,32,128,256]{3,2,1,0:T(8,128)(2,1)S(1)}, bf16[2,32,128,256]{3,2,1,0:T(8,128)(2,1)}, u32[]{:S(2)}) copy-start(bf16[2,32,128,256]{3,2,1,0:T(8,128)(2,1)} %get-tuple-element.10.turned_ref.next_turned_ref) | copy-start | bytes 12582916
  41.0 5.4 %copy-start.3 = (bf16[2,32,128,128]{3,2,1,0:T(8,128)(2,1)S(1)}, bf16[2,32,128,128]{3,2,1,0:T(8,128)(2,1)}, u32[]{:S(2)}) copy-start(bf16[2,32,128,128]{3,2,1,0:T(8,128)(2,1)} %get-tuple-element.11.schur_ref.next_schur_ref) | copy-start | bytes 6291460

commit v3 on v2

v3 whole, which is shorter than its diff:
```python
import functools

import jax
import jax.numpy as jnp
from jax import lax
from jax.experimental import pallas as pl
from jax.experimental.pallas import tpu as pltpu
from jax.sharding import PartitionSpec as P

BF = jnp.bfloat16
F32 = jnp.float32
MIB = 1024 * 1024


def passed_along(x, axis, by):
    devices = lax.axis_size(axis)
    pairs = [(i, i + by) for i in range(devices) if 0 <= i + by < devices]
    return lax.ppermute(x, axis, pairs)


def dot(a, b):
    return lax.dot_general(a, b, (((1,), (0,)), ((), ())), preferred_element_type=F32)


def marks_of(skel_row, rank, interp):
    rows, slots = interp.shape
    live = lax.broadcasted_iota(jnp.int32, (1, slots), 1) < rank
    picked_row = jnp.where(live, skel_row, -1).astype(F32).astype(BF)
    row = lax.broadcasted_iota(jnp.int32, (rows, slots), 0).astype(F32).astype(BF)
    live_row = jnp.where(live, F32(1.0), F32(0.0)).astype(BF)
    hit = jnp.where(row == picked_row, BF(1.0), BF(0.0))
    return hit, interp * live_row


def kept_cleared(hits, interps):
    slots = hits[0].shape[-1]
    ones = jnp.ones((slots, slots), BF)
    counts = [dot(hit, ones).astype(BF) for hit in hits]
    return [h + z * (BF(1.0) - n) for h, z, n in zip(hits, interps, counts)]


def bases_of(cells, layer, first, rank_ref, skel_ref, interp_ref):
    pairs = [
        marks_of(skel_ref[0, k : k + 1], rank_ref[layer, first + k], interp_ref[0, k])
        for k in range(cells)
    ]
    return kept_cleared([p[0] for p in pairs], [p[1] for p in pairs])


def scaled(turned, conduct):
    return turned * -conduct


def face_of(left, link, link_t, right):
    upper = jnp.concatenate([left, link], axis=1)
    lower = jnp.concatenate([link_t, right], axis=1)
    return jnp.concatenate([upper, lower], axis=0)


def project(turned, matrices, bases):
    inner = [dot(t, m).astype(BF) for t, m in zip(turned, matrices)]
    return [dot(i, b) for i, b in zip(inner, bases)]


def top_kernel(cells, rank_ref, skel_ref, interp_ref, out_ref):
    first = pl.program_id(0) * cells
    for k in range(cells):
        hit, interp = marks_of(skel_ref[0, k : k + 1], rank_ref[0, first + k], interp_ref[0, k])
        out_ref[k] = hit + interp * (BF(1.0) - hit)


def pack_masks(size):
    half = size // 2
    row = lax.broadcasted_iota(jnp.int32, (half, size), 0)
    lane = lax.broadcasted_iota(jnp.int32, (half, size), 1)
    ahead = lane - row
    upper = (ahead >= 0) & (ahead < half)
    return upper, ahead == 0, ahead == half


def main_kernel(
    cells, layers, chunks,
    rank_ref, skel_ref, interp_ref, matrix_ref,
    x_rank_ref, x_skel_ref, x_interp_ref, x_coup_ref,
    y_rank_ref, y_skel_ref, y_interp_ref, y_coup_ref,
    x_out_ref, y_out_ref, packed_ref, edge_ref, corner_ref, last_turned_ref, last_schur_ref,
    store_top, store_turned, store_schur,
):
    layer = layers - 1 - pl.program_id(0)
    chunk = chunks - 1 - pl.program_id(1)
    first = chunk * cells
    slots = skel_ref.shape[-1]
    half = slots // 2
    top = interp_ref.shape[2] // 2

    bases = bases_of(cells, layer, first, rank_ref, skel_ref, interp_ref)
    turned = [jnp.transpose(b) for b in bases]
    schurs = project(turned, [matrix_ref[0, k] for k in range(cells)], bases)
    schurs = [s.astype(BF) for s in schurs]

    def faces(out_ref, f_rank_ref, f_skel_ref, f_interp_ref, coup_ref, rights):
        found = bases_of(cells, layer, first, f_rank_ref, f_skel_ref, f_interp_ref)
        found_turned = [jnp.transpose(f) for f in found]
        matrices = []
        for k in range(cells):
            right_top, right_turned, right = rights[k]
            conduct = coup_ref[0, k : k + 1]
            link = dot(scaled(turned[k][:, top:], conduct), right_top).astype(BF)
            link_t = dot(scaled(right_turned, conduct), bases[k][top:]).astype(BF)
            matrices.append(face_of(schurs[k], link, link_t, right))
        results = project(found_turned, matrices, found)
        for k in range(cells):
            out_ref[0, k] = results[k].astype(BF)

    def stored(place):
        return store_top[place], store_turned[place], store_schur[place]

    after = jnp.minimum(first + cells, store_schur.shape[0] - 1)
    rights = [(bases[k][:top], turned[k][:, :top], schurs[k]) for k in range(1, cells)]
    faces(y_out_ref, y_rank_ref, y_skel_ref, y_interp_ref, y_coup_ref, rights + [stored(after)])

    @pl.when(layer < layers - 1)
    def _():
        rights = [stored(first + k) for k in range(cells)]
        faces(x_out_ref, x_rank_ref, x_skel_ref, x_interp_ref, x_coup_ref, rights)

    for k in range(cells):
        store_top[first + k] = bases[k][:top]
        store_turned[first + k] = turned[k][:, :top]
        store_schur[first + k] = schurs[k]

    @pl.when(layer == layers - 1)
    def _():
        for k in range(cells):
            last_turned_ref[k] = turned[k][:, top:]
            last_schur_ref[k] = schurs[k]

    @pl.when(layer == 0)
    def _():
        upper, _, opposite = pack_masks(slots)
        pad = packed_ref.shape[1] - cells * half - cells
        extras = []
        for k in range(cells):
            above = schurs[k][:half].astype(F32)
            below = schurs[k][half:].astype(F32)
            packed_ref[chunk, k * half : (k + 1) * half] = jnp.where(upper, above, below).astype(BF)
            extras.append(jnp.sum(jnp.where(opposite, above, F32(0.0)), axis=0, keepdims=True))
        rows = extras + [jnp.zeros((pad, slots), F32)]
        packed_ref[chunk, cells * half :] = jnp.concatenate(rows, axis=0).astype(BF)

    @pl.when(chunk == 0)
    def _():
        edge_ref[layer, 0] = bases[0][:top]
        edge_ref[layer, 1] = schurs[0]

    @pl.when(chunk == chunks - 1)
    def _():
        corner_ref[layer, 0] = turned[cells - 1][:, top:]
        corner_ref[layer, 1] = schurs[cells - 1]


def y_edge_kernel(layers, place, rank_ref, skel_ref, interp_ref, coup_ref, corner_ref, edge_ref, _, out_ref):
    row = place % skel_ref.shape[1]
    pairs = [
        marks_of(skel_ref[i, row : row + 1], rank_ref[i, place], interp_ref[i, 0])
        for i in range(layers)
    ]
    found = kept_cleared([p[0] for p in pairs], [p[1] for p in pairs])
    matrices = []
    for i in range(layers):
        link = dot(scaled(corner_ref[i, 0], coup_ref[i, row : row + 1]), edge_ref[i, 0]).astype(BF)
        matrices.append(face_of(corner_ref[i, 1], link, jnp.transpose(link), edge_ref[i, 1]))
    results = project([jnp.transpose(f) for f in found], matrices, found)
    for i in range(layers):
        out_ref[i, 0] = results[i].astype(BF)


def x_part_kernel(
    cells, layer, rank_ref, skel_ref, interp_ref, coup_ref, turned_ref, schur_ref, top_ref,
    part_ref, lower_ref, lower_turned_ref,
):
    half = top_ref.shape[-2]
    faces = bases_of(cells, layer, pl.program_id(0) * cells, rank_ref, skel_ref, interp_ref)
    turned = [jnp.transpose(f) for f in faces]
    for k in range(cells):
        lower_ref[k] = faces[k][half:]
        lower_turned_ref[k] = turned[k][:, half:]
    marked = [top_ref[k] for k in range(cells)]
    hits = [jnp.where(m == BF(1.0), BF(1.0), BF(0.0)) for m in marked]
    tops = kept_cleared(hits, marked)
    found = [
        dot(scaled(turned_ref[k], coup_ref[0, k : k + 1]), tops[k]).astype(BF)
        for k in range(cells)
    ]
    matrices = [
        face_of(schur_ref[k], found[k], jnp.transpose(found[k]), jnp.zeros_like(found[k]))
        for k in range(cells)
    ]
    results = project(turned, matrices, faces)
    for k in range(cells):
        part_ref[k] = results[k]


def x_last_kernel(cells, part_ref, lower_ref, lower_turned_ref, packed_ref, _, out_ref):
    slots = part_ref.shape[-1]
    half = slots // 2
    upper, same, opposite = pack_masks(slots)
    one, zero, mid = F32(1.0), F32(0.0), F32(0.5)
    top_scale = jnp.where(same, mid, jnp.where(upper, one, zero))
    low_scale = jnp.where(opposite, mid, jnp.where(upper, zero, one))
    opp_scale = jnp.where(opposite, one, zero)
    extras = packed_ref[0, cells * half :].astype(F32)
    schurs = []
    for k in range(cells):
        packed = packed_ref[0, k * half : (k + 1) * half].astype(F32)
        top = packed * top_scale + extras[k : k + 1] * opp_scale
        low = packed * low_scale
        tri = jnp.concatenate([top, low], axis=0).astype(BF)
        schurs.append(tri + jnp.transpose(tri))
    results = project(
        [lower_turned_ref[k] for k in range(cells)], schurs, [lower_ref[k] for k in range(cells)]
    )
    for k in range(cells):
        out_ref[0, k] = (part_ref[k] + results[k]).astype(BF)


def call(kernel, grid, in_specs, out_specs, out_shape, flops, moved, aliases=None, vmem=24, scratch=()):
    return pl.pallas_call(
        kernel,
        grid=grid,
        in_specs=in_specs,
        out_specs=out_specs,
        out_shape=out_shape,
        scratch_shapes=scratch,
        input_output_aliases=aliases or {},
        compiler_params=pltpu.CompilerParams(vmem_limit_bytes=vmem * MIB),
        cost_estimate=pl.CostEstimate(flops=flops, bytes_accessed=moved, transcendentals=0),
    )


def body(
    cell_matrix,
    x_coupling,
    y_coupling,
    cell_interp,
    cell_skel,
    cell_rank,
    x_face_interp,
    x_face_skel,
    x_face_rank,
    y_face_interp,
    y_face_skel,
    y_face_rank,
):
    nx, nj, rows, slots = cell_interp.shape
    half = rows // 2
    fslots = x_face_interp.shape[-1]
    cells = 8 if nj % 8 == 0 else nj
    chunks = nj // cells
    unit = 2 * nx * nj * slots * slots * slots
    smem = pl.BlockSpec(memory_space=pltpu.SMEM)
    shape = jax.ShapeDtypeStruct

    top = call(
        functools.partial(top_kernel, cells),
        (chunks,),
        [
            smem,
            pl.BlockSpec((1, cells, slots), lambda c: (0, c, 0)),
            pl.BlockSpec((1, cells, half, slots), lambda c: (0, c, 0, 0)),
        ],
        pl.BlockSpec((cells, half, slots), lambda c: (c, 0, 0)),
        shape((nj, half, slots), BF),
        0,
        4 * nj * half * slots,
        vmem=56,
    )(cell_rank, cell_skel, cell_interp)
    top_in = passed_along(top, "gx", -1)

    pack_rows = cells * slots // 2 + -(-cells // 16) * 16
    near = max(nx - 2, 0)

    def down(*dims):
        zeros = (0,) * len(dims)
        return pl.BlockSpec((1, cells) + dims, lambda i, c: (nx - 1 - i, chunks - 1 - c) + zeros)

    def down_x(*dims):
        zeros = (0,) * len(dims)

        def place(i, c):
            return (jnp.minimum(nx - 1 - i, near), jnp.where(i == 0, chunks - 1, chunks - 1 - c)) + zeros

        return pl.BlockSpec((1, cells) + dims, place)

    def whole(*dims):
        return pl.BlockSpec(dims, lambda i, c: (0,) * len(dims))

    def from_last(*dims):
        return pl.BlockSpec(
            (cells,) + dims, lambda i, c: (jnp.where(i == 0, chunks - 1 - c, 0),) + (0,) * len(dims)
        )

    x_out, y_out, packed, edge, corner, last_turned, last_schur = call(
        functools.partial(main_kernel, cells, nx, chunks),
        (nx, chunks),
        [
            smem, down(slots), down(rows, slots), down(rows, rows),
            smem, down_x(fslots), down_x(rows, fslots), down_x(half),
            smem, down(fslots), down(rows, fslots), down(half),
        ],
        [
            down_x(fslots, fslots),
            down(fslots, fslots),
            whole(chunks, pack_rows, slots),
            whole(nx, 2, half, slots),
            whole(nx, 2, slots, half),
            from_last(slots, half),
            from_last(slots, slots),
        ],
        [
            shape((nx, nj, fslots, fslots), BF),
            shape((nx, nj, fslots, fslots), BF),
            shape((chunks, pack_rows, slots), BF),
            shape((nx, 2, half, slots), BF),
            shape((nx, 2, slots, half), BF),
            shape((nj, slots, half), BF),
            shape((nj, slots, slots), BF),
        ],
        20 * unit,
        nx * nj * (rows * rows + 3 * rows * slots + 3 * slots * slots) * 2,
        vmem=56,
        scratch=[
            pltpu.VMEM((nj, half, slots), BF),
            pltpu.VMEM((nj, slots, half), BF),
            pltpu.VMEM((nj, slots, slots), BF),
        ],
    )(
        cell_rank, cell_skel, cell_interp, cell_matrix,
        x_face_rank, x_face_skel, x_face_interp, x_coupling,
        y_face_rank, y_face_skel, y_face_interp, y_coupling,
    )
    edge_in = passed_along(edge, "yz", -1)
    packed_in = passed_along(packed, "gx", -1)
    face_bytes = nj * (4 * rows * slots + 4 * slots * slots) * 2

    last = nx - 1
    tail = nj - 1
    group = tail // cells

    def last_block(*dims):
        return pl.BlockSpec((1, cells) + dims, lambda c: (last, c) + (0,) * len(dims))

    def plain(*dims):
        return pl.BlockSpec((cells,) + dims, lambda c: (c,) + (0,) * len(dims))

    part, lower, lower_turned = call(
        functools.partial(x_part_kernel, cells, last),
        (chunks,),
        [
            smem,
            last_block(fslots),
            last_block(rows, fslots),
            last_block(half),
            plain(slots, half),
            plain(slots, slots),
            plain(half, slots),
        ],
        [plain(fslots, fslots), plain(slots, fslots), plain(fslots, slots)],
        [
            shape((nj, fslots, fslots), F32),
            shape((nj, slots, fslots), BF),
            shape((nj, fslots, slots), BF),
        ],
        8 * unit // nx,
        face_bytes,
    )(x_face_rank, x_face_skel, x_face_interp, x_coupling, last_turned, last_schur, top_in)

    y_out = call(
        functools.partial(y_edge_kernel, nx, tail),
        (1,),
        [
            smem,
            pl.BlockSpec((nx, cells, fslots), lambda i: (0, group, 0)),
            pl.BlockSpec((nx, 1, rows, fslots), lambda i: (0, tail, 0, 0)),
            pl.BlockSpec((nx, cells, half), lambda i: (0, group, 0)),
            pl.BlockSpec((nx, 2, slots, half), lambda i: (0, 0, 0, 0)),
            pl.BlockSpec((nx, 2, half, slots), lambda i: (0, 0, 0, 0)),
            pl.BlockSpec(memory_space=pl.ANY),
        ],
        pl.BlockSpec((nx, 1, fslots, fslots), lambda i: (0, tail, 0, 0)),
        shape((nx, nj, fslots, fslots), BF),
        8 * unit // nj,
        nx * face_bytes // nj,
        {6: 0},
    )(y_face_rank, y_face_skel, y_face_interp, y_coupling, corner, edge_in, y_out)

    x_out = call(
        functools.partial(x_last_kernel, cells),
        (chunks,),
        [
            plain(fslots, fslots),
            plain(slots, fslots),
            plain(fslots, slots),
            pl.BlockSpec((1, pack_rows, slots), lambda c: (c, 0, 0)),
            pl.BlockSpec(memory_space=pl.ANY),
        ],
        last_block(fslots, fslots),
        shape((nx, nj, fslots, fslots), BF),
        3 * unit // nx,
        nj * slots * slots * 11,
        {4: 0},
    )(part, lower, lower_turned, packed_in, x_out)
    return (x_out, y_out)


def solution(mesh):
    return jax.shard_map(
        body,
        mesh=mesh,
        in_specs=(
            P("gx", "yz", None, None),
            P("gx", "yz", None),
            P("gx", "yz", None),
            P("gx", "yz", None, None),
            P("gx", "yz", None),
            P("gx", "yz"),
            P("gx", "yz", None, None),
            P("gx", "yz", None),
            P("gx", "yz"),
            P("gx", "yz", None, None),
            P("gx", "yz", None),
            P("gx", "yz"),
        ),
        out_specs=(P("gx", "yz", None, None), P("gx", "yz", None, None)),
        check_vma=False,
    )
```

time: 56.5 us -> 48.6 us (0.86)
  the two profiles are of different devices: /device:TPU:31 before, /device:TPU:9 now
where the time goes in v3:
time: 48.6 us; the launch traced here: 48.2 us
  Pallas kernels  32.8 us (67%)
  starting transfers between devices  7.95 us (16%)
  waiting for transfers between devices  4.74 us (10%)
  local copies, waits for them, and re-layouts  1.98 us (4%)
  between operations  0.73 us (2%)
    pallas_call x1, Pallas kernels, body(): call(functools.partial(main_kernel, cells, nx, chunks), (nx, chunks), [sm...  19.7 us
    ppermute x3, starting transfers between devices, passed_along(): return lax.ppermute(x, axis, pairs)  7.95 us
    pallas_call x1, Pallas kernels, body(): call(functools.partial(x_part_kernel, cells, last), (chunks,), [smem, las...  4.98 us
    ppermute x3, waiting for transfers between devices, passed_along(): return lax.ppermute(x, axis, pairs)  4.74 us
    pallas_call x1, Pallas kernels, body(): call(functools.partial(top_kernel, cells), (chunks,), [smem, pl.BlockSpec...  3.67 us
    pallas_call x1, Pallas kernels, body(): call(functools.partial(x_last_kernel, cells), (chunks,), [plain(fslots, f...  2.69 us
    unnamed x22, local copies, waits for them, and re-layouts  1.98 us
    pallas_call x1, Pallas kernels, body(): call(functools.partial(y_edge_kernel, nx, tail), (1,), [smem, pl.BlockSpe...  1.73 us
  transfers between devices with their start and end apart: 3, of which 1 were waited for; matrix products, arithmetic and copies ran while one was open for 0% of the time, Pallas kernels for 55%

profile of v3, /device:TPU:9, one launch (start us, length us, event | category | flops | bytes accessed | tf_op | source)
XLA Modules:
  0.0 48.2 jit_solution(10498325902073503324)
XLA Ops:
  0.6 3.7 %shard_map.132 = bf16[32,128,128]{2,1,0:T(8,128)(2,1)} custom-call(s32[2,32]{1,0:T(2,128)} %rank_ref.5, s32[2,32,128]{2,1,0:T(8,128)} %skel_ref.5, bf16[2,32,256,128]{3,2,1,0:T(8,128)(2,1)} %interp_ref.5), custom_call_target="tpu_custom_call" | custom-call | bytes 2097152 | tf_op jit(solution)/shard_map/pallas_call | solution.py:264
  4.3 3.2 %collective-permute-start = (bf16[32,128,128]{2,1,0:T(8,128)(2,1)}, bf16[32,128,128]{2,1,0:T(8,128)(2,1)S(1)}, u32[]{:S(2)}, u32[]{:S(2)}) collective-permute-start(bf16[32,128,128]{2,1,0:T(8,128)(2,1)} %shard_map.132), channel_id=1, source_target_pairs={{4,0},{8,4},{12,8},{16,12},{20,16},{24,20},{28,24},{5,1},{9,5},{13... | collective-permute-start | bytes 3145736 | tf_op jit(solution)/shard_map/ppermute | solution.py:18
  7.5 0.0 copy-start
  7.5 19.7 %shard_map.131 = (bf16[2,32,128,128]{3,2,1,0:T(8,128)(2,1)}, bf16[2,32,128,128]{3,2,1,0:T(8,128)(2,1)}, bf16[4,528,128]{2,1,0:T(8,128)(2,1)}, bf16[2,2,128,128]{...) custom-call(s32[2,32]{1,0:T(2,128)} %rank_ref.5, ...), custom_call_target="tpu_custom_call" | custom-call | flops 5368709120 | bytes 27262976 | tf_op jit(solution)/shard_map/pallas_call | solution.py:303
  27.2 1.9 %collective-permute-start.1 = (bf16[4,528,128]{2,1,0:T(8,128)(2,1)}, bf16[4,528,128]{2,1,0:T(8,128)(2,1)S(1)}, u32[]{:S(2)}, u32[]{:S(2)}) collective-permute-start(bf16[4,528,128]{2,1,0:T(8,128)(2,1)} %get-tuple-element.17), channel_id=1, source_target_pairs={{4,0},{8,4},{12,8},{16,12},{20,16},{24,20},{28,24},{5,1},{9,5},{13... | collective-permute-start | bytes 1622024 | tf_op jit(solution)/shard_map/ppermute | solution.py:18
  29.1 2.9 %collective-permute-start.2 = (bf16[2,2,128,128]{3,2,1,0:T(8,128)(2,1)}, bf16[2,2,128,128]{3,2,1,0:T(8,128)(2,1)S(1)}, u32[]{:S(2)}, u32[]{:S(2)}) collective-permute-start(bf16[2,2,128,128]{3,2,1,0:T(8,128)(2,1)} %get-tuple-element.20), channel_id=1, source_target_pairs={{1,0},{2,1},{3,2},{5,4},{6,5},{7,6},{9,8},{10,9},{11,10},{13,12},{... | collective-permute-start | bytes 393224 | tf_op jit(solution)/shard_map/ppermute | solution.py:18
  32.0 4.7 %collective-permute-done.2.edge_ref = bf16[2,2,128,128]{3,2,1,0:T(8,128)(2,1)S(1)} collective-permute-done((bf16[2,2,128,128]{3,2,1,0:T(8,128)(2,1)}, bf16[2,2,128,128]{3,2,1,0:T(8,128)(2,1)S(1)}, u32[]{:S(2)}, u32[]{:S(2)}) %collective-permute-start.2) | collective-permute-done | bytes 131104 | tf_op jit(solution)/shard_map/ppermute | solution.py:18
  36.8 0.0 copy-done.5
  36.8 0.0 copy-done.7
  36.8 0.0 copy-done.9
  36.8 0.0 copy-done
  36.8 0.0 copy-start.4
  36.8 0.9 %copy-done.4 = bf16[2,2,128,128]{3,2,1,0:T(8,128)(2,1)S(1)} copy-done((bf16[2,2,128,128]{3,2,1,0:T(8,128)(2,1)S(1)}, bf16[2,2,128,128]{3,2,1,0:T(8,128)(2,1)}, u32[]{:S(2)}) %copy-start.4) | copy-done | bytes 131096
  37.7 0.0 copy-start.8
  37.7 0.0 copy-start.10
  37.7 1.7 %shard_map.135 = bf16[2,32,128,128]{3,2,1,0:T(8,128)(2,1)} custom-call(s32[2,32]{1,0:T(2,128)S(1)} %copy-done.9, s32[2,32,128]{2,1,0:T(8,128)S(1)} %copy-done.5, bf16[2,32,256,128]{3,2,1,0:T(8,128)(2,1)S(1)} %copy-done, bf16[2,32,128]{2,1,0:T(8,128)(2,1)S(1)} %copy-done.7, bf16[2,2,128,128]{3,2,1,0:T(8,128)(2,1)S(1)} %copy-done.4, ...), custom_call_target="tpu_custom_call", output_to_operand_aliasing={{}: (6, {})} | custom-call | flops 67108864 | bytes 786432 | tf_op jit(solution)/shard_map/pallas_call | solution.py:378
  39.5 0.0 collective-permute-done.top_ref
  39.5 0.4 copy-done.1
  39.9 0.3 copy-done.2
  40.2 0.3 copy-done.3
  40.5 0.0 copy-done.6
  40.5 5.0 %shard_map.133 = (f32[32,128,128]{2,1,0:T(8,128)S(1)}, bf16[32,128,128]{2,1,0:T(8,128)(2,1)S(1)}, bf16[32,128,128]{2,1,0:T(8,128)(2,1)S(1)}) custom-call(s32[2,32]{1,0:T(2,128)S(1)} %copy-done.10, s32[2,32,128]{2,1,0:T(8,128)S(1)} %copy-done.6, bf16[2,32,256,128]{3,2,1,0:T(8,128)(2,1)S(1)} %copy-done.1, bf16[2,32,128]{2,1,0:T(8,128)(2,1)S(1)} %copy-done.8, ...), custom_call_target="tpu_custom_call" | custom-call | flops 1073741824 | bytes 12582912 | tf_op jit(solution)/shard_map/pallas_call | solution.py:356
  45.5 0.0 collective-permute-done.1.packed_ref
  45.5 2.7 %shard_map.134 = bf16[2,32,128,128]{3,2,1,0:T(8,128)(2,1)} custom-call(f32[32,128,128]{2,1,0:T(8,128)S(1)} %get-tuple-element.14.part_ref, bf16[32,128,128]{2,1,0:T(8,128)(2,1)S(1)} %get-tuple-element.15.lower_ref, bf16[32,128,128]{2,1,0:T(8,128)(2,1)S(1)} %get-tuple-element.16.lower_turned_ref, ...), custom_call_target="tpu_custom_call", output_to_operand_aliasing={{}: (4, {})} | custom-call | flops 402653184 | bytes 5767168 | tf_op jit(solution)/shard_map/pallas_call | solution.py:397
  (9 shorter events, 0.0 us)
Async XLA Ops:
  4.3 32.5 %copy-start.5 = (s32[2,32,128]{2,1,0:T(8,128)S(1)}, s32[2,32,128]{2,1,0:T(8,128)}, u32[]{:S(2)}) copy-start(s32[2,32,128]{2,1,0:T(8,128)} %skel_ref.7) | copy-start | bytes 98308
  4.3 32.5 %copy-start.7 = (bf16[2,32,128]{2,1,0:T(8,128)(2,1)S(1)}, bf16[2,32,128]{2,1,0:T(8,128)(2,1)}, u32[]{:S(2)}) copy-start(bf16[2,32,128]{2,1,0:T(8,128)(2,1)} %coup_ref.3) | copy-start | bytes 49156
  4.3 32.5 %copy-start.9 = (s32[2,32]{1,0:T(2,128)S(1)}, s32[2,32]{1,0:T(2,128)}, u32[]{:S(2)}) copy-start(s32[2,32]{1,0:T(2,128)} %rank_ref.7) | copy-start | bytes 772
  4.3 35.1 %collective-permute-start = (bf16[32,128,128]{2,1,0:T(8,128)(2,1)}, bf16[32,128,128]{2,1,0:T(8,128)(2,1)S(1)}, u32[]{:S(2)}, u32[]{:S(2)}) collective-permute-start(bf16[32,128,128]{2,1,0:T(8,128)(2,1)} %shard_map.132), channel_id=1, source_target_pairs={{4,0},{8,4},{12,8},{16,12},{20,16},{24,20},{28,24},{5,1},{9,5},{13... | collective-permute-start | bytes 3145736 | tf_op jit(solution)/shard_map/ppermute | solution.py:18
  7.5 29.3 %copy-start = (bf16[2,32,256,128]{3,2,1,0:T(8,128)(2,1)S(1)}, bf16[2,32,256,128]{3,2,1,0:T(8,128)(2,1)}, u32[]{:S(2)}) copy-start(bf16[2,32,256,128]{3,2,1,0:T(8,128)(2,1)} %interp_ref.7) | copy-start | bytes 12582916
  27.2 18.3 %collective-permute-start.1 = (bf16[4,528,128]{2,1,0:T(8,128)(2,1)}, bf16[4,528,128]{2,1,0:T(8,128)(2,1)S(1)}, u32[]{:S(2)}, u32[]{:S(2)}) collective-permute-start(bf16[4,528,128]{2,1,0:T(8,128)(2,1)} %get-tuple-element.17), channel_id=1, source_target_pairs={{4,0},{8,4},{12,8},{16,12},{20,16},{24,20},{28,24},{5,1},{9,5},{13... | collective-permute-start | bytes 1622024 | tf_op jit(solution)/shard_map/ppermute | solution.py:18
  29.1 7.6 %collective-permute-start.2 = (bf16[2,2,128,128]{3,2,1,0:T(8,128)(2,1)}, bf16[2,2,128,128]{3,2,1,0:T(8,128)(2,1)S(1)}, u32[]{:S(2)}, u32[]{:S(2)}) collective-permute-start(bf16[2,2,128,128]{3,2,1,0:T(8,128)(2,1)} %get-tuple-element.20), channel_id=1, source_target_pairs={{1,0},{2,1},{3,2},{5,4},{6,5},{7,6},{9,8},{10,9},{11,10},{13,12},{... | collective-permute-start | bytes 393224 | tf_op jit(solution)/shard_map/ppermute | solution.py:18
  36.8 0.9 %copy-start.4 = (bf16[2,2,128,128]{3,2,1,0:T(8,128)(2,1)S(1)}, bf16[2,2,128,128]{3,2,1,0:T(8,128)(2,1)}, u32[]{:S(2)}) copy-start(bf16[2,2,128,128]{3,2,1,0:T(8,128)(2,1)} %get-tuple-element.19.corner_ref) | copy-start | bytes 393220
  37.7 2.2 %copy-start.1 = (bf16[2,32,256,128]{3,2,1,0:T(8,128)(2,1)S(1)}, bf16[2,32,256,128]{3,2,1,0:T(8,128)(2,1)}, u32[]{:S(2)}) copy-start(bf16[2,32,256,128]{3,2,1,0:T(8,128)(2,1)} %interp_ref.6) | copy-start | bytes 12582916
  37.7 2.5 %copy-start.2 = (bf16[32,128,128]{2,1,0:T(8,128)(2,1)S(1)}, bf16[32,128,128]{2,1,0:T(8,128)(2,1)}, u32[]{:S(2)}) copy-start(bf16[32,128,128]{2,1,0:T(8,128)(2,1)} %get-tuple-element.12.turned_ref) | copy-start | bytes 3145732
  37.7 2.8 %copy-start.3 = (bf16[32,128,128]{2,1,0:T(8,128)(2,1)S(1)}, bf16[32,128,128]{2,1,0:T(8,128)(2,1)}, u32[]{:S(2)}) copy-start(bf16[32,128,128]{2,1,0:T(8,128)(2,1)} %get-tuple-element.13.schur_ref) | copy-start | bytes 3145732
  37.7 2.8 %copy-start.6 = (s32[2,32,128]{2,1,0:T(8,128)S(1)}, s32[2,32,128]{2,1,0:T(8,128)}, u32[]{:S(2)}) copy-start(s32[2,32,128]{2,1,0:T(8,128)} %skel_ref.6) | copy-start | bytes 98308
  37.7 2.8 %copy-start.8 = (bf16[2,32,128]{2,1,0:T(8,128)(2,1)S(1)}, bf16[2,32,128]{2,1,0:T(8,128)(2,1)}, u32[]{:S(2)}) copy-start(bf16[2,32,128]{2,1,0:T(8,128)(2,1)} %coup_ref.2) | copy-start | bytes 49156
  37.7 2.8 %copy-start.10 = (s32[2,32]{1,0:T(2,128)S(1)}, s32[2,32]{1,0:T(2,128)}, u32[]{:S(2)}) copy-start(s32[2,32]{1,0:T(2,128)} %rank_ref.6) | copy-start | bytes 772

commit v4 on v3

--- a/solution.py
+++ b/solution.py
@@ -62,11 +62,29 @@
     return [dot(i, b) for i, b in zip(inner, bases)]
 
 
-def top_kernel(cells, rank_ref, skel_ref, interp_ref, out_ref):
-    first = pl.program_id(0) * cells
-    for k in range(cells):
-        hit, interp = marks_of(skel_ref[0, k : k + 1], rank_ref[0, first + k], interp_ref[0, k])
-        out_ref[k] = hit + interp * (BF(1.0) - hit)
+def top_kernel(cells, rank_hbm, skel_hbm, interp_hbm, out_ref, rank_ref, skel_ref, held, small_sems, sems):
+    count, half, _ = out_ref.shape
+    small = [
+        pltpu.make_async_copy(rank_hbm, rank_ref, small_sems.at[0]),
+        pltpu.make_async_copy(skel_hbm.at[0], skel_ref, small_sems.at[1]),
+    ]
+    copies = []
+    for c in range(count // cells):
+        group = pl.ds(c * cells, cells)
+        copies.append(
+            pltpu.make_async_copy(
+                interp_hbm.at[0, group, pl.ds(0, half)], held.at[group], sems.at[c]
+            )
+        )
+    for copy in small + copies:
+        copy.start()
+    for copy in small:
+        copy.wait()
+    for c in range(count // cells):
+        copies[c].wait()
+        for k in range(c * cells, (c + 1) * cells):
+            hit, interp = marks_of(skel_ref[k : k + 1], rank_ref[0, k], held[k])
+            out_ref[k] = hit + interp * (BF(1.0) - hit)
 
 
 def pack_masks(size):
@@ -201,27 +219,39 @@
         part_ref[k] = results[k]
 
 
-def x_last_kernel(cells, part_ref, lower_ref, lower_turned_ref, packed_ref, _, out_ref):
-    slots = part_ref.shape[-1]
+def x_last_kernel(
+    cells, layer, part_ref, lower_ref, lower_turned_ref, packed_ref, _, out_ref, held, sems
+):
+    count, _, slots = part_ref.shape
     half = slots // 2
     upper, same, opposite = pack_masks(slots)
     one, zero, mid = F32(1.0), F32(0.0), F32(0.5)
     top_scale = jnp.where(same, mid, jnp.where(upper, one, zero))
     low_scale = jnp.where(opposite, mid, jnp.where(upper, zero, one))
     opp_scale = jnp.where(opposite, one, zero)
-    extras = packed_ref[0, cells * half :].astype(F32)
-    schurs = []
-    for k in range(cells):
-        packed = packed_ref[0, k * half : (k + 1) * half].astype(F32)
-        top = packed * top_scale + extras[k : k + 1] * opp_scale
-        low = packed * low_scale
-        tri = jnp.concatenate([top, low], axis=0).astype(BF)
-        schurs.append(tri + jnp.transpose(tri))
-    results = project(
-        [lower_turned_ref[k] for k in range(cells)], schurs, [lower_ref[k] for k in range(cells)]
-    )
-    for k in range(cells):
-        out_ref[0, k] = (part_ref[k] + results[k]).astype(BF)
+    copies = []
+    for c in range(count // cells):
+        extras = packed_ref[c, cells * half :].astype(F32)
+        places = range(c * cells, (c + 1) * cells)
+        schurs = []
+        for k in range(cells):
+            packed = packed_ref[c, k * half : (k + 1) * half].astype(F32)
+            top = packed * top_scale + extras[k : k + 1] * opp_scale
+            low = packed * low_scale
+            tri = jnp.concatenate([top, low], axis=0).astype(BF)
+            schurs.append(tri + jnp.transpose(tri))
+        results = project(
+            [lower_turned_ref[k] for k in places], schurs, [lower_ref[k] for k in places]
+        )
+        for k, result in zip(places, results):
+            held[k] = (part_ref[k] + result).astype(BF)
+        group = pl.ds(c * cells, cells)
+        copies.append(
+            pltpu.make_async_copy(held.at[group], out_ref.at[layer, group], sems.at[c])
+        )
+        copies[c].start()
+    for copy in copies:
+        copy.wait()
 
 
 def call(kernel, grid, in_specs, out_specs, out_shape, flops, moved, aliases=None, vmem=24, scratch=()):
@@ -236,6 +266,10 @@
         compiler_params=pltpu.CompilerParams(vmem_limit_bytes=vmem * MIB),
         cost_estimate=pl.CostEstimate(flops=flops, bytes_accessed=moved, transcendentals=0),
     )
+
+
+def in_hbm(x):
+    return pltpu.with_memory_space_constraint(x, pltpu.HBM)
 
 
 def body(
@@ -261,20 +295,25 @@
     smem = pl.BlockSpec(memory_space=pltpu.SMEM)
     shape = jax.ShapeDtypeStruct
 
+    hbm = pl.BlockSpec(memory_space=pltpu.HBM)
+    vmem = pl.BlockSpec(memory_space=pltpu.VMEM)
     top = call(
         functools.partial(top_kernel, cells),
-        (chunks,),
-        [
-            smem,
-            pl.BlockSpec((1, cells, slots), lambda c: (0, c, 0)),
-            pl.BlockSpec((1, cells, half, slots), lambda c: (0, c, 0, 0)),
-        ],
-        pl.BlockSpec((cells, half, slots), lambda c: (c, 0, 0)),
+        (),
+        [hbm, hbm, hbm],
+        vmem,
         shape((nj, half, slots), BF),
         0,
         4 * nj * half * slots,
-        vmem=56,
-    )(cell_rank, cell_skel, cell_interp)
+        vmem=8,
+        scratch=[
+            pltpu.SMEM((nx, nj), jnp.int32),
+            pltpu.VMEM((nj, slots), jnp.int32),
+            pltpu.VMEM((nj, half, slots), BF),
+            pltpu.SemaphoreType.DMA((2,)),
+            pltpu.SemaphoreType.DMA((chunks,)),
+        ],
+    )(in_hbm(cell_rank), in_hbm(cell_skel), in_hbm(cell_interp))
     top_in = passed_along(top, "gx", -1)
 
     pack_rows = cells * slots // 2 + -(-cells // 16) * 16
@@ -328,16 +367,16 @@
         ],
         20 * unit,
         nx * nj * (rows * rows + 3 * rows * slots + 3 * slots * slots) * 2,
-        vmem=56,
+        vmem=32,
         scratch=[
             pltpu.VMEM((nj, half, slots), BF),
             pltpu.VMEM((nj, slots, half), BF),
             pltpu.VMEM((nj, slots, slots), BF),
         ],
     )(
-        cell_rank, cell_skel, cell_interp, cell_matrix,
-        x_face_rank, x_face_skel, x_face_interp, x_coupling,
-        y_face_rank, y_face_skel, y_face_interp, y_coupling,
+        cell_rank, in_hbm(cell_skel), in_hbm(cell_interp), in_hbm(cell_matrix),
+        x_face_rank, in_hbm(x_face_skel), in_hbm(x_face_interp), in_hbm(x_coupling),
+        y_face_rank, in_hbm(y_face_skel), in_hbm(y_face_interp), in_hbm(y_coupling),
     )
     edge_in = passed_along(edge, "yz", -1)
     packed_in = passed_along(packed, "gx", -1)
@@ -375,6 +414,7 @@
         face_bytes,
     )(x_face_rank, x_face_skel, x_face_interp, x_coupling, last_turned, last_schur, top_in)
 
+    edge_in, part = lax.optimization_barrier((edge_in, part))
     y_out = call(
         functools.partial(y_edge_kernel, nx, tail),
         (1,),
@@ -392,23 +432,18 @@
         8 * unit // nj,
         nx * face_bytes // nj,
         {6: 0},
-    )(y_face_rank, y_face_skel, y_face_interp, y_coupling, corner, edge_in, y_out)
+    )(y_face_rank, y_face_skel, in_hbm(y_face_interp), y_coupling, corner, edge_in, y_out)
 
     x_out = call(
-        functools.partial(x_last_kernel, cells),
-        (chunks,),
-        [
-            plain(fslots, fslots),
-            plain(slots, fslots),
-            plain(fslots, slots),
-            pl.BlockSpec((1, pack_rows, slots), lambda c: (c, 0, 0)),
-            pl.BlockSpec(memory_space=pl.ANY),
-        ],
-        last_block(fslots, fslots),
+        functools.partial(x_last_kernel, cells, last),
+        (),
+        [vmem, vmem, vmem, vmem, hbm],
+        hbm,
         shape((nx, nj, fslots, fslots), BF),
         3 * unit // nx,
         nj * slots * slots * 11,
         {4: 0},
+        scratch=[pltpu.VMEM((nj, fslots, fslots), BF), pltpu.SemaphoreType.DMA((chunks,))],
     )(part, lower, lower_turned, packed_in, x_out)
     return (x_out, y_out)
 

time: 48.6 us -> 44.1 us (0.907)
  the two profiles are of different devices: /device:TPU:9 before, /device:TPU:0 now
where the time goes in v4:
time: 44.1 us; the launch traced here: 43.7 us
  Pallas kernels  29.2 us (66%)
  waiting for transfers between devices  9.75 us (22%)
  starting transfers between devices  3.87 us (9%)
  between operations  0.79 us (2%)
    pallas_call x1, Pallas kernels, body(): call(functools.partial(main_kernel, cells, nx, chunks), (nx, chunks), [sm...  18.7 us
    ppermute x3, waiting for transfers between devices, passed_along(): return lax.ppermute(x, axis, pairs)  9.75 us
    pallas_call x1, Pallas kernels, body(): call(functools.partial(x_part_kernel, cells, last), (chunks,), [smem, las...  5.03 us
    ppermute x3, starting transfers between devices, passed_along(): return lax.ppermute(x, axis, pairs)  3.87 us
    pallas_call x1, Pallas kernels, body(): call(functools.partial(y_edge_kernel, nx, tail), (1,), [smem, pl.BlockSpe...  2.11 us
    pallas_call x1, Pallas kernels, body(): call(functools.partial(x_last_kernel, cells, last), (), [vmem, vmem, vmem...  1.84 us
    pallas_call x1, Pallas kernels, body(): call(functools.partial(top_kernel, cells), (), [hbm, hbm, hbm], vmem, sha...  1.55 us
  transfers between devices with their start and end apart: 3, of which 2 were waited for; matrix products, arithmetic and copies ran while one was open for 0% of the time, Pallas kernels for 59%

profile of v4, /device:TPU:0, one launch (start us, length us, event | category | flops | bytes accessed | tf_op | source)
XLA Modules:
  0.0 43.7 jit_solution(4662345337803317026)
XLA Ops:
  0.6 0.0 copy-start.6
  0.6 0.0 copy-start.5
  0.7 0.0 copy-start.7
  0.7 1.6 %shard_map.132 = bf16[32,128,128]{2,1,0:T(8,128)(2,1)S(1)} custom-call(s32[2,32]{1,0:T(2,128)} %rank_hbm.1, s32[2,32,128]{2,1,0:T(8,128)} %skel_hbm.1, bf16[2,32,256,128]{3,2,1,0:T(8,128)(2,1)} %interp_hbm.1), custom_call_target="tpu_custom_call" | custom-call | bytes 2097152 | tf_op jit(solution)/shard_map/pallas_call | solution.py:300
  2.2 0.0 copy-start.1
  2.2 0.0 copy-start.3
  2.2 1.3 %collective-permute-start.1 = (bf16[32,128,128]{2,1,0:T(8,128)(2,1)S(1)}, bf16[32,128,128]{2,1,0:T(8,128)(2,1)S(1)}, u32[]{:S(2)}, u32[]{:S(2)}) collective-permute-start(bf16[32,128,128]{2,1,0:T(8,128)(2,1)S(1)} %shard_map.132), channel_id=1, source_target_pairs={{4,0},{8,4},{12,8},{16,12},{20,16},{24,20},{28,24},{5,1},{9,5},{13... | collective-permute-start | bytes 3145736 | tf_op jit(solution)/shard_map/ppermute | solution.py:18
  3.5 0.0 copy-done.6
  3.6 0.0 copy-done.5
  3.6 0.0 copy-done.7
  3.6 0.0 copy-start
  3.6 18.7 %shard_map.131 = (bf16[2,32,128,128]{3,2,1,0:T(8,128)(2,1)}, bf16[2,32,128,128]{3,2,1,0:T(8,128)(2,1)}, bf16[4,528,128]{2,1,0:T(8,128)(2,1)S(1)}, bf16[2,2,128,1...) custom-call(s32[2,32]{1,0:T(2,128)S(1)} %copy-done.6, ...), custom_call_target="tpu_custom_call" | custom-call | flops 5368709120 | bytes 27262976 | tf_op jit(solution)/shard_map/pallas_call | solution.py:342
  22.3 1.3 %collective-permute-start.2 = (bf16[4,528,128]{2,1,0:T(8,128)(2,1)S(1)}, bf16[4,528,128]{2,1,0:T(8,128)(2,1)S(1)}, u32[]{:S(2)}, u32[]{:S(2)}) collective-permute-start(bf16[4,528,128]{2,1,0:T(8,128)(2,1)S(1)} %get-tuple-element.21), channel_id=1, source_target_pairs={{4,0},{8,4},{12,8},{16,12},{20,16},{24,20},{28,24},{5,1},{9,5},{13... | collective-permute-start | bytes 1622024 | tf_op jit(solution)/shard_map/ppermute | solution.py:18
  23.6 1.3 %collective-permute-start = (bf16[2,2,128,128]{3,2,1,0:T(8,128)(2,1)S(1)}, bf16[2,2,128,128]{3,2,1,0:T(8,128)(2,1)S(1)}, u32[]{:S(2)}, u32[]{:S(2)}) collective-permute-start(bf16[2,2,128,128]{3,2,1,0:T(8,128)(2,1)S(1)} %get-tuple-element.14), channel_id=1, source_target_pairs={{1,0},{2,1},{3,2},{5,4},{6,5},{7,6},{9,8},{10,9},{11,10},{13,12},{... | collective-permute-start | bytes 393224 | tf_op jit(solution)/shard_map/ppermute | solution.py:18
  24.9 6.2 %collective-permute-done.1.top_ref = bf16[32,128,128]{2,1,0:T(8,128)(2,1)S(1)} collective-permute-done((bf16[32,128,128]{2,1,0:T(8,128)(2,1)S(1)}, bf16[32,128,128]{2,1,0:T(8,128)(2,1)S(1)}, u32[]{:S(2)}, u32[]{:S(2)}) %collective-permute-start.1) | collective-permute-done | bytes 1048608 | tf_op jit(solution)/shard_map/ppermute | solution.py:18
  31.1 0.0 copy-done.1
  31.1 0.0 copy-done
  31.1 0.0 copy-start.2
  31.1 0.0 copy-start.4
  31.1 5.0 %shard_map.133 = (f32[32,128,128]{2,1,0:T(8,128)S(1)}, bf16[32,128,128]{2,1,0:T(8,128)(2,1)S(1)}, bf16[32,128,128]{2,1,0:T(8,128)(2,1)S(1)}) custom-call(s32[2,32]{1,0:T(2,128)S(1)} %copy-done.7, s32[2,32,128]{2,1,0:T(8,128)S(1)} %copy-done.1, bf16[2,32,256,128]{3,2,1,0:T(8,128)(2,1)S(1)} %copy-done, bf16[2,32,128]{2,1,0:T(8,128)(2,1)S(1)} %copy-done.3, ...), custom_call_target="tpu_custom_call" | custom-call | flops 1073741824 | bytes 12582912 | tf_op jit(solution)/shard_map/pallas_call | solution.py:395
  36.2 0.0 collective-permute-done.edge_ref
  36.2 2.1 %shard_map.135 = bf16[2,32,128,128]{3,2,1,0:T(8,128)(2,1)} custom-call(s32[2,32]{1,0:T(2,128)S(1)} %copy-done.5, s32[2,32,128]{2,1,0:T(8,128)S(1)} %copy-done.2, bf16[2,32,256,128]{3,2,1,0:T(8,128)(2,1)} %interp_ref.5, bf16[2,32,128]{2,1,0:T(8,128)(2,1)S(1)} %copy-done.4, ...), custom_call_target="tpu_custom_call", output_to_operand_aliasing={{}: (6, {})} | custom-call | flops 67108864 | bytes 786432 | tf_op jit(solution)/shard_map/pallas_call | solution.py:418
  38.3 3.5 %collective-permute-done.2.packed_ref = bf16[4,528,128]{2,1,0:T(8,128)(2,1)S(1)} collective-permute-done((bf16[4,528,128]{2,1,0:T(8,128)(2,1)S(1)}, bf16[4,528,128]{2,1,0:T(8,128)(2,1)S(1)}, u32[]{:S(2)}, u32[]{:S(2)}) %collective-permute-start.2) | collective-permute-done | bytes 540704 | tf_op jit(solution)/shard_map/ppermute | solution.py:18
  41.9 1.8 %shard_map.134 = bf16[2,32,128,128]{3,2,1,0:T(8,128)(2,1)} custom-call(f32[32,128,128]{2,1,0:T(8,128)S(1)} %get-tuple-element.18.part_ref, bf16[32,128,128]{2,1,0:T(8,128)(2,1)S(1)} %get-tuple-element.19.lower_ref, bf16[32,128,128]{2,1,0:T(8,128)(2,1)S(1)} %get-tuple-element.20.lower_turned_ref, ...), custom_call_target="tpu_custom_call", output_to_operand_aliasing={{}: (4, {})} | custom-call | flops 402653184 | bytes 5767168 | tf_op jit(solution)/shard_map/pallas_call | solution.py:437
  (3 shorter events, 0.0 us)
Async XLA Ops:
  0.6 2.9 %copy-start.6 = (s32[2,32]{1,0:T(2,128)S(1)}, s32[2,32]{1,0:T(2,128)}, u32[]{:S(2)}) copy-start(s32[2,32]{1,0:T(2,128)} %rank_hbm.1) | copy-start | bytes 772
  0.6 2.9 %copy-start.5 = (s32[2,32]{1,0:T(2,128)S(1)}, s32[2,32]{1,0:T(2,128)}, u32[]{:S(2)}) copy-start(s32[2,32]{1,0:T(2,128)} %rank_ref.5) | copy-start | bytes 772
  0.7 2.9 %copy-start.7 = (s32[2,32]{1,0:T(2,128)S(1)}, s32[2,32]{1,0:T(2,128)}, u32[]{:S(2)}) copy-start(s32[2,32]{1,0:T(2,128)} %rank_ref.4) | copy-start | bytes 772
  2.2 28.9 %copy-start.1 = (s32[2,32,128]{2,1,0:T(8,128)S(1)}, s32[2,32,128]{2,1,0:T(8,128)}, u32[]{:S(2)}) copy-start(s32[2,32,128]{2,1,0:T(8,128)} %skel_ref.4) | copy-start | bytes 98308
  2.2 28.9 %copy-start.3 = (bf16[2,32,128]{2,1,0:T(8,128)(2,1)S(1)}, bf16[2,32,128]{2,1,0:T(8,128)(2,1)}, u32[]{:S(2)}) copy-start(bf16[2,32,128]{2,1,0:T(8,128)(2,1)} %coup_ref.2) | copy-start | bytes 49156
  2.2 28.9 %collective-permute-start.1 = (bf16[32,128,128]{2,1,0:T(8,128)(2,1)S(1)}, bf16[32,128,128]{2,1,0:T(8,128)(2,1)S(1)}, u32[]{:S(2)}, u32[]{:S(2)}) collective-permute-start(bf16[32,128,128]{2,1,0:T(8,128)(2,1)S(1)} %shard_map.132), channel_id=1, source_target_pairs={{4,0},{8,4},{12,8},{16,12},{20,16},{24,20},{28,24},{5,1},{9,5},{13... | collective-permute-start | bytes 3145736 | tf_op jit(solution)/shard_map/ppermute | solution.py:18
  3.6 27.5 %copy-start = (bf16[2,32,256,128]{3,2,1,0:T(8,128)(2,1)S(1)}, bf16[2,32,256,128]{3,2,1,0:T(8,128)(2,1)}, u32[]{:S(2)}) copy-start(bf16[2,32,256,128]{3,2,1,0:T(8,128)(2,1)} %interp_ref.4) | copy-start | bytes 12582916
  22.3 19.6 %collective-permute-start.2 = (bf16[4,528,128]{2,1,0:T(8,128)(2,1)S(1)}, bf16[4,528,128]{2,1,0:T(8,128)(2,1)S(1)}, u32[]{:S(2)}, u32[]{:S(2)}) collective-permute-start(bf16[4,528,128]{2,1,0:T(8,128)(2,1)S(1)} %get-tuple-element.21), channel_id=1, source_target_pairs={{4,0},{8,4},{12,8},{16,12},{20,16},{24,20},{28,24},{5,1},{9,5},{13... | collective-permute-start | bytes 1622024 | tf_op jit(solution)/shard_map/ppermute | solution.py:18
  23.6 12.6 %collective-permute-start = (bf16[2,2,128,128]{3,2,1,0:T(8,128)(2,1)S(1)}, bf16[2,2,128,128]{3,2,1,0:T(8,128)(2,1)S(1)}, u32[]{:S(2)}, u32[]{:S(2)}) collective-permute-start(bf16[2,2,128,128]{3,2,1,0:T(8,128)(2,1)S(1)} %get-tuple-element.14), channel_id=1, source_target_pairs={{1,0},{2,1},{3,2},{5,4},{6,5},{7,6},{9,8},{10,9},{11,10},{13,12},{... | collective-permute-start | bytes 393224 | tf_op jit(solution)/shard_map/ppermute | solution.py:18
  31.1 5.1 %copy-start.2 = (s32[2,32,128]{2,1,0:T(8,128)S(1)}, s32[2,32,128]{2,1,0:T(8,128)}, u32[]{:S(2)}) copy-start(s32[2,32,128]{2,1,0:T(8,128)} %skel_ref.5) | copy-start | bytes 98308
  31.1 5.1 %copy-start.4 = (bf16[2,32,128]{2,1,0:T(8,128)(2,1)S(1)}, bf16[2,32,128]{2,1,0:T(8,128)(2,1)}, u32[]{:S(2)}) copy-start(bf16[2,32,128]{2,1,0:T(8,128)(2,1)} %coup_ref.3) | copy-start | bytes 49156

commit v5 on v4

--- a/solution.py
+++ b/solution.py
@@ -28,13 +28,13 @@
     picked_row = jnp.where(live, skel_row, -1).astype(F32).astype(BF)
     row = lax.broadcasted_iota(jnp.int32, (rows, slots), 0).astype(F32).astype(BF)
     live_row = jnp.where(live, F32(1.0), F32(0.0)).astype(BF)
-    hit = jnp.where(row == picked_row, BF(1.0), BF(0.0))
-    return hit, interp * live_row
+    return row == picked_row, interp * live_row
 
 
 def kept_cleared(hits, interps):
     slots = hits[0].shape[-1]
     ones = jnp.ones((slots, slots), BF)
+    hits = [jnp.where(hit, BF(1.0), BF(0.0)) for hit in hits]
     counts = [dot(hit, ones).astype(BF) for hit in hits]
     return [h + z * (BF(1.0) - n) for h, z, n in zip(hits, interps, counts)]
 
@@ -84,7 +84,7 @@
         copies[c].wait()
         for k in range(c * cells, (c + 1) * cells):
             hit, interp = marks_of(skel_ref[k : k + 1], rank_ref[0, k], held[k])
-            out_ref[k] = hit + interp * (BF(1.0) - hit)
+            out_ref[k] = jnp.where(hit, BF(1.0), interp)
 
 
 def pack_masks(size):
@@ -101,8 +101,8 @@
     rank_ref, skel_ref, interp_ref, matrix_ref,
     x_rank_ref, x_skel_ref, x_interp_ref, x_coup_ref,
     y_rank_ref, y_skel_ref, y_interp_ref, y_coup_ref,
-    x_out_ref, y_out_ref, packed_ref, edge_ref, corner_ref, last_turned_ref, last_schur_ref,
-    store_top, store_turned, store_schur,
+    x_out_ref, y_out_ref, packed_ref, packed_last_ref, edge_ref, corner_ref, last_turned_ref, last_schur_ref,
+    store_top, store_turned, store_schur, store_extra,
 ):
     layer = layers - 1 - pl.program_id(0)
     chunk = chunks - 1 - pl.program_id(1)
@@ -155,16 +155,38 @@
 
     @pl.when(layer == 0)
     def _():
-        upper, _, opposite = pack_masks(slots)
-        pad = packed_ref.shape[1] - cells * half - cells
-        extras = []
-        for k in range(cells):
-            above = schurs[k][:half].astype(F32)
-            below = schurs[k][half:].astype(F32)
-            packed_ref[chunk, k * half : (k + 1) * half] = jnp.where(upper, above, below).astype(BF)
-            extras.append(jnp.sum(jnp.where(opposite, above, F32(0.0)), axis=0, keepdims=True))
-        rows = extras + [jnp.zeros((pad, slots), F32)]
-        packed_ref[chunk, cells * half :] = jnp.concatenate(rows, axis=0).astype(BF)
+        upper, same, opposite = pack_masks(slots)
+
+        def put(packed_ref, start):
+            for k in range(cells):
+                above, below = schurs[k][:half].astype(F32), schurs[k][half:].astype(F32)
+                place = pl.ds(pl.multiple_of(start + k * half, half), half)
+                packed_ref[place] = jnp.where(upper, above, below).astype(BF)
+
+        @pl.when(chunk < chunks - 1)
+        def _():
+            put(packed_ref, chunk * (cells * half))
+
+        @pl.when(chunk == chunks - 1)
+        def _():
+            put(packed_last_ref, 0)
+
+        for p in range(0, cells, 2):
+            extra = jnp.where(opposite, schurs[p][:half].astype(F32), F32(0.0))
+            if p + 1 < cells:
+                extra += jnp.where(same, schurs[p + 1][half:].astype(F32), F32(0.0))
+            store_extra[chunk, p // 2 : p // 2 + 1] = jnp.sum(extra, axis=0, keepdims=True)
+
+        @pl.when(chunk == 0)
+        def _():
+            pairs = -(-cells // 2)
+            for ref, places in ((packed_ref, range(chunks - 1)), (packed_last_ref, [chunks - 1])):
+                start = len(places) * cells * half
+                rows = [store_extra[c, :pairs] for c in places]
+                pad = ref.shape[0] - start - pairs * len(places)
+                if pad:
+                    rows.append(jnp.zeros((pad, slots), F32))
+                ref[start:] = jnp.concatenate(rows, axis=0).astype(BF)
 
     @pl.when(chunk == 0)
     def _():
@@ -204,8 +226,7 @@
         lower_ref[k] = faces[k][half:]
         lower_turned_ref[k] = turned[k][:, half:]
     marked = [top_ref[k] for k in range(cells)]
-    hits = [jnp.where(m == BF(1.0), BF(1.0), BF(0.0)) for m in marked]
-    tops = kept_cleared(hits, marked)
+    tops = kept_cleared([m == BF(1.0) for m in marked], marked)
     found = [
         dot(scaled(turned_ref[k], coup_ref[0, k : k + 1]), tops[k]).astype(BF)
         for k in range(cells)
@@ -220,36 +241,46 @@
 
 
 def x_last_kernel(
-    cells, layer, part_ref, lower_ref, lower_turned_ref, packed_ref, _, out_ref, held, sems
+    cells, layer, places, part_ref, lower_ref, lower_turned_ref, packed_ref, _, out_ref, held, sems
 ):
-    count, _, slots = part_ref.shape
+    slots = part_ref.shape[-1]
     half = slots // 2
     upper, same, opposite = pack_masks(slots)
     one, zero, mid = F32(1.0), F32(0.0), F32(0.5)
     top_scale = jnp.where(same, mid, jnp.where(upper, one, zero))
     low_scale = jnp.where(opposite, mid, jnp.where(upper, zero, one))
-    opp_scale = jnp.where(opposite, one, zero)
+    same_scale = jnp.where(same, one, zero)
+    opposite_scale = jnp.where(opposite, one, zero)
+    extras = packed_ref[len(places) * cells * half :].astype(F32)
+    pairs = -(-cells // 2)
     copies = []
-    for c in range(count // cells):
-        extras = packed_ref[c, cells * half :].astype(F32)
-        places = range(c * cells, (c + 1) * cells)
+    for n, c in enumerate(places):
+        group = range(c * cells, (c + 1) * cells)
         schurs = []
         for k in range(cells):
-            packed = packed_ref[c, k * half : (k + 1) * half].astype(F32)
-            top = packed * top_scale + extras[k : k + 1] * opp_scale
-            low = packed * low_scale
+            start = (n * cells + k) * half
+            packed = packed_ref[start : start + half].astype(F32)
+            extra = extras[n * pairs + k // 2 : n * pairs + k // 2 + 1]
+            top, low = packed * top_scale, packed * low_scale
+            if k % 2 == 0:
+                top += extra * opposite_scale
+            else:
+                low += extra * same_scale
             tri = jnp.concatenate([top, low], axis=0).astype(BF)
             schurs.append(tri + jnp.transpose(tri))
         results = project(
-            [lower_turned_ref[k] for k in places], schurs, [lower_ref[k] for k in places]
+            [lower_turned_ref[k] for k in group], schurs, [lower_ref[k] for k in group]
         )
-        for k, result in zip(places, results):
-            held[k] = (part_ref[k] + result).astype(BF)
-        group = pl.ds(c * cells, cells)
+        for k, result in enumerate(results):
+            held[n * cells + k] = (part_ref[c * cells + k] + result).astype(BF)
         copies.append(
-            pltpu.make_async_copy(held.at[group], out_ref.at[layer, group], sems.at[c])
+            pltpu.make_async_copy(
+                held.at[pl.ds(n * cells, cells)],
+                out_ref.at[layer, pl.ds(c * cells, cells)],
+                sems.at[n],
+            )
         )
-        copies[c].start()
+        copies[n].start()
     for copy in copies:
         copy.wait()
 
@@ -289,7 +320,7 @@
     nx, nj, rows, slots = cell_interp.shape
     half = rows // 2
     fslots = x_face_interp.shape[-1]
-    cells = 8 if nj % 8 == 0 else nj
+    cells = next(n for n in (8, 4, 2, 1) if nj % n == 0 and nj > n)
     chunks = nj // cells
     unit = 2 * nx * nj * slots * slots * slots
     smem = pl.BlockSpec(memory_space=pltpu.SMEM)
@@ -316,7 +347,11 @@
     )(in_hbm(cell_rank), in_hbm(cell_skel), in_hbm(cell_interp))
     top_in = passed_along(top, "gx", -1)
 
-    pack_rows = cells * slots // 2 + -(-cells // 16) * 16
+
+    def pack_rows(count):
+        extra = count * -(-cells // 2)
+        return count * cells * slots // 2 + -(-extra // 16) * 16
+
     near = max(nx - 2, 0)
 
     def down(*dims):
@@ -339,7 +374,7 @@
             (cells,) + dims, lambda i, c: (jnp.where(i == 0, chunks - 1 - c, 0),) + (0,) * len(dims)
         )
 
-    x_out, y_out, packed, edge, corner, last_turned, last_schur = call(
+    x_out, y_out, packed, packed_last, edge, corner, last_turned, last_schur = call(
         functools.partial(main_kernel, cells, nx, chunks),
         (nx, chunks),
         [
@@ -350,7 +385,8 @@
         [
             down_x(fslots, fslots),
             down(fslots, fslots),
-            whole(chunks, pack_rows, slots),
+            whole(pack_rows(chunks - 1), slots),
+            whole(pack_rows(1), slots),
             whole(nx, 2, half, slots),
             whole(nx, 2, slots, half),
             from_last(slots, half),
@@ -359,7 +395,8 @@
         [
             shape((nx, nj, fslots, fslots), BF),
             shape((nx, nj, fslots, fslots), BF),
-            shape((chunks, pack_rows, slots), BF),
+            shape((pack_rows(chunks - 1), slots), BF),
+            shape((pack_rows(1), slots), BF),
             shape((nx, 2, half, slots), BF),
             shape((nx, 2, slots, half), BF),
             shape((nj, slots, half), BF),
@@ -372,6 +409,7 @@
             pltpu.VMEM((nj, half, slots), BF),
             pltpu.VMEM((nj, slots, half), BF),
             pltpu.VMEM((nj, slots, slots), BF),
+            pltpu.VMEM((chunks, cells, slots), F32),
         ],
     )(
         cell_rank, in_hbm(cell_skel), in_hbm(cell_interp), in_hbm(cell_matrix),
@@ -414,6 +452,8 @@
         face_bytes,
     )(x_face_rank, x_face_skel, x_face_interp, x_coupling, last_turned, last_schur, top_in)
 
+    packed_last, part = lax.optimization_barrier((packed_last, part))
+    packed_last_in = passed_along(packed_last, "gx", -1)
     edge_in, part = lax.optimization_barrier((edge_in, part))
     y_out = call(
         functools.partial(y_edge_kernel, nx, tail),
@@ -434,17 +474,25 @@
         {6: 0},
     )(y_face_rank, y_face_skel, in_hbm(y_face_interp), y_coupling, corner, edge_in, y_out)
 
-    x_out = call(
-        functools.partial(x_last_kernel, cells, last),
-        (),
-        [vmem, vmem, vmem, vmem, hbm],
-        hbm,
-        shape((nx, nj, fslots, fslots), BF),
-        3 * unit // nx,
-        nj * slots * slots * 11,
-        {4: 0},
-        scratch=[pltpu.VMEM((nj, fslots, fslots), BF), pltpu.SemaphoreType.DMA((chunks,))],
-    )(part, lower, lower_turned, packed_in, x_out)
+    for places, arrived in (
+        (range(chunks - 1), packed_in),
+        (range(chunks - 1, chunks), packed_last_in),
+    ):
+        count = len(places)
+        x_out = call(
+            functools.partial(x_last_kernel, cells, last, places),
+            (),
+            [vmem, vmem, vmem, vmem, hbm],
+            hbm,
+            shape((nx, nj, fslots, fslots), BF),
+            3 * unit // nx * count // chunks,
+            nj * slots * slots * 11 * count // chunks,
+            {4: 0},
+            scratch=[
+                pltpu.VMEM((count * cells, fslots, fslots), BF),
+                pltpu.SemaphoreType.DMA((count,)),
+            ],
+        )(part, lower, lower_turned, arrived, x_out)
     return (x_out, y_out)
 
 

time: 44.1 us -> 45.3 us (1.027)
  starting transfers between devices: 3.87 us -> 5.16 us
  Pallas kernels: 29.2 us -> 30.1 us
  waiting for transfers between devices: 9.75 us -> 8.88 us
    ppermute x3 -> x4, starting transfers between devices: 3.87 us -> 5.16 us  [passed_along(): return lax.ppermute(x, axis, pairs)]
    pallas_call x1 -> x2, Pallas kernels: 1.84 us -> 2.73 us  [body(): call(functools.partial(x_last_kernel, cells, last, places), (), [vmem, vm...]
    ppermute x3 -> x4, waiting for transfers between devices: 9.75 us -> 8.88 us  [passed_along(): return lax.ppermute(x, axis, pairs)]
  transfers between devices with their start and end apart: 3 -> 4, of which waited for: 2 -> 2; matrix products, arithmetic and copies ran while one was open for 0% -> 0% of each run, Pallas kernels for 59% -> 61%
where the time goes in v5:
time: 45.3 us; the launch traced here: 44.9 us
  Pallas kernels  30.1 us (66%)
  waiting for transfers between devices  8.88 us (20%)
  starting transfers between devices  5.16 us (11%)
  between operations  0.8 us (2%)
    pallas_call x1, Pallas kernels, body(): call(functools.partial(main_kernel, cells, nx, chunks), (nx, chunks), [sm...  18.8 us
    ppermute x4, waiting for transfers between devices, passed_along(): return lax.ppermute(x, axis, pairs)  8.88 us
    ppermute x4, starting transfers between devices, passed_along(): return lax.ppermute(x, axis, pairs)  5.16 us
    pallas_call x1, Pallas kernels, body(): call(functools.partial(x_part_kernel, cells, last), (chunks,), [smem, las...  5.03 us
    pallas_call x2, Pallas kernels, body(): call(functools.partial(x_last_kernel, cells, last, places), (), [vmem, vm...  2.73 us
    pallas_call x1, Pallas kernels, body(): call(functools.partial(y_edge_kernel, nx, tail), (1,), [smem, pl.BlockSpe...  2.11 us
    pallas_call x1, Pallas kernels, body(): call(functools.partial(top_kernel, cells), (), [hbm, hbm, hbm], vmem, sha...  1.35 us
  transfers between devices with their start and end apart: 4, of which 2 were waited for; matrix products, arithmetic and copies ran while one was open for 0% of the time, Pallas kernels for 61%

profile of v5, /device:TPU:0, one launch (start us, length us, event | category | flops | bytes accessed | tf_op | source)
XLA Modules:
  0.0 44.9 jit_solution(7590977877485487951)
XLA Ops:
  0.6 0.0 copy-start.6
  0.7 1.3 %shard_map.132 = bf16[32,128,128]{2,1,0:T(8,128)(2,1)S(1)} custom-call(s32[2,32]{1,0:T(2,128)} %rank_hbm.1, s32[2,32,128]{2,1,0:T(8,128)} %skel_hbm.1, bf16[2,32,256,128]{3,2,1,0:T(8,128)(2,1)} %interp_hbm.1), custom_call_target="tpu_custom_call" | custom-call | bytes 2097152 | tf_op jit(solution)/shard_map/pallas_call | solution.py:331
  2.0 0.0 copy-start.1
  2.0 0.0 copy-start.3
  2.0 1.3 %collective-permute-start.1 = (bf16[32,128,128]{2,1,0:T(8,128)(2,1)S(1)}, bf16[32,128,128]{2,1,0:T(8,128)(2,1)S(1)}, u32[]{:S(2)}, u32[]{:S(2)}) collective-permute-start(bf16[32,128,128]{2,1,0:T(8,128)(2,1)S(1)} %shard_map.132), channel_id=1, source_target_pairs={{4,0},{8,4},{12,8},{16,12},{20,16},{24,20},{28,24},{5,1},{9,5},{13... | collective-permute-start | bytes 3145736 | tf_op jit(solution)/shard_map/ppermute | solution.py:18
  3.3 0.0 copy-done.6
  3.4 0.0 copy-done.5
  3.4 0.0 copy-done.7
  3.4 0.0 copy-start
  3.4 18.8 %shard_map.131 = (bf16[2,32,128,128]{3,2,1,0:T(8,128)(2,1)}, bf16[2,32,128,128]{3,2,1,0:T(8,128)(2,1)}, bf16[1552,128]{1,0:T(8,128)(2,1)S(1)}, bf16[528,128]{1,0...) custom-call(s32[2,32]{1,0:T(2,128)S(1)} %copy-done.6, ...), custom_call_target="tpu_custom_call" | custom-call | flops 5368709120 | bytes 27262976 | tf_op jit(solution)/shard_map/pallas_call | solution.py:377
  22.2 1.3 %collective-permute-start.3 = (bf16[1552,128]{1,0:T(8,128)(2,1)S(1)}, bf16[1552,128]{1,0:T(8,128)(2,1)S(1)}, u32[]{:S(2)}, u32[]{:S(2)}) collective-permute-start(bf16[1552,128]{1,0:T(8,128)(2,1)S(1)} %get-tuple-element.27), channel_id=1, source_target_pairs={{4,0},{8,4},{12,8},{16,12},{20,16},{24,20},{28,24},{5,1},{9,5},{13... | collective-permute-start | bytes 1191944 | tf_op jit(solution)/shard_map/ppermute | solution.py:18
  23.5 1.3 %collective-permute-start = (bf16[2,2,128,128]{3,2,1,0:T(8,128)(2,1)S(1)}, bf16[2,2,128,128]{3,2,1,0:T(8,128)(2,1)S(1)}, u32[]{:S(2)}, u32[]{:S(2)}) collective-permute-start(bf16[2,2,128,128]{3,2,1,0:T(8,128)(2,1)S(1)} %get-tuple-element.17), channel_id=1, source_target_pairs={{1,0},{2,1},{3,2},{5,4},{6,5},{7,6},{9,8},{10,9},{11,10},{13,12},{... | collective-permute-start | bytes 393224 | tf_op jit(solution)/shard_map/ppermute | solution.py:18
  24.8 6.1 %collective-permute-done.1.top_ref = bf16[32,128,128]{2,1,0:T(8,128)(2,1)S(1)} collective-permute-done((bf16[32,128,128]{2,1,0:T(8,128)(2,1)S(1)}, bf16[32,128,128]{2,1,0:T(8,128)(2,1)S(1)}, u32[]{:S(2)}, u32[]{:S(2)}) %collective-permute-start.1) | collective-permute-done | bytes 1048608 | tf_op jit(solution)/shard_map/ppermute | solution.py:18
  30.9 0.0 copy-done
  30.9 0.0 copy-start.2
  30.9 0.0 copy-start.4
  30.9 5.0 %shard_map.133 = (f32[32,128,128]{2,1,0:T(8,128)S(1)}, bf16[32,128,128]{2,1,0:T(8,128)(2,1)S(1)}, bf16[32,128,128]{2,1,0:T(8,128)(2,1)S(1)}) custom-call(s32[2,32]{1,0:T(2,128)S(1)} %copy-done.7, s32[2,32,128]{2,1,0:T(8,128)S(1)} %copy-done.1, bf16[2,32,256,128]{3,2,1,0:T(8,128)(2,1)S(1)} %copy-done, bf16[2,32,128]{2,1,0:T(8,128)(2,1)S(1)} %copy-done.3, ...), custom_call_target="tpu_custom_call" | custom-call | flops 1073741824 | bytes 12582912 | tf_op jit(solution)/shard_map/pallas_call | solution.py:433
  36.0 1.3 %collective-permute-start.2 = (bf16[528,128]{1,0:T(8,128)(2,1)S(1)}, bf16[528,128]{1,0:T(8,128)(2,1)S(1)}, u32[]{:S(2)}, u32[]{:S(2)}) collective-permute-start(bf16[528,128]{1,0:T(8,128)(2,1)S(1)} %get-tuple-element.26), channel_id=1, source_target_pairs={{4,0},{8,4},{12,8},{16,12},{20,16},{24,20},{28,24},{5,1},{9,5},{13... | collective-permute-start | bytes 405512 | tf_op jit(solution)/shard_map/ppermute | solution.py:18
  37.3 0.0 collective-permute-done.edge_ref
  37.3 2.1 %shard_map.136 = bf16[2,32,128,128]{3,2,1,0:T(8,128)(2,1)} custom-call(s32[2,32]{1,0:T(2,128)S(1)} %copy-done.5, s32[2,32,128]{2,1,0:T(8,128)S(1)} %copy-done.2, bf16[2,32,256,128]{3,2,1,0:T(8,128)(2,1)} %interp_ref.5, bf16[2,32,128]{2,1,0:T(8,128)(2,1)S(1)} %copy-done.4, ...), custom_call_target="tpu_custom_call", output_to_operand_aliasing={{}: (6, {})} | custom-call | flops 67108864 | bytes 786432 | tf_op jit(solution)/shard_map/pallas_call | solution.py:458
  39.4 0.0 collective-permute-done.3.packed_ref
  39.4 1.6 %shard_map.134._ = bf16[2,32,128,128]{3,2,1,0:T(8,128)(2,1)} custom-call(f32[32,128,128]{2,1,0:T(8,128)S(1)} %get-tuple-element.23.part_ref, bf16[32,128,128]{2,1,0:T(8,128)(2,1)S(1)} %get-tuple-element.24.lower_ref, bf16[32,128,128]{2,1,0:T(8,128)(2,1)S(1)} %get-tuple-element.25.lower_turned_ref, ...), custom_call_target="tpu_custom_call", output_to_operand_aliasing={{}: (4, {})} | custom-call | flops 301989888 | bytes 4325376 | tf_op jit(solution)/shard_map/pallas_call | solution.py:482
  41.0 2.8 %collective-permute-done.2.packed_ref = bf16[528,128]{1,0:T(8,128)(2,1)S(1)} collective-permute-done((bf16[528,128]{1,0:T(8,128)(2,1)S(1)}, bf16[528,128]{1,0:T(8,128)(2,1)S(1)}, u32[]{:S(2)}, u32[]{:S(2)}) %collective-permute-start.2) | collective-permute-done | bytes 135200 | tf_op jit(solution)/shard_map/ppermute | solution.py:18
  43.8 1.1 %shard_map.135 = bf16[2,32,128,128]{3,2,1,0:T(8,128)(2,1)} custom-call(f32[32,128,128]{2,1,0:T(8,128)S(1)} %get-tuple-element.23.part_ref, bf16[32,128,128]{2,1,0:T(8,128)(2,1)S(1)} %get-tuple-element.24.lower_ref, bf16[32,128,128]{2,1,0:T(8,128)(2,1)S(1)} %get-tuple-element.25.lower_turned_ref, ...), custom_call_target="tpu_custom_call", output_to_operand_aliasing={{}: (4, {})} | custom-call | flops 100663296 | bytes 1441792 | tf_op jit(solution)/shard_map/pallas_call | solution.py:482
  (6 shorter events, 0.0 us)
Async XLA Ops:
  0.6 2.7 %copy-start.6 = (s32[2,32]{1,0:T(2,128)S(1)}, s32[2,32]{1,0:T(2,128)}, u32[]{:S(2)}) copy-start(s32[2,32]{1,0:T(2,128)} %rank_hbm.1) | copy-start | bytes 772
  0.6 2.7 %copy-start.5 = (s32[2,32]{1,0:T(2,128)S(1)}, s32[2,32]{1,0:T(2,128)}, u32[]{:S(2)}) copy-start(s32[2,32]{1,0:T(2,128)} %rank_ref.5) | copy-start | bytes 772
  0.7 2.7 %copy-start.7 = (s32[2,32]{1,0:T(2,128)S(1)}, s32[2,32]{1,0:T(2,128)}, u32[]{:S(2)}) copy-start(s32[2,32]{1,0:T(2,128)} %rank_ref.4) | copy-start | bytes 772
  2.0 28.9 %copy-start.1 = (s32[2,32,128]{2,1,0:T(8,128)S(1)}, s32[2,32,128]{2,1,0:T(8,128)}, u32[]{:S(2)}) copy-start(s32[2,32,128]{2,1,0:T(8,128)} %skel_ref.4) | copy-start | bytes 98308
  2.0 28.9 %copy-start.3 = (bf16[2,32,128]{2,1,0:T(8,128)(2,1)S(1)}, bf16[2,32,128]{2,1,0:T(8,128)(2,1)}, u32[]{:S(2)}) copy-start(bf16[2,32,128]{2,1,0:T(8,128)(2,1)} %coup_ref.2) | copy-start | bytes 49156
  2.0 28.9 %collective-permute-start.1 = (bf16[32,128,128]{2,1,0:T(8,128)(2,1)S(1)}, bf16[32,128,128]{2,1,0:T(8,128)(2,1)S(1)}, u32[]{:S(2)}, u32[]{:S(2)}) collective-permute-start(bf16[32,128,128]{2,1,0:T(8,128)(2,1)S(1)} %shard_map.132), channel_id=1, source_target_pairs={{4,0},{8,4},{12,8},{16,12},{20,16},{24,20},{28,24},{5,1},{9,5},{13... | collective-permute-start | bytes 3145736 | tf_op jit(solution)/shard_map/ppermute | solution.py:18
  3.4 27.5 %copy-start = (bf16[2,32,256,128]{3,2,1,0:T(8,128)(2,1)S(1)}, bf16[2,32,256,128]{3,2,1,0:T(8,128)(2,1)}, u32[]{:S(2)}) copy-start(bf16[2,32,256,128]{3,2,1,0:T(8,128)(2,1)} %interp_ref.4) | copy-start | bytes 12582916
  22.2 17.2 %collective-permute-start.3 = (bf16[1552,128]{1,0:T(8,128)(2,1)S(1)}, bf16[1552,128]{1,0:T(8,128)(2,1)S(1)}, u32[]{:S(2)}, u32[]{:S(2)}) collective-permute-start(bf16[1552,128]{1,0:T(8,128)(2,1)S(1)} %get-tuple-element.27), channel_id=1, source_target_pairs={{4,0},{8,4},{12,8},{16,12},{20,16},{24,20},{28,24},{5,1},{9,5},{13... | collective-permute-start | bytes 1191944 | tf_op jit(solution)/shard_map/ppermute | solution.py:18
  23.5 13.8 %collective-permute-start = (bf16[2,2,128,128]{3,2,1,0:T(8,128)(2,1)S(1)}, bf16[2,2,128,128]{3,2,1,0:T(8,128)(2,1)S(1)}, u32[]{:S(2)}, u32[]{:S(2)}) collective-permute-start(bf16[2,2,128,128]{3,2,1,0:T(8,128)(2,1)S(1)} %get-tuple-element.17), channel_id=1, source_target_pairs={{1,0},{2,1},{3,2},{5,4},{6,5},{7,6},{9,8},{10,9},{11,10},{13,12},{... | collective-permute-start | bytes 393224 | tf_op jit(solution)/shard_map/ppermute | solution.py:18
  30.9 6.4 %copy-start.2 = (s32[2,32,128]{2,1,0:T(8,128)S(1)}, s32[2,32,128]{2,1,0:T(8,128)}, u32[]{:S(2)}) copy-start(s32[2,32,128]{2,1,0:T(8,128)} %skel_ref.5) | copy-start | bytes 98308
  30.9 6.4 %copy-start.4 = (bf16[2,32,128]{2,1,0:T(8,128)(2,1)S(1)}, bf16[2,32,128]{2,1,0:T(8,128)(2,1)}, u32[]{:S(2)}) copy-start(bf16[2,32,128]{2,1,0:T(8,128)(2,1)} %coup_ref.3) | copy-start | bytes 49156
  36.0 7.8 %collective-permute-start.2 = (bf16[528,128]{1,0:T(8,128)(2,1)S(1)}, bf16[528,128]{1,0:T(8,128)(2,1)S(1)}, u32[]{:S(2)}, u32[]{:S(2)}) collective-permute-start(bf16[528,128]{1,0:T(8,128)(2,1)S(1)} %get-tuple-element.26), channel_id=1, source_target_pairs={{4,0},{8,4},{12,8},{16,12},{20,16},{24,20},{28,24},{5,1},{9,5},{13... | collective-permute-start | bytes 405512 | tf_op jit(solution)/shard_map/ppermute | solution.py:18

commit v6 on v5

--- a/solution.py
+++ b/solution.py
@@ -418,6 +418,7 @@
     )
     edge_in = passed_along(edge, "yz", -1)
     packed_in = passed_along(packed, "gx", -1)
+    packed_last_in = passed_along(packed_last, "gx", -1)
     face_bytes = nj * (4 * rows * slots + 4 * slots * slots) * 2
 
     last = nx - 1
@@ -452,8 +453,6 @@
         face_bytes,
     )(x_face_rank, x_face_skel, x_face_interp, x_coupling, last_turned, last_schur, top_in)
 
-    packed_last, part = lax.optimization_barrier((packed_last, part))
-    packed_last_in = passed_along(packed_last, "gx", -1)
     edge_in, part = lax.optimization_barrier((edge_in, part))
     y_out = call(
         functools.partial(y_edge_kernel, nx, tail),

time: 45.3 us -> 43 us (0.949)
  waiting for transfers between devices: 8.88 us -> 6.54 us
    ppermute x4, waiting for transfers between devices: 8.88 us -> 6.54 us  [passed_along(): return lax.ppermute(x, axis, pairs)]
  transfers between devices with their start and end apart: 4 -> 4, of which waited for: 2 -> 3; matrix products, arithmetic and copies ran while one was open for 0% -> 0% of each run, Pallas kernels for 61% -> 65%
where the time goes in v6:
time: 43 us; the launch traced here: 42.6 us
  Pallas kernels  30.1 us (70%)
  waiting for transfers between devices  6.54 us (15%)
  starting transfers between devices  5.16 us (12%)
  between operations  0.8 us (2%)
    pallas_call x1, Pallas kernels, body(): call(functools.partial(main_kernel, cells, nx, chunks), (nx, chunks), [sm...  18.8 us
    ppermute x4, waiting for transfers between devices, passed_along(): return lax.ppermute(x, axis, pairs)  6.54 us
    ppermute x4, starting transfers between devices, passed_along(): return lax.ppermute(x, axis, pairs)  5.16 us
    pallas_call x1, Pallas kernels, body(): call(functools.partial(x_part_kernel, cells, last), (chunks,), [smem, las...  5.03 us
    pallas_call x2, Pallas kernels, body(): call(functools.partial(x_last_kernel, cells, last, places), (), [vmem, vm...  2.73 us
    pallas_call x1, Pallas kernels, body(): call(functools.partial(y_edge_kernel, nx, tail), (1,), [smem, pl.BlockSpe...  2.11 us
    pallas_call x1, Pallas kernels, body(): call(functools.partial(top_kernel, cells), (), [hbm, hbm, hbm], vmem, sha...  1.35 us
  transfers between devices with their start and end apart: 4, of which 3 were waited for; matrix products, arithmetic and copies ran while one was open for 0% of the time, Pallas kernels for 65%

profile of v6, /device:TPU:0, one launch (start us, length us, event | category | flops | bytes accessed | tf_op | source)
XLA Modules:
  0.0 42.6 jit_solution(17276957252464350356)
XLA Ops:
  0.6 0.0 copy-start.6
  0.7 1.3 %shard_map.132 = bf16[32,128,128]{2,1,0:T(8,128)(2,1)S(1)} custom-call(s32[2,32]{1,0:T(2,128)} %rank_hbm.1, s32[2,32,128]{2,1,0:T(8,128)} %skel_hbm.1, bf16[2,32,256,128]{3,2,1,0:T(8,128)(2,1)} %interp_hbm.1), custom_call_target="tpu_custom_call" | custom-call | bytes 2097152 | tf_op jit(solution)/shard_map/pallas_call | solution.py:331
  2.0 0.0 copy-start.1
  2.0 0.0 copy-start.3
  2.0 1.3 %collective-permute-start.1 = (bf16[32,128,128]{2,1,0:T(8,128)(2,1)S(1)}, bf16[32,128,128]{2,1,0:T(8,128)(2,1)S(1)}, u32[]{:S(2)}, u32[]{:S(2)}) collective-permute-start(bf16[32,128,128]{2,1,0:T(8,128)(2,1)S(1)} %shard_map.132), channel_id=1, source_target_pairs={{4,0},{8,4},{12,8},{16,12},{20,16},{24,20},{28,24},{5,1},{9,5},{13... | collective-permute-start | bytes 3145736 | tf_op jit(solution)/shard_map/ppermute | solution.py:18
  3.3 0.0 copy-done.6
  3.4 0.0 copy-done.5
  3.4 0.0 copy-done.7
  3.4 0.0 copy-start
  3.4 18.8 %shard_map.131 = (bf16[2,32,128,128]{3,2,1,0:T(8,128)(2,1)}, bf16[2,32,128,128]{3,2,1,0:T(8,128)(2,1)}, bf16[1552,128]{1,0:T(8,128)(2,1)S(1)}, bf16[528,128]{1,0...) custom-call(s32[2,32]{1,0:T(2,128)S(1)} %copy-done.6, ...), custom_call_target="tpu_custom_call" | custom-call | flops 5368709120 | bytes 27262976 | tf_op jit(solution)/shard_map/pallas_call | solution.py:377
  22.2 1.3 %collective-permute-start.3 = (bf16[1552,128]{1,0:T(8,128)(2,1)S(1)}, bf16[1552,128]{1,0:T(8,128)(2,1)S(1)}, u32[]{:S(2)}, u32[]{:S(2)}) collective-permute-start(bf16[1552,128]{1,0:T(8,128)(2,1)S(1)} %get-tuple-element.23), channel_id=1, source_target_pairs={{4,0},{8,4},{12,8},{16,12},{20,16},{24,20},{28,24},{5,1},{9,5},{13... | collective-permute-start | bytes 1191944 | tf_op jit(solution)/shard_map/ppermute | solution.py:18
  23.5 1.3 %collective-permute-start = (bf16[2,2,128,128]{3,2,1,0:T(8,128)(2,1)S(1)}, bf16[2,2,128,128]{3,2,1,0:T(8,128)(2,1)S(1)}, u32[]{:S(2)}, u32[]{:S(2)}) collective-permute-start(bf16[2,2,128,128]{3,2,1,0:T(8,128)(2,1)S(1)} %get-tuple-element.15), channel_id=1, source_target_pairs={{1,0},{2,1},{3,2},{5,4},{6,5},{7,6},{9,8},{10,9},{11,10},{13,12},{... | collective-permute-start | bytes 393224 | tf_op jit(solution)/shard_map/ppermute | solution.py:18
  24.8 1.3 %collective-permute-start.2 = (bf16[528,128]{1,0:T(8,128)(2,1)S(1)}, bf16[528,128]{1,0:T(8,128)(2,1)S(1)}, u32[]{:S(2)}, u32[]{:S(2)}) collective-permute-start(bf16[528,128]{1,0:T(8,128)(2,1)S(1)} %get-tuple-element.22), channel_id=1, source_target_pairs={{4,0},{8,4},{12,8},{16,12},{20,16},{24,20},{28,24},{5,1},{9,5},{13... | collective-permute-start | bytes 405512 | tf_op jit(solution)/shard_map/ppermute | solution.py:18
  26.1 4.8 %collective-permute-done.1.top_ref = bf16[32,128,128]{2,1,0:T(8,128)(2,1)S(1)} collective-permute-done((bf16[32,128,128]{2,1,0:T(8,128)(2,1)S(1)}, bf16[32,128,128]{2,1,0:T(8,128)(2,1)S(1)}, u32[]{:S(2)}, u32[]{:S(2)}) %collective-permute-start.1) | collective-permute-done | bytes 1048608 | tf_op jit(solution)/shard_map/ppermute | solution.py:18
  30.9 0.0 copy-done
  30.9 0.0 copy-start.2
  30.9 0.0 copy-start.4
  30.9 5.0 %shard_map.133 = (f32[32,128,128]{2,1,0:T(8,128)S(1)}, bf16[32,128,128]{2,1,0:T(8,128)(2,1)S(1)}, bf16[32,128,128]{2,1,0:T(8,128)(2,1)S(1)}) custom-call(s32[2,32]{1,0:T(2,128)S(1)} %copy-done.7, s32[2,32,128]{2,1,0:T(8,128)S(1)} %copy-done.1, bf16[2,32,256,128]{3,2,1,0:T(8,128)(2,1)S(1)} %copy-done, bf16[2,32,128]{2,1,0:T(8,128)(2,1)S(1)} %copy-done.3, ...), custom_call_target="tpu_custom_call" | custom-call | flops 1073741824 | bytes 12582912 | tf_op jit(solution)/shard_map/pallas_call | solution.py:434
  36.0 0.0 collective-permute-done.edge_ref
  36.0 2.1 %shard_map.136 = bf16[2,32,128,128]{3,2,1,0:T(8,128)(2,1)} custom-call(s32[2,32]{1,0:T(2,128)S(1)} %copy-done.5, s32[2,32,128]{2,1,0:T(8,128)S(1)} %copy-done.2, bf16[2,32,256,128]{3,2,1,0:T(8,128)(2,1)} %interp_ref.5, bf16[2,32,128]{2,1,0:T(8,128)(2,1)S(1)} %copy-done.4, ...), custom_call_target="tpu_custom_call", output_to_operand_aliasing={{}: (6, {})} | custom-call | flops 67108864 | bytes 786432 | tf_op jit(solution)/shard_map/pallas_call | solution.py:457
  38.1 1.3 %collective-permute-done.3.packed_ref = bf16[1552,128]{1,0:T(8,128)(2,1)S(1)} collective-permute-done((bf16[1552,128]{1,0:T(8,128)(2,1)S(1)}, bf16[1552,128]{1,0:T(8,128)(2,1)S(1)}, u32[]{:S(2)}, u32[]{:S(2)}) %collective-permute-start.3) | collective-permute-done | bytes 397344 | tf_op jit(solution)/shard_map/ppermute | solution.py:18
  39.4 1.6 %shard_map.134._ = bf16[2,32,128,128]{3,2,1,0:T(8,128)(2,1)} custom-call(f32[32,128,128]{2,1,0:T(8,128)S(1)} %get-tuple-element.19.part_ref, bf16[32,128,128]{2,1,0:T(8,128)(2,1)S(1)} %get-tuple-element.20.lower_ref, bf16[32,128,128]{2,1,0:T(8,128)(2,1)S(1)} %get-tuple-element.21.lower_turned_ref, ...), custom_call_target="tpu_custom_call", output_to_operand_aliasing={{}: (4, {})} | custom-call | flops 301989888 | bytes 4325376 | tf_op jit(solution)/shard_map/pallas_call | solution.py:481
  41.0 0.5 %collective-permute-done.2.packed_ref = bf16[528,128]{1,0:T(8,128)(2,1)S(1)} collective-permute-done((bf16[528,128]{1,0:T(8,128)(2,1)S(1)}, bf16[528,128]{1,0:T(8,128)(2,1)S(1)}, u32[]{:S(2)}, u32[]{:S(2)}) %collective-permute-start.2) | collective-permute-done | bytes 135200 | tf_op jit(solution)/shard_map/ppermute | solution.py:18
  41.5 1.1 %shard_map.135 = bf16[2,32,128,128]{3,2,1,0:T(8,128)(2,1)} custom-call(f32[32,128,128]{2,1,0:T(8,128)S(1)} %get-tuple-element.19.part_ref, bf16[32,128,128]{2,1,0:T(8,128)(2,1)S(1)} %get-tuple-element.20.lower_ref, bf16[32,128,128]{2,1,0:T(8,128)(2,1)S(1)} %get-tuple-element.21.lower_turned_ref, ...), custom_call_target="tpu_custom_call", output_to_operand_aliasing={{}: (4, {})} | custom-call | flops 100663296 | bytes 1441792 | tf_op jit(solution)/shard_map/pallas_call | solution.py:481
  (6 shorter events, 0.0 us)
Async XLA Ops:
  0.6 2.7 %copy-start.6 = (s32[2,32]{1,0:T(2,128)S(1)}, s32[2,32]{1,0:T(2,128)}, u32[]{:S(2)}) copy-start(s32[2,32]{1,0:T(2,128)} %rank_hbm.1) | copy-start | bytes 772
  0.6 2.7 %copy-start.5 = (s32[2,32]{1,0:T(2,128)S(1)}, s32[2,32]{1,0:T(2,128)}, u32[]{:S(2)}) copy-start(s32[2,32]{1,0:T(2,128)} %rank_ref.5) | copy-start | bytes 772
  0.7 2.7 %copy-start.7 = (s32[2,32]{1,0:T(2,128)S(1)}, s32[2,32]{1,0:T(2,128)}, u32[]{:S(2)}) copy-start(s32[2,32]{1,0:T(2,128)} %rank_ref.4) | copy-start | bytes 772
  2.0 28.9 %copy-start.1 = (s32[2,32,128]{2,1,0:T(8,128)S(1)}, s32[2,32,128]{2,1,0:T(8,128)}, u32[]{:S(2)}) copy-start(s32[2,32,128]{2,1,0:T(8,128)} %skel_ref.4) | copy-start | bytes 98308
  2.0 28.9 %copy-start.3 = (bf16[2,32,128]{2,1,0:T(8,128)(2,1)S(1)}, bf16[2,32,128]{2,1,0:T(8,128)(2,1)}, u32[]{:S(2)}) copy-start(bf16[2,32,128]{2,1,0:T(8,128)(2,1)} %coup_ref.2) | copy-start | bytes 49156
  2.0 28.9 %collective-permute-start.1 = (bf16[32,128,128]{2,1,0:T(8,128)(2,1)S(1)}, bf16[32,128,128]{2,1,0:T(8,128)(2,1)S(1)}, u32[]{:S(2)}, u32[]{:S(2)}) collective-permute-start(bf16[32,128,128]{2,1,0:T(8,128)(2,1)S(1)} %shard_map.132), channel_id=1, source_target_pairs={{4,0},{8,4},{12,8},{16,12},{20,16},{24,20},{28,24},{5,1},{9,5},{13... | collective-permute-start | bytes 3145736 | tf_op jit(solution)/shard_map/ppermute | solution.py:18
  3.4 27.5 %copy-start = (bf16[2,32,256,128]{3,2,1,0:T(8,128)(2,1)S(1)}, bf16[2,32,256,128]{3,2,1,0:T(8,128)(2,1)}, u32[]{:S(2)}) copy-start(bf16[2,32,256,128]{3,2,1,0:T(8,128)(2,1)} %interp_ref.4) | copy-start | bytes 12582916
  22.2 17.2 %collective-permute-start.3 = (bf16[1552,128]{1,0:T(8,128)(2,1)S(1)}, bf16[1552,128]{1,0:T(8,128)(2,1)S(1)}, u32[]{:S(2)}, u32[]{:S(2)}) collective-permute-start(bf16[1552,128]{1,0:T(8,128)(2,1)S(1)} %get-tuple-element.23), channel_id=1, source_target_pairs={{4,0},{8,4},{12,8},{16,12},{20,16},{24,20},{28,24},{5,1},{9,5},{13... | collective-permute-start | bytes 1191944 | tf_op jit(solution)/shard_map/ppermute | solution.py:18
  23.5 12.5 %collective-permute-start = (bf16[2,2,128,128]{3,2,1,0:T(8,128)(2,1)S(1)}, bf16[2,2,128,128]{3,2,1,0:T(8,128)(2,1)S(1)}, u32[]{:S(2)}, u32[]{:S(2)}) collective-permute-start(bf16[2,2,128,128]{3,2,1,0:T(8,128)(2,1)S(1)} %get-tuple-element.15), channel_id=1, source_target_pairs={{1,0},{2,1},{3,2},{5,4},{6,5},{7,6},{9,8},{10,9},{11,10},{13,12},{... | collective-permute-start | bytes 393224 | tf_op jit(solution)/shard_map/ppermute | solution.py:18
  24.8 16.7 %collective-permute-start.2 = (bf16[528,128]{1,0:T(8,128)(2,1)S(1)}, bf16[528,128]{1,0:T(8,128)(2,1)S(1)}, u32[]{:S(2)}, u32[]{:S(2)}) collective-permute-start(bf16[528,128]{1,0:T(8,128)(2,1)S(1)} %get-tuple-element.22), channel_id=1, source_target_pairs={{4,0},{8,4},{12,8},{16,12},{20,16},{24,20},{28,24},{5,1},{9,5},{13... | collective-permute-start | bytes 405512 | tf_op jit(solution)/shard_map/ppermute | solution.py:18
  30.9 5.1 %copy-start.2 = (s32[2,32,128]{2,1,0:T(8,128)S(1)}, s32[2,32,128]{2,1,0:T(8,128)}, u32[]{:S(2)}) copy-start(s32[2,32,128]{2,1,0:T(8,128)} %skel_ref.5) | copy-start | bytes 98308
  30.9 5.1 %copy-start.4 = (bf16[2,32,128]{2,1,0:T(8,128)(2,1)S(1)}, bf16[2,32,128]{2,1,0:T(8,128)(2,1)}, u32[]{:S(2)}) copy-start(bf16[2,32,128]{2,1,0:T(8,128)(2,1)} %coup_ref.3) | copy-start | bytes 49156

commit v7 on v6

--- a/solution.py
+++ b/solution.py
@@ -31,11 +31,22 @@
     return row == picked_row, interp * live_row
 
 
+def pair_ones(slots):
+    row = lax.broadcasted_iota(jnp.int32, (2 * slots, 2 * slots), 0) < slots
+    lane = lax.broadcasted_iota(jnp.int32, (2 * slots, 2 * slots), 1) < slots
+    return jnp.where(row == lane, F32(1.0), F32(0.0)).astype(BF)
+
+
 def kept_cleared(hits, interps):
     slots = hits[0].shape[-1]
-    ones = jnp.ones((slots, slots), BF)
+    ones = pair_ones(slots)
     hits = [jnp.where(hit, BF(1.0), BF(0.0)) for hit in hits]
-    counts = [dot(hit, ones).astype(BF) for hit in hits]
+    counts = []
+    for k in range(0, len(hits) - 1, 2):
+        both = dot(jnp.concatenate(hits[k : k + 2], axis=1), ones).astype(BF)
+        counts += [both[:, :slots], both[:, slots:]]
+    if len(hits) % 2:
+        counts.append(dot(hits[-1], ones[:slots, :slots]).astype(BF))
     return [h + z * (BF(1.0) - n) for h, z, n in zip(hits, interps, counts)]
 
 
@@ -199,20 +210,19 @@
         corner_ref[layer, 1] = schurs[cells - 1]
 
 
-def y_edge_kernel(layers, place, rank_ref, skel_ref, interp_ref, coup_ref, corner_ref, edge_ref, _, out_ref):
-    row = place % skel_ref.shape[1]
+def y_edge_parts(place, rank_ref, skel_ref, interps, coup_ref, corner_ref, edge_ref):
+    layers = skel_ref.shape[0]
     pairs = [
-        marks_of(skel_ref[i, row : row + 1], rank_ref[i, place], interp_ref[i, 0])
+        marks_of(skel_ref[i, place : place + 1], rank_ref[i, place], interps[i])
         for i in range(layers)
     ]
     found = kept_cleared([p[0] for p in pairs], [p[1] for p in pairs])
     matrices = []
     for i in range(layers):
-        link = dot(scaled(corner_ref[i, 0], coup_ref[i, row : row + 1]), edge_ref[i, 0]).astype(BF)
+        conduct = coup_ref[i, place : place + 1]
+        link = dot(scaled(corner_ref[i, 0], conduct), edge_ref[i, 0]).astype(BF)
         matrices.append(face_of(corner_ref[i, 1], link, jnp.transpose(link), edge_ref[i, 1]))
-    results = project([jnp.transpose(f) for f in found], matrices, found)
-    for i in range(layers):
-        out_ref[i, 0] = results[i].astype(BF)
+    return [jnp.transpose(f) for f in found], matrices, found
 
 
 def x_part_kernel(
@@ -240,9 +250,7 @@
         part_ref[k] = results[k]
 
 
-def x_last_kernel(
-    cells, layer, places, part_ref, lower_ref, lower_turned_ref, packed_ref, _, out_ref, held, sems
-):
+def x_last_chunk(cells, layer, n, places, part_ref, lower_ref, lower_turned_ref, packed_ref, out_ref, held, sems, more):
     slots = part_ref.shape[-1]
     half = slots // 2
     upper, same, opposite = pack_masks(slots)
@@ -253,34 +261,79 @@
     opposite_scale = jnp.where(opposite, one, zero)
     extras = packed_ref[len(places) * cells * half :].astype(F32)
     pairs = -(-cells // 2)
+    c = places[n]
+    group = range(c * cells, (c + 1) * cells)
+    schurs = []
+    for k in range(cells):
+        start = (n * cells + k) * half
+        packed = packed_ref[start : start + half].astype(F32)
+        extra = extras[n * pairs + k // 2 : n * pairs + k // 2 + 1]
+        top, low = packed * top_scale, packed * low_scale
+        if k % 2 == 0:
+            top += extra * opposite_scale
+        else:
+            low += extra * same_scale
+        tri = jnp.concatenate([top, low], axis=0).astype(BF)
+        schurs.append(tri + jnp.transpose(tri))
+    results = project(
+        [lower_turned_ref[k] for k in group] + more[0],
+        schurs + more[1],
+        [lower_ref[k] for k in group] + more[2],
+    )
+    for k in range(cells):
+        held[n * cells + k] = (part_ref[c * cells + k] + results[k]).astype(BF)
+    copy = pltpu.make_async_copy(
+        held.at[pl.ds(n * cells, cells)], out_ref.at[layer, pl.ds(c * cells, cells)], sems.at[n]
+    )
+    copy.start()
+    return copy, results[cells:]
+
+
+def x_last_kernel(
+    cells, layer, places, part_ref, lower_ref, lower_turned_ref, packed_ref, _, out_ref, held, sems
+):
     copies = []
-    for n, c in enumerate(places):
-        group = range(c * cells, (c + 1) * cells)
-        schurs = []
-        for k in range(cells):
-            start = (n * cells + k) * half
-            packed = packed_ref[start : start + half].astype(F32)
-            extra = extras[n * pairs + k // 2 : n * pairs + k // 2 + 1]
-            top, low = packed * top_scale, packed * low_scale
-            if k % 2 == 0:
-                top += extra * opposite_scale
-            else:
-                low += extra * same_scale
-            tri = jnp.concatenate([top, low], axis=0).astype(BF)
-            schurs.append(tri + jnp.transpose(tri))
-        results = project(
-            [lower_turned_ref[k] for k in group], schurs, [lower_ref[k] for k in group]
+    for n in range(len(places)):
+        copy, _ = x_last_chunk(
+            cells, layer, n, places, part_ref, lower_ref, lower_turned_ref, packed_ref, out_ref, held, sems,
+            ([], [], []),
         )
-        for k, result in enumerate(results):
-            held[n * cells + k] = (part_ref[c * cells + k] + result).astype(BF)
+        copies.append(copy)
+    for copy in copies:
+        copy.wait()
+
+
+def x_last_y_edge_kernel(
+    cells, layer, places, place, part_ref, lower_ref, lower_turned_ref, packed_ref, _,
+    rank_ref, skel_ref, interp_hbm, coup_ref, corner_ref, edge_ref, __,
+    out_ref, y_out_ref, held, sems, interp_ref, y_held, y_sems,
+):
+    layers = skel_ref.shape[0]
+    fetches = [
+        pltpu.make_async_copy(interp_hbm.at[i, place], interp_ref.at[i], y_sems.at[i])
+        for i in range(layers)
+    ]
+    for fetch in fetches:
+        fetch.start()
+    copies = []
+    for n in range(len(places)):
+        more = ([], [], [])
+        if n == len(places) - 1:
+            for fetch in fetches:
+                fetch.wait()
+            more = y_edge_parts(
+                place, rank_ref, skel_ref, [interp_ref[i] for i in range(layers)], coup_ref, corner_ref, edge_ref
+            )
+        copy, results = x_last_chunk(
+            cells, layer, n, places, part_ref, lower_ref, lower_turned_ref, packed_ref, out_ref, held, sems, more
+        )
+        copies.append(copy)
+    for i in range(layers):
+        y_held[i] = results[i].astype(BF)
         copies.append(
-            pltpu.make_async_copy(
-                held.at[pl.ds(n * cells, cells)],
-                out_ref.at[layer, pl.ds(c * cells, cells)],
-                sems.at[n],
-            )
+            pltpu.make_async_copy(y_held.at[i], y_out_ref.at[i, place], y_sems.at[layers + i])
         )
-        copies[n].start()
+        copies[-1].start()
     for copy in copies:
         copy.wait()
 
@@ -423,7 +476,6 @@
 
     last = nx - 1
     tail = nj - 1
-    group = tail // cells
 
     def last_block(*dims):
         return pl.BlockSpec((1, cells) + dims, lambda c: (last, c) + (0,) * len(dims))
@@ -453,45 +505,39 @@
         face_bytes,
     )(x_face_rank, x_face_skel, x_face_interp, x_coupling, last_turned, last_schur, top_in)
 
-    edge_in, part = lax.optimization_barrier((edge_in, part))
-    y_out = call(
-        functools.partial(y_edge_kernel, nx, tail),
-        (1,),
-        [
-            smem,
-            pl.BlockSpec((nx, cells, fslots), lambda i: (0, group, 0)),
-            pl.BlockSpec((nx, 1, rows, fslots), lambda i: (0, tail, 0, 0)),
-            pl.BlockSpec((nx, cells, half), lambda i: (0, group, 0)),
-            pl.BlockSpec((nx, 2, slots, half), lambda i: (0, 0, 0, 0)),
-            pl.BlockSpec((nx, 2, half, slots), lambda i: (0, 0, 0, 0)),
-            pl.BlockSpec(memory_space=pl.ANY),
-        ],
-        pl.BlockSpec((nx, 1, fslots, fslots), lambda i: (0, tail, 0, 0)),
-        shape((nx, nj, fslots, fslots), BF),
-        8 * unit // nj,
-        nx * face_bytes // nj,
-        {6: 0},
-    )(y_face_rank, y_face_skel, in_hbm(y_face_interp), y_coupling, corner, edge_in, y_out)
-
-    for places, arrived in (
-        (range(chunks - 1), packed_in),
-        (range(chunks - 1, chunks), packed_last_in),
-    ):
-        count = len(places)
-        x_out = call(
-            functools.partial(x_last_kernel, cells, last, places),
-            (),
-            [vmem, vmem, vmem, vmem, hbm],
-            hbm,
-            shape((nx, nj, fslots, fslots), BF),
-            3 * unit // nx * count // chunks,
-            nj * slots * slots * 11 * count // chunks,
-            {4: 0},
-            scratch=[
-                pltpu.VMEM((count * cells, fslots, fslots), BF),
-                pltpu.SemaphoreType.DMA((count,)),
-            ],
-        )(part, lower, lower_turned, arrived, x_out)
+    count = chunks - 1
+    out_shape = shape((nx, nj, fslots, fslots), BF)
+    x_out, y_out = call(
+        functools.partial(x_last_y_edge_kernel, cells, last, range(count), tail),
+        (),
+        [vmem, vmem, vmem, vmem, hbm, smem, vmem, hbm, vmem, vmem, vmem, hbm],
+        [hbm, hbm],
+        [out_shape, out_shape],
+        3 * unit // nx,
+        nj * slots * slots * 11,
+        {4: 0, 11: 1},
+        scratch=[
+            pltpu.VMEM((count * cells, fslots, fslots), BF),
+            pltpu.SemaphoreType.DMA((count,)),
+            pltpu.VMEM((nx, rows, fslots), BF),
+            pltpu.VMEM((nx, fslots, fslots), BF),
+            pltpu.SemaphoreType.DMA((2 * nx,)),
+        ],
+    )(
+        part, lower, lower_turned, packed_in, x_out,
+        y_face_rank, y_face_skel, in_hbm(y_face_interp), y_coupling, corner, edge_in, y_out,
+    )
+    x_out = call(
+        functools.partial(x_last_kernel, cells, last, range(count, chunks)),
+        (),
+        [vmem, vmem, vmem, vmem, hbm],
+        hbm,
+        out_shape,
+        3 * unit // nx // chunks,
+        nj * slots * slots * 11 // chunks,
+        {4: 0},
+        scratch=[pltpu.VMEM((cells, fslots, fslots), BF), pltpu.SemaphoreType.DMA((1,))],
+    )(part, lower, lower_turned, packed_last_in, x_out)
     return (x_out, y_out)
 
 

time: 43 us -> 43.7 us (1.016)
  waiting for transfers between devices: 6.54 us -> 8.01 us
  Pallas kernels: 30.1 us -> 29.3 us
    ppermute x4, waiting for transfers between devices: 6.54 us -> 8.01 us  [passed_along(): return lax.ppermute(x, axis, pairs)]
    pallas_call x3 -> x2, Pallas kernels: 4.84 us -> 3.87 us  [the longest x1 2.74 us: body(): call(functools.partial(x_last_y_edge_kernel, cells, last, range(count), t...]
  transfers between devices with their start and end apart: 4 -> 4, of which waited for: 3 -> 2; matrix products, arithmetic and copies ran while one was open for 0% -> 0% of each run, Pallas kernels for 65% -> 62%
where the time goes in v7:
time: 43.7 us; the launch traced here: 43.3 us
  Pallas kernels  29.3 us (67%)
  waiting for transfers between devices  8.01 us (18%)
  starting transfers between devices  5.16 us (12%)
  between operations  0.8 us (2%)
    pallas_call x1, Pallas kernels, body(): call(functools.partial(main_kernel, cells, nx, chunks), (nx, chunks), [sm...  19.1 us
    ppermute x4, waiting for transfers between devices, passed_along(): return lax.ppermute(x, axis, pairs)  8.01 us
    ppermute x4, starting transfers between devices, passed_along(): return lax.ppermute(x, axis, pairs)  5.16 us
    pallas_call x1, Pallas kernels, body(): call(functools.partial(x_part_kernel, cells, last), (chunks,), [smem, las...  4.98 us
    pallas_call x1, Pallas kernels, body(): call(functools.partial(x_last_y_edge_kernel, cells, last, range(count), t...  2.74 us
    pallas_call x1, Pallas kernels, body(): call(functools.partial(top_kernel, cells), (), [hbm, hbm, hbm], vmem, sha...  1.35 us
    pallas_call x1, Pallas kernels, body(): call(functools.partial(x_last_kernel, cells, last, range(count, chunks)),...  1.13 us
  transfers between devices with their start and end apart: 4, of which 2 were waited for; matrix products, arithmetic and copies ran while one was open for 0% of the time, Pallas kernels for 62%

profile of v7, /device:TPU:0, one launch (start us, length us, event | category | flops | bytes accessed | tf_op | source)
XLA Modules:
  0.0 43.3 jit_solution(3775156676397337905)
XLA Ops:
  0.6 0.0 copy-start.6
  0.6 0.0 copy-start.5
  0.7 0.0 copy-start.7
  0.7 1.3 %shard_map.132 = bf16[32,128,128]{2,1,0:T(8,128)(2,1)S(1)} custom-call(s32[2,32]{1,0:T(2,128)} %rank_hbm.1, s32[2,32,128]{2,1,0:T(8,128)} %skel_hbm.1, bf16[2,32,256,128]{3,2,1,0:T(8,128)(2,1)} %interp_hbm.2), custom_call_target="tpu_custom_call" | custom-call | bytes 2097152 | tf_op jit(solution)/shard_map/pallas_call | solution.py:384
  2.0 0.0 copy-start.1
  2.0 0.0 copy-start.3
  2.0 1.3 %collective-permute-start = (bf16[32,128,128]{2,1,0:T(8,128)(2,1)S(1)}, bf16[32,128,128]{2,1,0:T(8,128)(2,1)S(1)}, u32[]{:S(2)}, u32[]{:S(2)}) collective-permute-start(bf16[32,128,128]{2,1,0:T(8,128)(2,1)S(1)} %shard_map.132), channel_id=1, source_target_pairs={{4,0},{8,4},{12,8},{16,12},{20,16},{24,20},{28,24},{5,1},{9,5},{13... | collective-permute-start | bytes 3145736 | tf_op jit(solution)/shard_map/ppermute | solution.py:18
  3.3 0.0 copy-done.6
  3.4 0.0 copy-done.5
  3.4 0.0 copy-done.7
  3.4 0.0 copy-start
  3.4 19.1 %shard_map.131 = (bf16[2,32,128,128]{3,2,1,0:T(8,128)(2,1)}, bf16[2,32,128,128]{3,2,1,0:T(8,128)(2,1)}, bf16[1552,128]{1,0:T(8,128)(2,1)S(1)}, bf16[528,128]{1,0...) custom-call(s32[2,32]{1,0:T(2,128)S(1)} %copy-done.6, ...), custom_call_target="tpu_custom_call" | custom-call | flops 5368709120 | bytes 27262976 | tf_op jit(solution)/shard_map/pallas_call | solution.py:430
  22.5 1.3 %collective-permute-start.2 = (bf16[1552,128]{1,0:T(8,128)(2,1)S(1)}, bf16[1552,128]{1,0:T(8,128)(2,1)S(1)}, u32[]{:S(2)}, u32[]{:S(2)}) collective-permute-start(bf16[1552,128]{1,0:T(8,128)(2,1)S(1)} %get-tuple-element.21), channel_id=1, source_target_pairs={{4,0},{8,4},{12,8},{16,12},{20,16},{24,20},{28,24},{5,1},{9,5},{13... | collective-permute-start | bytes 1191944 | tf_op jit(solution)/shard_map/ppermute | solution.py:18
  23.8 1.3 %collective-permute-start.3 = (bf16[2,2,128,128]{3,2,1,0:T(8,128)(2,1)S(1)}, bf16[2,2,128,128]{3,2,1,0:T(8,128)(2,1)S(1)}, u32[]{:S(2)}, u32[]{:S(2)}) collective-permute-start(bf16[2,2,128,128]{3,2,1,0:T(8,128)(2,1)S(1)} %get-tuple-element.24), channel_id=1, source_target_pairs={{1,0},{2,1},{3,2},{5,4},{6,5},{7,6},{9,8},{10,9},{11,10},{13,12},{... | collective-permute-start | bytes 393224 | tf_op jit(solution)/shard_map/ppermute | solution.py:18
  25.1 1.3 %collective-permute-start.1 = (bf16[528,128]{1,0:T(8,128)(2,1)S(1)}, bf16[528,128]{1,0:T(8,128)(2,1)S(1)}, u32[]{:S(2)}, u32[]{:S(2)}) collective-permute-start(bf16[528,128]{1,0:T(8,128)(2,1)S(1)} %get-tuple-element.20), channel_id=1, source_target_pairs={{4,0},{8,4},{12,8},{16,12},{20,16},{24,20},{28,24},{5,1},{9,5},{13... | collective-permute-start | bytes 405512 | tf_op jit(solution)/shard_map/ppermute | solution.py:18
  26.4 4.5 %collective-permute-done.top_ref = bf16[32,128,128]{2,1,0:T(8,128)(2,1)S(1)} collective-permute-done((bf16[32,128,128]{2,1,0:T(8,128)(2,1)S(1)}, bf16[32,128,128]{2,1,0:T(8,128)(2,1)S(1)}, u32[]{:S(2)}, u32[]{:S(2)}) %collective-permute-start) | collective-permute-done | bytes 1048608 | tf_op jit(solution)/shard_map/ppermute | solution.py:18
  30.9 0.0 copy-start.2
  30.9 0.0 copy-start.4
  30.9 5.0 %shard_map.133 = (f32[32,128,128]{2,1,0:T(8,128)S(1)}, bf16[32,128,128]{2,1,0:T(8,128)(2,1)S(1)}, bf16[32,128,128]{2,1,0:T(8,128)(2,1)S(1)}) custom-call(s32[2,32]{1,0:T(2,128)S(1)} %copy-done.7, s32[2,32,128]{2,1,0:T(8,128)S(1)} %copy-done.1, bf16[2,32,256,128]{3,2,1,0:T(8,128)(2,1)S(1)} %copy-done, bf16[2,32,128]{2,1,0:T(8,128)(2,1)S(1)} %copy-done.3, ...), custom_call_target="tpu_custom_call" | custom-call | flops 1073741824 | bytes 12582912 | tf_op jit(solution)/shard_map/pallas_call | solution.py:486
  35.9 0.0 collective-permute-done.3.edge_ref
  35.9 3.5 %collective-permute-done.2.packed_ref = bf16[1552,128]{1,0:T(8,128)(2,1)S(1)} collective-permute-done((bf16[1552,128]{1,0:T(8,128)(2,1)S(1)}, bf16[1552,128]{1,0:T(8,128)(2,1)S(1)}, u32[]{:S(2)}, u32[]{:S(2)}) %collective-permute-start.2) | collective-permute-done | bytes 397344 | tf_op jit(solution)/shard_map/ppermute | solution.py:18
  39.4 2.7 %shard_map.134 = (bf16[2,32,128,128]{3,2,1,0:T(8,128)(2,1)}, bf16[2,32,128,128]{3,2,1,0:T(8,128)(2,1)}) custom-call(f32[32,128,128]{2,1,0:T(8,128)S(1)} %get-tuple-element.17.part_ref, bf16[32,128,128]{2,1,0:T(8,128)(2,1)S(1)} %get-tuple-element.18.lower_ref, ...), custom_call_target="tpu_custom_call", output_to_operand_aliasing={{0}: (4, {}), {1}: (11, {})} | custom-call | flops 402653184 | bytes 5767168 | tf_op jit(solution)/shard_map/pallas_call | solution.py:510
  42.2 0.0 collective-permute-done.1.packed_ref
  42.2 1.1 %shard_map.135 = bf16[2,32,128,128]{3,2,1,0:T(8,128)(2,1)} custom-call(f32[32,128,128]{2,1,0:T(8,128)S(1)} %get-tuple-element.17.part_ref, bf16[32,128,128]{2,1,0:T(8,128)(2,1)S(1)} %get-tuple-element.18.lower_ref, bf16[32,128,128]{2,1,0:T(8,128)(2,1)S(1)} %get-tuple-element.19.lower_turned_ref, ...), custom_call_target="tpu_custom_call", output_to_operand_aliasing={{}: (4, {})} | custom-call | flops 100663296 | bytes 1441792 | tf_op jit(solution)/shard_map/pallas_call | solution.py:530
  (5 shorter events, 0.0 us)
Async XLA Ops:
  0.6 2.7 %copy-start.6 = (s32[2,32]{1,0:T(2,128)S(1)}, s32[2,32]{1,0:T(2,128)}, u32[]{:S(2)}) copy-start(s32[2,32]{1,0:T(2,128)} %rank_hbm.1) | copy-start | bytes 772
  0.6 2.7 %copy-start.5 = (s32[2,32]{1,0:T(2,128)S(1)}, s32[2,32]{1,0:T(2,128)}, u32[]{:S(2)}) copy-start(s32[2,32]{1,0:T(2,128)} %rank_ref.5) | copy-start | bytes 772
  0.7 2.7 %copy-start.7 = (s32[2,32]{1,0:T(2,128)S(1)}, s32[2,32]{1,0:T(2,128)}, u32[]{:S(2)}) copy-start(s32[2,32]{1,0:T(2,128)} %rank_ref.4) | copy-start | bytes 772
  2.0 28.9 %copy-start.1 = (s32[2,32,128]{2,1,0:T(8,128)S(1)}, s32[2,32,128]{2,1,0:T(8,128)}, u32[]{:S(2)}) copy-start(s32[2,32,128]{2,1,0:T(8,128)} %skel_ref.4) | copy-start | bytes 98308
  2.0 28.9 %copy-start.3 = (bf16[2,32,128]{2,1,0:T(8,128)(2,1)S(1)}, bf16[2,32,128]{2,1,0:T(8,128)(2,1)}, u32[]{:S(2)}) copy-start(bf16[2,32,128]{2,1,0:T(8,128)(2,1)} %coup_ref.2) | copy-start | bytes 49156
  2.0 28.9 %collective-permute-start = (bf16[32,128,128]{2,1,0:T(8,128)(2,1)S(1)}, bf16[32,128,128]{2,1,0:T(8,128)(2,1)S(1)}, u32[]{:S(2)}, u32[]{:S(2)}) collective-permute-start(bf16[32,128,128]{2,1,0:T(8,128)(2,1)S(1)} %shard_map.132), channel_id=1, source_target_pairs={{4,0},{8,4},{12,8},{16,12},{20,16},{24,20},{28,24},{5,1},{9,5},{13... | collective-permute-start | bytes 3145736 | tf_op jit(solution)/shard_map/ppermute | solution.py:18
  3.4 27.5 %copy-start = (bf16[2,32,256,128]{3,2,1,0:T(8,128)(2,1)S(1)}, bf16[2,32,256,128]{3,2,1,0:T(8,128)(2,1)}, u32[]{:S(2)}) copy-start(bf16[2,32,256,128]{3,2,1,0:T(8,128)(2,1)} %interp_ref.3) | copy-start | bytes 12582916
  22.5 16.9 %collective-permute-start.2 = (bf16[1552,128]{1,0:T(8,128)(2,1)S(1)}, bf16[1552,128]{1,0:T(8,128)(2,1)S(1)}, u32[]{:S(2)}, u32[]{:S(2)}) collective-permute-start(bf16[1552,128]{1,0:T(8,128)(2,1)S(1)} %get-tuple-element.21), channel_id=1, source_target_pairs={{4,0},{8,4},{12,8},{16,12},{20,16},{24,20},{28,24},{5,1},{9,5},{13... | collective-permute-start | bytes 1191944 | tf_op jit(solution)/shard_map/ppermute | solution.py:18
  23.8 12.2 %collective-permute-start.3 = (bf16[2,2,128,128]{3,2,1,0:T(8,128)(2,1)S(1)}, bf16[2,2,128,128]{3,2,1,0:T(8,128)(2,1)S(1)}, u32[]{:S(2)}, u32[]{:S(2)}) collective-permute-start(bf16[2,2,128,128]{3,2,1,0:T(8,128)(2,1)S(1)} %get-tuple-element.24), channel_id=1, source_target_pairs={{1,0},{2,1},{3,2},{5,4},{6,5},{7,6},{9,8},{10,9},{11,10},{13,12},{... | collective-permute-start | bytes 393224 | tf_op jit(solution)/shard_map/ppermute | solution.py:18
  25.1 17.1 %collective-permute-start.1 = (bf16[528,128]{1,0:T(8,128)(2,1)S(1)}, bf16[528,128]{1,0:T(8,128)(2,1)S(1)}, u32[]{:S(2)}, u32[]{:S(2)}) collective-permute-start(bf16[528,128]{1,0:T(8,128)(2,1)S(1)} %get-tuple-element.20), channel_id=1, source_target_pairs={{4,0},{8,4},{12,8},{16,12},{20,16},{24,20},{28,24},{5,1},{9,5},{13... | collective-permute-start | bytes 405512 | tf_op jit(solution)/shard_map/ppermute | solution.py:18
  30.9 8.5 %copy-start.2 = (s32[2,32,128]{2,1,0:T(8,128)S(1)}, s32[2,32,128]{2,1,0:T(8,128)}, u32[]{:S(2)}) copy-start(s32[2,32,128]{2,1,0:T(8,128)} %skel_ref.5) | copy-start | bytes 98308
  30.9 8.5 %copy-start.4 = (bf16[2,32,128]{2,1,0:T(8,128)(2,1)S(1)}, bf16[2,32,128]{2,1,0:T(8,128)(2,1)}, u32[]{:S(2)}) copy-start(bf16[2,32,128]{2,1,0:T(8,128)(2,1)} %coup_ref.3) | copy-start | bytes 49156

commit v8 on v6

--- a/solution.py
+++ b/solution.py
@@ -16,6 +16,10 @@
     devices = lax.axis_size(axis)
     pairs = [(i, i + by) for i in range(devices) if 0 <= i + by < devices]
     return lax.ppermute(x, axis, pairs)
+
+
+def dot_nt(a, b):
+    return lax.dot_general(a, b, (((1,), (1,)), ((), ())), preferred_element_type=F32)
 
 
 def dot(a, b):
@@ -31,20 +35,23 @@
     return row == picked_row, interp * live_row
 
 
-def kept_cleared(hits, interps):
-    slots = hits[0].shape[-1]
-    ones = jnp.ones((slots, slots), BF)
-    hits = [jnp.where(hit, BF(1.0), BF(0.0)) for hit in hits]
-    counts = [dot(hit, ones).astype(BF) for hit in hits]
-    return [h + z * (BF(1.0) - n) for h, z, n in zip(hits, interps, counts)]
+def kept_cleared(turned):
+    most = jnp.max(turned, axis=0, keepdims=True)
+    least = jnp.where(most.astype(F32) == 1.0, F32(1.0), F32(-2.0)).astype(BF)
+    return jnp.where(turned >= least, turned, BF(0.0))
+
+
+def marked_of(skel_row, rank, interp):
+    hit, live = marks_of(skel_row, rank, interp)
+    return jnp.where(hit, BF(1.0), live)
 
 
 def bases_of(cells, layer, first, rank_ref, skel_ref, interp_ref):
-    pairs = [
-        marks_of(skel_ref[0, k : k + 1], rank_ref[layer, first + k], interp_ref[0, k])
+    marked = [
+        marked_of(skel_ref[0, k : k + 1], rank_ref[layer, first + k], interp_ref[0, k])
         for k in range(cells)
     ]
-    return kept_cleared([p[0] for p in pairs], [p[1] for p in pairs])
+    return [kept_cleared(t) for t in [jnp.transpose(m) for m in marked]]
 
 
 def scaled(turned, conduct):
@@ -57,9 +64,9 @@
     return jnp.concatenate([upper, lower], axis=0)
 
 
-def project(turned, matrices, bases):
+def project(turned, matrices):
     inner = [dot(t, m).astype(BF) for t, m in zip(turned, matrices)]
-    return [dot(i, b) for i, b in zip(inner, bases)]
+    return [dot_nt(i, t) for i, t in zip(inner, turned)]
 
 
 def top_kernel(cells, rank_hbm, skel_hbm, interp_hbm, out_ref, rank_ref, skel_ref, held, small_sems, sems):
@@ -83,8 +90,7 @@
     for c in range(count // cells):
         copies[c].wait()
         for k in range(c * cells, (c + 1) * cells):
-            hit, interp = marks_of(skel_ref[k : k + 1], rank_ref[0, k], held[k])
-            out_ref[k] = jnp.where(hit, BF(1.0), interp)
+            out_ref[k] = marked_of(skel_ref[k : k + 1], rank_ref[0, k], held[k])
 
 
 def pack_masks(size):
@@ -102,7 +108,7 @@
     x_rank_ref, x_skel_ref, x_interp_ref, x_coup_ref,
     y_rank_ref, y_skel_ref, y_interp_ref, y_coup_ref,
     x_out_ref, y_out_ref, packed_ref, packed_last_ref, edge_ref, corner_ref, last_turned_ref, last_schur_ref,
-    store_top, store_turned, store_schur, store_extra,
+    store_turned, store_schur, store_extra,
 ):
     layer = layers - 1 - pl.program_id(0)
     chunk = chunks - 1 - pl.program_id(1)
@@ -111,30 +117,29 @@
     half = slots // 2
     top = interp_ref.shape[2] // 2
 
-    bases = bases_of(cells, layer, first, rank_ref, skel_ref, interp_ref)
-    turned = [jnp.transpose(b) for b in bases]
-    schurs = project(turned, [matrix_ref[0, k] for k in range(cells)], bases)
+    turned = bases_of(cells, layer, first, rank_ref, skel_ref, interp_ref)
+    schurs = project(turned, [matrix_ref[0, k] for k in range(cells)])
     schurs = [s.astype(BF) for s in schurs]
 
     def faces(out_ref, f_rank_ref, f_skel_ref, f_interp_ref, coup_ref, rights):
         found = bases_of(cells, layer, first, f_rank_ref, f_skel_ref, f_interp_ref)
-        found_turned = [jnp.transpose(f) for f in found]
         matrices = []
         for k in range(cells):
-            right_top, right_turned, right = rights[k]
+            right_turned, right = rights[k]
             conduct = coup_ref[0, k : k + 1]
-            link = dot(scaled(turned[k][:, top:], conduct), right_top).astype(BF)
-            link_t = dot(scaled(right_turned, conduct), bases[k][top:]).astype(BF)
+            lower = turned[k][:, top:]
+            link = dot_nt(scaled(lower, conduct), right_turned).astype(BF)
+            link_t = dot_nt(scaled(right_turned, conduct), lower).astype(BF)
             matrices.append(face_of(schurs[k], link, link_t, right))
-        results = project(found_turned, matrices, found)
+        results = project(found, matrices)
         for k in range(cells):
             out_ref[0, k] = results[k].astype(BF)
 
     def stored(place):
-        return store_top[place], store_turned[place], store_schur[place]
+        return store_turned[place], store_schur[place]
 
     after = jnp.minimum(first + cells, store_schur.shape[0] - 1)
-    rights = [(bases[k][:top], turned[k][:, :top], schurs[k]) for k in range(1, cells)]
+    rights = [(turned[k][:, :top], schurs[k]) for k in range(1, cells)]
     faces(y_out_ref, y_rank_ref, y_skel_ref, y_interp_ref, y_coup_ref, rights + [stored(after)])
 
     @pl.when(layer < layers - 1)
@@ -143,7 +148,6 @@
         faces(x_out_ref, x_rank_ref, x_skel_ref, x_interp_ref, x_coup_ref, rights)
 
     for k in range(cells):
-        store_top[first + k] = bases[k][:top]
         store_turned[first + k] = turned[k][:, :top]
         store_schur[first + k] = schurs[k]
 
@@ -190,7 +194,7 @@
 
     @pl.when(chunk == 0)
     def _():
-        edge_ref[layer, 0] = bases[0][:top]
+        edge_ref[layer, 0] = turned[0][:, :top]
         edge_ref[layer, 1] = schurs[0]
 
     @pl.when(chunk == chunks - 1)
@@ -201,47 +205,44 @@
 
 def y_edge_kernel(layers, place, rank_ref, skel_ref, interp_ref, coup_ref, corner_ref, edge_ref, _, out_ref):
     row = place % skel_ref.shape[1]
-    pairs = [
-        marks_of(skel_ref[i, row : row + 1], rank_ref[i, place], interp_ref[i, 0])
+    marked = [
+        marked_of(skel_ref[i, row : row + 1], rank_ref[i, place], interp_ref[i, 0])
         for i in range(layers)
     ]
-    found = kept_cleared([p[0] for p in pairs], [p[1] for p in pairs])
+    found = [kept_cleared(jnp.transpose(m)) for m in marked]
     matrices = []
     for i in range(layers):
-        link = dot(scaled(corner_ref[i, 0], coup_ref[i, row : row + 1]), edge_ref[i, 0]).astype(BF)
-        matrices.append(face_of(corner_ref[i, 1], link, jnp.transpose(link), edge_ref[i, 1]))
-    results = project([jnp.transpose(f) for f in found], matrices, found)
+        conduct = coup_ref[i, row : row + 1]
+        link = dot_nt(scaled(corner_ref[i, 0], conduct), edge_ref[i, 0]).astype(BF)
+        link_t = dot_nt(scaled(edge_ref[i, 0], conduct), corner_ref[i, 0]).astype(BF)
+        matrices.append(face_of(corner_ref[i, 1], link, link_t, edge_ref[i, 1]))
+    results = project(found, matrices)
     for i in range(layers):
         out_ref[i, 0] = results[i].astype(BF)
 
 
 def x_part_kernel(
     cells, layer, rank_ref, skel_ref, interp_ref, coup_ref, turned_ref, schur_ref, top_ref,
-    part_ref, lower_ref, lower_turned_ref,
+    part_ref, lower_turned_ref,
 ):
     half = top_ref.shape[-2]
     faces = bases_of(cells, layer, pl.program_id(0) * cells, rank_ref, skel_ref, interp_ref)
-    turned = [jnp.transpose(f) for f in faces]
     for k in range(cells):
-        lower_ref[k] = faces[k][half:]
-        lower_turned_ref[k] = turned[k][:, half:]
-    marked = [top_ref[k] for k in range(cells)]
-    tops = kept_cleared([m == BF(1.0) for m in marked], marked)
-    found = [
-        dot(scaled(turned_ref[k], coup_ref[0, k : k + 1]), tops[k]).astype(BF)
-        for k in range(cells)
-    ]
-    matrices = [
-        face_of(schur_ref[k], found[k], jnp.transpose(found[k]), jnp.zeros_like(found[k]))
-        for k in range(cells)
-    ]
-    results = project(turned, matrices, faces)
+        lower_turned_ref[k] = faces[k][:, half:]
+    tops = [kept_cleared(t) for t in [jnp.transpose(top_ref[k]) for k in range(cells)]]
+    matrices = []
+    for k in range(cells):
+        conduct = coup_ref[0, k : k + 1]
+        link = dot_nt(scaled(turned_ref[k], conduct), tops[k]).astype(BF)
+        link_t = dot_nt(scaled(tops[k], conduct), turned_ref[k]).astype(BF)
+        matrices.append(face_of(schur_ref[k], link, link_t, jnp.zeros_like(link)))
+    results = project(faces, matrices)
     for k in range(cells):
         part_ref[k] = results[k]
 
 
 def x_last_kernel(
-    cells, layer, places, part_ref, lower_ref, lower_turned_ref, packed_ref, _, out_ref, held, sems
+    cells, layer, places, part_ref, lower_turned_ref, packed_ref, _, out_ref, held, sems
 ):
     slots = part_ref.shape[-1]
     half = slots // 2
@@ -256,7 +257,7 @@
     copies = []
     for n, c in enumerate(places):
         group = range(c * cells, (c + 1) * cells)
-        schurs = []
+        halves = []
         for k in range(cells):
             start = (n * cells + k) * half
             packed = packed_ref[start : start + half].astype(F32)
@@ -266,11 +267,10 @@
                 top += extra * opposite_scale
             else:
                 low += extra * same_scale
-            tri = jnp.concatenate([top, low], axis=0).astype(BF)
-            schurs.append(tri + jnp.transpose(tri))
-        results = project(
-            [lower_turned_ref[k] for k in group], schurs, [lower_ref[k] for k in group]
-        )
+            halves.append(jnp.concatenate([top, low], axis=0).astype(BF))
+        turned = [lower_turned_ref[k] for k in group]
+        inner = [(dot(t, h) + dot_nt(t, h)).astype(BF) for t, h in zip(turned, halves)]
+        results = [dot_nt(i, t) for i, t in zip(inner, turned)]
         for k, result in enumerate(results):
             held[n * cells + k] = (part_ref[c * cells + k] + result).astype(BF)
         copies.append(
@@ -387,7 +387,7 @@
             down(fslots, fslots),
             whole(pack_rows(chunks - 1), slots),
             whole(pack_rows(1), slots),
-            whole(nx, 2, half, slots),
+            whole(nx, 2, slots, half),
             whole(nx, 2, slots, half),
             from_last(slots, half),
             from_last(slots, slots),
@@ -397,7 +397,7 @@
             shape((nx, nj, fslots, fslots), BF),
             shape((pack_rows(chunks - 1), slots), BF),
             shape((pack_rows(1), slots), BF),
-            shape((nx, 2, half, slots), BF),
+            shape((nx, 2, slots, half), BF),
             shape((nx, 2, slots, half), BF),
             shape((nj, slots, half), BF),
             shape((nj, slots, slots), BF),
@@ -406,7 +406,6 @@
         nx * nj * (rows * rows + 3 * rows * slots + 3 * slots * slots) * 2,
         vmem=32,
         scratch=[
-            pltpu.VMEM((nj, half, slots), BF),
             pltpu.VMEM((nj, slots, half), BF),
             pltpu.VMEM((nj, slots, slots), BF),
             pltpu.VMEM((chunks, cells, slots), F32),
@@ -431,7 +430,7 @@
     def plain(*dims):
         return pl.BlockSpec((cells,) + dims, lambda c: (c,) + (0,) * len(dims))
 
-    part, lower, lower_turned = call(
+    part, lower_turned = call(
         functools.partial(x_part_kernel, cells, last),
         (chunks,),
         [
@@ -443,10 +442,9 @@
             plain(slots, slots),
             plain(half, slots),
         ],
-        [plain(fslots, fslots), plain(slots, fslots), plain(fslots, slots)],
+        [plain(fslots, fslots), plain(fslots, slots)],
         [
             shape((nj, fslots, fslots), F32),
-            shape((nj, slots, fslots), BF),
             shape((nj, fslots, slots), BF),
         ],
         8 * unit // nx,
@@ -463,7 +461,7 @@
             pl.BlockSpec((nx, 1, rows, fslots), lambda i: (0, tail, 0, 0)),
             pl.BlockSpec((nx, cells, half), lambda i: (0, group, 0)),
             pl.BlockSpec((nx, 2, slots, half), lambda i: (0, 0, 0, 0)),
-            pl.BlockSpec((nx, 2, half, slots), lambda i: (0, 0, 0, 0)),
+            pl.BlockSpec((nx, 2, slots, half), lambda i: (0, 0, 0, 0)),
             pl.BlockSpec(memory_space=pl.ANY),
         ],
         pl.BlockSpec((nx, 1, fslots, fslots), lambda i: (0, tail, 0, 0)),
@@ -481,17 +479,17 @@
         x_out = call(
             functools.partial(x_last_kernel, cells, last, places),
             (),
-            [vmem, vmem, vmem, vmem, hbm],
+            [vmem, vmem, vmem, hbm],
             hbm,
             shape((nx, nj, fslots, fslots), BF),
             3 * unit // nx * count // chunks,
             nj * slots * slots * 11 * count // chunks,
-            {4: 0},
+            {3: 0},
             scratch=[
                 pltpu.VMEM((count * cells, fslots, fslots), BF),
                 pltpu.SemaphoreType.DMA((count,)),
             ],
-        )(part, lower, lower_turned, arrived, x_out)
+        )(part, lower_turned, arrived, x_out)
     return (x_out, y_out)
 
 

time: 43 us -> 43.4 us (level)
  waiting for transfers between devices: 6.54 us -> 8.58 us
  Pallas kernels: 30.1 us -> 28.4 us
    ppermute x4, waiting for transfers between devices: 6.54 us -> 8.58 us  [passed_along(): return lax.ppermute(x, axis, pairs)]
    pallas_call x1, Pallas kernels: 18.8 us -> 17.1 us  [body(): call(functools.partial(main_kernel, cells, nx, chunks), (nx, chunks), [sm...]
    pallas_call x2, Pallas kernels: 2.73 us -> 3.58 us  [body(): call(functools.partial(x_last_kernel, cells, last, places), (), [vmem, vm...]
    pallas_call x1, Pallas kernels: 5.03 us -> 4.33 us  [body(): call(functools.partial(x_part_kernel, cells, last), (chunks,), [smem, las...]
  transfers between devices with their start and end apart: 4 -> 4, of which waited for: 3 -> 2; matrix products, arithmetic and copies ran while one was open for 0% -> 0% of each run, Pallas kernels for 65% -> 60%
where the time goes in v8:
time: 43.4 us; the launch traced here: 43 us
  Pallas kernels  28.4 us (65%)
  waiting for transfers between devices  8.58 us (20%)
  starting transfers between devices  5.16 us (12%)
  between operations  0.81 us (2%)
    pallas_call x1, Pallas kernels, body(): call(functools.partial(main_kernel, cells, nx, chunks), (nx, chunks), [sm...  17.1 us
    ppermute x4, waiting for transfers between devices, passed_along(): return lax.ppermute(x, axis, pairs)  8.58 us
    ppermute x4, starting transfers between devices, passed_along(): return lax.ppermute(x, axis, pairs)  5.16 us
    pallas_call x1, Pallas kernels, body(): call(functools.partial(x_part_kernel, cells, last), (chunks,), [smem, las...  4.33 us
    pallas_call x2, Pallas kernels, body(): call(functools.partial(x_last_kernel, cells, last, places), (), [vmem, vm...  3.58 us
    pallas_call x1, Pallas kernels, body(): call(functools.partial(y_edge_kernel, nx, tail), (1,), [smem, pl.BlockSpe...  2.05 us
    pallas_call x1, Pallas kernels, body(): call(functools.partial(top_kernel, cells), (), [hbm, hbm, hbm], vmem, sha...  1.35 us
  transfers between devices with their start and end apart: 4, of which 2 were waited for; matrix products, arithmetic and copies ran while one was open for 0% of the time, Pallas kernels for 60%

profile of v8, /device:TPU:0, one launch (start us, length us, event | category | flops | bytes accessed | tf_op | source)
XLA Modules:
  0.0 43.0 jit_solution(10835222018383147327)
XLA Ops:
  0.6 0.0 copy-start.6
  0.6 0.0 copy-start.5
  0.7 0.0 copy-start.7
  0.7 1.3 %shard_map.132 = bf16[32,128,128]{2,1,0:T(8,128)(2,1)S(1)} custom-call(s32[2,32]{1,0:T(2,128)} %rank_hbm.1, s32[2,32,128]{2,1,0:T(8,128)} %skel_hbm.1, bf16[2,32,256,128]{3,2,1,0:T(8,128)(2,1)} %interp_hbm.1), custom_call_target="tpu_custom_call" | custom-call | bytes 2097152 | tf_op jit(solution)/shard_map/pallas_call | solution.py:331
  2.0 0.0 copy-start.1
  2.0 0.0 copy-start.3
  2.0 1.3 %collective-permute-start.1 = (bf16[32,128,128]{2,1,0:T(8,128)(2,1)S(1)}, bf16[32,128,128]{2,1,0:T(8,128)(2,1)S(1)}, u32[]{:S(2)}, u32[]{:S(2)}) collective-permute-start(bf16[32,128,128]{2,1,0:T(8,128)(2,1)S(1)} %shard_map.132), channel_id=1, source_target_pairs={{4,0},{8,4},{12,8},{16,12},{20,16},{24,20},{28,24},{5,1},{9,5},{13... | collective-permute-start | bytes 3145736 | tf_op jit(solution)/shard_map/ppermute | solution.py:18
  3.3 0.0 copy-done.6
  3.4 0.0 copy-done.5
  3.4 0.0 copy-start
  3.4 17.1 %shard_map.131 = (bf16[2,32,128,128]{3,2,1,0:T(8,128)(2,1)}, bf16[2,32,128,128]{3,2,1,0:T(8,128)(2,1)}, bf16[1552,128]{1,0:T(8,128)(2,1)S(1)}, bf16[528,128]{1,0...) custom-call(s32[2,32]{1,0:T(2,128)S(1)} %copy-done.6, ...), custom_call_target="tpu_custom_call" | custom-call | flops 5368709120 | bytes 27262976 | tf_op jit(solution)/shard_map/pallas_call | solution.py:377
  20.5 1.3 %collective-permute-start.3 = (bf16[1552,128]{1,0:T(8,128)(2,1)S(1)}, bf16[1552,128]{1,0:T(8,128)(2,1)S(1)}, u32[]{:S(2)}, u32[]{:S(2)}) collective-permute-start(bf16[1552,128]{1,0:T(8,128)(2,1)S(1)} %get-tuple-element.21), channel_id=1, source_target_pairs={{4,0},{8,4},{12,8},{16,12},{20,16},{24,20},{28,24},{5,1},{9,5},{13... | collective-permute-start | bytes 1191944 | tf_op jit(solution)/shard_map/ppermute | solution.py:18
  21.8 1.3 %collective-permute-start = (bf16[2,2,128,128]{3,2,1,0:T(8,128)(2,1)S(1)}, bf16[2,2,128,128]{3,2,1,0:T(8,128)(2,1)S(1)}, u32[]{:S(2)}, u32[]{:S(2)}) collective-permute-start(bf16[2,2,128,128]{3,2,1,0:T(8,128)(2,1)S(1)} %get-tuple-element.14), channel_id=1, source_target_pairs={{1,0},{2,1},{3,2},{5,4},{6,5},{7,6},{9,8},{10,9},{11,10},{13,12},{... | collective-permute-start | bytes 393224 | tf_op jit(solution)/shard_map/ppermute | solution.py:18
  23.1 1.3 %collective-permute-start.2 = (bf16[528,128]{1,0:T(8,128)(2,1)S(1)}, bf16[528,128]{1,0:T(8,128)(2,1)S(1)}, u32[]{:S(2)}, u32[]{:S(2)}) collective-permute-start(bf16[528,128]{1,0:T(8,128)(2,1)S(1)} %get-tuple-element.20), channel_id=1, source_target_pairs={{4,0},{8,4},{12,8},{16,12},{20,16},{24,20},{28,24},{5,1},{9,5},{13... | collective-permute-start | bytes 405512 | tf_op jit(solution)/shard_map/ppermute | solution.py:18
  24.4 6.5 %collective-permute-done.1.top_ref = bf16[32,128,128]{2,1,0:T(8,128)(2,1)S(1)} collective-permute-done((bf16[32,128,128]{2,1,0:T(8,128)(2,1)S(1)}, bf16[32,128,128]{2,1,0:T(8,128)(2,1)S(1)}, u32[]{:S(2)}, u32[]{:S(2)}) %collective-permute-start.1) | collective-permute-done | bytes 1048608 | tf_op jit(solution)/shard_map/ppermute | solution.py:18
  30.9 0.0 copy-start.2
  30.9 0.0 copy-start.4
  30.9 4.3 %shard_map.133 = (f32[32,128,128]{2,1,0:T(8,128)S(1)}, bf16[32,128,128]{2,1,0:T(8,128)(2,1)S(1)}) custom-call(s32[2,32]{1,0:T(2,128)S(1)} %copy-done.7, s32[2,32,128]{2,1,0:T(8,128)S(1)} %copy-done.1, bf16[2,32,256,128]{3,2,1,0:T(8,128)(2,1)S(1)} %copy-done, bf16[2,32,128]{2,1,0:T(8,128)(2,1)S(1)} %copy-done.3, ...), custom_call_target="tpu_custom_call" | custom-call | flops 1073741824 | bytes 12582912 | tf_op jit(solution)/shard_map/pallas_call | solution.py:433
  35.3 0.0 collective-permute-done.edge_ref
  35.3 2.1 %shard_map.136 = bf16[2,32,128,128]{3,2,1,0:T(8,128)(2,1)} custom-call(s32[2,32]{1,0:T(2,128)S(1)} %copy-done.5, s32[2,32,128]{2,1,0:T(8,128)S(1)} %copy-done.2, bf16[2,32,256,128]{3,2,1,0:T(8,128)(2,1)} %interp_ref.5, bf16[2,32,128]{2,1,0:T(8,128)(2,1)S(1)} %copy-done.4, ...), custom_call_target="tpu_custom_call", output_to_operand_aliasing={{}: (6, {})} | custom-call | flops 67108864 | bytes 786432 | tf_op jit(solution)/shard_map/pallas_call | solution.py:455
  37.3 2.1 %collective-permute-done.3.packed_ref = bf16[1552,128]{1,0:T(8,128)(2,1)S(1)} collective-permute-done((bf16[1552,128]{1,0:T(8,128)(2,1)S(1)}, bf16[1552,128]{1,0:T(8,128)(2,1)S(1)}, u32[]{:S(2)}, u32[]{:S(2)}) %collective-permute-start.3) | collective-permute-done | bytes 397344 | tf_op jit(solution)/shard_map/ppermute | solution.py:18
  39.4 2.3 %shard_map.134._ = bf16[2,32,128,128]{3,2,1,0:T(8,128)(2,1)} custom-call(f32[32,128,128]{2,1,0:T(8,128)S(1)} %get-tuple-element.18.part_ref, bf16[32,128,128]{2,1,0:T(8,128)(2,1)S(1)} %get-tuple-element.19.lower_turned_ref, bf16[1552,128]{1,0:T(8,128)(2,1)S(1)} %collective-permute-done.3.packed_ref, ...), custom_call_target="tpu_custom_call", output_to_operand_aliasing={{}: (3, {})} | custom-call | flops 301989888 | bytes 4325376 | tf_op jit(solution)/shard_map/pallas_call | solution.py:479
  41.7 0.0 collective-permute-done.2.packed_ref
  41.7 1.3 %shard_map.135 = bf16[2,32,128,128]{3,2,1,0:T(8,128)(2,1)} custom-call(f32[32,128,128]{2,1,0:T(8,128)S(1)} %get-tuple-element.18.part_ref, bf16[32,128,128]{2,1,0:T(8,128)(2,1)S(1)} %get-tuple-element.19.lower_turned_ref, bf16[528,128]{1,0:T(8,128)(2,1)S(1)} %collective-permute-done.2.packed_ref, ...), custom_call_target="tpu_custom_call", output_to_operand_aliasing={{}: (3, {})} | custom-call | flops 100663296 | bytes 1441792 | tf_op jit(solution)/shard_map/pallas_call | solution.py:479
  (6 shorter events, 0.0 us)
Async XLA Ops:
  0.6 2.7 %copy-start.6 = (s32[2,32]{1,0:T(2,128)S(1)}, s32[2,32]{1,0:T(2,128)}, u32[]{:S(2)}) copy-start(s32[2,32]{1,0:T(2,128)} %rank_hbm.1) | copy-start | bytes 772
  0.6 2.7 %copy-start.5 = (s32[2,32]{1,0:T(2,128)S(1)}, s32[2,32]{1,0:T(2,128)}, u32[]{:S(2)}) copy-start(s32[2,32]{1,0:T(2,128)} %rank_ref.5) | copy-start | bytes 772
  0.7 2.7 %copy-start.7 = (s32[2,32]{1,0:T(2,128)S(1)}, s32[2,32]{1,0:T(2,128)}, u32[]{:S(2)}) copy-start(s32[2,32]{1,0:T(2,128)} %rank_ref.4) | copy-start | bytes 772
  2.0 28.9 %copy-start.1 = (s32[2,32,128]{2,1,0:T(8,128)S(1)}, s32[2,32,128]{2,1,0:T(8,128)}, u32[]{:S(2)}) copy-start(s32[2,32,128]{2,1,0:T(8,128)} %skel_ref.4) | copy-start | bytes 98308
  2.0 28.9 %copy-start.3 = (bf16[2,32,128]{2,1,0:T(8,128)(2,1)S(1)}, bf16[2,32,128]{2,1,0:T(8,128)(2,1)}, u32[]{:S(2)}) copy-start(bf16[2,32,128]{2,1,0:T(8,128)(2,1)} %coup_ref.2) | copy-start | bytes 49156
  2.0 28.9 %collective-permute-start.1 = (bf16[32,128,128]{2,1,0:T(8,128)(2,1)S(1)}, bf16[32,128,128]{2,1,0:T(8,128)(2,1)S(1)}, u32[]{:S(2)}, u32[]{:S(2)}) collective-permute-start(bf16[32,128,128]{2,1,0:T(8,128)(2,1)S(1)} %shard_map.132), channel_id=1, source_target_pairs={{4,0},{8,4},{12,8},{16,12},{20,16},{24,20},{28,24},{5,1},{9,5},{13... | collective-permute-start | bytes 3145736 | tf_op jit(solution)/shard_map/ppermute | solution.py:18
  3.4 27.5 %copy-start = (bf16[2,32,256,128]{3,2,1,0:T(8,128)(2,1)S(1)}, bf16[2,32,256,128]{3,2,1,0:T(8,128)(2,1)}, u32[]{:S(2)}) copy-start(bf16[2,32,256,128]{3,2,1,0:T(8,128)(2,1)} %interp_ref.4) | copy-start | bytes 12582916
  20.5 18.9 %collective-permute-start.3 = (bf16[1552,128]{1,0:T(8,128)(2,1)S(1)}, bf16[1552,128]{1,0:T(8,128)(2,1)S(1)}, u32[]{:S(2)}, u32[]{:S(2)}) collective-permute-start(bf16[1552,128]{1,0:T(8,128)(2,1)S(1)} %get-tuple-element.21), channel_id=1, source_target_pairs={{4,0},{8,4},{12,8},{16,12},{20,16},{24,20},{28,24},{5,1},{9,5},{13... | collective-permute-start | bytes 1191944 | tf_op jit(solution)/shard_map/ppermute | solution.py:18
  21.8 13.5 %collective-permute-start = (bf16[2,2,128,128]{3,2,1,0:T(8,128)(2,1)S(1)}, bf16[2,2,128,128]{3,2,1,0:T(8,128)(2,1)S(1)}, u32[]{:S(2)}, u32[]{:S(2)}) collective-permute-start(bf16[2,2,128,128]{3,2,1,0:T(8,128)(2,1)S(1)} %get-tuple-element.14), channel_id=1, source_target_pairs={{1,0},{2,1},{3,2},{5,4},{6,5},{7,6},{9,8},{10,9},{11,10},{13,12},{... | collective-permute-start | bytes 393224 | tf_op jit(solution)/shard_map/ppermute | solution.py:18
  23.1 18.6 %collective-permute-start.2 = (bf16[528,128]{1,0:T(8,128)(2,1)S(1)}, bf16[528,128]{1,0:T(8,128)(2,1)S(1)}, u32[]{:S(2)}, u32[]{:S(2)}) collective-permute-start(bf16[528,128]{1,0:T(8,128)(2,1)S(1)} %get-tuple-element.20), channel_id=1, source_target_pairs={{4,0},{8,4},{12,8},{16,12},{20,16},{24,20},{28,24},{5,1},{9,5},{13... | collective-permute-start | bytes 405512 | tf_op jit(solution)/shard_map/ppermute | solution.py:18
  30.9 4.4 %copy-start.2 = (s32[2,32,128]{2,1,0:T(8,128)S(1)}, s32[2,32,128]{2,1,0:T(8,128)}, u32[]{:S(2)}) copy-start(s32[2,32,128]{2,1,0:T(8,128)} %skel_ref.5) | copy-start | bytes 98308
  30.9 4.4 %copy-start.4 = (bf16[2,32,128]{2,1,0:T(8,128)(2,1)S(1)}, bf16[2,32,128]{2,1,0:T(8,128)(2,1)}, u32[]{:S(2)}) copy-start(bf16[2,32,128]{2,1,0:T(8,128)(2,1)} %coup_ref.3) | copy-start | bytes 49156

commit v9 on v8

--- a/solution.py
+++ b/solution.py
@@ -46,9 +46,9 @@
     return jnp.where(hit, BF(1.0), live)
 
 
-def bases_of(cells, layer, first, rank_ref, skel_ref, interp_ref):
+def bases_of(cells, layer, first, rank_ref, skel, interp_ref):
     marked = [
-        marked_of(skel_ref[0, k : k + 1], rank_ref[layer, first + k], interp_ref[0, k])
+        marked_of(skel[k : k + 1], rank_ref[layer, first + k], interp_ref[0, k])
         for k in range(cells)
     ]
     return [kept_cleared(t) for t in [jnp.transpose(m) for m in marked]]
@@ -108,7 +108,7 @@
     x_rank_ref, x_skel_ref, x_interp_ref, x_coup_ref,
     y_rank_ref, y_skel_ref, y_interp_ref, y_coup_ref,
     x_out_ref, y_out_ref, packed_ref, packed_last_ref, edge_ref, corner_ref, last_turned_ref, last_schur_ref,
-    store_turned, store_schur, store_extra,
+    store_turned, store_schur, store_extra, x_coup_held, y_coup_held,
 ):
     layer = layers - 1 - pl.program_id(0)
     chunk = chunks - 1 - pl.program_id(1)
@@ -117,16 +117,24 @@
     half = slots // 2
     top = interp_ref.shape[2] // 2
 
-    turned = bases_of(cells, layer, first, rank_ref, skel_ref, interp_ref)
+    rows = pl.ds(pl.multiple_of(first, cells), cells)
+
+    @pl.when((pl.program_id(0) == 0) & (pl.program_id(1) == 0))
+    def _():
+        x_coup_held[...] = x_coup_ref[...].astype(F32)
+        y_coup_held[...] = y_coup_ref[...].astype(F32)
+
+    turned = bases_of(cells, layer, first, rank_ref, skel_ref[layer, rows], interp_ref)
     schurs = project(turned, [matrix_ref[0, k] for k in range(cells)])
     schurs = [s.astype(BF) for s in schurs]
 
-    def faces(out_ref, f_rank_ref, f_skel_ref, f_interp_ref, coup_ref, rights):
-        found = bases_of(cells, layer, first, f_rank_ref, f_skel_ref, f_interp_ref)
+    def faces(out_ref, f_rank_ref, f_skel_ref, f_interp_ref, coup_held, rights):
+        found = bases_of(cells, layer, first, f_rank_ref, f_skel_ref[layer, rows], f_interp_ref)
+        conducts = coup_held[layer, rows].astype(BF)
         matrices = []
         for k in range(cells):
             right_turned, right = rights[k]
-            conduct = coup_ref[0, k : k + 1]
+            conduct = conducts[k : k + 1]
             lower = turned[k][:, top:]
             link = dot_nt(scaled(lower, conduct), right_turned).astype(BF)
             link_t = dot_nt(scaled(right_turned, conduct), lower).astype(BF)
@@ -140,12 +148,12 @@
 
     after = jnp.minimum(first + cells, store_schur.shape[0] - 1)
     rights = [(turned[k][:, :top], schurs[k]) for k in range(1, cells)]
-    faces(y_out_ref, y_rank_ref, y_skel_ref, y_interp_ref, y_coup_ref, rights + [stored(after)])
+    faces(y_out_ref, y_rank_ref, y_skel_ref, y_interp_ref, y_coup_held, rights + [stored(after)])
 
     @pl.when(layer < layers - 1)
     def _():
         rights = [stored(first + k) for k in range(cells)]
-        faces(x_out_ref, x_rank_ref, x_skel_ref, x_interp_ref, x_coup_ref, rights)
+        faces(x_out_ref, x_rank_ref, x_skel_ref, x_interp_ref, x_coup_held, rights)
 
     for k in range(cells):
         store_turned[first + k] = turned[k][:, :top]
@@ -154,8 +162,8 @@
     @pl.when(layer == layers - 1)
     def _():
         for k in range(cells):
-            last_turned_ref[k] = turned[k][:, top:]
-            last_schur_ref[k] = schurs[k]
+            last_turned_ref[first + k] = turned[k][:, top:]
+            last_schur_ref[first + k] = schurs[k]
 
     @pl.when(layer == 0)
     def _():
@@ -226,7 +234,7 @@
     part_ref, lower_turned_ref,
 ):
     half = top_ref.shape[-2]
-    faces = bases_of(cells, layer, pl.program_id(0) * cells, rank_ref, skel_ref, interp_ref)
+    faces = bases_of(cells, layer, pl.program_id(0) * cells, rank_ref, skel_ref[0], interp_ref)
     for k in range(cells):
         lower_turned_ref[k] = faces[k][:, half:]
     tops = [kept_cleared(t) for t in [jnp.transpose(top_ref[k]) for k in range(cells)]]
@@ -257,7 +265,7 @@
     copies = []
     for n, c in enumerate(places):
         group = range(c * cells, (c + 1) * cells)
-        halves = []
+        schurs = []
         for k in range(cells):
             start = (n * cells + k) * half
             packed = packed_ref[start : start + half].astype(F32)
@@ -267,10 +275,9 @@
                 top += extra * opposite_scale
             else:
                 low += extra * same_scale
-            halves.append(jnp.concatenate([top, low], axis=0).astype(BF))
-        turned = [lower_turned_ref[k] for k in group]
-        inner = [(dot(t, h) + dot_nt(t, h)).astype(BF) for t, h in zip(turned, halves)]
-        results = [dot_nt(i, t) for i, t in zip(inner, turned)]
+            tri = jnp.concatenate([top, low], axis=0).astype(BF)
+            schurs.append(tri + jnp.transpose(tri))
+        results = project([lower_turned_ref[k] for k in group], schurs)
         for k, result in enumerate(results):
             held[n * cells + k] = (part_ref[c * cells + k] + result).astype(BF)
         copies.append(
@@ -366,31 +373,18 @@
 
         return pl.BlockSpec((1, cells) + dims, place)
 
-    def whole(*dims):
-        return pl.BlockSpec(dims, lambda i, c: (0,) * len(dims))
-
-    def from_last(*dims):
-        return pl.BlockSpec(
-            (cells,) + dims, lambda i, c: (jnp.where(i == 0, chunks - 1 - c, 0),) + (0,) * len(dims)
-        )
-
     x_out, y_out, packed, packed_last, edge, corner, last_turned, last_schur = call(
         functools.partial(main_kernel, cells, nx, chunks),
         (nx, chunks),
         [
-            smem, down(slots), down(rows, slots), down(rows, rows),
-            smem, down_x(fslots), down_x(rows, fslots), down_x(half),
-            smem, down(fslots), down(rows, fslots), down(half),
+            smem, vmem, down(rows, slots), down(rows, rows),
+            smem, vmem, down_x(rows, fslots), vmem,
+            smem, vmem, down(rows, fslots), vmem,
         ],
         [
             down_x(fslots, fslots),
             down(fslots, fslots),
-            whole(pack_rows(chunks - 1), slots),
-            whole(pack_rows(1), slots),
-            whole(nx, 2, slots, half),
-            whole(nx, 2, slots, half),
-            from_last(slots, half),
-            from_last(slots, slots),
+            vmem, vmem, vmem, vmem, vmem, vmem,
         ],
         [
             shape((nx, nj, fslots, fslots), BF),
@@ -409,11 +403,13 @@
             pltpu.VMEM((nj, slots, half), BF),
             pltpu.VMEM((nj, slots, slots), BF),
             pltpu.VMEM((chunks, cells, slots), F32),
+            pltpu.VMEM((nx, nj, half), F32),
+            pltpu.VMEM((nx, nj, half), F32),
         ],
     )(
-        cell_rank, in_hbm(cell_skel), in_hbm(cell_interp), in_hbm(cell_matrix),
-        x_face_rank, in_hbm(x_face_skel), in_hbm(x_face_interp), in_hbm(x_coupling),
-        y_face_rank, in_hbm(y_face_skel), in_hbm(y_face_interp), in_hbm(y_coupling),
+        cell_rank, cell_skel, in_hbm(cell_interp), in_hbm(cell_matrix),
+        x_face_rank, x_face_skel, in_hbm(x_face_interp), x_coupling,
+        y_face_rank, y_face_skel, in_hbm(y_face_interp), y_coupling,
     )
     edge_in = passed_along(edge, "yz", -1)
     packed_in = passed_along(packed, "gx", -1)

time: 43.4 us -> 43.1 us (level)
  Pallas kernels: 28.4 us -> 27.7 us
  waiting for transfers between devices: 8.58 us -> 9.02 us
    pallas_call x2, Pallas kernels: 3.58 us -> 3 us  [body(): call(functools.partial(x_last_kernel, cells, last, places), (), [vmem, vm...]
    ppermute x4, waiting for transfers between devices: 8.58 us -> 9.02 us  [passed_along(): return lax.ppermute(x, axis, pairs)]
  transfers between devices with their start and end apart: 4 -> 4, of which waited for: 2 -> 3; matrix products, arithmetic and copies ran while one was open for 0% -> 0% of each run, Pallas kernels for 60% -> 59%
where the time goes in v9:
time: 43.1 us; the launch traced here: 42.7 us
  Pallas kernels  27.7 us (64%)
  waiting for transfers between devices  9.02 us (21%)
  starting transfers between devices  5.16 us (12%)
  between operations  0.83 us (2%)
    pallas_call x1, Pallas kernels, body(): call(functools.partial(main_kernel, cells, nx, chunks), (nx, chunks), [sm...  16.9 us
    ppermute x4, waiting for transfers between devices, passed_along(): return lax.ppermute(x, axis, pairs)  9.02 us
    ppermute x4, starting transfers between devices, passed_along(): return lax.ppermute(x, axis, pairs)  5.16 us
    pallas_call x1, Pallas kernels, body(): call(functools.partial(x_part_kernel, cells, last), (chunks,), [smem, las...  4.3 us
    pallas_call x2, Pallas kernels, body(): call(functools.partial(x_last_kernel, cells, last, places), (), [vmem, vm...  3 us
    pallas_call x1, Pallas kernels, body(): call(functools.partial(y_edge_kernel, nx, tail), (1,), [smem, pl.BlockSpe...  2.05 us
    pallas_call x1, Pallas kernels, body(): call(functools.partial(top_kernel, cells), (), [hbm, hbm, hbm], vmem, sha...  1.39 us
  transfers between devices with their start and end apart: 4, of which 3 were waited for; matrix products, arithmetic and copies ran while one was open for 0% of the time, Pallas kernels for 59%

profile of v9, /device:TPU:0, one launch (start us, length us, event | category | flops | bytes accessed | tf_op | source)
XLA Modules:
  0.0 42.7 jit_solution(3000149314934228012)
XLA Ops:
  0.6 0.0 copy-start.7
  0.6 0.0 copy-start.1
  0.7 0.0 copy-start.6
  0.7 0.0 copy-start.3
  0.7 0.0 copy-start.8
  0.7 0.0 copy-start.2
  0.7 0.0 copy-start.5
  0.7 0.0 copy-start.4
  0.7 1.4 %shard_map.132 = bf16[32,128,128]{2,1,0:T(8,128)(2,1)S(1)} custom-call(s32[2,32]{1,0:T(2,128)} %rank_hbm.1, s32[2,32,128]{2,1,0:T(8,128)} %skel_hbm.1, bf16[2,32,256,128]{3,2,1,0:T(8,128)(2,1)} %interp_hbm.1), custom_call_target="tpu_custom_call" | custom-call | bytes 2097152 | tf_op jit(solution)/shard_map/pallas_call | solution.py:338
  2.1 1.3 %collective-permute-start.1 = (bf16[32,128,128]{2,1,0:T(8,128)(2,1)S(1)}, bf16[32,128,128]{2,1,0:T(8,128)(2,1)S(1)}, u32[]{:S(2)}, u32[]{:S(2)}) collective-permute-start(bf16[32,128,128]{2,1,0:T(8,128)(2,1)S(1)} %shard_map.132), channel_id=1, source_target_pairs={{4,0},{8,4},{12,8},{16,12},{20,16},{24,20},{28,24},{5,1},{9,5},{13... | collective-permute-start | bytes 3145736 | tf_op jit(solution)/shard_map/ppermute | solution.py:18
  3.4 0.0 copy-done.7
  3.5 0.0 copy-start
  3.5 16.9 %shard_map.131 = (bf16[2,32,128,128]{3,2,1,0:T(8,128)(2,1)}, bf16[2,32,128,128]{3,2,1,0:T(8,128)(2,1)}, bf16[1552,128]{1,0:T(8,128)(2,1)S(1)}, bf16[528,128]{1,0...) custom-call(s32[2,32]{1,0:T(2,128)S(1)} %copy-done.7, ...), custom_call_target="tpu_custom_call" | custom-call | flops 5368709120 | bytes 27262976 | tf_op jit(solution)/shard_map/pallas_call | solution.py:376
  20.4 1.3 %collective-permute-start.3 = (bf16[1552,128]{1,0:T(8,128)(2,1)S(1)}, bf16[1552,128]{1,0:T(8,128)(2,1)S(1)}, u32[]{:S(2)}, u32[]{:S(2)}) collective-permute-start(bf16[1552,128]{1,0:T(8,128)(2,1)S(1)} %get-tuple-element.21), channel_id=1, source_target_pairs={{4,0},{8,4},{12,8},{16,12},{20,16},{24,20},{28,24},{5,1},{9,5},{13... | collective-permute-start | bytes 1191944 | tf_op jit(solution)/shard_map/ppermute | solution.py:18
  21.7 1.3 %collective-permute-start = (bf16[2,2,128,128]{3,2,1,0:T(8,128)(2,1)S(1)}, bf16[2,2,128,128]{3,2,1,0:T(8,128)(2,1)S(1)}, u32[]{:S(2)}, u32[]{:S(2)}) collective-permute-start(bf16[2,2,128,128]{3,2,1,0:T(8,128)(2,1)S(1)} %get-tuple-element.14), channel_id=1, source_target_pairs={{1,0},{2,1},{3,2},{5,4},{6,5},{7,6},{9,8},{10,9},{11,10},{13,12},{... | collective-permute-start | bytes 393224 | tf_op jit(solution)/shard_map/ppermute | solution.py:18
  23.0 1.3 %collective-permute-start.2 = (bf16[528,128]{1,0:T(8,128)(2,1)S(1)}, bf16[528,128]{1,0:T(8,128)(2,1)S(1)}, u32[]{:S(2)}, u32[]{:S(2)}) collective-permute-start(bf16[528,128]{1,0:T(8,128)(2,1)S(1)} %get-tuple-element.20), channel_id=1, source_target_pairs={{4,0},{8,4},{12,8},{16,12},{20,16},{24,20},{28,24},{5,1},{9,5},{13... | collective-permute-start | bytes 405512 | tf_op jit(solution)/shard_map/ppermute | solution.py:18
  24.3 6.6 %collective-permute-done.1.top_ref = bf16[32,128,128]{2,1,0:T(8,128)(2,1)S(1)} collective-permute-done((bf16[32,128,128]{2,1,0:T(8,128)(2,1)S(1)}, bf16[32,128,128]{2,1,0:T(8,128)(2,1)S(1)}, u32[]{:S(2)}, u32[]{:S(2)}) %collective-permute-start.1) | collective-permute-done | bytes 1048608 | tf_op jit(solution)/shard_map/ppermute | solution.py:18
  31.0 4.3 %shard_map.133 = (f32[32,128,128]{2,1,0:T(8,128)S(1)}, bf16[32,128,128]{2,1,0:T(8,128)(2,1)S(1)}) custom-call(s32[2,32]{1,0:T(2,128)S(1)} %copy-done.8, s32[2,32,128]{2,1,0:T(8,128)S(1)} %copy-done.2, bf16[2,32,256,128]{3,2,1,0:T(8,128)(2,1)S(1)} %copy-done, bf16[2,32,128]{2,1,0:T(8,128)(2,1)S(1)} %copy-done.4, ...), custom_call_target="tpu_custom_call" | custom-call | flops 1073741824 | bytes 12582912 | tf_op jit(solution)/shard_map/pallas_call | solution.py:429
  35.3 0.0 collective-permute-done.edge_ref
  35.3 2.1 %shard_map.136 = bf16[2,32,128,128]{3,2,1,0:T(8,128)(2,1)} custom-call(s32[2,32]{1,0:T(2,128)S(1)} %copy-done.6, s32[2,32,128]{2,1,0:T(8,128)S(1)} %copy-done.3, bf16[2,32,256,128]{3,2,1,0:T(8,128)(2,1)} %interp_ref.5, bf16[2,32,128]{2,1,0:T(8,128)(2,1)S(1)} %copy-done.5, ...), custom_call_target="tpu_custom_call", output_to_operand_aliasing={{}: (6, {})} | custom-call | flops 67108864 | bytes 786432 | tf_op jit(solution)/shard_map/pallas_call | solution.py:451
  37.3 2.1 %collective-permute-done.3.packed_ref = bf16[1552,128]{1,0:T(8,128)(2,1)S(1)} collective-permute-done((bf16[1552,128]{1,0:T(8,128)(2,1)S(1)}, bf16[1552,128]{1,0:T(8,128)(2,1)S(1)}, u32[]{:S(2)}, u32[]{:S(2)}) %collective-permute-start.3) | collective-permute-done | bytes 397344 | tf_op jit(solution)/shard_map/ppermute | solution.py:18
  39.5 1.8 %shard_map.134._ = bf16[2,32,128,128]{3,2,1,0:T(8,128)(2,1)} custom-call(f32[32,128,128]{2,1,0:T(8,128)S(1)} %get-tuple-element.18.part_ref, bf16[32,128,128]{2,1,0:T(8,128)(2,1)S(1)} %get-tuple-element.19.lower_turned_ref, bf16[1552,128]{1,0:T(8,128)(2,1)S(1)} %collective-permute-done.3.packed_ref, ...), custom_call_target="tpu_custom_call", output_to_operand_aliasing={{}: (3, {})} | custom-call | flops 301989888 | bytes 4325376 | tf_op jit(solution)/shard_map/pallas_call | solution.py:475
  41.3 0.2 collective-permute-done.2.packed_ref
  41.5 1.2 %shard_map.135 = bf16[2,32,128,128]{3,2,1,0:T(8,128)(2,1)} custom-call(f32[32,128,128]{2,1,0:T(8,128)S(1)} %get-tuple-element.18.part_ref, bf16[32,128,128]{2,1,0:T(8,128)(2,1)S(1)} %get-tuple-element.19.lower_turned_ref, bf16[528,128]{1,0:T(8,128)(2,1)S(1)} %collective-permute-done.2.packed_ref, ...), custom_call_target="tpu_custom_call", output_to_operand_aliasing={{}: (3, {})} | custom-call | flops 100663296 | bytes 1441792 | tf_op jit(solution)/shard_map/pallas_call | solution.py:475
  (8 shorter events, 0.0 us)
Async XLA Ops:
  0.6 2.8 %copy-start.7 = (s32[2,32]{1,0:T(2,128)S(1)}, s32[2,32]{1,0:T(2,128)}, u32[]{:S(2)}) copy-start(s32[2,32]{1,0:T(2,128)} %rank_hbm.1) | copy-start | bytes 772
  0.6 2.8 %copy-start.1 = (s32[2,32,128]{2,1,0:T(8,128)S(1)}, s32[2,32,128]{2,1,0:T(8,128)}, u32[]{:S(2)}) copy-start(s32[2,32,128]{2,1,0:T(8,128)} %skel_hbm.1) | copy-start | bytes 98308
  0.7 2.8 %copy-start.6 = (s32[2,32]{1,0:T(2,128)S(1)}, s32[2,32]{1,0:T(2,128)}, u32[]{:S(2)}) copy-start(s32[2,32]{1,0:T(2,128)} %rank_ref.5) | copy-start | bytes 772
  0.7 2.8 %copy-start.3 = (s32[2,32,128]{2,1,0:T(8,128)S(1)}, s32[2,32,128]{2,1,0:T(8,128)}, u32[]{:S(2)}) copy-start(s32[2,32,128]{2,1,0:T(8,128)} %skel_ref.5) | copy-start | bytes 98308
  0.7 2.8 %copy-start.8 = (s32[2,32]{1,0:T(2,128)S(1)}, s32[2,32]{1,0:T(2,128)}, u32[]{:S(2)}) copy-start(s32[2,32]{1,0:T(2,128)} %rank_ref.4) | copy-start | bytes 772
  0.7 2.8 %copy-start.2 = (s32[2,32,128]{2,1,0:T(8,128)S(1)}, s32[2,32,128]{2,1,0:T(8,128)}, u32[]{:S(2)}) copy-start(s32[2,32,128]{2,1,0:T(8,128)} %skel_ref.4) | copy-start | bytes 98308
  0.7 2.8 %copy-start.5 = (bf16[2,32,128]{2,1,0:T(8,128)(2,1)S(1)}, bf16[2,32,128]{2,1,0:T(8,128)(2,1)}, u32[]{:S(2)}) copy-start(bf16[2,32,128]{2,1,0:T(8,128)(2,1)} %coup_ref.3) | copy-start | bytes 49156
  0.7 2.8 %copy-start.4 = (bf16[2,32,128]{2,1,0:T(8,128)(2,1)S(1)}, bf16[2,32,128]{2,1,0:T(8,128)(2,1)}, u32[]{:S(2)}) copy-start(bf16[2,32,128]{2,1,0:T(8,128)(2,1)} %coup_ref.2) | copy-start | bytes 49156
  2.1 28.9 %collective-permute-start.1 = (bf16[32,128,128]{2,1,0:T(8,128)(2,1)S(1)}, bf16[32,128,128]{2,1,0:T(8,128)(2,1)S(1)}, u32[]{:S(2)}, u32[]{:S(2)}) collective-permute-start(bf16[32,128,128]{2,1,0:T(8,128)(2,1)S(1)} %shard_map.132), channel_id=1, source_target_pairs={{4,0},{8,4},{12,8},{16,12},{20,16},{24,20},{28,24},{5,1},{9,5},{13... | collective-permute-start | bytes 3145736 | tf_op jit(solution)/shard_map/ppermute | solution.py:18
  3.5 27.5 %copy-start = (bf16[2,32,256,128]{3,2,1,0:T(8,128)(2,1)S(1)}, bf16[2,32,256,128]{3,2,1,0:T(8,128)(2,1)}, u32[]{:S(2)}) copy-start(bf16[2,32,256,128]{3,2,1,0:T(8,128)(2,1)} %interp_ref.4) | copy-start | bytes 12582916
  20.4 19.0 %collective-permute-start.3 = (bf16[1552,128]{1,0:T(8,128)(2,1)S(1)}, bf16[1552,128]{1,0:T(8,128)(2,1)S(1)}, u32[]{:S(2)}, u32[]{:S(2)}) collective-permute-start(bf16[1552,128]{1,0:T(8,128)(2,1)S(1)} %get-tuple-element.21), channel_id=1, source_target_pairs={{4,0},{8,4},{12,8},{16,12},{20,16},{24,20},{28,24},{5,1},{9,5},{13... | collective-permute-start | bytes 1191944 | tf_op jit(solution)/shard_map/ppermute | solution.py:18
  21.7 13.5 %collective-permute-start = (bf16[2,2,128,128]{3,2,1,0:T(8,128)(2,1)S(1)}, bf16[2,2,128,128]{3,2,1,0:T(8,128)(2,1)S(1)}, u32[]{:S(2)}, u32[]{:S(2)}) collective-permute-start(bf16[2,2,128,128]{3,2,1,0:T(8,128)(2,1)S(1)} %get-tuple-element.14), channel_id=1, source_target_pairs={{1,0},{2,1},{3,2},{5,4},{6,5},{7,6},{9,8},{10,9},{11,10},{13,12},{... | collective-permute-start | bytes 393224 | tf_op jit(solution)/shard_map/ppermute | solution.py:18
  23.0 18.5 %collective-permute-start.2 = (bf16[528,128]{1,0:T(8,128)(2,1)S(1)}, bf16[528,128]{1,0:T(8,128)(2,1)S(1)}, u32[]{:S(2)}, u32[]{:S(2)}) collective-permute-start(bf16[528,128]{1,0:T(8,128)(2,1)S(1)} %get-tuple-element.20), channel_id=1, source_target_pairs={{4,0},{8,4},{12,8},{16,12},{20,16},{24,20},{28,24},{5,1},{9,5},{13... | collective-permute-start | bytes 405512 | tf_op jit(solution)/shard_map/ppermute | solution.py:18

commit v10 on v9

v10 whole, which is shorter than its diff:
```python
import functools

import jax
import jax.numpy as jnp
from jax import lax
from jax.experimental import pallas as pl
from jax.experimental.pallas import tpu as pltpu
from jax.sharding import PartitionSpec as P

BF = jnp.bfloat16
F32 = jnp.float32
MIB = 1024 * 1024


def passed_along(x, axis, by):
    devices = lax.axis_size(axis)
    pairs = [(i, i + by) for i in range(devices) if 0 <= i + by < devices]
    return lax.ppermute(x, axis, pairs)


def dot_nt(a, b):
    return lax.dot_general(a, b, (((1,), (1,)), ((), ())), preferred_element_type=F32)


def dot(a, b):
    return lax.dot_general(a, b, (((1,), (0,)), ((), ())), preferred_element_type=F32)


def marked_of(skel_row, rank, interp):
    rows, slots = interp.shape
    live = lax.broadcasted_iota(jnp.int32, (1, slots), 1) < rank
    picked_row = jnp.where(live, skel_row, -1).astype(F32).astype(BF)
    row = lax.broadcasted_iota(jnp.int32, (rows, slots), 0).astype(F32).astype(BF)
    live_row = jnp.where(live, F32(1.0), F32(0.0)).astype(BF)
    return jnp.where(row == picked_row, BF(1.0), interp * live_row)


def kept_cleared(turned):
    most = jnp.max(turned, axis=0, keepdims=True)
    least = jnp.where(most.astype(F32) == 1.0, F32(1.0), F32(-2.0)).astype(BF)
    return jnp.where(turned >= least, turned, BF(0.0))


def bases_of(cells, layer, first, rank_ref, skel_ref, interp_of):
    marked = [
        marked_of(skel_ref[layer, pl.ds(first + k, 1)], rank_ref[layer, first + k], interp_of(k))
        for k in range(cells)
    ]
    return [kept_cleared(t) for t in [jnp.transpose(m) for m in marked]]


def scaled(turned, conduct):
    return turned * -conduct.astype(BF)


def face_of(left, link, link_t, right):
    upper = jnp.concatenate([left, link], axis=1)
    lower = jnp.concatenate([link_t, right], axis=1)
    return jnp.concatenate([upper, lower], axis=0)


def joined(lower, conduct, right_turned, left, right):
    link = dot_nt(scaled(lower, conduct), right_turned).astype(BF)
    link_t = dot_nt(scaled(right_turned, conduct), lower).astype(BF)
    return face_of(left, link, link_t, right)


def project(turned, matrices):
    inner = [dot(t, m).astype(BF) for t, m in zip(turned, matrices)]
    return [dot_nt(i, t) for i, t in zip(inner, turned)]


def pack_masks(size):
    half = size // 2
    row = lax.broadcasted_iota(jnp.int32, (half, size), 0)
    lane = lax.broadcasted_iota(jnp.int32, (half, size), 1)
    ahead = lane - row
    upper = (ahead >= 0) & (ahead < half)
    return upper, ahead == 0, ahead == half


def top_kernel(cells, rank_hbm, skel_hbm, interp_hbm, out_ref, rank_ref, skel_ref, held, small_sems, sems):
    count, half, _ = out_ref.shape
    small = [
        pltpu.make_async_copy(rank_hbm, rank_ref, small_sems.at[0]),
        pltpu.make_async_copy(skel_hbm, skel_ref, small_sems.at[1]),
    ]

    def fetch(c):
        group = pl.ds(c * cells, cells)
        return pltpu.make_async_copy(
            interp_hbm.at[0, group, pl.ds(0, half)], held.at[group], sems.at[c]
        )

    for copy in small:
        copy.start()
    for c in range(count // cells):
        fetch(c).start()
    for copy in small:
        copy.wait()

    def step(c, _):
        fetch(c).wait()
        for k in range(cells):
            place = c * cells + k
            out_ref[place] = marked_of(skel_ref[0, pl.ds(place, 1)], rank_ref[0, place], held[place])
        return 0

    lax.fori_loop(0, count // cells, step, 0)


def main_kernel(
    cells, layers, chunks, late,
    rank_ref, skel_ref, interp_ref, matrix_ref,
    x_rank_ref, x_skel_ref, x_interp_ref, x_coup_ref,
    y_rank_ref, y_skel_ref, y_interp_ref, y_coup_ref,
    x_out_ref, y_out_ref, packed_ref, packed_late_ref, edge_ref, corner_ref, last_turned_ref, last_schur_ref,
    store_turned, store_schur, store_extra, x_coup_held, y_coup_held,
):
    layer = layers - 1 - pl.program_id(0)
    chunk = chunks - 1 - pl.program_id(1)
    first = chunk * cells
    slots = skel_ref.shape[-1]
    half = slots // 2
    pairs = -(-cells // 2)
    top = interp_ref.shape[2] // 2

    @pl.when((pl.program_id(0) == 0) & (pl.program_id(1) == 0))
    def _():
        x_coup_held[...] = x_coup_ref[...].astype(F32)
        y_coup_held[...] = y_coup_ref[...].astype(F32)

    turned = bases_of(cells, layer, first, rank_ref, skel_ref, lambda k: interp_ref[0, k])
    schurs = project(turned, [matrix_ref[0, k] for k in range(cells)])
    schurs = [s.astype(BF) for s in schurs]

    def faces(out_ref, f_rank_ref, f_skel_ref, f_interp_ref, coup_held, rights):
        found = bases_of(cells, layer, first, f_rank_ref, f_skel_ref, lambda k: f_interp_ref[0, k])
        matrices = [
            joined(
                turned[k][:, top:], coup_held[layer, pl.ds(first + k, 1)], rights[k][0], schurs[k], rights[k][1]
            )
            for k in range(cells)
        ]
        results = project(found, matrices)
        for k in range(cells):
            out_ref[0, k] = results[k].astype(BF)

    def stored(place):
        return store_turned[place], store_schur[place]

    after = jnp.minimum(first + cells, store_schur.shape[0] - 1)
    rights = [(turned[k][:, :top], schurs[k]) for k in range(1, cells)]
    faces(y_out_ref, y_rank_ref, y_skel_ref, y_interp_ref, y_coup_held, rights + [stored(after)])

    @pl.when(layer < layers - 1)
    def _():
        rights = [stored(first + k) for k in range(cells)]
        faces(x_out_ref, x_rank_ref, x_skel_ref, x_interp_ref, x_coup_held, rights)

    for k in range(cells):
        store_turned[first + k] = turned[k][:, :top]
        store_schur[first + k] = schurs[k]

    @pl.when(layer == layers - 1)
    def _():
        for k in range(cells):
            last_turned_ref[first + k] = turned[k][:, top:]
            last_schur_ref[first + k] = schurs[k]

    @pl.when(layer == 0)
    def _():
        upper, same, opposite = pack_masks(slots)
        packs = []
        for k in range(cells):
            above, below = schurs[k][:half].astype(F32), schurs[k][half:].astype(F32)
            packs.append(jnp.where(upper, above, below).astype(BF))

        def put(ref, start):
            for k in range(cells):
                ref[pl.ds(pl.multiple_of(start + k * half, half), half)] = packs[k]

        @pl.when(chunk < chunks - late)
        def _():
            put(packed_ref, chunk * (cells * half))

        @pl.when(chunk >= chunks - late)
        def _():
            put(packed_late_ref, (chunk - (chunks - late)) * (cells * half))

        for p in range(0, cells, 2):
            extra = jnp.where(opposite, schurs[p][:half].astype(F32), F32(0.0))
            if p + 1 < cells:
                extra += jnp.where(same, schurs[p + 1][half:].astype(F32), F32(0.0))
            store_extra[chunk, p // 2 : p // 2 + 1] = jnp.sum(extra, axis=0, keepdims=True)

        @pl.when(chunk == 0)
        def _():
            for ref, places in ((packed_ref, range(chunks - late)), (packed_late_ref, range(chunks - late, chunks))):
                start = len(places) * cells * half
                rows = [store_extra[c, :pairs] for c in places]
                pad = ref.shape[0] - start - pairs * len(places)
                if pad:
                    rows.append(jnp.zeros((pad, slots), F32))
                ref[start:] = jnp.concatenate(rows, axis=0).astype(BF)

    @pl.when(chunk == 0)
    def _():
        edge_ref[layer, 0] = turned[0][:, :top]
        edge_ref[layer, 1] = schurs[0]

    @pl.when(chunk == chunks - 1)
    def _():
        corner_ref[layer, 0] = turned[cells - 1][:, top:]
        corner_ref[layer, 1] = schurs[cells - 1]


def y_edge_kernel(layers, place, rank_ref, skel_ref, interp_ref, coup_ref, corner_ref, edge_ref, _, out_ref):
    marked = [
        marked_of(skel_ref[i, place : place + 1], rank_ref[i, place], interp_ref[i, 0])
        for i in range(layers)
    ]
    found = [kept_cleared(jnp.transpose(m)) for m in marked]
    matrices = [
        joined(corner_ref[i, 0], coup_ref[i, place : place + 1], edge_ref[i, 0], corner_ref[i, 1], edge_ref[i, 1])
        for i in range(layers)
    ]
    results = project(found, matrices)
    for i in range(layers):
        out_ref[i, 0] = results[i].astype(BF)


def x_part_kernel(
    cells, layer, rank_ref, skel_ref, interp_ref, coup_ref, turned_ref, schur_ref, top_ref,
    part_ref, lower_ref, coup_held,
):
    first = pl.program_id(0) * cells
    half = top_ref.shape[-2]

    @pl.when(pl.program_id(0) == 0)
    def _():
        coup_held[...] = coup_ref[...].astype(F32)

    faces = bases_of(cells, layer, first, rank_ref, skel_ref, lambda k: interp_ref[0, k])
    for k in range(cells):
        lower_ref[first + k] = faces[k][:, half:]
    tops = [kept_cleared(t) for t in [jnp.transpose(top_ref[first + k]) for k in range(cells)]]
    nothing = jnp.zeros(schur_ref.shape[1:], BF)
    matrices = [
        joined(
            turned_ref[first + k], coup_held[layer, pl.ds(first + k, 1)], tops[k], schur_ref[first + k], nothing
        )
        for k in range(cells)
    ]
    results = project(faces, matrices)
    for k in range(cells):
        part_ref[first + k] = results[k]


def x_last_kernel(
    cells, layer, begin, end, part_ref, lower_ref, packed_ref, _, out_ref, held, extra_ref, sems
):
    slots = part_ref.shape[-1]
    half = slots // 2
    pairs = -(-cells // 2)
    upper, same, opposite = pack_masks(slots)
    one, zero, mid = F32(1.0), F32(0.0), F32(0.5)
    top_scale = jnp.where(same, mid, jnp.where(upper, one, zero))
    low_scale = jnp.where(opposite, mid, jnp.where(upper, zero, one))
    same_scale = jnp.where(same, one, zero)
    opposite_scale = jnp.where(opposite, one, zero)
    extra_ref[...] = packed_ref[(end - begin) * cells * half :].astype(F32)

    def out_copy(n):
        return pltpu.make_async_copy(
            held.at[pl.ds(n * cells, cells)],
            out_ref.at[layer, pl.ds((begin + n) * cells, cells)],
            sems.at[n],
        )

    def step(n, _):
        schurs = []
        for k in range(cells):
            start = pl.multiple_of((n * cells + k) * half, half)
            packed = packed_ref[pl.ds(start, half)].astype(F32)
            extra = extra_ref[pl.ds(n * pairs + k // 2, 1)]
            top, low = packed * top_scale, packed * low_scale
            if k % 2 == 0:
                top += extra * opposite_scale
            else:
                low += extra * same_scale
            tri = jnp.concatenate([top, low], axis=0).astype(BF)
            schurs.append(tri + jnp.transpose(tri))
        places = [(begin + n) * cells + k for k in range(cells)]
        results = project([lower_ref[k] for k in places], schurs)
        for k in range(cells):
            held[n * cells + k] = (part_ref[places[k]] + results[k]).astype(BF)
        out_copy(n).start()
        return 0

    lax.fori_loop(0, end - begin, step, 0)
    for n in range(end - begin):
        out_copy(n).wait()


def call(kernel, grid, in_specs, out_specs, out_shape, flops, moved, aliases=None, vmem=24, scratch=()):
    return pl.pallas_call(
        kernel,
        grid=grid,
        in_specs=in_specs,
        out_specs=out_specs,
        out_shape=out_shape,
        scratch_shapes=scratch,
        input_output_aliases=aliases or {},
        compiler_params=pltpu.CompilerParams(vmem_limit_bytes=vmem * MIB),
        cost_estimate=pl.CostEstimate(flops=flops, bytes_accessed=moved, transcendentals=0),
    )


def in_hbm(x):
    return pltpu.with_memory_space_constraint(x, pltpu.HBM)


def body(
    cell_matrix,
    x_coupling,
    y_coupling,
    cell_interp,
    cell_skel,
    cell_rank,
    x_face_interp,
    x_face_skel,
    x_face_rank,
    y_face_interp,
    y_face_skel,
    y_face_rank,
):
    nx, nj, rows, slots = cell_interp.shape
    half = rows // 2
    fslots = x_face_interp.shape[-1]
    cells = next(n for n in (4, 2, 1) if nj % n == 0 and nj > n)
    chunks = nj // cells
    late = max(1, chunks // 4)
    early = chunks - late
    last = nx - 1
    tail = nj - 1
    unit = 2 * nx * nj * slots * slots * slots
    face_bytes = nj * (4 * rows * slots + 4 * slots * slots) * 2
    smem = pl.BlockSpec(memory_space=pltpu.SMEM)
    hbm = pl.BlockSpec(memory_space=pltpu.HBM)
    vmem = pl.BlockSpec(memory_space=pltpu.VMEM)
    shape = jax.ShapeDtypeStruct
    faces_shape = shape((nx, nj, fslots, fslots), BF)

    top = call(
        functools.partial(top_kernel, cells),
        (),
        [hbm, hbm, hbm],
        vmem,
        shape((nj, half, slots), BF),
        0,
        4 * nj * half * slots,
        vmem=8,
        scratch=[
            pltpu.SMEM((nx, nj), jnp.int32),
            pltpu.VMEM((nx, nj, slots), jnp.int32),
            pltpu.VMEM((nj, half, slots), BF),
            pltpu.SemaphoreType.DMA((2,)),
            pltpu.SemaphoreType.DMA((chunks,)),
        ],
    )(in_hbm(cell_rank), in_hbm(cell_skel), in_hbm(cell_interp))
    top_in = passed_along(top, "gx", -1)

    def pack_rows(count):
        extra = count * -(-cells // 2)
        return count * cells * slots // 2 + -(-extra // 16) * 16

    near = max(nx - 2, 0)

    def down(*dims):
        zeros = (0,) * len(dims)
        return pl.BlockSpec((1, cells) + dims, lambda i, c: (nx - 1 - i, chunks - 1 - c) + zeros)

    def down_x(*dims):
        zeros = (0,) * len(dims)

        def place(i, c):
            return (jnp.minimum(nx - 1 - i, near), jnp.where(i == 0, chunks - 1, chunks - 1 - c)) + zeros

        return pl.BlockSpec((1, cells) + dims, place)

    x_out, y_out, packed, packed_late, edge, corner, last_turned, last_schur = call(
        functools.partial(main_kernel, cells, nx, chunks, late),
        (nx, chunks),
        [
            smem, vmem, down(rows, slots), down(rows, rows),
            smem, vmem, down_x(rows, fslots), vmem,
            smem, vmem, down(rows, fslots), vmem,
        ],
        [down_x(fslots, fslots), down(fslots, fslots), vmem, vmem, vmem, vmem, vmem, vmem],
        [
            faces_shape,
            faces_shape,
            shape((pack_rows(early), slots), BF),
            shape((pack_rows(late), slots), BF),
            shape((nx, 2, slots, half), BF),
            shape((nx, 2, slots, half), BF),
            shape((nj, slots, half), BF),
            shape((nj, slots, slots), BF),
        ],
        20 * unit,
        nx * nj * (rows * rows + 3 * rows * slots + 3 * slots * slots) * 2,
        vmem=32,
        scratch=[
            pltpu.VMEM((nj, slots, half), BF),
            pltpu.VMEM((nj, slots, slots), BF),
            pltpu.VMEM((chunks, 8 * -(-cells // 16), slots), F32),
            pltpu.VMEM((nx, nj, half), F32),
            pltpu.VMEM((nx, nj, half), F32),
        ],
    )(
        cell_rank, cell_skel, in_hbm(cell_interp), in_hbm(cell_matrix),
        x_face_rank, x_face_skel, in_hbm(x_face_interp), x_coupling,
        y_face_rank, y_face_skel, in_hbm(y_face_interp), y_coupling,
    )
    edge_in = passed_along(edge, "yz", -1)
    packed_in = passed_along(packed, "gx", -1)
    packed_late_in = passed_along(packed_late, "gx", -1)

    part, lower = call(
        functools.partial(x_part_kernel, cells, last),
        (chunks,),
        [
            smem, vmem, pl.BlockSpec((1, cells, rows, fslots), lambda c: (last, c, 0, 0)), vmem,
            vmem, vmem, vmem,
        ],
        [vmem, vmem],
        [shape((nj, fslots, fslots), F32), shape((nj, fslots, slots), BF)],
        8 * unit // nx,
        face_bytes,
        scratch=[pltpu.VMEM((nx, nj, half), F32)],
    )(x_face_rank, x_face_skel, in_hbm(x_face_interp), x_coupling, last_turned, last_schur, top_in)

    edge_in, part = lax.optimization_barrier((edge_in, part))
    y_out = call(
        functools.partial(y_edge_kernel, nx, tail),
        (1,),
        [
            smem, vmem, pl.BlockSpec((nx, 1, rows, fslots), lambda i: (0, tail, 0, 0)), vmem,
            vmem, vmem, pl.BlockSpec(memory_space=pl.ANY),
        ],
        pl.BlockSpec((nx, 1, fslots, fslots), lambda i: (0, tail, 0, 0)),
        faces_shape,
        8 * unit // nj,
        nx * face_bytes // nj,
        {6: 0},
    )(y_face_rank, y_face_skel, in_hbm(y_face_interp), y_coupling, corner, edge_in, y_out)

    for begin, end, arrived in ((0, early, packed_in), (early, chunks, packed_late_in)):
        count = end - begin
        x_out = call(
            functools.partial(x_last_kernel, cells, last, begin, end),
            (),
            [vmem, vmem, vmem, hbm],
            hbm,
            faces_shape,
            3 * unit // nx * count // chunks,
            nj * slots * slots * 11 * count // chunks,
            {3: 0},
            scratch=[
                pltpu.VMEM((count * cells, fslots, fslots), BF),
                pltpu.VMEM((pack_rows(count) - count * cells * slots // 2, slots), F32),
                pltpu.SemaphoreType.DMA((count,)),
            ],
        )(part, lower, arrived, x_out)
    return (x_out, y_out)


def solution(mesh):
    return jax.shard_map(
        body,
        mesh=mesh,
        in_specs=(
            P("gx", "yz", None, None),
            P("gx", "yz", None),
            P("gx", "yz", None),
            P("gx", "yz", None, None),
            P("gx", "yz", None),
            P("gx", "yz"),
            P("gx", "yz", None, None),
            P("gx", "yz", None),
            P("gx", "yz"),
            P("gx", "yz", None, None),
            P("gx", "yz", None),
            P("gx", "yz"),
        ),
        out_specs=(P("gx", "yz", None, None), P("gx", "yz", None, None)),
        check_vma=False,
    )
```

time: 43.1 us -> 51.9 us (1.20)
  the two profiles are of different devices: /device:TPU:0 before, /device:TPU:25 now
where the time goes in v10:
time: 51.9 us; the launch traced here: 51.3 us
  Pallas kernels  39 us (75%)
  starting transfers between devices  11.3 us (22%)
  between operations  0.84 us (2%)
    pallas_call x1, Pallas kernels, body(): call(functools.partial(main_kernel, cells, nx, chunks, late), (nx, chunks...  23.6 us
    ppermute x4, starting transfers between devices, passed_along(): return lax.ppermute(x, axis, pairs)  11.3 us
    pallas_call x1, Pallas kernels, body(): call(functools.partial(x_part_kernel, cells, last), (chunks,), [smem, vme...  7.35 us
    pallas_call x2, Pallas kernels, body(): call(functools.partial(x_last_kernel, cells, last, begin, end), (), [vmem...  4.44 us
    pallas_call x1, Pallas kernels, body(): call(functools.partial(y_edge_kernel, nx, tail), (1,), [smem, vmem, pl.Bl...  2.05 us
    pallas_call x1, Pallas kernels, body(): call(functools.partial(top_kernel, cells), (), [hbm, hbm, hbm], vmem, sha...  1.64 us
  transfers between devices with their start and end apart: 4, of which 0 were waited for; matrix products, arithmetic and copies ran while one was open for 0% of the time, Pallas kernels for 70%

profile of v10, /device:TPU:25, one launch (start us, length us, event | category | flops | bytes accessed | tf_op | source)
XLA Modules:
  0.0 51.3 jit_solution(15443009044248991726)
XLA Ops:
  0.6 0.0 copy-start.6
  0.6 0.0 copy-start
  0.7 1.6 %shard_map.132 = bf16[32,128,128]{2,1,0:T(8,128)(2,1)S(1)} custom-call(s32[2,32]{1,0:T(2,128)} %rank_hbm.1, s32[2,32,128]{2,1,0:T(8,128)} %skel_hbm.1, bf16[2,32,256,128]{3,2,1,0:T(8,128)(2,1)} %interp_hbm.1), custom_call_target="tpu_custom_call" | custom-call | bytes 2097152 | tf_op jit(solution)/shard_map/pallas_call | solution.py:355
  2.4 3.0 %collective-permute-start.1 = (bf16[32,128,128]{2,1,0:T(8,128)(2,1)S(1)}, bf16[32,128,128]{2,1,0:T(8,128)(2,1)S(1)}, u32[]{:S(2)}, u32[]{:S(2)}) collective-permute-start(bf16[32,128,128]{2,1,0:T(8,128)(2,1)S(1)} %shard_map.132), channel_id=1, source_target_pairs={{4,0},{8,4},{12,8},{16,12},{20,16},{24,20},{28,24},{5,1},{9,5},{13... | collective-permute-start | bytes 3145736 | tf_op jit(solution)/shard_map/ppermute | solution.py:18
  5.4 0.0 copy-done.6
  5.4 0.0 copy-done
  5.4 0.0 copy-done.5
  5.4 0.0 copy-done.2
  5.4 0.0 copy-done.7
  5.4 0.0 copy-done.1
  5.5 0.0 copy-done.4
  5.5 0.0 copy-done.3
  5.5 23.6 %shard_map.131 = (bf16[2,32,128,128]{3,2,1,0:T(8,128)(2,1)}, bf16[2,32,128,128]{3,2,1,0:T(8,128)(2,1)}, bf16[1552,128]{1,0:T(8,128)(2,1)S(1)}, bf16[528,128]{1,0...) custom-call(s32[2,32]{1,0:T(2,128)S(1)} %copy-done.6, ...), custom_call_target="tpu_custom_call" | custom-call | flops 5368709120 | bytes 27262976 | tf_op jit(solution)/shard_map/pallas_call | solution.py:392
  29.0 2.1 %collective-permute-start.3 = (bf16[1552,128]{1,0:T(8,128)(2,1)S(1)}, bf16[1552,128]{1,0:T(8,128)(2,1)S(1)}, u32[]{:S(2)}, u32[]{:S(2)}) collective-permute-start(bf16[1552,128]{1,0:T(8,128)(2,1)S(1)} %get-tuple-element.21), channel_id=1, source_target_pairs={{4,0},{8,4},{12,8},{16,12},{20,16},{24,20},{28,24},{5,1},{9,5},{13... | collective-permute-start | bytes 1191944 | tf_op jit(solution)/shard_map/ppermute | solution.py:18
  31.2 3.1 %collective-permute-start = (bf16[2,2,128,128]{3,2,1,0:T(8,128)(2,1)S(1)}, bf16[2,2,128,128]{3,2,1,0:T(8,128)(2,1)S(1)}, u32[]{:S(2)}, u32[]{:S(2)}) collective-permute-start(bf16[2,2,128,128]{3,2,1,0:T(8,128)(2,1)S(1)} %get-tuple-element.14), channel_id=1, source_target_pairs={{1,0},{2,1},{3,2},{5,4},{6,5},{7,6},{9,8},{10,9},{11,10},{13,12},{... | collective-permute-start | bytes 393224 | tf_op jit(solution)/shard_map/ppermute | solution.py:18
  34.3 3.0 %collective-permute-start.2 = (bf16[528,128]{1,0:T(8,128)(2,1)S(1)}, bf16[528,128]{1,0:T(8,128)(2,1)S(1)}, u32[]{:S(2)}, u32[]{:S(2)}) collective-permute-start(bf16[528,128]{1,0:T(8,128)(2,1)S(1)} %get-tuple-element.20), channel_id=1, source_target_pairs={{4,0},{8,4},{12,8},{16,12},{20,16},{24,20},{28,24},{5,1},{9,5},{13... | collective-permute-start | bytes 405512 | tf_op jit(solution)/shard_map/ppermute | solution.py:18
  37.4 0.0 collective-permute-done.1.top_ref
  37.4 7.4 %shard_map.133 = (f32[32,128,128]{2,1,0:T(8,128)S(1)}, bf16[32,128,128]{2,1,0:T(8,128)(2,1)S(1)}) custom-call(s32[2,32]{1,0:T(2,128)S(1)} %copy-done.7, s32[2,32,128]{2,1,0:T(8,128)S(1)} %copy-done.1, bf16[2,32,256,128]{3,2,1,0:T(8,128)(2,1)} %interp_ref.4, bf16[2,32,128]{2,1,0:T(8,128)(2,1)S(1)} %copy-done.3, ...), custom_call_target="tpu_custom_call" | custom-call | flops 1073741824 | bytes 12582912 | tf_op jit(solution)/shard_map/pallas_call | solution.py:430
  44.8 0.0 collective-permute-done.edge_ref
  44.8 2.0 %shard_map.136 = bf16[2,32,128,128]{3,2,1,0:T(8,128)(2,1)} custom-call(s32[2,32]{1,0:T(2,128)S(1)} %copy-done.5, s32[2,32,128]{2,1,0:T(8,128)S(1)} %copy-done.2, bf16[2,32,256,128]{3,2,1,0:T(8,128)(2,1)} %interp_ref.5, bf16[2,32,128]{2,1,0:T(8,128)(2,1)S(1)} %copy-done.4, ...), custom_call_target="tpu_custom_call", output_to_operand_aliasing={{}: (6, {})} | custom-call | flops 67108864 | bytes 786432 | tf_op jit(solution)/shard_map/pallas_call | solution.py:445
  46.8 0.0 collective-permute-done.3.packed_ref
  46.8 3.0 %shard_map.134._ = bf16[2,32,128,128]{3,2,1,0:T(8,128)(2,1)} custom-call(f32[32,128,128]{2,1,0:T(8,128)S(1)} %get-tuple-element.18.part_ref, bf16[32,128,128]{2,1,0:T(8,128)(2,1)S(1)} %get-tuple-element.19.lower_ref, bf16[1552,128]{1,0:T(8,128)(2,1)S(1)} %collective-permute-done.3.packed_ref, ...), custom_call_target="tpu_custom_call", output_to_operand_aliasing={{}: (3, {})} | custom-call | flops 301989888 | bytes 4325376 | tf_op jit(solution)/shard_map/pallas_call | solution.py:461
  49.8 0.0 collective-permute-done.2.packed_ref
  49.8 1.4 %shard_map.135 = bf16[2,32,128,128]{3,2,1,0:T(8,128)(2,1)} custom-call(f32[32,128,128]{2,1,0:T(8,128)S(1)} %get-tuple-element.18.part_ref, bf16[32,128,128]{2,1,0:T(8,128)(2,1)S(1)} %get-tuple-element.19.lower_ref, bf16[528,128]{1,0:T(8,128)(2,1)S(1)} %collective-permute-done.2.packed_ref, ...), custom_call_target="tpu_custom_call", output_to_operand_aliasing={{}: (3, {})} | custom-call | flops 100663296 | bytes 1441792 | tf_op jit(solution)/shard_map/pallas_call | solution.py:461
  (6 shorter events, 0.0 us)
Async XLA Ops:
  0.6 4.8 %copy-start.6 = (s32[2,32]{1,0:T(2,128)S(1)}, s32[2,32]{1,0:T(2,128)}, u32[]{:S(2)}) copy-start(s32[2,32]{1,0:T(2,128)} %rank_hbm.1) | copy-start | bytes 772
  0.6 4.8 %copy-start = (s32[2,32,128]{2,1,0:T(8,128)S(1)}, s32[2,32,128]{2,1,0:T(8,128)}, u32[]{:S(2)}) copy-start(s32[2,32,128]{2,1,0:T(8,128)} %skel_hbm.1) | copy-start | bytes 98308
  0.7 4.8 %copy-start.5 = (s32[2,32]{1,0:T(2,128)S(1)}, s32[2,32]{1,0:T(2,128)}, u32[]{:S(2)}) copy-start(s32[2,32]{1,0:T(2,128)} %rank_ref.5) | copy-start | bytes 772
  0.7 4.8 %copy-start.2 = (s32[2,32,128]{2,1,0:T(8,128)S(1)}, s32[2,32,128]{2,1,0:T(8,128)}, u32[]{:S(2)}) copy-start(s32[2,32,128]{2,1,0:T(8,128)} %skel_ref.5) | copy-start | bytes 98308
  0.7 4.8 %copy-start.7 = (s32[2,32]{1,0:T(2,128)S(1)}, s32[2,32]{1,0:T(2,128)}, u32[]{:S(2)}) copy-start(s32[2,32]{1,0:T(2,128)} %rank_ref.4) | copy-start | bytes 772
  0.7 4.8 %copy-start.1 = (s32[2,32,128]{2,1,0:T(8,128)S(1)}, s32[2,32,128]{2,1,0:T(8,128)}, u32[]{:S(2)}) copy-start(s32[2,32,128]{2,1,0:T(8,128)} %skel_ref.4) | copy-start | bytes 98308
  0.7 4.8 %copy-start.4 = (bf16[2,32,128]{2,1,0:T(8,128)(2,1)S(1)}, bf16[2,32,128]{2,1,0:T(8,128)(2,1)}, u32[]{:S(2)}) copy-start(bf16[2,32,128]{2,1,0:T(8,128)(2,1)} %coup_ref.3) | copy-start | bytes 49156
  0.7 4.8 %copy-start.3 = (bf16[2,32,128]{2,1,0:T(8,128)(2,1)S(1)}, bf16[2,32,128]{2,1,0:T(8,128)(2,1)}, u32[]{:S(2)}) copy-start(bf16[2,32,128]{2,1,0:T(8,128)(2,1)} %coup_ref.2) | copy-start | bytes 49156
  2.4 35.0 %collective-permute-start.1 = (bf16[32,128,128]{2,1,0:T(8,128)(2,1)S(1)}, bf16[32,128,128]{2,1,0:T(8,128)(2,1)S(1)}, u32[]{:S(2)}, u32[]{:S(2)}) collective-permute-start(bf16[32,128,128]{2,1,0:T(8,128)(2,1)S(1)} %shard_map.132), channel_id=1, source_target_pairs={{4,0},{8,4},{12,8},{16,12},{20,16},{24,20},{28,24},{5,1},{9,5},{13... | collective-permute-start | bytes 3145736 | tf_op jit(solution)/shard_map/ppermute | solution.py:18
  29.0 17.8 %collective-permute-start.3 = (bf16[1552,128]{1,0:T(8,128)(2,1)S(1)}, bf16[1552,128]{1,0:T(8,128)(2,1)S(1)}, u32[]{:S(2)}, u32[]{:S(2)}) collective-permute-start(bf16[1552,128]{1,0:T(8,128)(2,1)S(1)} %get-tuple-element.21), channel_id=1, source_target_pairs={{4,0},{8,4},{12,8},{16,12},{20,16},{24,20},{28,24},{5,1},{9,5},{13... | collective-permute-start | bytes 1191944 | tf_op jit(solution)/shard_map/ppermute | solution.py:18
  31.2 13.6 %collective-permute-start = (bf16[2,2,128,128]{3,2,1,0:T(8,128)(2,1)S(1)}, bf16[2,2,128,128]{3,2,1,0:T(8,128)(2,1)S(1)}, u32[]{:S(2)}, u32[]{:S(2)}) collective-permute-start(bf16[2,2,128,128]{3,2,1,0:T(8,128)(2,1)S(1)} %get-tuple-element.14), channel_id=1, source_target_pairs={{1,0},{2,1},{3,2},{5,4},{6,5},{7,6},{9,8},{10,9},{11,10},{13,12},{... | collective-permute-start | bytes 393224 | tf_op jit(solution)/shard_map/ppermute | solution.py:18
  34.3 15.5 %collective-permute-start.2 = (bf16[528,128]{1,0:T(8,128)(2,1)S(1)}, bf16[528,128]{1,0:T(8,128)(2,1)S(1)}, u32[]{:S(2)}, u32[]{:S(2)}) collective-permute-start(bf16[528,128]{1,0:T(8,128)(2,1)S(1)} %get-tuple-element.20), channel_id=1, source_target_pairs={{4,0},{8,4},{12,8},{16,12},{20,16},{24,20},{28,24},{5,1},{9,5},{13... | collective-permute-start | bytes 405512 | tf_op jit(solution)/shard_map/ppermute | solution.py:18

commit v11 on v9

--- a/solution.py
+++ b/solution.py
@@ -72,8 +72,8 @@
 def top_kernel(cells, rank_hbm, skel_hbm, interp_hbm, out_ref, rank_ref, skel_ref, held, small_sems, sems):
     count, half, _ = out_ref.shape
     small = [
-        pltpu.make_async_copy(rank_hbm, rank_ref, small_sems.at[0]),
-        pltpu.make_async_copy(skel_hbm.at[0], skel_ref, small_sems.at[1]),
+        pltpu.make_async_copy(skel_hbm.at[0], skel_ref, small_sems.at[0]),
+        pltpu.make_async_copy(rank_hbm, rank_ref, small_sems.at[1]),
     ]
     copies = []
     for c in range(count // cells):
@@ -128,7 +128,7 @@
     schurs = project(turned, [matrix_ref[0, k] for k in range(cells)])
     schurs = [s.astype(BF) for s in schurs]
 
-    def faces(out_ref, f_rank_ref, f_skel_ref, f_interp_ref, coup_held, rights):
+    def bases_and_matrices(f_rank_ref, f_skel_ref, f_interp_ref, coup_held, rights):
         found = bases_of(cells, layer, first, f_rank_ref, f_skel_ref[layer, rows], f_interp_ref)
         conducts = coup_held[layer, rows].astype(BF)
         matrices = []
@@ -139,21 +139,30 @@
             link = dot_nt(scaled(lower, conduct), right_turned).astype(BF)
             link_t = dot_nt(scaled(right_turned, conduct), lower).astype(BF)
             matrices.append(face_of(schurs[k], link, link_t, right))
-        results = project(found, matrices)
-        for k in range(cells):
-            out_ref[0, k] = results[k].astype(BF)
+        return found, matrices
 
     def stored(place):
         return store_turned[place], store_schur[place]
 
-    after = jnp.minimum(first + cells, store_schur.shape[0] - 1)
-    rights = [(turned[k][:, :top], schurs[k]) for k in range(1, cells)]
-    faces(y_out_ref, y_rank_ref, y_skel_ref, y_interp_ref, y_coup_held, rights + [stored(after)])
+    def y_faces():
+        after = jnp.minimum(first + cells, store_schur.shape[0] - 1)
+        rights = [(turned[k][:, :top], schurs[k]) for k in range(1, cells)] + [stored(after)]
+        return bases_and_matrices(y_rank_ref, y_skel_ref, y_interp_ref, y_coup_held, rights)
+
+    @pl.when(layer == layers - 1)
+    def _():
+        for k, result in enumerate(project(*y_faces())):
+            y_out_ref[0, k] = result.astype(BF)
 
     @pl.when(layer < layers - 1)
     def _():
         rights = [stored(first + k) for k in range(cells)]
-        faces(x_out_ref, x_rank_ref, x_skel_ref, x_interp_ref, x_coup_held, rights)
+        x_found, x_matrices = bases_and_matrices(x_rank_ref, x_skel_ref, x_interp_ref, x_coup_held, rights)
+        y_found, y_matrices = y_faces()
+        results = project(x_found + y_found, x_matrices + y_matrices)
+        for k in range(cells):
+            x_out_ref[0, k] = results[k].astype(BF)
+            y_out_ref[0, k] = results[cells + k].astype(BF)
 
     for k in range(cells):
         store_turned[first + k] = turned[k][:, :top]
@@ -233,20 +242,26 @@
     cells, layer, rank_ref, skel_ref, interp_ref, coup_ref, turned_ref, schur_ref, top_ref,
     part_ref, lower_turned_ref,
 ):
-    half = top_ref.shape[-2]
-    faces = bases_of(cells, layer, pl.program_id(0) * cells, rank_ref, skel_ref[0], interp_ref)
-    for k in range(cells):
-        lower_turned_ref[k] = faces[k][:, half:]
-    tops = [kept_cleared(t) for t in [jnp.transpose(top_ref[k]) for k in range(cells)]]
-    matrices = []
-    for k in range(cells):
-        conduct = coup_ref[0, k : k + 1]
-        link = dot_nt(scaled(turned_ref[k], conduct), tops[k]).astype(BF)
-        link_t = dot_nt(scaled(tops[k], conduct), turned_ref[k]).astype(BF)
-        matrices.append(face_of(schur_ref[k], link, link_t, jnp.zeros_like(link)))
-    results = project(faces, matrices)
-    for k in range(cells):
-        part_ref[k] = results[k]
+    count, slots, half = turned_ref.shape
+    nothing = jnp.zeros((slots, slots), BF)
+    for first in range(0, count, cells):
+        group = range(first, first + cells)
+        skel = skel_ref[layer, first : first + cells]
+        marked = [
+            marked_of(skel[k - first : k - first + 1], rank_ref[layer, k], interp_ref[layer, k]) for k in group
+        ]
+        faces = [kept_cleared(t) for t in [jnp.transpose(m) for m in marked]]
+        for k in group:
+            lower_turned_ref[k] = faces[k - first][:, half:]
+        tops = [kept_cleared(t) for t in [jnp.transpose(top_ref[k]) for k in group]]
+        matrices = []
+        for k, top in zip(group, tops):
+            conduct = coup_ref[layer, k : k + 1]
+            link = dot_nt(scaled(turned_ref[k], conduct), top).astype(BF)
+            link_t = dot_nt(scaled(top, conduct), turned_ref[k]).astype(BF)
+            matrices.append(face_of(schur_ref[k], link, link_t, nothing))
+        for k, result in zip(group, project(faces, matrices)):
+            part_ref[k] = result
 
 
 def x_last_kernel(
@@ -329,14 +344,16 @@
     fslots = x_face_interp.shape[-1]
     cells = next(n for n in (8, 4, 2, 1) if nj % n == 0 and nj > n)
     chunks = nj // cells
+    face_bytes = nj * (4 * rows * slots + 4 * slots * slots) * 2
     unit = 2 * nx * nj * slots * slots * slots
     smem = pl.BlockSpec(memory_space=pltpu.SMEM)
     shape = jax.ShapeDtypeStruct
 
     hbm = pl.BlockSpec(memory_space=pltpu.HBM)
     vmem = pl.BlockSpec(memory_space=pltpu.VMEM)
+    fine = next(n for n in (4, 2, 1) if nj % n == 0)
     top = call(
-        functools.partial(top_kernel, cells),
+        functools.partial(top_kernel, fine),
         (),
         [hbm, hbm, hbm],
         vmem,
@@ -349,11 +366,15 @@
             pltpu.VMEM((nj, slots), jnp.int32),
             pltpu.VMEM((nj, half, slots), BF),
             pltpu.SemaphoreType.DMA((2,)),
-            pltpu.SemaphoreType.DMA((chunks,)),
+            pltpu.SemaphoreType.DMA((nj // fine,)),
         ],
     )(in_hbm(cell_rank), in_hbm(cell_skel), in_hbm(cell_interp))
+    (
+        top, cell_rank, cell_skel, x_coupling, y_coupling, x_face_skel, x_face_rank, y_face_skel, y_face_rank
+    ) = lax.optimization_barrier(
+        (top, cell_rank, cell_skel, x_coupling, y_coupling, x_face_skel, x_face_rank, y_face_skel, y_face_rank)
+    )
     top_in = passed_along(top, "gx", -1)
-
 
     def pack_rows(count):
         extra = count * -(-cells // 2)
@@ -414,37 +435,20 @@
     edge_in = passed_along(edge, "yz", -1)
     packed_in = passed_along(packed, "gx", -1)
     packed_last_in = passed_along(packed_last, "gx", -1)
-    face_bytes = nj * (4 * rows * slots + 4 * slots * slots) * 2
 
     last = nx - 1
     tail = nj - 1
     group = tail // cells
 
-    def last_block(*dims):
-        return pl.BlockSpec((1, cells) + dims, lambda c: (last, c) + (0,) * len(dims))
-
-    def plain(*dims):
-        return pl.BlockSpec((cells,) + dims, lambda c: (c,) + (0,) * len(dims))
-
     part, lower_turned = call(
         functools.partial(x_part_kernel, cells, last),
-        (chunks,),
-        [
-            smem,
-            last_block(fslots),
-            last_block(rows, fslots),
-            last_block(half),
-            plain(slots, half),
-            plain(slots, slots),
-            plain(half, slots),
-        ],
-        [plain(fslots, fslots), plain(fslots, slots)],
-        [
-            shape((nj, fslots, fslots), F32),
-            shape((nj, fslots, slots), BF),
-        ],
+        (),
+        [smem, vmem, vmem, vmem, vmem, vmem, vmem],
+        [vmem, vmem],
+        [shape((nj, fslots, fslots), F32), shape((nj, fslots, slots), BF)],
         8 * unit // nx,
         face_bytes,
+        vmem=16,
     )(x_face_rank, x_face_skel, x_face_interp, x_coupling, last_turned, last_schur, top_in)
 
     edge_in, part = lax.optimization_barrier((edge_in, part))

time: 43.1 us -> 43.2 us (level)
    pallas_call x1, Pallas kernels: 16.9 us -> 18.1 us  [body(): call(functools.partial(main_kernel, cells, nx, chunks), (nx, chunks), [sm...]
    pallas_call x2, Pallas kernels: 5.69 us -> 4.79 us  [the longest x1 3.24 us: body(): call(functools.partial(x_part_kernel, cells, last), (), [smem, vmem, vmem...]
where the time goes in v11:
time: 43.2 us; the launch traced here: 42.9 us
  Pallas kernels  27.9 us (65%)
  waiting for transfers between devices  8.97 us (21%)
  starting transfers between devices  5.16 us (12%)
  between operations  0.83 us (2%)
    pallas_call x1, Pallas kernels, body(): call(functools.partial(main_kernel, cells, nx, chunks), (nx, chunks), [sm...  18.1 us
    ppermute x4, waiting for transfers between devices, passed_along(): return lax.ppermute(x, axis, pairs)  8.97 us
    ppermute x4, starting transfers between devices, passed_along(): return lax.ppermute(x, axis, pairs)  5.16 us
    pallas_call x1, Pallas kernels, body(): call(functools.partial(x_part_kernel, cells, last), (), [smem, vmem, vmem...  3.24 us
    pallas_call x2, Pallas kernels, body(): call(functools.partial(x_last_kernel, cells, last, places), (), [vmem, vm...  2.99 us
    pallas_call x1, Pallas kernels, body(): call(functools.partial(y_edge_kernel, nx, tail), (1,), [smem, pl.BlockSpe...  2.05 us
    pallas_call x1, Pallas kernels, body(): call(functools.partial(top_kernel, fine), (), [hbm, hbm, hbm], vmem, shap...  1.54 us
  transfers between devices with their start and end apart: 4, of which 3 were waited for; matrix products, arithmetic and copies ran while one was open for 0% of the time, Pallas kernels for 59%

profile of v11, /device:TPU:0, one launch (start us, length us, event | category | flops | bytes accessed | tf_op | source)
XLA Modules:
  0.0 42.9 jit_solution(15831555888203397025)
XLA Ops:
  0.6 0.0 copy-start.7
  0.6 0.0 copy-start.1
  0.7 0.0 copy-start.6
  0.7 0.0 copy-start.3
  0.7 0.0 copy-start.8
  0.7 0.0 copy-start.2
  0.7 0.0 copy-start.5
  0.7 0.0 copy-start.4
  0.7 1.5 %shard_map.131 = bf16[32,128,128]{2,1,0:T(8,128)(2,1)S(1)} custom-call(s32[2,32]{1,0:T(2,128)} %rank_ref, s32[2,32,128]{2,1,0:T(8,128)} %skel_ref, bf16[2,32,256,128]{3,2,1,0:T(8,128)(2,1)} %interp_ref.3), custom_call_target="tpu_custom_call" | custom-call | bytes 2097152 | tf_op jit(solution)/shard_map/pallas_call | solution.py:355
  2.3 1.3 %collective-permute-start.1 = (bf16[32,128,128]{2,1,0:T(8,128)(2,1)S(1)}, bf16[32,128,128]{2,1,0:T(8,128)(2,1)S(1)}, u32[]{:S(2)}, u32[]{:S(2)}) collective-permute-start(bf16[32,128,128]{2,1,0:T(8,128)(2,1)S(1)} %shard_map.131), channel_id=1, source_target_pairs={{4,0},{8,4},{12,8},{16,12},{20,16},{24,20},{28,24},{5,1},{9,5},{13... | collective-permute-start | bytes 3145736 | tf_op jit(solution)/shard_map/ppermute | solution.py:18
  3.6 0.0 copy-done.7
  3.6 0.0 copy-start
  3.7 18.1 %shard_map.132 = (bf16[2,32,128,128]{3,2,1,0:T(8,128)(2,1)}, bf16[2,32,128,128]{3,2,1,0:T(8,128)(2,1)}, bf16[1552,128]{1,0:T(8,128)(2,1)S(1)}, bf16[528,128]{1,0...) custom-call(s32[2,32]{1,0:T(2,128)S(1)} %copy-done.7, ...), custom_call_target="tpu_custom_call" | custom-call | flops 5368709120 | bytes 27262976 | tf_op jit(solution)/shard_map/pallas_call | solution.py:397
  21.7 1.3 %collective-permute-start.3 = (bf16[1552,128]{1,0:T(8,128)(2,1)S(1)}, bf16[1552,128]{1,0:T(8,128)(2,1)S(1)}, u32[]{:S(2)}, u32[]{:S(2)}) collective-permute-start(bf16[1552,128]{1,0:T(8,128)(2,1)S(1)} %get-tuple-element.39), channel_id=1, source_target_pairs={{4,0},{8,4},{12,8},{16,12},{20,16},{24,20},{28,24},{5,1},{9,5},{13... | collective-permute-start | bytes 1191944 | tf_op jit(solution)/shard_map/ppermute | solution.py:18
  23.0 1.3 %collective-permute-start = (bf16[2,2,128,128]{3,2,1,0:T(8,128)(2,1)S(1)}, bf16[2,2,128,128]{3,2,1,0:T(8,128)(2,1)S(1)}, u32[]{:S(2)}, u32[]{:S(2)}) collective-permute-start(bf16[2,2,128,128]{3,2,1,0:T(8,128)(2,1)S(1)} %get-tuple-element.31), channel_id=1, source_target_pairs={{1,0},{2,1},{3,2},{5,4},{6,5},{7,6},{9,8},{10,9},{11,10},{13,12},{... | collective-permute-start | bytes 393224 | tf_op jit(solution)/shard_map/ppermute | solution.py:18
  24.3 1.3 %collective-permute-start.2 = (bf16[528,128]{1,0:T(8,128)(2,1)S(1)}, bf16[528,128]{1,0:T(8,128)(2,1)S(1)}, u32[]{:S(2)}, u32[]{:S(2)}) collective-permute-start(bf16[528,128]{1,0:T(8,128)(2,1)S(1)} %get-tuple-element.38), channel_id=1, source_target_pairs={{4,0},{8,4},{12,8},{16,12},{20,16},{24,20},{28,24},{5,1},{9,5},{13... | collective-permute-start | bytes 405512 | tf_op jit(solution)/shard_map/ppermute | solution.py:18
  25.6 5.5 %collective-permute-done.1.top_ref = bf16[32,128,128]{2,1,0:T(8,128)(2,1)S(1)} collective-permute-done((bf16[32,128,128]{2,1,0:T(8,128)(2,1)S(1)}, bf16[32,128,128]{2,1,0:T(8,128)(2,1)S(1)}, u32[]{:S(2)}, u32[]{:S(2)}) %collective-permute-start.1) | collective-permute-done | bytes 1048608 | tf_op jit(solution)/shard_map/ppermute | solution.py:18
  31.1 3.2 %shard_map.133 = (f32[32,128,128]{2,1,0:T(8,128)S(1)}, bf16[32,128,128]{2,1,0:T(8,128)(2,1)S(1)}) custom-call(s32[2,32]{1,0:T(2,128)S(1)} %copy-done.8, s32[2,32,128]{2,1,0:T(8,128)S(1)} %copy-done.2, bf16[2,32,256,128]{3,2,1,0:T(8,128)(2,1)S(1)} %copy-done, bf16[2,32,128]{2,1,0:T(8,128)(2,1)S(1)} %copy-done.4, ...), custom_call_target="tpu_custom_call" | custom-call | flops 1073741824 | bytes 12582912 | tf_op jit(solution)/shard_map/pallas_call | solution.py:443
  34.4 0.0 collective-permute-done.edge_ref
  34.4 2.1 %shard_map.136 = bf16[2,32,128,128]{3,2,1,0:T(8,128)(2,1)} custom-call(s32[2,32]{1,0:T(2,128)S(1)} %copy-done.6, s32[2,32,128]{2,1,0:T(8,128)S(1)} %copy-done.3, bf16[2,32,256,128]{3,2,1,0:T(8,128)(2,1)} %interp_ref.5, bf16[2,32,128]{2,1,0:T(8,128)(2,1)S(1)} %copy-done.5, ...), custom_call_target="tpu_custom_call", output_to_operand_aliasing={{}: (6, {})} | custom-call | flops 67108864 | bytes 786432 | tf_op jit(solution)/shard_map/pallas_call | solution.py:455
  36.4 3.2 %collective-permute-done.3.packed_ref = bf16[1552,128]{1,0:T(8,128)(2,1)S(1)} collective-permute-done((bf16[1552,128]{1,0:T(8,128)(2,1)S(1)}, bf16[1552,128]{1,0:T(8,128)(2,1)S(1)}, u32[]{:S(2)}, u32[]{:S(2)}) %collective-permute-start.3) | collective-permute-done | bytes 397344 | tf_op jit(solution)/shard_map/ppermute | solution.py:18
  39.6 1.8 %shard_map.134._ = bf16[2,32,128,128]{3,2,1,0:T(8,128)(2,1)} custom-call(f32[32,128,128]{2,1,0:T(8,128)S(1)} %get-tuple-element.36.part_ref, bf16[32,128,128]{2,1,0:T(8,128)(2,1)S(1)} %get-tuple-element.37.lower_turned_ref, bf16[1552,128]{1,0:T(8,128)(2,1)S(1)} %collective-permute-done.3.packed_ref, ...), custom_call_target="tpu_custom_call", output_to_operand_aliasing={{}: (3, {})} | custom-call | flops 301989888 | bytes 4325376 | tf_op jit(solution)/shard_map/pallas_call | solution.py:479
  41.4 0.3 collective-permute-done.2.packed_ref
  41.7 1.2 %shard_map.135 = bf16[2,32,128,128]{3,2,1,0:T(8,128)(2,1)} custom-call(f32[32,128,128]{2,1,0:T(8,128)S(1)} %get-tuple-element.36.part_ref, bf16[32,128,128]{2,1,0:T(8,128)(2,1)S(1)} %get-tuple-element.37.lower_turned_ref, bf16[528,128]{1,0:T(8,128)(2,1)S(1)} %collective-permute-done.2.packed_ref, ...), custom_call_target="tpu_custom_call", output_to_operand_aliasing={{}: (3, {})} | custom-call | flops 100663296 | bytes 1441792 | tf_op jit(solution)/shard_map/pallas_call | solution.py:479
  (8 shorter events, 0.0 us)
Async XLA Ops:
  0.6 2.9 %copy-start.7 = (s32[2,32]{1,0:T(2,128)S(1)}, s32[2,32]{1,0:T(2,128)}, u32[]{:S(2)}) copy-start(s32[2,32]{1,0:T(2,128)} %rank_ref) | copy-start | bytes 772
  0.6 2.9 %copy-start.1 = (s32[2,32,128]{2,1,0:T(8,128)S(1)}, s32[2,32,128]{2,1,0:T(8,128)}, u32[]{:S(2)}) copy-start(s32[2,32,128]{2,1,0:T(8,128)} %skel_ref) | copy-start | bytes 98308
  0.7 2.9 %copy-start.6 = (s32[2,32]{1,0:T(2,128)S(1)}, s32[2,32]{1,0:T(2,128)}, u32[]{:S(2)}) copy-start(s32[2,32]{1,0:T(2,128)} %rank_ref.2) | copy-start | bytes 772
  0.7 2.9 %copy-start.3 = (s32[2,32,128]{2,1,0:T(8,128)S(1)}, s32[2,32,128]{2,1,0:T(8,128)}, u32[]{:S(2)}) copy-start(s32[2,32,128]{2,1,0:T(8,128)} %skel_ref.2) | copy-start | bytes 98308
  0.7 2.9 %copy-start.8 = (s32[2,32]{1,0:T(2,128)S(1)}, s32[2,32]{1,0:T(2,128)}, u32[]{:S(2)}) copy-start(s32[2,32]{1,0:T(2,128)} %rank_ref.1) | copy-start | bytes 772
  0.7 2.9 %copy-start.2 = (s32[2,32,128]{2,1,0:T(8,128)S(1)}, s32[2,32,128]{2,1,0:T(8,128)}, u32[]{:S(2)}) copy-start(s32[2,32,128]{2,1,0:T(8,128)} %skel_ref.1) | copy-start | bytes 98308
  0.7 2.9 %copy-start.5 = (bf16[2,32,128]{2,1,0:T(8,128)(2,1)S(1)}, bf16[2,32,128]{2,1,0:T(8,128)(2,1)}, u32[]{:S(2)}) copy-start(bf16[2,32,128]{2,1,0:T(8,128)(2,1)} %coup_ref.1) | copy-start | bytes 49156
  0.7 2.9 %copy-start.4 = (bf16[2,32,128]{2,1,0:T(8,128)(2,1)S(1)}, bf16[2,32,128]{2,1,0:T(8,128)(2,1)}, u32[]{:S(2)}) copy-start(bf16[2,32,128]{2,1,0:T(8,128)(2,1)} %coup_ref) | copy-start | bytes 49156
  2.3 28.9 %collective-permute-start.1 = (bf16[32,128,128]{2,1,0:T(8,128)(2,1)S(1)}, bf16[32,128,128]{2,1,0:T(8,128)(2,1)S(1)}, u32[]{:S(2)}, u32[]{:S(2)}) collective-permute-start(bf16[32,128,128]{2,1,0:T(8,128)(2,1)S(1)} %shard_map.131), channel_id=1, source_target_pairs={{4,0},{8,4},{12,8},{16,12},{20,16},{24,20},{28,24},{5,1},{9,5},{13... | collective-permute-start | bytes 3145736 | tf_op jit(solution)/shard_map/ppermute | solution.py:18
  3.6 27.5 %copy-start = (bf16[2,32,256,128]{3,2,1,0:T(8,128)(2,1)S(1)}, bf16[2,32,256,128]{3,2,1,0:T(8,128)(2,1)}, u32[]{:S(2)}) copy-start(bf16[2,32,256,128]{3,2,1,0:T(8,128)(2,1)} %interp_ref.4) | copy-start | bytes 12582916
  21.7 17.9 %collective-permute-start.3 = (bf16[1552,128]{1,0:T(8,128)(2,1)S(1)}, bf16[1552,128]{1,0:T(8,128)(2,1)S(1)}, u32[]{:S(2)}, u32[]{:S(2)}) collective-permute-start(bf16[1552,128]{1,0:T(8,128)(2,1)S(1)} %get-tuple-element.39), channel_id=1, source_target_pairs={{4,0},{8,4},{12,8},{16,12},{20,16},{24,20},{28,24},{5,1},{9,5},{13... | collective-permute-start | bytes 1191944 | tf_op jit(solution)/shard_map/ppermute | solution.py:18
  23.0 11.4 %collective-permute-start = (bf16[2,2,128,128]{3,2,1,0:T(8,128)(2,1)S(1)}, bf16[2,2,128,128]{3,2,1,0:T(8,128)(2,1)S(1)}, u32[]{:S(2)}, u32[]{:S(2)}) collective-permute-start(bf16[2,2,128,128]{3,2,1,0:T(8,128)(2,1)S(1)} %get-tuple-element.31), channel_id=1, source_target_pairs={{1,0},{2,1},{3,2},{5,4},{6,5},{7,6},{9,8},{10,9},{11,10},{13,12},{... | collective-permute-start | bytes 393224 | tf_op jit(solution)/shard_map/ppermute | solution.py:18
  24.3 17.4 %collective-permute-start.2 = (bf16[528,128]{1,0:T(8,128)(2,1)S(1)}, bf16[528,128]{1,0:T(8,128)(2,1)S(1)}, u32[]{:S(2)}, u32[]{:S(2)}) collective-permute-start(bf16[528,128]{1,0:T(8,128)(2,1)S(1)} %get-tuple-element.38), channel_id=1, source_target_pairs={{4,0},{8,4},{12,8},{16,12},{20,16},{24,20},{28,24},{5,1},{9,5},{13... | collective-permute-start | bytes 405512 | tf_op jit(solution)/shard_map/ppermute | solution.py:18

commit v12 on v11

--- a/solution.py
+++ b/solution.py
@@ -72,8 +72,8 @@
 def top_kernel(cells, rank_hbm, skel_hbm, interp_hbm, out_ref, rank_ref, skel_ref, held, small_sems, sems):
     count, half, _ = out_ref.shape
     small = [
-        pltpu.make_async_copy(skel_hbm.at[0], skel_ref, small_sems.at[0]),
-        pltpu.make_async_copy(rank_hbm, rank_ref, small_sems.at[1]),
+        pltpu.make_async_copy(rank_hbm, rank_ref, small_sems.at[0]),
+        pltpu.make_async_copy(skel_hbm.at[0], skel_ref, small_sems.at[1]),
     ]
     copies = []
     for c in range(count // cells):
@@ -128,7 +128,7 @@
     schurs = project(turned, [matrix_ref[0, k] for k in range(cells)])
     schurs = [s.astype(BF) for s in schurs]
 
-    def bases_and_matrices(f_rank_ref, f_skel_ref, f_interp_ref, coup_held, rights):
+    def faces(out_ref, f_rank_ref, f_skel_ref, f_interp_ref, coup_held, rights):
         found = bases_of(cells, layer, first, f_rank_ref, f_skel_ref[layer, rows], f_interp_ref)
         conducts = coup_held[layer, rows].astype(BF)
         matrices = []
@@ -139,30 +139,21 @@
             link = dot_nt(scaled(lower, conduct), right_turned).astype(BF)
             link_t = dot_nt(scaled(right_turned, conduct), lower).astype(BF)
             matrices.append(face_of(schurs[k], link, link_t, right))
-        return found, matrices
+        results = project(found, matrices)
+        for k in range(cells):
+            out_ref[0, k] = results[k].astype(BF)
 
     def stored(place):
         return store_turned[place], store_schur[place]
 
-    def y_faces():
-        after = jnp.minimum(first + cells, store_schur.shape[0] - 1)
-        rights = [(turned[k][:, :top], schurs[k]) for k in range(1, cells)] + [stored(after)]
-        return bases_and_matrices(y_rank_ref, y_skel_ref, y_interp_ref, y_coup_held, rights)
-
-    @pl.when(layer == layers - 1)
-    def _():
-        for k, result in enumerate(project(*y_faces())):
-            y_out_ref[0, k] = result.astype(BF)
+    after = jnp.minimum(first + cells, store_schur.shape[0] - 1)
+    rights = [(turned[k][:, :top], schurs[k]) for k in range(1, cells)]
+    faces(y_out_ref, y_rank_ref, y_skel_ref, y_interp_ref, y_coup_held, rights + [stored(after)])
 
     @pl.when(layer < layers - 1)
     def _():
         rights = [stored(first + k) for k in range(cells)]
-        x_found, x_matrices = bases_and_matrices(x_rank_ref, x_skel_ref, x_interp_ref, x_coup_held, rights)
-        y_found, y_matrices = y_faces()
-        results = project(x_found + y_found, x_matrices + y_matrices)
-        for k in range(cells):
-            x_out_ref[0, k] = results[k].astype(BF)
-            y_out_ref[0, k] = results[cells + k].astype(BF)
+        faces(x_out_ref, x_rank_ref, x_skel_ref, x_interp_ref, x_coup_held, rights)
 
     for k in range(cells):
         store_turned[first + k] = turned[k][:, :top]
@@ -293,16 +284,17 @@
             tri = jnp.concatenate([top, low], axis=0).astype(BF)
             schurs.append(tri + jnp.transpose(tri))
         results = project([lower_turned_ref[k] for k in group], schurs)
-        for k, result in enumerate(results):
-            held[n * cells + k] = (part_ref[c * cells + k] + result).astype(BF)
-        copies.append(
-            pltpu.make_async_copy(
-                held.at[pl.ds(n * cells, cells)],
-                out_ref.at[layer, pl.ds(c * cells, cells)],
-                sems.at[n],
+        part_cells = max(1, cells // 2)
+        for start in range(0, cells, part_cells):
+            for k in range(start, start + part_cells):
+                held[n * cells + k] = (part_ref[c * cells + k] + results[k]).astype(BF)
+            copy = pltpu.make_async_copy(
+                held.at[pl.ds(n * cells + start, part_cells)],
+                out_ref.at[layer, pl.ds(c * cells + start, part_cells)],
+                sems.at[n, start // part_cells],
             )
-        )
-        copies[n].start()
+            copy.start()
+            copies.append(copy)
     for copy in copies:
         copy.wait()
 
@@ -344,16 +336,15 @@
     fslots = x_face_interp.shape[-1]
     cells = next(n for n in (8, 4, 2, 1) if nj % n == 0 and nj > n)
     chunks = nj // cells
-    face_bytes = nj * (4 * rows * slots + 4 * slots * slots) * 2
     unit = 2 * nx * nj * slots * slots * slots
     smem = pl.BlockSpec(memory_space=pltpu.SMEM)
     shape = jax.ShapeDtypeStruct
 
     hbm = pl.BlockSpec(memory_space=pltpu.HBM)
     vmem = pl.BlockSpec(memory_space=pltpu.VMEM)
-    fine = next(n for n in (4, 2, 1) if nj % n == 0)
+    large = next(n for n in (16, 8, 4, 2, 1) if nj % n == 0)
     top = call(
-        functools.partial(top_kernel, fine),
+        functools.partial(top_kernel, large),
         (),
         [hbm, hbm, hbm],
         vmem,
@@ -366,15 +357,11 @@
             pltpu.VMEM((nj, slots), jnp.int32),
             pltpu.VMEM((nj, half, slots), BF),
             pltpu.SemaphoreType.DMA((2,)),
-            pltpu.SemaphoreType.DMA((nj // fine,)),
+            pltpu.SemaphoreType.DMA((nj // large,)),
         ],
     )(in_hbm(cell_rank), in_hbm(cell_skel), in_hbm(cell_interp))
-    (
-        top, cell_rank, cell_skel, x_coupling, y_coupling, x_face_skel, x_face_rank, y_face_skel, y_face_rank
-    ) = lax.optimization_barrier(
-        (top, cell_rank, cell_skel, x_coupling, y_coupling, x_face_skel, x_face_rank, y_face_skel, y_face_rank)
-    )
     top_in = passed_along(top, "gx", -1)
+
 
     def pack_rows(count):
         extra = count * -(-cells // 2)
@@ -435,6 +422,7 @@
     edge_in = passed_along(edge, "yz", -1)
     packed_in = passed_along(packed, "gx", -1)
     packed_last_in = passed_along(packed_last, "gx", -1)
+    face_bytes = nj * (4 * rows * slots + 4 * slots * slots) * 2
 
     last = nx - 1
     tail = nj - 1
@@ -487,7 +475,7 @@
             {3: 0},
             scratch=[
                 pltpu.VMEM((count * cells, fslots, fslots), BF),
-                pltpu.SemaphoreType.DMA((count,)),
+                pltpu.SemaphoreType.DMA((count, 2)),
             ],
         )(part, lower_turned, arrived, x_out)
     return (x_out, y_out)

time: 43.2 us -> 43.1 us (level)
  Pallas kernels: 27.9 us -> 26.6 us
  waiting for transfers between devices: 8.97 us -> 10.1 us
    ppermute x4, waiting for transfers between devices: 8.97 us -> 10.1 us  [passed_along(): return lax.ppermute(x, axis, pairs)]
    pallas_call x1, Pallas kernels: 18.1 us -> 16.9 us  [body(): call(functools.partial(main_kernel, cells, nx, chunks), (nx, chunks), [sm...]
  transfers between devices with their start and end apart: 4 -> 4, of which waited for: 3 -> 3; matrix products, arithmetic and copies ran while one was open for 0% -> 0% of each run, Pallas kernels for 59% -> 56%
where the time goes in v12:
time: 43.1 us; the launch traced here: 42.8 us
  Pallas kernels  26.6 us (62%)
  waiting for transfers between devices  10.1 us (23%)
  starting transfers between devices  5.16 us (12%)
  between operations  0.83 us (2%)
    pallas_call x1, Pallas kernels, body(): call(functools.partial(main_kernel, cells, nx, chunks), (nx, chunks), [sm...  16.9 us
    ppermute x4, waiting for transfers between devices, passed_along(): return lax.ppermute(x, axis, pairs)  10.1 us
    ppermute x4, starting transfers between devices, passed_along(): return lax.ppermute(x, axis, pairs)  5.16 us
    pallas_call x1, Pallas kernels, body(): call(functools.partial(x_part_kernel, cells, last), (), [smem, vmem, vmem...  3.25 us
    pallas_call x2, Pallas kernels, body(): call(functools.partial(x_last_kernel, cells, last, places), (), [vmem, vm...  2.94 us
    pallas_call x1, Pallas kernels, body(): call(functools.partial(y_edge_kernel, nx, tail), (1,), [smem, pl.BlockSpe...  2.05 us
    pallas_call x1, Pallas kernels, body(): call(functools.partial(top_kernel, large), (), [hbm, hbm, hbm], vmem, sha...  1.45 us
  transfers between devices with their start and end apart: 4, of which 3 were waited for; matrix products, arithmetic and copies ran while one was open for 0% of the time, Pallas kernels for 56%

profile of v12, /device:TPU:0, one launch (start us, length us, event | category | flops | bytes accessed | tf_op | source)
XLA Modules:
  0.0 42.8 jit_solution(2924775580353142805)
XLA Ops:
  0.6 0.0 copy-start.7
  0.6 0.0 copy-start.1
  0.7 0.0 copy-start.6
  0.7 0.0 copy-start.3
  0.7 0.0 copy-start.8
  0.7 0.0 copy-start.2
  0.7 0.0 copy-start.5
  0.7 0.0 copy-start.4
  0.7 1.4 %shard_map.132 = bf16[32,128,128]{2,1,0:T(8,128)(2,1)S(1)} custom-call(s32[2,32]{1,0:T(2,128)} %rank_hbm.1, s32[2,32,128]{2,1,0:T(8,128)} %skel_hbm.1, bf16[2,32,256,128]{3,2,1,0:T(8,128)(2,1)} %interp_hbm.1), custom_call_target="tpu_custom_call" | custom-call | bytes 2097152 | tf_op jit(solution)/shard_map/pallas_call | solution.py:346
  2.2 1.3 %collective-permute-start.1 = (bf16[32,128,128]{2,1,0:T(8,128)(2,1)S(1)}, bf16[32,128,128]{2,1,0:T(8,128)(2,1)S(1)}, u32[]{:S(2)}, u32[]{:S(2)}) collective-permute-start(bf16[32,128,128]{2,1,0:T(8,128)(2,1)S(1)} %shard_map.132), channel_id=1, source_target_pairs={{4,0},{8,4},{12,8},{16,12},{20,16},{24,20},{28,24},{5,1},{9,5},{13... | collective-permute-start | bytes 3145736 | tf_op jit(solution)/shard_map/ppermute | solution.py:18
  3.5 0.0 copy-done.7
  3.5 0.0 copy-start
  3.6 16.9 %shard_map.131 = (bf16[2,32,128,128]{3,2,1,0:T(8,128)(2,1)}, bf16[2,32,128,128]{3,2,1,0:T(8,128)(2,1)}, bf16[1552,128]{1,0:T(8,128)(2,1)S(1)}, bf16[528,128]{1,0...) custom-call(s32[2,32]{1,0:T(2,128)S(1)} %copy-done.7, ...), custom_call_target="tpu_custom_call" | custom-call | flops 5368709120 | bytes 27262976 | tf_op jit(solution)/shard_map/pallas_call | solution.py:384
  20.5 1.3 %collective-permute-start.3 = (bf16[1552,128]{1,0:T(8,128)(2,1)S(1)}, bf16[1552,128]{1,0:T(8,128)(2,1)S(1)}, u32[]{:S(2)}, u32[]{:S(2)}) collective-permute-start(bf16[1552,128]{1,0:T(8,128)(2,1)S(1)} %get-tuple-element.21), channel_id=1, source_target_pairs={{4,0},{8,4},{12,8},{16,12},{20,16},{24,20},{28,24},{5,1},{9,5},{13... | collective-permute-start | bytes 1191944 | tf_op jit(solution)/shard_map/ppermute | solution.py:18
  21.8 1.3 %collective-permute-start = (bf16[2,2,128,128]{3,2,1,0:T(8,128)(2,1)S(1)}, bf16[2,2,128,128]{3,2,1,0:T(8,128)(2,1)S(1)}, u32[]{:S(2)}, u32[]{:S(2)}) collective-permute-start(bf16[2,2,128,128]{3,2,1,0:T(8,128)(2,1)S(1)} %get-tuple-element.14), channel_id=1, source_target_pairs={{1,0},{2,1},{3,2},{5,4},{6,5},{7,6},{9,8},{10,9},{11,10},{13,12},{... | collective-permute-start | bytes 393224 | tf_op jit(solution)/shard_map/ppermute | solution.py:18
  23.1 1.3 %collective-permute-start.2 = (bf16[528,128]{1,0:T(8,128)(2,1)S(1)}, bf16[528,128]{1,0:T(8,128)(2,1)S(1)}, u32[]{:S(2)}, u32[]{:S(2)}) collective-permute-start(bf16[528,128]{1,0:T(8,128)(2,1)S(1)} %get-tuple-element.20), channel_id=1, source_target_pairs={{4,0},{8,4},{12,8},{16,12},{20,16},{24,20},{28,24},{5,1},{9,5},{13... | collective-permute-start | bytes 405512 | tf_op jit(solution)/shard_map/ppermute | solution.py:18
  24.4 6.6 %collective-permute-done.1.top_ref = bf16[32,128,128]{2,1,0:T(8,128)(2,1)S(1)} collective-permute-done((bf16[32,128,128]{2,1,0:T(8,128)(2,1)S(1)}, bf16[32,128,128]{2,1,0:T(8,128)(2,1)S(1)}, u32[]{:S(2)}, u32[]{:S(2)}) %collective-permute-start.1) | collective-permute-done | bytes 1048608 | tf_op jit(solution)/shard_map/ppermute | solution.py:18
  31.0 3.2 %shard_map.133 = (f32[32,128,128]{2,1,0:T(8,128)S(1)}, bf16[32,128,128]{2,1,0:T(8,128)(2,1)S(1)}) custom-call(s32[2,32]{1,0:T(2,128)S(1)} %copy-done.8, s32[2,32,128]{2,1,0:T(8,128)S(1)} %copy-done.2, bf16[2,32,256,128]{3,2,1,0:T(8,128)(2,1)S(1)} %copy-done, bf16[2,32,128]{2,1,0:T(8,128)(2,1)S(1)} %copy-done.4, ...), custom_call_target="tpu_custom_call" | custom-call | flops 1073741824 | bytes 12582912 | tf_op jit(solution)/shard_map/pallas_call | solution.py:431
  34.3 0.0 collective-permute-done.edge_ref
  34.3 2.0 %shard_map.136 = bf16[2,32,128,128]{3,2,1,0:T(8,128)(2,1)} custom-call(s32[2,32]{1,0:T(2,128)S(1)} %copy-done.6, s32[2,32,128]{2,1,0:T(8,128)S(1)} %copy-done.3, bf16[2,32,256,128]{3,2,1,0:T(8,128)(2,1)} %interp_ref.5, bf16[2,32,128]{2,1,0:T(8,128)(2,1)S(1)} %copy-done.5, ...), custom_call_target="tpu_custom_call", output_to_operand_aliasing={{}: (6, {})} | custom-call | flops 67108864 | bytes 786432 | tf_op jit(solution)/shard_map/pallas_call | solution.py:443
  36.3 3.2 %collective-permute-done.3.packed_ref = bf16[1552,128]{1,0:T(8,128)(2,1)S(1)} collective-permute-done((bf16[1552,128]{1,0:T(8,128)(2,1)S(1)}, bf16[1552,128]{1,0:T(8,128)(2,1)S(1)}, u32[]{:S(2)}, u32[]{:S(2)}) %collective-permute-start.3) | collective-permute-done | bytes 397344 | tf_op jit(solution)/shard_map/ppermute | solution.py:18
  39.5 1.8 %shard_map.134._ = bf16[2,32,128,128]{3,2,1,0:T(8,128)(2,1)} custom-call(f32[32,128,128]{2,1,0:T(8,128)S(1)} %get-tuple-element.18.part_ref, bf16[32,128,128]{2,1,0:T(8,128)(2,1)S(1)} %get-tuple-element.19.lower_turned_ref, bf16[1552,128]{1,0:T(8,128)(2,1)S(1)} %collective-permute-done.3.packed_ref, ...), custom_call_target="tpu_custom_call", output_to_operand_aliasing={{}: (3, {})} | custom-call | flops 301989888 | bytes 4325376 | tf_op jit(solution)/shard_map/pallas_call | solution.py:467
  41.3 0.3 collective-permute-done.2.packed_ref
  41.6 1.2 %shard_map.135 = bf16[2,32,128,128]{3,2,1,0:T(8,128)(2,1)} custom-call(f32[32,128,128]{2,1,0:T(8,128)S(1)} %get-tuple-element.18.part_ref, bf16[32,128,128]{2,1,0:T(8,128)(2,1)S(1)} %get-tuple-element.19.lower_turned_ref, bf16[528,128]{1,0:T(8,128)(2,1)S(1)} %collective-permute-done.2.packed_ref, ...), custom_call_target="tpu_custom_call", output_to_operand_aliasing={{}: (3, {})} | custom-call | flops 100663296 | bytes 1441792 | tf_op jit(solution)/shard_map/pallas_call | solution.py:467
  (8 shorter events, 0.0 us)
Async XLA Ops:
  0.6 2.8 %copy-start.7 = (s32[2,32]{1,0:T(2,128)S(1)}, s32[2,32]{1,0:T(2,128)}, u32[]{:S(2)}) copy-start(s32[2,32]{1,0:T(2,128)} %rank_hbm.1) | copy-start | bytes 772
  0.6 2.8 %copy-start.1 = (s32[2,32,128]{2,1,0:T(8,128)S(1)}, s32[2,32,128]{2,1,0:T(8,128)}, u32[]{:S(2)}) copy-start(s32[2,32,128]{2,1,0:T(8,128)} %skel_hbm.1) | copy-start | bytes 98308
  0.7 2.8 %copy-start.6 = (s32[2,32]{1,0:T(2,128)S(1)}, s32[2,32]{1,0:T(2,128)}, u32[]{:S(2)}) copy-start(s32[2,32]{1,0:T(2,128)} %rank_ref.5) | copy-start | bytes 772
  0.7 2.8 %copy-start.3 = (s32[2,32,128]{2,1,0:T(8,128)S(1)}, s32[2,32,128]{2,1,0:T(8,128)}, u32[]{:S(2)}) copy-start(s32[2,32,128]{2,1,0:T(8,128)} %skel_ref.5) | copy-start | bytes 98308
  0.7 2.8 %copy-start.8 = (s32[2,32]{1,0:T(2,128)S(1)}, s32[2,32]{1,0:T(2,128)}, u32[]{:S(2)}) copy-start(s32[2,32]{1,0:T(2,128)} %rank_ref.4) | copy-start | bytes 772
  0.7 2.8 %copy-start.2 = (s32[2,32,128]{2,1,0:T(8,128)S(1)}, s32[2,32,128]{2,1,0:T(8,128)}, u32[]{:S(2)}) copy-start(s32[2,32,128]{2,1,0:T(8,128)} %skel_ref.4) | copy-start | bytes 98308
  0.7 2.8 %copy-start.5 = (bf16[2,32,128]{2,1,0:T(8,128)(2,1)S(1)}, bf16[2,32,128]{2,1,0:T(8,128)(2,1)}, u32[]{:S(2)}) copy-start(bf16[2,32,128]{2,1,0:T(8,128)(2,1)} %coup_ref.3) | copy-start | bytes 49156
  0.7 2.8 %copy-start.4 = (bf16[2,32,128]{2,1,0:T(8,128)(2,1)S(1)}, bf16[2,32,128]{2,1,0:T(8,128)(2,1)}, u32[]{:S(2)}) copy-start(bf16[2,32,128]{2,1,0:T(8,128)(2,1)} %coup_ref.2) | copy-start | bytes 49156
  2.2 28.9 %collective-permute-start.1 = (bf16[32,128,128]{2,1,0:T(8,128)(2,1)S(1)}, bf16[32,128,128]{2,1,0:T(8,128)(2,1)S(1)}, u32[]{:S(2)}, u32[]{:S(2)}) collective-permute-start(bf16[32,128,128]{2,1,0:T(8,128)(2,1)S(1)} %shard_map.132), channel_id=1, source_target_pairs={{4,0},{8,4},{12,8},{16,12},{20,16},{24,20},{28,24},{5,1},{9,5},{13... | collective-permute-start | bytes 3145736 | tf_op jit(solution)/shard_map/ppermute | solution.py:18
  3.5 27.5 %copy-start = (bf16[2,32,256,128]{3,2,1,0:T(8,128)(2,1)S(1)}, bf16[2,32,256,128]{3,2,1,0:T(8,128)(2,1)}, u32[]{:S(2)}) copy-start(bf16[2,32,256,128]{3,2,1,0:T(8,128)(2,1)} %interp_ref.4) | copy-start | bytes 12582916
  20.5 19.0 %collective-permute-start.3 = (bf16[1552,128]{1,0:T(8,128)(2,1)S(1)}, bf16[1552,128]{1,0:T(8,128)(2,1)S(1)}, u32[]{:S(2)}, u32[]{:S(2)}) collective-permute-start(bf16[1552,128]{1,0:T(8,128)(2,1)S(1)} %get-tuple-element.21), channel_id=1, source_target_pairs={{4,0},{8,4},{12,8},{16,12},{20,16},{24,20},{28,24},{5,1},{9,5},{13... | collective-permute-start | bytes 1191944 | tf_op jit(solution)/shard_map/ppermute | solution.py:18
  21.8 12.5 %collective-permute-start = (bf16[2,2,128,128]{3,2,1,0:T(8,128)(2,1)S(1)}, bf16[2,2,128,128]{3,2,1,0:T(8,128)(2,1)S(1)}, u32[]{:S(2)}, u32[]{:S(2)}) collective-permute-start(bf16[2,2,128,128]{3,2,1,0:T(8,128)(2,1)S(1)} %get-tuple-element.14), channel_id=1, source_target_pairs={{1,0},{2,1},{3,2},{5,4},{6,5},{7,6},{9,8},{10,9},{11,10},{13,12},{... | collective-permute-start | bytes 393224 | tf_op jit(solution)/shard_map/ppermute | solution.py:18
  23.1 18.5 %collective-permute-start.2 = (bf16[528,128]{1,0:T(8,128)(2,1)S(1)}, bf16[528,128]{1,0:T(8,128)(2,1)S(1)}, u32[]{:S(2)}, u32[]{:S(2)}) collective-permute-start(bf16[528,128]{1,0:T(8,128)(2,1)S(1)} %get-tuple-element.20), channel_id=1, source_target_pairs={{4,0},{8,4},{12,8},{16,12},{20,16},{24,20},{28,24},{5,1},{9,5},{13... | collective-permute-start | bytes 405512 | tf_op jit(solution)/shard_map/ppermute | solution.py:18

commit v13 on v12

--- a/solution.py
+++ b/solution.py
@@ -108,7 +108,7 @@
     x_rank_ref, x_skel_ref, x_interp_ref, x_coup_ref,
     y_rank_ref, y_skel_ref, y_interp_ref, y_coup_ref,
     x_out_ref, y_out_ref, packed_ref, packed_last_ref, edge_ref, corner_ref, last_turned_ref, last_schur_ref,
-    store_turned, store_schur, store_extra, x_coup_held, y_coup_held,
+    store_turned, store_schur, store_extra,
 ):
     layer = layers - 1 - pl.program_id(0)
     chunk = chunks - 1 - pl.program_id(1)
@@ -117,24 +117,16 @@
     half = slots // 2
     top = interp_ref.shape[2] // 2
 
-    rows = pl.ds(pl.multiple_of(first, cells), cells)
-
-    @pl.when((pl.program_id(0) == 0) & (pl.program_id(1) == 0))
-    def _():
-        x_coup_held[...] = x_coup_ref[...].astype(F32)
-        y_coup_held[...] = y_coup_ref[...].astype(F32)
-
-    turned = bases_of(cells, layer, first, rank_ref, skel_ref[layer, rows], interp_ref)
+    turned = bases_of(cells, layer, first, rank_ref, skel_ref[0], interp_ref)
     schurs = project(turned, [matrix_ref[0, k] for k in range(cells)])
     schurs = [s.astype(BF) for s in schurs]
 
-    def faces(out_ref, f_rank_ref, f_skel_ref, f_interp_ref, coup_held, rights):
-        found = bases_of(cells, layer, first, f_rank_ref, f_skel_ref[layer, rows], f_interp_ref)
-        conducts = coup_held[layer, rows].astype(BF)
+    def faces(out_ref, f_rank_ref, f_skel_ref, f_interp_ref, coup_ref, rights):
+        found = bases_of(cells, layer, first, f_rank_ref, f_skel_ref[0], f_interp_ref)
         matrices = []
         for k in range(cells):
             right_turned, right = rights[k]
-            conduct = conducts[k : k + 1]
+            conduct = coup_ref[0, k : k + 1]
             lower = turned[k][:, top:]
             link = dot_nt(scaled(lower, conduct), right_turned).astype(BF)
             link_t = dot_nt(scaled(right_turned, conduct), lower).astype(BF)
@@ -148,12 +140,12 @@
 
     after = jnp.minimum(first + cells, store_schur.shape[0] - 1)
     rights = [(turned[k][:, :top], schurs[k]) for k in range(1, cells)]
-    faces(y_out_ref, y_rank_ref, y_skel_ref, y_interp_ref, y_coup_held, rights + [stored(after)])
+    faces(y_out_ref, y_rank_ref, y_skel_ref, y_interp_ref, y_coup_ref, rights + [stored(after)])
 
     @pl.when(layer < layers - 1)
     def _():
         rights = [stored(first + k) for k in range(cells)]
-        faces(x_out_ref, x_rank_ref, x_skel_ref, x_interp_ref, x_coup_held, rights)
+        faces(x_out_ref, x_rank_ref, x_skel_ref, x_interp_ref, x_coup_ref, rights)
 
     for k in range(cells):
         store_turned[first + k] = turned[k][:, :top]
@@ -231,7 +223,7 @@
 
 def x_part_kernel(
     cells, layer, rank_ref, skel_ref, interp_ref, coup_ref, turned_ref, schur_ref, top_ref,
-    part_ref, lower_turned_ref,
+    part_ref, lower_ref, lower_turned_ref,
 ):
     count, slots, half = turned_ref.shape
     nothing = jnp.zeros((slots, slots), BF)
@@ -244,6 +236,7 @@
         faces = [kept_cleared(t) for t in [jnp.transpose(m) for m in marked]]
         for k in group:
             lower_turned_ref[k] = faces[k - first][:, half:]
+            lower_ref[k] = jnp.transpose(faces[k - first][:, half:])
         tops = [kept_cleared(t) for t in [jnp.transpose(top_ref[k]) for k in group]]
         matrices = []
         for k, top in zip(group, tops):
@@ -256,7 +249,7 @@
 
 
 def x_last_kernel(
-    cells, layer, places, part_ref, lower_turned_ref, packed_ref, _, out_ref, held, sems
+    cells, layer, places, part_ref, lower_ref, lower_turned_ref, packed_ref, _, out_ref, held, sems
 ):
     slots = part_ref.shape[-1]
     half = slots // 2
@@ -283,7 +276,8 @@
                 low += extra * same_scale
             tri = jnp.concatenate([top, low], axis=0).astype(BF)
             schurs.append(tri + jnp.transpose(tri))
-        results = project([lower_turned_ref[k] for k in group], schurs)
+        inner = [dot(lower_turned_ref[k], h).astype(BF) for k, h in zip(group, schurs)]
+        results = [dot(i, lower_ref[k]) for k, i in zip(group, inner)]
         part_cells = max(1, cells // 2)
         for start in range(0, cells, part_cells):
             for k in range(start, start + part_cells):
@@ -342,9 +336,8 @@
 
     hbm = pl.BlockSpec(memory_space=pltpu.HBM)
     vmem = pl.BlockSpec(memory_space=pltpu.VMEM)
-    large = next(n for n in (16, 8, 4, 2, 1) if nj % n == 0)
     top = call(
-        functools.partial(top_kernel, large),
+        functools.partial(top_kernel, cells),
         (),
         [hbm, hbm, hbm],
         vmem,
@@ -357,7 +350,7 @@
             pltpu.VMEM((nj, slots), jnp.int32),
             pltpu.VMEM((nj, half, slots), BF),
             pltpu.SemaphoreType.DMA((2,)),
-            pltpu.SemaphoreType.DMA((nj // large,)),
+            pltpu.SemaphoreType.DMA((chunks,)),
         ],
     )(in_hbm(cell_rank), in_hbm(cell_skel), in_hbm(cell_interp))
     top_in = passed_along(top, "gx", -1)
@@ -385,9 +378,9 @@
         functools.partial(main_kernel, cells, nx, chunks),
         (nx, chunks),
         [
-            smem, vmem, down(rows, slots), down(rows, rows),
-            smem, vmem, down_x(rows, fslots), vmem,
-            smem, vmem, down(rows, fslots), vmem,
+            smem, down(slots), down(rows, slots), down(rows, rows),
+            smem, down_x(fslots), down_x(rows, fslots), down_x(half),
+            smem, down(fslots), down(rows, fslots), down(half),
         ],
         [
             down_x(fslots, fslots),
@@ -411,13 +404,11 @@
             pltpu.VMEM((nj, slots, half), BF),
             pltpu.VMEM((nj, slots, slots), BF),
             pltpu.VMEM((chunks, cells, slots), F32),
-            pltpu.VMEM((nx, nj, half), F32),
-            pltpu.VMEM((nx, nj, half), F32),
         ],
     )(
-        cell_rank, cell_skel, in_hbm(cell_interp), in_hbm(cell_matrix),
-        x_face_rank, x_face_skel, in_hbm(x_face_interp), x_coupling,
-        y_face_rank, y_face_skel, in_hbm(y_face_interp), y_coupling,
+        cell_rank, in_hbm(cell_skel), in_hbm(cell_interp), in_hbm(cell_matrix),
+        x_face_rank, in_hbm(x_face_skel), in_hbm(x_face_interp), in_hbm(x_coupling),
+        y_face_rank, in_hbm(y_face_skel), in_hbm(y_face_interp), in_hbm(y_coupling),
     )
     edge_in = passed_along(edge, "yz", -1)
     packed_in = passed_along(packed, "gx", -1)
@@ -428,12 +419,16 @@
     tail = nj - 1
     group = tail // cells
 
-    part, lower_turned = call(
+    part, lower, lower_turned = call(
         functools.partial(x_part_kernel, cells, last),
         (),
         [smem, vmem, vmem, vmem, vmem, vmem, vmem],
-        [vmem, vmem],
-        [shape((nj, fslots, fslots), F32), shape((nj, fslots, slots), BF)],
+        [vmem, vmem, vmem],
+        [
+            shape((nj, fslots, fslots), F32),
+            shape((nj, slots, fslots), BF),
+            shape((nj, fslots, slots), BF),
+        ],
         8 * unit // nx,
         face_bytes,
         vmem=16,
@@ -467,17 +462,17 @@
         x_out = call(
             functools.partial(x_last_kernel, cells, last, places),
             (),
-            [vmem, vmem, vmem, hbm],
+            [vmem, vmem, vmem, vmem, hbm],
             hbm,
             shape((nx, nj, fslots, fslots), BF),
             3 * unit // nx * count // chunks,
             nj * slots * slots * 11 * count // chunks,
-            {3: 0},
+            {4: 0},
             scratch=[
                 pltpu.VMEM((count * cells, fslots, fslots), BF),
                 pltpu.SemaphoreType.DMA((count, 2)),
             ],
-        )(part, lower_turned, arrived, x_out)
+        )(part, lower, lower_turned, arrived, x_out)
     return (x_out, y_out)
 
 

time: 43.1 us -> 42.9 us (level)
  no operation moved by 1% of the time
where the time goes in v13:
time: 42.9 us; the launch traced here: 42.6 us
  Pallas kernels  26.5 us (62%)
  waiting for transfers between devices  10.1 us (24%)
  starting transfers between devices  5.16 us (12%)
  between operations  0.8 us (2%)
    pallas_call x1, Pallas kernels, body(): call(functools.partial(main_kernel, cells, nx, chunks), (nx, chunks), [sm...  17.1 us
    ppermute x4, waiting for transfers between devices, passed_along(): return lax.ppermute(x, axis, pairs)  10.1 us
    ppermute x4, starting transfers between devices, passed_along(): return lax.ppermute(x, axis, pairs)  5.16 us
    pallas_call x1, Pallas kernels, body(): call(functools.partial(x_part_kernel, cells, last), (), [smem, vmem, vmem...  3.32 us
    pallas_call x2, Pallas kernels, body(): call(functools.partial(x_last_kernel, cells, last, places), (), [vmem, vm...  2.68 us
    pallas_call x1, Pallas kernels, body(): call(functools.partial(y_edge_kernel, nx, tail), (1,), [smem, pl.BlockSpe...  2.05 us
    pallas_call x1, Pallas kernels, body(): call(functools.partial(top_kernel, cells), (), [hbm, hbm, hbm], vmem, sha...  1.35 us
  transfers between devices with their start and end apart: 4, of which 3 were waited for; matrix products, arithmetic and copies ran while one was open for 0% of the time, Pallas kernels for 56%

profile of v13, /device:TPU:0, one launch (start us, length us, event | category | flops | bytes accessed | tf_op | source)
XLA Modules:
  0.0 42.6 jit_solution(2687289580012988809)
XLA Ops:
  0.6 0.0 copy-start.6
  0.6 0.0 copy-start.5
  0.7 0.0 copy-start.7
  0.7 1.3 %shard_map.132 = bf16[32,128,128]{2,1,0:T(8,128)(2,1)S(1)} custom-call(s32[2,32]{1,0:T(2,128)} %rank_hbm.1, s32[2,32,128]{2,1,0:T(8,128)} %skel_hbm.1, bf16[2,32,256,128]{3,2,1,0:T(8,128)(2,1)} %interp_hbm.1), custom_call_target="tpu_custom_call" | custom-call | bytes 2097152 | tf_op jit(solution)/shard_map/pallas_call | solution.py:339
  2.0 0.0 copy-start.1
  2.0 0.0 copy-start.3
  2.0 1.3 %collective-permute-start.1 = (bf16[32,128,128]{2,1,0:T(8,128)(2,1)S(1)}, bf16[32,128,128]{2,1,0:T(8,128)(2,1)S(1)}, u32[]{:S(2)}, u32[]{:S(2)}) collective-permute-start(bf16[32,128,128]{2,1,0:T(8,128)(2,1)S(1)} %shard_map.132), channel_id=1, source_target_pairs={{4,0},{8,4},{12,8},{16,12},{20,16},{24,20},{28,24},{5,1},{9,5},{13... | collective-permute-start | bytes 3145736 | tf_op jit(solution)/shard_map/ppermute | solution.py:18
  3.3 0.0 copy-done.6
  3.4 0.0 copy-done.5
  3.4 0.0 copy-start
  3.4 17.1 %shard_map.131 = (bf16[2,32,128,128]{3,2,1,0:T(8,128)(2,1)}, bf16[2,32,128,128]{3,2,1,0:T(8,128)(2,1)}, bf16[1552,128]{1,0:T(8,128)(2,1)S(1)}, bf16[528,128]{1,0...) custom-call(s32[2,32]{1,0:T(2,128)S(1)} %copy-done.6, ...), custom_call_target="tpu_custom_call" | custom-call | flops 5368709120 | bytes 27262976 | tf_op jit(solution)/shard_map/pallas_call | solution.py:377
  20.5 1.3 %collective-permute-start.3 = (bf16[1552,128]{1,0:T(8,128)(2,1)S(1)}, bf16[1552,128]{1,0:T(8,128)(2,1)S(1)}, u32[]{:S(2)}, u32[]{:S(2)}) collective-permute-start(bf16[1552,128]{1,0:T(8,128)(2,1)S(1)} %get-tuple-element.23), channel_id=1, source_target_pairs={{4,0},{8,4},{12,8},{16,12},{20,16},{24,20},{28,24},{5,1},{9,5},{13... | collective-permute-start | bytes 1191944 | tf_op jit(solution)/shard_map/ppermute | solution.py:18
  21.8 1.3 %collective-permute-start = (bf16[2,2,128,128]{3,2,1,0:T(8,128)(2,1)S(1)}, bf16[2,2,128,128]{3,2,1,0:T(8,128)(2,1)S(1)}, u32[]{:S(2)}, u32[]{:S(2)}) collective-permute-start(bf16[2,2,128,128]{3,2,1,0:T(8,128)(2,1)S(1)} %get-tuple-element.15), channel_id=1, source_target_pairs={{1,0},{2,1},{3,2},{5,4},{6,5},{7,6},{9,8},{10,9},{11,10},{13,12},{... | collective-permute-start | bytes 393224 | tf_op jit(solution)/shard_map/ppermute | solution.py:18
  23.1 1.3 %collective-permute-start.2 = (bf16[528,128]{1,0:T(8,128)(2,1)S(1)}, bf16[528,128]{1,0:T(8,128)(2,1)S(1)}, u32[]{:S(2)}, u32[]{:S(2)}) collective-permute-start(bf16[528,128]{1,0:T(8,128)(2,1)S(1)} %get-tuple-element.22), channel_id=1, source_target_pairs={{4,0},{8,4},{12,8},{16,12},{20,16},{24,20},{28,24},{5,1},{9,5},{13... | collective-permute-start | bytes 405512 | tf_op jit(solution)/shard_map/ppermute | solution.py:18
  24.4 6.5 %collective-permute-done.1.top_ref = bf16[32,128,128]{2,1,0:T(8,128)(2,1)S(1)} collective-permute-done((bf16[32,128,128]{2,1,0:T(8,128)(2,1)S(1)}, bf16[32,128,128]{2,1,0:T(8,128)(2,1)S(1)}, u32[]{:S(2)}, u32[]{:S(2)}) %collective-permute-start.1) | collective-permute-done | bytes 1048608 | tf_op jit(solution)/shard_map/ppermute | solution.py:18
  30.9 0.0 copy-start.2
  30.9 0.0 copy-start.4
  30.9 3.3 %shard_map.133 = (f32[32,128,128]{2,1,0:T(8,128)S(1)}, bf16[32,128,128]{2,1,0:T(8,128)(2,1)S(1)}, bf16[32,128,128]{2,1,0:T(8,128)(2,1)S(1)}) custom-call(s32[2,32]{1,0:T(2,128)S(1)} %copy-done.7, s32[2,32,128]{2,1,0:T(8,128)S(1)} %copy-done.1, bf16[2,32,256,128]{3,2,1,0:T(8,128)(2,1)S(1)} %copy-done, bf16[2,32,128]{2,1,0:T(8,128)(2,1)S(1)} %copy-done.3, ...), custom_call_target="tpu_custom_call" | custom-call | flops 1073741824 | bytes 12582912 | tf_op jit(solution)/shard_map/pallas_call | solution.py:422
  34.3 0.0 collective-permute-done.edge_ref
  34.3 2.1 %shard_map.136 = bf16[2,32,128,128]{3,2,1,0:T(8,128)(2,1)} custom-call(s32[2,32]{1,0:T(2,128)S(1)} %copy-done.5, s32[2,32,128]{2,1,0:T(8,128)S(1)} %copy-done.2, bf16[2,32,256,128]{3,2,1,0:T(8,128)(2,1)} %interp_ref.5, bf16[2,32,128]{2,1,0:T(8,128)(2,1)S(1)} %copy-done.4, ...), custom_call_target="tpu_custom_call", output_to_operand_aliasing={{}: (6, {})} | custom-call | flops 67108864 | bytes 786432 | tf_op jit(solution)/shard_map/pallas_call | solution.py:438
  36.3 3.1 %collective-permute-done.3.packed_ref = bf16[1552,128]{1,0:T(8,128)(2,1)S(1)} collective-permute-done((bf16[1552,128]{1,0:T(8,128)(2,1)S(1)}, bf16[1552,128]{1,0:T(8,128)(2,1)S(1)}, u32[]{:S(2)}, u32[]{:S(2)}) %collective-permute-start.3) | collective-permute-done | bytes 397344 | tf_op jit(solution)/shard_map/ppermute | solution.py:18
  39.4 1.6 %shard_map.134._ = bf16[2,32,128,128]{3,2,1,0:T(8,128)(2,1)} custom-call(f32[32,128,128]{2,1,0:T(8,128)S(1)} %get-tuple-element.19.part_ref, bf16[32,128,128]{2,1,0:T(8,128)(2,1)S(1)} %get-tuple-element.20.lower_ref, bf16[32,128,128]{2,1,0:T(8,128)(2,1)S(1)} %get-tuple-element.21.lower_turned_ref, ...), custom_call_target="tpu_custom_call", output_to_operand_aliasing={{}: (4, {})} | custom-call | flops 301989888 | bytes 4325376 | tf_op jit(solution)/shard_map/pallas_call | solution.py:462
  41.0 0.5 %collective-permute-done.2.packed_ref = bf16[528,128]{1,0:T(8,128)(2,1)S(1)} collective-permute-done((bf16[528,128]{1,0:T(8,128)(2,1)S(1)}, bf16[528,128]{1,0:T(8,128)(2,1)S(1)}, u32[]{:S(2)}, u32[]{:S(2)}) %collective-permute-start.2) | collective-permute-done | bytes 135200 | tf_op jit(solution)/shard_map/ppermute | solution.py:18
  41.5 1.1 %shard_map.135 = bf16[2,32,128,128]{3,2,1,0:T(8,128)(2,1)} custom-call(f32[32,128,128]{2,1,0:T(8,128)S(1)} %get-tuple-element.19.part_ref, bf16[32,128,128]{2,1,0:T(8,128)(2,1)S(1)} %get-tuple-element.20.lower_ref, bf16[32,128,128]{2,1,0:T(8,128)(2,1)S(1)} %get-tuple-element.21.lower_turned_ref, ...), custom_call_target="tpu_custom_call", output_to_operand_aliasing={{}: (4, {})} | custom-call | flops 100663296 | bytes 1441792 | tf_op jit(solution)/shard_map/pallas_call | solution.py:462
  (6 shorter events, 0.0 us)
Async XLA Ops:
  0.6 2.7 %copy-start.6 = (s32[2,32]{1,0:T(2,128)S(1)}, s32[2,32]{1,0:T(2,128)}, u32[]{:S(2)}) copy-start(s32[2,32]{1,0:T(2,128)} %rank_hbm.1) | copy-start | bytes 772
  0.6 2.7 %copy-start.5 = (s32[2,32]{1,0:T(2,128)S(1)}, s32[2,32]{1,0:T(2,128)}, u32[]{:S(2)}) copy-start(s32[2,32]{1,0:T(2,128)} %rank_ref.5) | copy-start | bytes 772
  0.7 2.7 %copy-start.7 = (s32[2,32]{1,0:T(2,128)S(1)}, s32[2,32]{1,0:T(2,128)}, u32[]{:S(2)}) copy-start(s32[2,32]{1,0:T(2,128)} %rank_ref.4) | copy-start | bytes 772
  2.0 28.9 %copy-start.1 = (s32[2,32,128]{2,1,0:T(8,128)S(1)}, s32[2,32,128]{2,1,0:T(8,128)}, u32[]{:S(2)}) copy-start(s32[2,32,128]{2,1,0:T(8,128)} %skel_ref.4) | copy-start | bytes 98308
  2.0 28.9 %copy-start.3 = (bf16[2,32,128]{2,1,0:T(8,128)(2,1)S(1)}, bf16[2,32,128]{2,1,0:T(8,128)(2,1)}, u32[]{:S(2)}) copy-start(bf16[2,32,128]{2,1,0:T(8,128)(2,1)} %coup_ref.2) | copy-start | bytes 49156
  2.0 28.9 %collective-permute-start.1 = (bf16[32,128,128]{2,1,0:T(8,128)(2,1)S(1)}, bf16[32,128,128]{2,1,0:T(8,128)(2,1)S(1)}, u32[]{:S(2)}, u32[]{:S(2)}) collective-permute-start(bf16[32,128,128]{2,1,0:T(8,128)(2,1)S(1)} %shard_map.132), channel_id=1, source_target_pairs={{4,0},{8,4},{12,8},{16,12},{20,16},{24,20},{28,24},{5,1},{9,5},{13... | collective-permute-start | bytes 3145736 | tf_op jit(solution)/shard_map/ppermute | solution.py:18
  3.4 27.5 %copy-start = (bf16[2,32,256,128]{3,2,1,0:T(8,128)(2,1)S(1)}, bf16[2,32,256,128]{3,2,1,0:T(8,128)(2,1)}, u32[]{:S(2)}) copy-start(bf16[2,32,256,128]{3,2,1,0:T(8,128)(2,1)} %interp_ref.4) | copy-start | bytes 12582916
  20.5 18.9 %collective-permute-start.3 = (bf16[1552,128]{1,0:T(8,128)(2,1)S(1)}, bf16[1552,128]{1,0:T(8,128)(2,1)S(1)}, u32[]{:S(2)}, u32[]{:S(2)}) collective-permute-start(bf16[1552,128]{1,0:T(8,128)(2,1)S(1)} %get-tuple-element.23), channel_id=1, source_target_pairs={{4,0},{8,4},{12,8},{16,12},{20,16},{24,20},{28,24},{5,1},{9,5},{13... | collective-permute-start | bytes 1191944 | tf_op jit(solution)/shard_map/ppermute | solution.py:18
  21.8 12.5 %collective-permute-start = (bf16[2,2,128,128]{3,2,1,0:T(8,128)(2,1)S(1)}, bf16[2,2,128,128]{3,2,1,0:T(8,128)(2,1)S(1)}, u32[]{:S(2)}, u32[]{:S(2)}) collective-permute-start(bf16[2,2,128,128]{3,2,1,0:T(8,128)(2,1)S(1)} %get-tuple-element.15), channel_id=1, source_target_pairs={{1,0},{2,1},{3,2},{5,4},{6,5},{7,6},{9,8},{10,9},{11,10},{13,12},{... | collective-permute-start | bytes 393224 | tf_op jit(solution)/shard_map/ppermute | solution.py:18
  23.1 18.4 %collective-permute-start.2 = (bf16[528,128]{1,0:T(8,128)(2,1)S(1)}, bf16[528,128]{1,0:T(8,128)(2,1)S(1)}, u32[]{:S(2)}, u32[]{:S(2)}) collective-permute-start(bf16[528,128]{1,0:T(8,128)(2,1)S(1)} %get-tuple-element.22), channel_id=1, source_target_pairs={{4,0},{8,4},{12,8},{16,12},{20,16},{24,20},{28,24},{5,1},{9,5},{13... | collective-permute-start | bytes 405512 | tf_op jit(solution)/shard_map/ppermute | solution.py:18
  30.9 3.4 %copy-start.2 = (s32[2,32,128]{2,1,0:T(8,128)S(1)}, s32[2,32,128]{2,1,0:T(8,128)}, u32[]{:S(2)}) copy-start(s32[2,32,128]{2,1,0:T(8,128)} %skel_ref.5) | copy-start | bytes 98308
  30.9 3.4 %copy-start.4 = (bf16[2,32,128]{2,1,0:T(8,128)(2,1)S(1)}, bf16[2,32,128]{2,1,0:T(8,128)(2,1)}, u32[]{:S(2)}) copy-start(bf16[2,32,128]{2,1,0:T(8,128)(2,1)} %coup_ref.3) | copy-start | bytes 49156

commit v14 on v13

--- a/solution.py
+++ b/solution.py
@@ -275,10 +275,14 @@
             else:
                 low += extra * same_scale
             tri = jnp.concatenate([top, low], axis=0).astype(BF)
-            schurs.append(tri + jnp.transpose(tri))
-        inner = [dot(lower_turned_ref[k], h).astype(BF) for k, h in zip(group, schurs)]
+            schurs.append(tri + jnp.transpose(tri) if k % 2 == 0 else tri)
+        inner = []
+        for k, h in zip(group, schurs):
+            turned = lower_turned_ref[k]
+            both = dot(turned, h) if k % 2 == 0 else dot(turned, h) + dot_nt(turned, h)
+            inner.append(both.astype(BF))
         results = [dot(i, lower_ref[k]) for k, i in zip(group, inner)]
-        part_cells = max(1, cells // 2)
+        part_cells = max(1, cells // 4)
         for start in range(0, cells, part_cells):
             for k in range(start, start + part_cells):
                 held[n * cells + k] = (part_ref[c * cells + k] + results[k]).astype(BF)
@@ -470,7 +474,7 @@
             {4: 0},
             scratch=[
                 pltpu.VMEM((count * cells, fslots, fslots), BF),
-                pltpu.SemaphoreType.DMA((count, 2)),
+                pltpu.SemaphoreType.DMA((count, 4)),
             ],
         )(part, lower, lower_turned, arrived, x_out)
     return (x_out, y_out)

time: 42.9 us -> 43 us (level)
  transfers between devices with their start and end apart: 4 -> 4, of which waited for: 3 -> 3; matrix products, arithmetic and copies ran while one was open for 0% -> 0% of each run, Pallas kernels for 56% -> 57%
where the time goes in v14:
time: 43 us; the launch traced here: 42.6 us
  Pallas kernels  26.8 us (62%)
  waiting for transfers between devices  9.86 us (23%)
  starting transfers between devices  5.16 us (12%)
  between operations  0.8 us (2%)
    pallas_call x1, Pallas kernels, body(): call(functools.partial(main_kernel, cells, nx, chunks), (nx, chunks), [sm...  17.1 us
    ppermute x4, waiting for transfers between devices, passed_along(): return lax.ppermute(x, axis, pairs)  9.86 us
    ppermute x4, starting transfers between devices, passed_along(): return lax.ppermute(x, axis, pairs)  5.16 us
    pallas_call x1, Pallas kernels, body(): call(functools.partial(x_part_kernel, cells, last), (), [smem, vmem, vmem...  3.32 us
    pallas_call x2, Pallas kernels, body(): call(functools.partial(x_last_kernel, cells, last, places), (), [vmem, vm...  2.97 us
    pallas_call x1, Pallas kernels, body(): call(functools.partial(y_edge_kernel, nx, tail), (1,), [smem, pl.BlockSpe...  2.05 us
    pallas_call x1, Pallas kernels, body(): call(functools.partial(top_kernel, cells), (), [hbm, hbm, hbm], vmem, sha...  1.35 us
  transfers between devices with their start and end apart: 4, of which 3 were waited for; matrix products, arithmetic and copies ran while one was open for 0% of the time, Pallas kernels for 57%

profile of v14, /device:TPU:0, one launch (start us, length us, event | category | flops | bytes accessed | tf_op | source)
XLA Modules:
  0.0 42.6 jit_solution(15907491298170420513)
XLA Ops:
  0.6 0.0 copy-start.6
  0.6 0.0 copy-start.5
  0.7 0.0 copy-start.7
  0.7 1.3 %shard_map.132 = bf16[32,128,128]{2,1,0:T(8,128)(2,1)S(1)} custom-call(s32[2,32]{1,0:T(2,128)} %rank_hbm.1, s32[2,32,128]{2,1,0:T(8,128)} %skel_hbm.1, bf16[2,32,256,128]{3,2,1,0:T(8,128)(2,1)} %interp_hbm.1), custom_call_target="tpu_custom_call" | custom-call | bytes 2097152 | tf_op jit(solution)/shard_map/pallas_call | solution.py:343
  2.0 0.0 copy-start.1
  2.0 0.0 copy-start.3
  2.0 1.3 %collective-permute-start.1 = (bf16[32,128,128]{2,1,0:T(8,128)(2,1)S(1)}, bf16[32,128,128]{2,1,0:T(8,128)(2,1)S(1)}, u32[]{:S(2)}, u32[]{:S(2)}) collective-permute-start(bf16[32,128,128]{2,1,0:T(8,128)(2,1)S(1)} %shard_map.132), channel_id=1, source_target_pairs={{4,0},{8,4},{12,8},{16,12},{20,16},{24,20},{28,24},{5,1},{9,5},{13... | collective-permute-start | bytes 3145736 | tf_op jit(solution)/shard_map/ppermute | solution.py:18
  3.3 0.0 copy-done.6
  3.4 0.0 copy-start
  3.4 17.1 %shard_map.131 = (bf16[2,32,128,128]{3,2,1,0:T(8,128)(2,1)}, bf16[2,32,128,128]{3,2,1,0:T(8,128)(2,1)}, bf16[1552,128]{1,0:T(8,128)(2,1)S(1)}, bf16[528,128]{1,0...) custom-call(s32[2,32]{1,0:T(2,128)S(1)} %copy-done.6, ...), custom_call_target="tpu_custom_call" | custom-call | flops 5368709120 | bytes 27262976 | tf_op jit(solution)/shard_map/pallas_call | solution.py:381
  20.5 1.3 %collective-permute-start.3 = (bf16[1552,128]{1,0:T(8,128)(2,1)S(1)}, bf16[1552,128]{1,0:T(8,128)(2,1)S(1)}, u32[]{:S(2)}, u32[]{:S(2)}) collective-permute-start(bf16[1552,128]{1,0:T(8,128)(2,1)S(1)} %get-tuple-element.23), channel_id=1, source_target_pairs={{4,0},{8,4},{12,8},{16,12},{20,16},{24,20},{28,24},{5,1},{9,5},{13... | collective-permute-start | bytes 1191944 | tf_op jit(solution)/shard_map/ppermute | solution.py:18
  21.8 1.3 %collective-permute-start = (bf16[2,2,128,128]{3,2,1,0:T(8,128)(2,1)S(1)}, bf16[2,2,128,128]{3,2,1,0:T(8,128)(2,1)S(1)}, u32[]{:S(2)}, u32[]{:S(2)}) collective-permute-start(bf16[2,2,128,128]{3,2,1,0:T(8,128)(2,1)S(1)} %get-tuple-element.15), channel_id=1, source_target_pairs={{1,0},{2,1},{3,2},{5,4},{6,5},{7,6},{9,8},{10,9},{11,10},{13,12},{... | collective-permute-start | bytes 393224 | tf_op jit(solution)/shard_map/ppermute | solution.py:18
  23.1 1.3 %collective-permute-start.2 = (bf16[528,128]{1,0:T(8,128)(2,1)S(1)}, bf16[528,128]{1,0:T(8,128)(2,1)S(1)}, u32[]{:S(2)}, u32[]{:S(2)}) collective-permute-start(bf16[528,128]{1,0:T(8,128)(2,1)S(1)} %get-tuple-element.22), channel_id=1, source_target_pairs={{4,0},{8,4},{12,8},{16,12},{20,16},{24,20},{28,24},{5,1},{9,5},{13... | collective-permute-start | bytes 405512 | tf_op jit(solution)/shard_map/ppermute | solution.py:18
  24.4 6.5 %collective-permute-done.1.top_ref = bf16[32,128,128]{2,1,0:T(8,128)(2,1)S(1)} collective-permute-done((bf16[32,128,128]{2,1,0:T(8,128)(2,1)S(1)}, bf16[32,128,128]{2,1,0:T(8,128)(2,1)S(1)}, u32[]{:S(2)}, u32[]{:S(2)}) %collective-permute-start.1) | collective-permute-done | bytes 1048608 | tf_op jit(solution)/shard_map/ppermute | solution.py:18
  30.9 0.0 copy-done.3
  30.9 0.0 copy-start.2
  30.9 0.0 copy-start.4
  30.9 3.3 %shard_map.133 = (f32[32,128,128]{2,1,0:T(8,128)S(1)}, bf16[32,128,128]{2,1,0:T(8,128)(2,1)S(1)}, bf16[32,128,128]{2,1,0:T(8,128)(2,1)S(1)}) custom-call(s32[2,32]{1,0:T(2,128)S(1)} %copy-done.7, s32[2,32,128]{2,1,0:T(8,128)S(1)} %copy-done.1, bf16[2,32,256,128]{3,2,1,0:T(8,128)(2,1)S(1)} %copy-done, bf16[2,32,128]{2,1,0:T(8,128)(2,1)S(1)} %copy-done.3, ...), custom_call_target="tpu_custom_call" | custom-call | flops 1073741824 | bytes 12582912 | tf_op jit(solution)/shard_map/pallas_call | solution.py:426
  34.3 0.0 collective-permute-done.edge_ref
  34.3 2.1 %shard_map.136 = bf16[2,32,128,128]{3,2,1,0:T(8,128)(2,1)} custom-call(s32[2,32]{1,0:T(2,128)S(1)} %copy-done.5, s32[2,32,128]{2,1,0:T(8,128)S(1)} %copy-done.2, bf16[2,32,256,128]{3,2,1,0:T(8,128)(2,1)} %interp_ref.5, bf16[2,32,128]{2,1,0:T(8,128)(2,1)S(1)} %copy-done.4, ...), custom_call_target="tpu_custom_call", output_to_operand_aliasing={{}: (6, {})} | custom-call | flops 67108864 | bytes 786432 | tf_op jit(solution)/shard_map/pallas_call | solution.py:442
  36.3 3.1 %collective-permute-done.3.packed_ref = bf16[1552,128]{1,0:T(8,128)(2,1)S(1)} collective-permute-done((bf16[1552,128]{1,0:T(8,128)(2,1)S(1)}, bf16[1552,128]{1,0:T(8,128)(2,1)S(1)}, u32[]{:S(2)}, u32[]{:S(2)}) %collective-permute-start.3) | collective-permute-done | bytes 397344 | tf_op jit(solution)/shard_map/ppermute | solution.py:18
  39.4 1.8 %shard_map.134._ = bf16[2,32,128,128]{3,2,1,0:T(8,128)(2,1)} custom-call(f32[32,128,128]{2,1,0:T(8,128)S(1)} %get-tuple-element.19.part_ref, bf16[32,128,128]{2,1,0:T(8,128)(2,1)S(1)} %get-tuple-element.20.lower_ref, bf16[32,128,128]{2,1,0:T(8,128)(2,1)S(1)} %get-tuple-element.21.lower_turned_ref, ...), custom_call_target="tpu_custom_call", output_to_operand_aliasing={{}: (4, {})} | custom-call | flops 301989888 | bytes 4325376 | tf_op jit(solution)/shard_map/pallas_call | solution.py:466
  41.2 0.3 collective-permute-done.2.packed_ref
  41.5 1.2 %shard_map.135 = bf16[2,32,128,128]{3,2,1,0:T(8,128)(2,1)} custom-call(f32[32,128,128]{2,1,0:T(8,128)S(1)} %get-tuple-element.19.part_ref, bf16[32,128,128]{2,1,0:T(8,128)(2,1)S(1)} %get-tuple-element.20.lower_ref, bf16[32,128,128]{2,1,0:T(8,128)(2,1)S(1)} %get-tuple-element.21.lower_turned_ref, ...), custom_call_target="tpu_custom_call", output_to_operand_aliasing={{}: (4, {})} | custom-call | flops 100663296 | bytes 1441792 | tf_op jit(solution)/shard_map/pallas_call | solution.py:466
  (6 shorter events, 0.0 us)
Async XLA Ops:
  0.6 2.7 %copy-start.6 = (s32[2,32]{1,0:T(2,128)S(1)}, s32[2,32]{1,0:T(2,128)}, u32[]{:S(2)}) copy-start(s32[2,32]{1,0:T(2,128)} %rank_hbm.1) | copy-start | bytes 772
  0.6 2.7 %copy-start.5 = (s32[2,32]{1,0:T(2,128)S(1)}, s32[2,32]{1,0:T(2,128)}, u32[]{:S(2)}) copy-start(s32[2,32]{1,0:T(2,128)} %rank_ref.5) | copy-start | bytes 772
  0.7 2.7 %copy-start.7 = (s32[2,32]{1,0:T(2,128)S(1)}, s32[2,32]{1,0:T(2,128)}, u32[]{:S(2)}) copy-start(s32[2,32]{1,0:T(2,128)} %rank_ref.4) | copy-start | bytes 772
  2.0 28.9 %copy-start.1 = (s32[2,32,128]{2,1,0:T(8,128)S(1)}, s32[2,32,128]{2,1,0:T(8,128)}, u32[]{:S(2)}) copy-start(s32[2,32,128]{2,1,0:T(8,128)} %skel_ref.4) | copy-start | bytes 98308
  2.0 28.9 %copy-start.3 = (bf16[2,32,128]{2,1,0:T(8,128)(2,1)S(1)}, bf16[2,32,128]{2,1,0:T(8,128)(2,1)}, u32[]{:S(2)}) copy-start(bf16[2,32,128]{2,1,0:T(8,128)(2,1)} %coup_ref.2) | copy-start | bytes 49156
  2.0 28.9 %collective-permute-start.1 = (bf16[32,128,128]{2,1,0:T(8,128)(2,1)S(1)}, bf16[32,128,128]{2,1,0:T(8,128)(2,1)S(1)}, u32[]{:S(2)}, u32[]{:S(2)}) collective-permute-start(bf16[32,128,128]{2,1,0:T(8,128)(2,1)S(1)} %shard_map.132), channel_id=1, source_target_pairs={{4,0},{8,4},{12,8},{16,12},{20,16},{24,20},{28,24},{5,1},{9,5},{13... | collective-permute-start | bytes 3145736 | tf_op jit(solution)/shard_map/ppermute | solution.py:18
  3.4 27.5 %copy-start = (bf16[2,32,256,128]{3,2,1,0:T(8,128)(2,1)S(1)}, bf16[2,32,256,128]{3,2,1,0:T(8,128)(2,1)}, u32[]{:S(2)}) copy-start(bf16[2,32,256,128]{3,2,1,0:T(8,128)(2,1)} %interp_ref.4) | copy-start | bytes 12582916
  20.5 18.9 %collective-permute-start.3 = (bf16[1552,128]{1,0:T(8,128)(2,1)S(1)}, bf16[1552,128]{1,0:T(8,128)(2,1)S(1)}, u32[]{:S(2)}, u32[]{:S(2)}) collective-permute-start(bf16[1552,128]{1,0:T(8,128)(2,1)S(1)} %get-tuple-element.23), channel_id=1, source_target_pairs={{4,0},{8,4},{12,8},{16,12},{20,16},{24,20},{28,24},{5,1},{9,5},{13... | collective-permute-start | bytes 1191944 | tf_op jit(solution)/shard_map/ppermute | solution.py:18
  21.8 12.5 %collective-permute-start = (bf16[2,2,128,128]{3,2,1,0:T(8,128)(2,1)S(1)}, bf16[2,2,128,128]{3,2,1,0:T(8,128)(2,1)S(1)}, u32[]{:S(2)}, u32[]{:S(2)}) collective-permute-start(bf16[2,2,128,128]{3,2,1,0:T(8,128)(2,1)S(1)} %get-tuple-element.15), channel_id=1, source_target_pairs={{1,0},{2,1},{3,2},{5,4},{6,5},{7,6},{9,8},{10,9},{11,10},{13,12},{... | collective-permute-start | bytes 393224 | tf_op jit(solution)/shard_map/ppermute | solution.py:18
  23.1 18.4 %collective-permute-start.2 = (bf16[528,128]{1,0:T(8,128)(2,1)S(1)}, bf16[528,128]{1,0:T(8,128)(2,1)S(1)}, u32[]{:S(2)}, u32[]{:S(2)}) collective-permute-start(bf16[528,128]{1,0:T(8,128)(2,1)S(1)} %get-tuple-element.22), channel_id=1, source_target_pairs={{4,0},{8,4},{12,8},{16,12},{20,16},{24,20},{28,24},{5,1},{9,5},{13... | collective-permute-start | bytes 405512 | tf_op jit(solution)/shard_map/ppermute | solution.py:18
  30.9 3.4 %copy-start.2 = (s32[2,32,128]{2,1,0:T(8,128)S(1)}, s32[2,32,128]{2,1,0:T(8,128)}, u32[]{:S(2)}) copy-start(s32[2,32,128]{2,1,0:T(8,128)} %skel_ref.5) | copy-start | bytes 98308
  30.9 3.4 %copy-start.4 = (bf16[2,32,128]{2,1,0:T(8,128)(2,1)S(1)}, bf16[2,32,128]{2,1,0:T(8,128)(2,1)}, u32[]{:S(2)}) copy-start(bf16[2,32,128]{2,1,0:T(8,128)(2,1)} %coup_ref.3) | copy-start | bytes 49156

commit v15 on v13

--- a/solution.py
+++ b/solution.py
@@ -87,10 +87,17 @@
         copy.start()
     for copy in small:
         copy.wait()
+    slots = skel_ref.shape[-1]
+    ranks = jnp.transpose(jnp.broadcast_to(rank_ref[0:1].astype(F32), (slots, count)))
+    live = lax.broadcasted_iota(jnp.int32, (count, slots), 1).astype(F32) < ranks
+    picked = jnp.where(live, skel_ref[...].astype(F32), F32(-1.0))
+    lives = jnp.where(live, F32(1.0), F32(0.0))
+    row = lax.broadcasted_iota(jnp.int32, (half, slots), 0).astype(F32).astype(BF)
     for c in range(count // cells):
         copies[c].wait()
         for k in range(c * cells, (c + 1) * cells):
-            out_ref[k] = marked_of(skel_ref[k : k + 1], rank_ref[0, k], held[k])
+            interp = held[k] * lives[k : k + 1].astype(BF)
+            out_ref[k] = jnp.where(row == picked[k : k + 1].astype(BF), BF(1.0), interp)
 
 
 def pack_masks(size):
@@ -346,7 +353,7 @@
         4 * nj * half * slots,
         vmem=8,
         scratch=[
-            pltpu.SMEM((nx, nj), jnp.int32),
+            pltpu.VMEM((nx, nj), jnp.int32),
             pltpu.VMEM((nj, slots), jnp.int32),
             pltpu.VMEM((nj, half, slots), BF),
             pltpu.SemaphoreType.DMA((2,)),

time: 42.9 us -> 43 us (level)
  no operation moved by 1% of the time
where the time goes in v15:
time: 43 us; the launch traced here: 42.6 us
  Pallas kernels  26.5 us (62%)
  waiting for transfers between devices  10.1 us (23%)
  starting transfers between devices  5.16 us (12%)
  between operations  0.8 us (2%)
    pallas_call x1, Pallas kernels, body(): call(functools.partial(main_kernel, cells, nx, chunks), (nx, chunks), [sm...  17.1 us
    ppermute x4, waiting for transfers between devices, passed_along(): return lax.ppermute(x, axis, pairs)  10.1 us
    ppermute x4, starting transfers between devices, passed_along(): return lax.ppermute(x, axis, pairs)  5.16 us
    pallas_call x1, Pallas kernels, body(): call(functools.partial(x_part_kernel, cells, last), (), [smem, vmem, vmem...  3.32 us
    pallas_call x2, Pallas kernels, body(): call(functools.partial(x_last_kernel, cells, last, places), (), [vmem, vm...  2.68 us
    pallas_call x1, Pallas kernels, body(): call(functools.partial(y_edge_kernel, nx, tail), (1,), [smem, pl.BlockSpe...  2.05 us
    pallas_call x1, Pallas kernels, body(): call(functools.partial(top_kernel, cells), (), [hbm, hbm, hbm], vmem, sha...  1.4 us
  transfers between devices with their start and end apart: 4, of which 3 were waited for; matrix products, arithmetic and copies ran while one was open for 0% of the time, Pallas kernels for 56%

profile of v15, /device:TPU:0, one launch (start us, length us, event | category | flops | bytes accessed | tf_op | source)
XLA Modules:
  0.0 42.6 jit_solution(1578827098476300872)
XLA Ops:
  0.6 0.0 copy-start.6
  0.6 0.0 copy-start.5
  0.7 0.0 copy-start.7
  0.7 1.4 %shard_map.132 = bf16[32,128,128]{2,1,0:T(8,128)(2,1)S(1)} custom-call(s32[2,32]{1,0:T(2,128)} %rank_hbm.1, s32[2,32,128]{2,1,0:T(8,128)} %skel_hbm.1, bf16[2,32,256,128]{3,2,1,0:T(8,128)(2,1)} %interp_hbm.1), custom_call_target="tpu_custom_call" | custom-call | bytes 2097152 | tf_op jit(solution)/shard_map/pallas_call | solution.py:346
  2.1 0.0 copy-start.1
  2.1 0.0 copy-start.3
  2.1 1.3 %collective-permute-start.1 = (bf16[32,128,128]{2,1,0:T(8,128)(2,1)S(1)}, bf16[32,128,128]{2,1,0:T(8,128)(2,1)S(1)}, u32[]{:S(2)}, u32[]{:S(2)}) collective-permute-start(bf16[32,128,128]{2,1,0:T(8,128)(2,1)S(1)} %shard_map.132), channel_id=1, source_target_pairs={{4,0},{8,4},{12,8},{16,12},{20,16},{24,20},{28,24},{5,1},{9,5},{13... | collective-permute-start | bytes 3145736 | tf_op jit(solution)/shard_map/ppermute | solution.py:18
  3.4 0.0 copy-done.6
  3.4 0.0 copy-done.5
  3.4 0.0 copy-start
  3.4 17.1 %shard_map.131 = (bf16[2,32,128,128]{3,2,1,0:T(8,128)(2,1)}, bf16[2,32,128,128]{3,2,1,0:T(8,128)(2,1)}, bf16[1552,128]{1,0:T(8,128)(2,1)S(1)}, bf16[528,128]{1,0...) custom-call(s32[2,32]{1,0:T(2,128)S(1)} %copy-done.6, ...), custom_call_target="tpu_custom_call" | custom-call | flops 5368709120 | bytes 27262976 | tf_op jit(solution)/shard_map/pallas_call | solution.py:384
  20.5 1.3 %collective-permute-start.3 = (bf16[1552,128]{1,0:T(8,128)(2,1)S(1)}, bf16[1552,128]{1,0:T(8,128)(2,1)S(1)}, u32[]{:S(2)}, u32[]{:S(2)}) collective-permute-start(bf16[1552,128]{1,0:T(8,128)(2,1)S(1)} %get-tuple-element.23), channel_id=1, source_target_pairs={{4,0},{8,4},{12,8},{16,12},{20,16},{24,20},{28,24},{5,1},{9,5},{13... | collective-permute-start | bytes 1191944 | tf_op jit(solution)/shard_map/ppermute | solution.py:18
  21.8 1.3 %collective-permute-start = (bf16[2,2,128,128]{3,2,1,0:T(8,128)(2,1)S(1)}, bf16[2,2,128,128]{3,2,1,0:T(8,128)(2,1)S(1)}, u32[]{:S(2)}, u32[]{:S(2)}) collective-permute-start(bf16[2,2,128,128]{3,2,1,0:T(8,128)(2,1)S(1)} %get-tuple-element.15), channel_id=1, source_target_pairs={{1,0},{2,1},{3,2},{5,4},{6,5},{7,6},{9,8},{10,9},{11,10},{13,12},{... | collective-permute-start | bytes 393224 | tf_op jit(solution)/shard_map/ppermute | solution.py:18
  23.1 1.3 %collective-permute-start.2 = (bf16[528,128]{1,0:T(8,128)(2,1)S(1)}, bf16[528,128]{1,0:T(8,128)(2,1)S(1)}, u32[]{:S(2)}, u32[]{:S(2)}) collective-permute-start(bf16[528,128]{1,0:T(8,128)(2,1)S(1)} %get-tuple-element.22), channel_id=1, source_target_pairs={{4,0},{8,4},{12,8},{16,12},{20,16},{24,20},{28,24},{5,1},{9,5},{13... | collective-permute-start | bytes 405512 | tf_op jit(solution)/shard_map/ppermute | solution.py:18
  24.4 6.5 %collective-permute-done.1.top_ref = bf16[32,128,128]{2,1,0:T(8,128)(2,1)S(1)} collective-permute-done((bf16[32,128,128]{2,1,0:T(8,128)(2,1)S(1)}, bf16[32,128,128]{2,1,0:T(8,128)(2,1)S(1)}, u32[]{:S(2)}, u32[]{:S(2)}) %collective-permute-start.1) | collective-permute-done | bytes 1048608 | tf_op jit(solution)/shard_map/ppermute | solution.py:18
  31.0 0.0 copy-start.2
  31.0 0.0 copy-start.4
  31.0 3.3 %shard_map.133 = (f32[32,128,128]{2,1,0:T(8,128)S(1)}, bf16[32,128,128]{2,1,0:T(8,128)(2,1)S(1)}, bf16[32,128,128]{2,1,0:T(8,128)(2,1)S(1)}) custom-call(s32[2,32]{1,0:T(2,128)S(1)} %copy-done.7, s32[2,32,128]{2,1,0:T(8,128)S(1)} %copy-done.1, bf16[2,32,256,128]{3,2,1,0:T(8,128)(2,1)S(1)} %copy-done, bf16[2,32,128]{2,1,0:T(8,128)(2,1)S(1)} %copy-done.3, ...), custom_call_target="tpu_custom_call" | custom-call | flops 1073741824 | bytes 12582912 | tf_op jit(solution)/shard_map/pallas_call | solution.py:429
  34.3 0.0 collective-permute-done.edge_ref
  34.3 2.1 %shard_map.136 = bf16[2,32,128,128]{3,2,1,0:T(8,128)(2,1)} custom-call(s32[2,32]{1,0:T(2,128)S(1)} %copy-done.5, s32[2,32,128]{2,1,0:T(8,128)S(1)} %copy-done.2, bf16[2,32,256,128]{3,2,1,0:T(8,128)(2,1)} %interp_ref.5, bf16[2,32,128]{2,1,0:T(8,128)(2,1)S(1)} %copy-done.4, ...), custom_call_target="tpu_custom_call", output_to_operand_aliasing={{}: (6, {})} | custom-call | flops 67108864 | bytes 786432 | tf_op jit(solution)/shard_map/pallas_call | solution.py:445
  36.4 3.1 %collective-permute-done.3.packed_ref = bf16[1552,128]{1,0:T(8,128)(2,1)S(1)} collective-permute-done((bf16[1552,128]{1,0:T(8,128)(2,1)S(1)}, bf16[1552,128]{1,0:T(8,128)(2,1)S(1)}, u32[]{:S(2)}, u32[]{:S(2)}) %collective-permute-start.3) | collective-permute-done | bytes 397344 | tf_op jit(solution)/shard_map/ppermute | solution.py:18
  39.5 1.6 %shard_map.134._ = bf16[2,32,128,128]{3,2,1,0:T(8,128)(2,1)} custom-call(f32[32,128,128]{2,1,0:T(8,128)S(1)} %get-tuple-element.19.part_ref, bf16[32,128,128]{2,1,0:T(8,128)(2,1)S(1)} %get-tuple-element.20.lower_ref, bf16[32,128,128]{2,1,0:T(8,128)(2,1)S(1)} %get-tuple-element.21.lower_turned_ref, ...), custom_call_target="tpu_custom_call", output_to_operand_aliasing={{}: (4, {})} | custom-call | flops 301989888 | bytes 4325376 | tf_op jit(solution)/shard_map/pallas_call | solution.py:469
  41.1 0.5 %collective-permute-done.2.packed_ref = bf16[528,128]{1,0:T(8,128)(2,1)S(1)} collective-permute-done((bf16[528,128]{1,0:T(8,128)(2,1)S(1)}, bf16[528,128]{1,0:T(8,128)(2,1)S(1)}, u32[]{:S(2)}, u32[]{:S(2)}) %collective-permute-start.2) | collective-permute-done | bytes 135200 | tf_op jit(solution)/shard_map/ppermute | solution.py:18
  41.5 1.1 %shard_map.135 = bf16[2,32,128,128]{3,2,1,0:T(8,128)(2,1)} custom-call(f32[32,128,128]{2,1,0:T(8,128)S(1)} %get-tuple-element.19.part_ref, bf16[32,128,128]{2,1,0:T(8,128)(2,1)S(1)} %get-tuple-element.20.lower_ref, bf16[32,128,128]{2,1,0:T(8,128)(2,1)S(1)} %get-tuple-element.21.lower_turned_ref, ...), custom_call_target="tpu_custom_call", output_to_operand_aliasing={{}: (4, {})} | custom-call | flops 100663296 | bytes 1441792 | tf_op jit(solution)/shard_map/pallas_call | solution.py:469
  (6 shorter events, 0.0 us)
Async XLA Ops:
  0.6 2.8 %copy-start.6 = (s32[2,32]{1,0:T(2,128)S(1)}, s32[2,32]{1,0:T(2,128)}, u32[]{:S(2)}) copy-start(s32[2,32]{1,0:T(2,128)} %rank_hbm.1) | copy-start | bytes 772
  0.6 2.8 %copy-start.5 = (s32[2,32]{1,0:T(2,128)S(1)}, s32[2,32]{1,0:T(2,128)}, u32[]{:S(2)}) copy-start(s32[2,32]{1,0:T(2,128)} %rank_ref.5) | copy-start | bytes 772
  0.7 2.8 %copy-start.7 = (s32[2,32]{1,0:T(2,128)S(1)}, s32[2,32]{1,0:T(2,128)}, u32[]{:S(2)}) copy-start(s32[2,32]{1,0:T(2,128)} %rank_ref.4) | copy-start | bytes 772
  2.1 28.9 %copy-start.1 = (s32[2,32,128]{2,1,0:T(8,128)S(1)}, s32[2,32,128]{2,1,0:T(8,128)}, u32[]{:S(2)}) copy-start(s32[2,32,128]{2,1,0:T(8,128)} %skel_ref.4) | copy-start | bytes 98308
  2.1 28.9 %copy-start.3 = (bf16[2,32,128]{2,1,0:T(8,128)(2,1)S(1)}, bf16[2,32,128]{2,1,0:T(8,128)(2,1)}, u32[]{:S(2)}) copy-start(bf16[2,32,128]{2,1,0:T(8,128)(2,1)} %coup_ref.2) | copy-start | bytes 49156
  2.1 28.9 %collective-permute-start.1 = (bf16[32,128,128]{2,1,0:T(8,128)(2,1)S(1)}, bf16[32,128,128]{2,1,0:T(8,128)(2,1)S(1)}, u32[]{:S(2)}, u32[]{:S(2)}) collective-permute-start(bf16[32,128,128]{2,1,0:T(8,128)(2,1)S(1)} %shard_map.132), channel_id=1, source_target_pairs={{4,0},{8,4},{12,8},{16,12},{20,16},{24,20},{28,24},{5,1},{9,5},{13... | collective-permute-start | bytes 3145736 | tf_op jit(solution)/shard_map/ppermute | solution.py:18
  3.4 27.5 %copy-start = (bf16[2,32,256,128]{3,2,1,0:T(8,128)(2,1)S(1)}, bf16[2,32,256,128]{3,2,1,0:T(8,128)(2,1)}, u32[]{:S(2)}) copy-start(bf16[2,32,256,128]{3,2,1,0:T(8,128)(2,1)} %interp_ref.4) | copy-start | bytes 12582916
  20.5 18.9 %collective-permute-start.3 = (bf16[1552,128]{1,0:T(8,128)(2,1)S(1)}, bf16[1552,128]{1,0:T(8,128)(2,1)S(1)}, u32[]{:S(2)}, u32[]{:S(2)}) collective-permute-start(bf16[1552,128]{1,0:T(8,128)(2,1)S(1)} %get-tuple-element.23), channel_id=1, source_target_pairs={{4,0},{8,4},{12,8},{16,12},{20,16},{24,20},{28,24},{5,1},{9,5},{13... | collective-permute-start | bytes 1191944 | tf_op jit(solution)/shard_map/ppermute | solution.py:18
  21.8 12.5 %collective-permute-start = (bf16[2,2,128,128]{3,2,1,0:T(8,128)(2,1)S(1)}, bf16[2,2,128,128]{3,2,1,0:T(8,128)(2,1)S(1)}, u32[]{:S(2)}, u32[]{:S(2)}) collective-permute-start(bf16[2,2,128,128]{3,2,1,0:T(8,128)(2,1)S(1)} %get-tuple-element.15), channel_id=1, source_target_pairs={{1,0},{2,1},{3,2},{5,4},{6,5},{7,6},{9,8},{10,9},{11,10},{13,12},{... | collective-permute-start | bytes 393224 | tf_op jit(solution)/shard_map/ppermute | solution.py:18
  23.1 18.4 %collective-permute-start.2 = (bf16[528,128]{1,0:T(8,128)(2,1)S(1)}, bf16[528,128]{1,0:T(8,128)(2,1)S(1)}, u32[]{:S(2)}, u32[]{:S(2)}) collective-permute-start(bf16[528,128]{1,0:T(8,128)(2,1)S(1)} %get-tuple-element.22), channel_id=1, source_target_pairs={{4,0},{8,4},{12,8},{16,12},{20,16},{24,20},{28,24},{5,1},{9,5},{13... | collective-permute-start | bytes 405512 | tf_op jit(solution)/shard_map/ppermute | solution.py:18
  31.0 3.4 %copy-start.2 = (s32[2,32,128]{2,1,0:T(8,128)S(1)}, s32[2,32,128]{2,1,0:T(8,128)}, u32[]{:S(2)}) copy-start(s32[2,32,128]{2,1,0:T(8,128)} %skel_ref.5) | copy-start | bytes 98308
  31.0 3.4 %copy-start.4 = (bf16[2,32,128]{2,1,0:T(8,128)(2,1)S(1)}, bf16[2,32,128]{2,1,0:T(8,128)(2,1)}, u32[]{:S(2)}) copy-start(bf16[2,32,128]{2,1,0:T(8,128)(2,1)} %coup_ref.3) | copy-start | bytes 49156

commit v16 on v13

--- a/solution.py
+++ b/solution.py
@@ -26,24 +26,22 @@
     return lax.dot_general(a, b, (((1,), (0,)), ((), ())), preferred_element_type=F32)
 
 
-def marks_of(skel_row, rank, interp):
-    rows, slots = interp.shape
-    live = lax.broadcasted_iota(jnp.int32, (1, slots), 1) < rank
-    picked_row = jnp.where(live, skel_row, -1).astype(F32).astype(BF)
-    row = lax.broadcasted_iota(jnp.int32, (rows, slots), 0).astype(F32).astype(BF)
-    live_row = jnp.where(live, F32(1.0), F32(0.0)).astype(BF)
-    return row == picked_row, interp * live_row
-
-
 def kept_cleared(turned):
     most = jnp.max(turned, axis=0, keepdims=True)
     least = jnp.where(most.astype(F32) == 1.0, F32(1.0), F32(-2.0)).astype(BF)
     return jnp.where(turned >= least, turned, BF(0.0))
 
 
+def marked_with(skel_row, live, interp):
+    rows, slots = interp.shape
+    picked_row = jnp.where(live, skel_row, -1).astype(F32).astype(BF)
+    row = lax.broadcasted_iota(jnp.int32, (rows, slots), 0).astype(F32).astype(BF)
+    live_row = jnp.where(live, F32(1.0), F32(0.0)).astype(BF)
+    return jnp.where(row == picked_row, BF(1.0), interp * live_row)
+
+
 def marked_of(skel_row, rank, interp):
-    hit, live = marks_of(skel_row, rank, interp)
-    return jnp.where(hit, BF(1.0), live)
+    return marked_with(skel_row, lax.broadcasted_iota(jnp.int32, skel_row.shape, 1) < rank, interp)
 
 
 def bases_of(cells, layer, first, rank_ref, skel, interp_ref):
@@ -67,30 +65,6 @@
 def project(turned, matrices):
     inner = [dot(t, m).astype(BF) for t, m in zip(turned, matrices)]
     return [dot_nt(i, t) for i, t in zip(inner, turned)]
-
-
-def top_kernel(cells, rank_hbm, skel_hbm, interp_hbm, out_ref, rank_ref, skel_ref, held, small_sems, sems):
-    count, half, _ = out_ref.shape
-    small = [
-        pltpu.make_async_copy(rank_hbm, rank_ref, small_sems.at[0]),
-        pltpu.make_async_copy(skel_hbm.at[0], skel_ref, small_sems.at[1]),
-    ]
-    copies = []
-    for c in range(count // cells):
-        group = pl.ds(c * cells, cells)
-        copies.append(
-            pltpu.make_async_copy(
-                interp_hbm.at[0, group, pl.ds(0, half)], held.at[group], sems.at[c]
-            )
-        )
-    for copy in small + copies:
-        copy.start()
-    for copy in small:
-        copy.wait()
-    for c in range(count // cells):
-        copies[c].wait()
-        for k in range(c * cells, (c + 1) * cells):
-            out_ref[k] = marked_of(skel_ref[k : k + 1], rank_ref[0, k], held[k])
 
 
 def pack_masks(size):
@@ -222,7 +196,7 @@
 
 
 def x_part_kernel(
-    cells, layer, rank_ref, skel_ref, interp_ref, coup_ref, turned_ref, schur_ref, top_ref,
+    cells, layer, rank_ref, skel_ref, interp_ref, coup_ref, turned_ref, schur_ref, top_ref, picks_ref,
     part_ref, lower_ref, lower_turned_ref,
 ):
     count, slots, half = turned_ref.shape
@@ -237,7 +211,10 @@
         for k in group:
             lower_turned_ref[k] = faces[k - first][:, half:]
             lower_ref[k] = jnp.transpose(faces[k - first][:, half:])
-        tops = [kept_cleared(t) for t in [jnp.transpose(top_ref[k]) for k in group]]
+        tops = []
+        for k in group:
+            picks = picks_ref[k : k + 1]
+            tops.append(kept_cleared(jnp.transpose(marked_with(picks - 1, picks > 0, top_ref[k]))))
         matrices = []
         for k, top in zip(group, tops):
             conduct = coup_ref[layer, k : k + 1]
@@ -336,25 +313,11 @@
 
     hbm = pl.BlockSpec(memory_space=pltpu.HBM)
     vmem = pl.BlockSpec(memory_space=pltpu.VMEM)
-    top = call(
-        functools.partial(top_kernel, cells),
-        (),
-        [hbm, hbm, hbm],
-        vmem,
-        shape((nj, half, slots), BF),
-        0,
-        4 * nj * half * slots,
-        vmem=8,
-        scratch=[
-            pltpu.SMEM((nx, nj), jnp.int32),
-            pltpu.VMEM((nj, slots), jnp.int32),
-            pltpu.VMEM((nj, half, slots), BF),
-            pltpu.SemaphoreType.DMA((2,)),
-            pltpu.SemaphoreType.DMA((chunks,)),
-        ],
-    )(in_hbm(cell_rank), in_hbm(cell_skel), in_hbm(cell_interp))
-    top_in = passed_along(top, "gx", -1)
-
+    top_in = passed_along(cell_interp[0, :, :half], "gx", -1)
+    live = lax.broadcasted_iota(jnp.int32, (nj, slots), 1) < cell_rank[0, :, None]
+    gathered = lax.all_gather(jnp.where(live, cell_skel[0] + 1, 0), "gx")
+    gathered = jnp.concatenate([gathered, jnp.zeros_like(gathered[:1])], axis=0)
+    picks_in = lax.dynamic_index_in_dim(gathered, lax.axis_index("gx") + 1, 0, keepdims=False)
 
     def pack_rows(count):
         extra = count * -(-cells // 2)
@@ -422,7 +385,7 @@
     part, lower, lower_turned = call(
         functools.partial(x_part_kernel, cells, last),
         (),
-        [smem, vmem, vmem, vmem, vmem, vmem, vmem],
+        [smem, vmem, vmem, vmem, vmem, vmem, vmem, vmem],
         [vmem, vmem, vmem],
         [
             shape((nj, fslots, fslots), F32),
@@ -432,7 +395,7 @@
         8 * unit // nx,
         face_bytes,
         vmem=16,
-    )(x_face_rank, x_face_skel, x_face_interp, x_coupling, last_turned, last_schur, top_in)
+    )(x_face_rank, x_face_skel, x_face_interp, x_coupling, last_turned, last_schur, top_in, picks_in)
 
     edge_in, part = lax.optimization_barrier((edge_in, part))
     y_out = call(

time: 42.9 us -> 81.6 us (1.90)
  blocking collectives: 0 us -> 41.2 us
  waiting for transfers between devices: 10.1 us -> 0.01 us
  local copies, waits for them, and re-layouts: 0.04 us -> 6.69 us
    all_gather x0 -> x1, blocking collectives: none -> 41.2 us  [body(): gathered = lax.all_gather(jnp.where(live, cell_skel[0] + 1, 0), 'gx')]
    ppermute x4, waiting for transfers between devices: 10.1 us -> 0.01 us  [passed_along(): return lax.ppermute(x, axis, pairs)]
    unnamed x16 -> x20, local copies, waits for them, and re-layouts: 0.04 us -> 4.34 us
    squeeze x0 -> x2, local copies, waits for them, and re-layouts: none -> 2.34 us  [the longest x1 2.34 us: body(): top_in = passed_along(cell_interp[0, :, :half], 'gx', -1)]
    pallas_call x1 -> x0, Pallas kernels: 1.35 us -> none  [body(): call(functools.partial(top_kernel, cells), (), [hbm, hbm, hbm], vmem, sha...]
    pallas_call x2, Pallas kernels: 2.68 us -> 3.59 us  [body(): call(functools.partial(x_last_kernel, cells, last, places), (), [vmem, vm...]
  transfers between devices with their start and end apart: 4 -> 4, of which waited for: 3 -> 0; matrix products, arithmetic and copies ran while one was open for 0% -> 1% of each run, Pallas kernels for 56% -> 30%
where the time goes in v16:
time: 81.6 us; the launch traced here: 81.1 us
  blocking collectives  41.2 us (50%)
  Pallas kernels  26.4 us (32%)
  local copies, waits for them, and re-layouts  6.69 us (8%)
  starting transfers between devices  5.14 us (6%)
    all_gather x1, blocking collectives, body(): gathered = lax.all_gather(jnp.where(live, cell_skel[0] + 1, 0), 'gx')  41.2 us
    pallas_call x1, Pallas kernels, body(): call(functools.partial(main_kernel, cells, nx, chunks), (nx, chunks), [sm...  17.3 us
    ppermute x4, starting transfers between devices, passed_along(): return lax.ppermute(x, axis, pairs)  5.14 us
    unnamed x20, local copies, waits for them, and re-layouts  4.34 us
    pallas_call x2, Pallas kernels, body(): call(functools.partial(x_last_kernel, cells, last, places), (), [vmem, vm...  3.59 us
    pallas_call x1, Pallas kernels, body(): call(functools.partial(x_part_kernel, cells, last), (), [smem, vmem, vmem...  3.45 us
    squeeze x1, local copies, waits for them, and re-layouts, body(): top_in = passed_along(cell_interp[0, :, :half], 'gx', -1)  2.34 us
    pallas_call x1, Pallas kernels, body(): call(functools.partial(y_edge_kernel, nx, tail), (1,), [smem, pl.BlockSpe...  2.12 us
  transfers between devices with their start and end apart: 4, of which 0 were waited for; matrix products, arithmetic and copies ran while one was open for 1% of the time, Pallas kernels for 30%

profile of v16, /device:TPU:0, one launch (start us, length us, event | category | flops | bytes accessed | tf_op | source)
XLA Modules:
  0.0 81.1 jit_solution(9111089082187273728)
XLA Ops:
  0.7 2.3 %slice_bitcast_fusion = bf16[32,128,128]{2,1,0:T(8,128)(2,1)} fusion(bf16[2,32,256,128]{3,2,1,0:T(8,128)(2,1)} %interp_ref.3), kind=kLoop, calls=%fused_computation | loop fusion | bytes 2097152 | tf_op jit(solution)/shard_map/squeeze | solution.py:316
  3.0 1.3 %collective-permute-start.1 = (bf16[32,128,128]{2,1,0:T(8,128)(2,1)}, bf16[32,128,128]{2,1,0:T(8,128)(2,1)S(1)}, u32[]{:S(2)}, u32[]{:S(2)}) collective-permute-start(bf16[32,128,128]{2,1,0:T(8,128)(2,1)} %slice_bitcast_fusion), channel_id=1, source_target_pairs={{4,0},{8,4},{12,8},{16,12},{20,16},{24,20},{28,24},{5,1},{9,5},{13... | collective-permute-start | bytes 3145736 | tf_op jit(solution)/shard_map/ppermute | solution.py:18
  4.3 0.0 copy-done.7
  4.3 0.0 copy-done.8
  4.3 0.0 copy-done.9
  4.3 17.3 %shard_map.131 = (bf16[2,32,128,128]{3,2,1,0:T(8,128)(2,1)}, bf16[2,32,128,128]{3,2,1,0:T(8,128)(2,1)}, bf16[1552,128]{1,0:T(8,128)(2,1)}, bf16[528,128]{1,0:T(8...) custom-call(s32[2,32]{1,0:T(2,128)S(1)} %copy-done.9, ...), custom_call_target="tpu_custom_call" | custom-call | flops 5368709120 | bytes 27262976 | tf_op jit(solution)/shard_map/pallas_call | solution.py:340
  21.6 0.7 copy-done.1
  22.3 1.3 %collective-permute-start = (bf16[2,2,128,128]{3,2,1,0:T(8,128)(2,1)}, bf16[2,2,128,128]{3,2,1,0:T(8,128)(2,1)}, u32[]{:S(2)}, u32[]{:S(2)}) collective-permute-start(bf16[2,2,128,128]{3,2,1,0:T(8,128)(2,1)} %get-tuple-element.15), channel_id=1, source_target_pairs={{1,0},{2,1},{3,2},{5,4},{6,5},{7,6},{9,8},{10,9},{11,10},{13,12},{... | collective-permute-start | bytes 393224 | tf_op jit(solution)/shard_map/ppermute | solution.py:18
  23.5 1.3 %collective-permute-start.2 = (bf16[528,128]{1,0:T(8,128)(2,1)}, bf16[528,128]{1,0:T(8,128)(2,1)}, u32[]{:S(2)}, u32[]{:S(2)}) collective-permute-start(bf16[528,128]{1,0:T(8,128)(2,1)} %get-tuple-element.22), channel_id=1, source_target_pairs={{4,0},{8,4},{12,8},{16,12},{20,16},{24,20},{28,24},{5,1},{9,5},{13... | collective-permute-start | bytes 405512 | tf_op jit(solution)/shard_map/ppermute | solution.py:18
  24.8 1.3 %collective-permute-start.3 = (bf16[1552,128]{1,0:T(8,128)(2,1)}, bf16[1552,128]{1,0:T(8,128)(2,1)S(1)}, u32[]{:S(2)}, u32[]{:S(2)}) collective-permute-start(bf16[1552,128]{1,0:T(8,128)(2,1)} %get-tuple-element.23), channel_id=1, source_target_pairs={{4,0},{8,4},{12,8},{16,12},{20,16},{24,20},{28,24},{5,1},{9,5},{13... | collective-permute-start | bytes 1191944 | tf_op jit(solution)/shard_map/ppermute | solution.py:18
  26.2 0.8 add_select_fusion
  27.0 41.2 %all_gather.4 = s32[8,32,128]{2,1,0:T(8,128)S(1)} all-gather(s32[1,32,128]{2,1,0:T(8,128)S(1)} %add_select_fusion), channel_id=1, replica_groups=mesh['gx'=8,'yz'=4] {'gx'}, dimensions={0}, use_global_device_ids=true | all-gather | bytes 147456 | tf_op jit(solution)/shard_map/all_gather | solution.py:318
  68.2 0.0 collective-permute-done.1.top_ref
  68.2 0.0 copy-start
  68.2 2.2 %copy-done = bf16[2,32,256,128]{3,2,1,0:T(8,128)(2,1)S(1)} copy-done((bf16[2,32,256,128]{3,2,1,0:T(8,128)(2,1)S(1)}, bf16[2,32,256,128]{3,2,1,0:T(8,128)(2,1)}, u32[]{:S(2)}) %copy-start) | copy-done | bytes 4194328
  70.4 0.8 copy-done.3
  71.1 0.7 copy-done.5
  71.8 3.5 %shard_map.132 = (f32[32,128,128]{2,1,0:T(8,128)S(1)}, bf16[32,128,128]{2,1,0:T(8,128)(2,1)S(1)}, bf16[32,128,128]{2,1,0:T(8,128)(2,1)S(1)}) custom-call(s32[2,32]{1,0:T(2,128)S(1)} %copy-done.8, s32[2,32,128]{2,1,0:T(8,128)S(1)} %copy-done.3, bf16[2,32,256,128]{3,2,1,0:T(8,128)(2,1)S(1)} %copy-done, bf16[2,32,128]{2,1,0:T(8,128)(2,1)S(1)} %copy-done.5, ...), custom_call_target="tpu_custom_call" | custom-call | flops 1073741824 | bytes 12582912 | tf_op jit(solution)/shard_map/pallas_call | solution.py:385
  75.3 0.0 collective-permute-done.edge_ref
  75.3 2.1 %shard_map.135 = bf16[2,32,128,128]{3,2,1,0:T(8,128)(2,1)} custom-call(s32[2,32]{1,0:T(2,128)S(1)} %copy-done.7, s32[2,32,128]{2,1,0:T(8,128)S(1)} %copy-done.4, bf16[2,32,256,128]{3,2,1,0:T(8,128)(2,1)} %interp_ref.5, bf16[2,32,128]{2,1,0:T(8,128)(2,1)S(1)} %copy-done.6, bf16[2,2,128,128]{3,2,1,0:T(8,128)(2,1)S(1)} %copy-done.2, ...), custom_call_target="tpu_custom_call", output_to_operand_aliasing={{}: (6, {})} | custom-call | flops 67108864 | bytes 786432 | tf_op jit(solution)/shard_map/pallas_call | solution.py:401
  77.5 0.0 collective-permute-done.3.packed_ref
  77.5 1.6 %shard_map.133._ = bf16[2,32,128,128]{3,2,1,0:T(8,128)(2,1)} custom-call(f32[32,128,128]{2,1,0:T(8,128)S(1)} %get-tuple-element.19.part_ref, bf16[32,128,128]{2,1,0:T(8,128)(2,1)S(1)} %get-tuple-element.20.lower_ref, bf16[32,128,128]{2,1,0:T(8,128)(2,1)S(1)} %get-tuple-element.21.lower_turned_ref, ...), custom_call_target="tpu_custom_call", output_to_operand_aliasing={{}: (4, {})} | custom-call | flops 301989888 | bytes 4325376 | tf_op jit(solution)/shard_map/pallas_call | solution.py:425
  79.1 0.0 collective-permute-done.2.packed_ref
  79.1 2.0 %shard_map.134 = bf16[2,32,128,128]{3,2,1,0:T(8,128)(2,1)} custom-call(f32[32,128,128]{2,1,0:T(8,128)S(1)} %get-tuple-element.19.part_ref, bf16[32,128,128]{2,1,0:T(8,128)(2,1)S(1)} %get-tuple-element.20.lower_ref, bf16[32,128,128]{2,1,0:T(8,128)(2,1)S(1)} %get-tuple-element.21.lower_turned_ref, ...), custom_call_target="tpu_custom_call", output_to_operand_aliasing={{}: (4, {})} | custom-call | flops 100663296 | bytes 1441792 | tf_op jit(solution)/shard_map/pallas_call | solution.py:425
  (14 shorter events, 0.0 us)
Async XLA Ops:
  0.6 3.7 %copy-start.7 = (s32[2,32]{1,0:T(2,128)S(1)}, s32[2,32]{1,0:T(2,128)}, u32[]{:S(2)}) copy-start(s32[2,32]{1,0:T(2,128)} %rank_ref.5) | copy-start | bytes 772
  0.6 3.7 %copy-start.8 = (s32[2,32]{1,0:T(2,128)S(1)}, s32[2,32]{1,0:T(2,128)}, u32[]{:S(2)}) copy-start(s32[2,32]{1,0:T(2,128)} %rank_ref.4) | copy-start | bytes 772
  0.7 3.7 %copy-start.9 = (s32[2,32]{1,0:T(2,128)S(1)}, s32[2,32]{1,0:T(2,128)}, u32[]{:S(2)}) copy-start(s32[2,32]{1,0:T(2,128)} %rank_ref.3) | copy-start | bytes 772
  3.0 65.2 %collective-permute-start.1 = (bf16[32,128,128]{2,1,0:T(8,128)(2,1)}, bf16[32,128,128]{2,1,0:T(8,128)(2,1)S(1)}, u32[]{:S(2)}, u32[]{:S(2)}) collective-permute-start(bf16[32,128,128]{2,1,0:T(8,128)(2,1)} %slice_bitcast_fusion), channel_id=1, source_target_pairs={{4,0},{8,4},{12,8},{16,12},{20,16},{24,20},{28,24},{5,1},{9,5},{13... | collective-permute-start | bytes 3145736 | tf_op jit(solution)/shard_map/ppermute | solution.py:18
  21.6 0.7 copy-start.1
  22.3 53.0 %collective-permute-start = (bf16[2,2,128,128]{3,2,1,0:T(8,128)(2,1)}, bf16[2,2,128,128]{3,2,1,0:T(8,128)(2,1)}, u32[]{:S(2)}, u32[]{:S(2)}) collective-permute-start(bf16[2,2,128,128]{3,2,1,0:T(8,128)(2,1)} %get-tuple-element.15), channel_id=1, source_target_pairs={{1,0},{2,1},{3,2},{5,4},{6,5},{7,6},{9,8},{10,9},{11,10},{13,12},{... | collective-permute-start | bytes 393224 | tf_op jit(solution)/shard_map/ppermute | solution.py:18
  23.5 55.5 %collective-permute-start.2 = (bf16[528,128]{1,0:T(8,128)(2,1)}, bf16[528,128]{1,0:T(8,128)(2,1)}, u32[]{:S(2)}, u32[]{:S(2)}) collective-permute-start(bf16[528,128]{1,0:T(8,128)(2,1)} %get-tuple-element.22), channel_id=1, source_target_pairs={{4,0},{8,4},{12,8},{16,12},{20,16},{24,20},{28,24},{5,1},{9,5},{13... | collective-permute-start | bytes 405512 | tf_op jit(solution)/shard_map/ppermute | solution.py:18
  24.8 52.6 %collective-permute-start.3 = (bf16[1552,128]{1,0:T(8,128)(2,1)}, bf16[1552,128]{1,0:T(8,128)(2,1)S(1)}, u32[]{:S(2)}, u32[]{:S(2)}) collective-permute-start(bf16[1552,128]{1,0:T(8,128)(2,1)} %get-tuple-element.23), channel_id=1, source_target_pairs={{4,0},{8,4},{12,8},{16,12},{20,16},{24,20},{28,24},{5,1},{9,5},{13... | collective-permute-start | bytes 1191944 | tf_op jit(solution)/shard_map/ppermute | solution.py:18
  68.2 2.2 %copy-start = (bf16[2,32,256,128]{3,2,1,0:T(8,128)(2,1)S(1)}, bf16[2,32,256,128]{3,2,1,0:T(8,128)(2,1)}, u32[]{:S(2)}) copy-start(bf16[2,32,256,128]{3,2,1,0:T(8,128)(2,1)} %interp_ref.4) | copy-start | bytes 12582916
  70.4 0.8 copy-start.3
  71.1 0.7 copy-start.5
  71.8 3.5 %copy-start.2 = (bf16[2,2,128,128]{3,2,1,0:T(8,128)(2,1)S(1)}, bf16[2,2,128,128]{3,2,1,0:T(8,128)(2,1)}, u32[]{:S(2)}) copy-start(bf16[2,2,128,128]{3,2,1,0:T(8,128)(2,1)} %copy-done.1) | copy-start | bytes 393220
  71.8 3.5 %copy-start.4 = (s32[2,32,128]{2,1,0:T(8,128)S(1)}, s32[2,32,128]{2,1,0:T(8,128)}, u32[]{:S(2)}) copy-start(s32[2,32,128]{2,1,0:T(8,128)} %skel_ref.5) | copy-start | bytes 98308
  71.8 3.5 %copy-start.6 = (bf16[2,32,128]{2,1,0:T(8,128)(2,1)S(1)}, bf16[2,32,128]{2,1,0:T(8,128)(2,1)}, u32[]{:S(2)}) copy-start(bf16[2,32,128]{2,1,0:T(8,128)(2,1)} %coup_ref.3) | copy-start | bytes 49156

commit v17 on v13

--- a/solution.py
+++ b/solution.py
@@ -184,13 +184,12 @@
         @pl.when(chunk == 0)
         def _():
             pairs = -(-cells // 2)
-            for ref, places in ((packed_ref, range(chunks - 1)), (packed_last_ref, [chunks - 1])):
-                start = len(places) * cells * half
-                rows = [store_extra[c, :pairs] for c in places]
-                pad = ref.shape[0] - start - pairs * len(places)
-                if pad:
-                    rows.append(jnp.zeros((pad, slots), F32))
-                ref[start:] = jnp.concatenate(rows, axis=0).astype(BF)
+            start = (chunks - 1) * cells * half
+            rows = [store_extra[c, :pairs] for c in range(chunks)]
+            pad = packed_ref.shape[0] - start - pairs * chunks
+            if pad:
+                rows.append(jnp.zeros((pad, slots), F32))
+            packed_ref[start:] = jnp.concatenate(rows, axis=0).astype(BF)
 
     @pl.when(chunk == 0)
     def _():
@@ -249,7 +248,7 @@
 
 
 def x_last_kernel(
-    cells, layer, places, part_ref, lower_ref, lower_turned_ref, packed_ref, _, out_ref, held, sems
+    cells, layer, places, part_ref, lower_ref, lower_turned_ref, extra_ref, packed_ref, _, out_ref, held, sems
 ):
     slots = part_ref.shape[-1]
     half = slots // 2
@@ -259,7 +258,7 @@
     low_scale = jnp.where(opposite, mid, jnp.where(upper, zero, one))
     same_scale = jnp.where(same, one, zero)
     opposite_scale = jnp.where(opposite, one, zero)
-    extras = packed_ref[len(places) * cells * half :].astype(F32)
+    extras = extra_ref[(part_ref.shape[0] // cells - 1) * cells * half :].astype(F32)
     pairs = -(-cells // 2)
     copies = []
     for n, c in enumerate(places):
@@ -268,7 +267,7 @@
         for k in range(cells):
             start = (n * cells + k) * half
             packed = packed_ref[start : start + half].astype(F32)
-            extra = extras[n * pairs + k // 2 : n * pairs + k // 2 + 1]
+            extra = extras[c * pairs + k // 2 : c * pairs + k // 2 + 1]
             top, low = packed * top_scale, packed * low_scale
             if k % 2 == 0:
                 top += extra * opposite_scale
@@ -356,9 +355,8 @@
     top_in = passed_along(top, "gx", -1)
 
 
-    def pack_rows(count):
-        extra = count * -(-cells // 2)
-        return count * cells * slots // 2 + -(-extra // 16) * 16
+    late_rows = cells * slots // 2
+    early_rows = (chunks - 1) * late_rows + -(-chunks * -(-cells // 2) // 16) * 16
 
     near = max(nx - 2, 0)
 
@@ -390,8 +388,8 @@
         [
             shape((nx, nj, fslots, fslots), BF),
             shape((nx, nj, fslots, fslots), BF),
-            shape((pack_rows(chunks - 1), slots), BF),
-            shape((pack_rows(1), slots), BF),
+            shape((early_rows, slots), BF),
+            shape((late_rows, slots), BF),
             shape((nx, 2, slots, half), BF),
             shape((nx, 2, slots, half), BF),
             shape((nj, slots, half), BF),
@@ -462,17 +460,17 @@
         x_out = call(
             functools.partial(x_last_kernel, cells, last, places),
             (),
-            [vmem, vmem, vmem, vmem, hbm],
+            [vmem, vmem, vmem, vmem, vmem, hbm],
             hbm,
             shape((nx, nj, fslots, fslots), BF),
             3 * unit // nx * count // chunks,
             nj * slots * slots * 11 * count // chunks,
-            {4: 0},
+            {5: 0},
             scratch=[
                 pltpu.VMEM((count * cells, fslots, fslots), BF),
                 pltpu.SemaphoreType.DMA((count, 2)),
             ],
-        )(part, lower, lower_turned, arrived, x_out)
+        )(part, lower, lower_turned, packed_in, arrived, x_out)
     return (x_out, y_out)
 
 

time: 42.9 us -> 42.9 us (level)
  no operation moved by 1% of the time
where the time goes in v17:
time: 42.9 us; the launch traced here: 42.5 us
  Pallas kernels  26.4 us (62%)
  waiting for transfers between devices  10.1 us (24%)
  starting transfers between devices  5.16 us (12%)
  between operations  0.8 us (2%)
    pallas_call x1, Pallas kernels, body(): call(functools.partial(main_kernel, cells, nx, chunks), (nx, chunks), [sm...  17.1 us
    ppermute x4, waiting for transfers between devices, passed_along(): return lax.ppermute(x, axis, pairs)  10.1 us
    ppermute x4, starting transfers between devices, passed_along(): return lax.ppermute(x, axis, pairs)  5.16 us
    pallas_call x1, Pallas kernels, body(): call(functools.partial(x_part_kernel, cells, last), (), [smem, vmem, vmem...  3.22 us
    pallas_call x2, Pallas kernels, body(): call(functools.partial(x_last_kernel, cells, last, places), (), [vmem, vm...  2.68 us
    pallas_call x1, Pallas kernels, body(): call(functools.partial(y_edge_kernel, nx, tail), (1,), [smem, pl.BlockSpe...  2.05 us
    pallas_call x1, Pallas kernels, body(): call(functools.partial(top_kernel, cells), (), [hbm, hbm, hbm], vmem, sha...  1.35 us
  transfers between devices with their start and end apart: 4, of which 3 were waited for; matrix products, arithmetic and copies ran while one was open for 0% of the time, Pallas kernels for 56%

profile of v17, /device:TPU:0, one launch (start us, length us, event | category | flops | bytes accessed | tf_op | source)
XLA Modules:
  0.0 42.5 jit_solution(13759024109626572451)
XLA Ops:
  0.6 0.0 copy-start.6
  0.6 0.0 copy-start.5
  0.7 0.0 copy-start.7
  0.7 1.3 %shard_map.132 = bf16[32,128,128]{2,1,0:T(8,128)(2,1)S(1)} custom-call(s32[2,32]{1,0:T(2,128)} %rank_hbm.1, s32[2,32,128]{2,1,0:T(8,128)} %skel_hbm.1, bf16[2,32,256,128]{3,2,1,0:T(8,128)(2,1)} %interp_hbm.1), custom_call_target="tpu_custom_call" | custom-call | bytes 2097152 | tf_op jit(solution)/shard_map/pallas_call | solution.py:338
  2.0 0.0 copy-start.1
  2.0 0.0 copy-start.3
  2.0 1.3 %collective-permute-start.1 = (bf16[32,128,128]{2,1,0:T(8,128)(2,1)S(1)}, bf16[32,128,128]{2,1,0:T(8,128)(2,1)S(1)}, u32[]{:S(2)}, u32[]{:S(2)}) collective-permute-start(bf16[32,128,128]{2,1,0:T(8,128)(2,1)S(1)} %shard_map.132), channel_id=1, source_target_pairs={{4,0},{8,4},{12,8},{16,12},{20,16},{24,20},{28,24},{5,1},{9,5},{13... | collective-permute-start | bytes 3145736 | tf_op jit(solution)/shard_map/ppermute | solution.py:18
  3.3 0.0 copy-done.6
  3.4 0.0 copy-done.5
  3.4 0.0 copy-start
  3.4 17.1 %shard_map.131 = (bf16[2,32,128,128]{3,2,1,0:T(8,128)(2,1)}, bf16[2,32,128,128]{3,2,1,0:T(8,128)(2,1)}, bf16[1552,128]{1,0:T(8,128)(2,1)S(1)}, bf16[512,128]{1,0...) custom-call(s32[2,32]{1,0:T(2,128)S(1)} %copy-done.6, ...), custom_call_target="tpu_custom_call" | custom-call | flops 5368709120 | bytes 27262976 | tf_op jit(solution)/shard_map/pallas_call | solution.py:375
  20.5 1.3 %collective-permute-start.2 = (bf16[1552,128]{1,0:T(8,128)(2,1)S(1)}, bf16[1552,128]{1,0:T(8,128)(2,1)S(1)}, u32[]{:S(2)}, u32[]{:S(2)}) collective-permute-start(bf16[1552,128]{1,0:T(8,128)(2,1)S(1)} %get-tuple-element.22), channel_id=1, source_target_pairs={{4,0},{8,4},{12,8},{16,12},{20,16},{24,20},{28,24},{5,1},{9,5},{13... | collective-permute-start | bytes 1191944 | tf_op jit(solution)/shard_map/ppermute | solution.py:18
  21.8 1.3 %collective-permute-start = (bf16[2,2,128,128]{3,2,1,0:T(8,128)(2,1)S(1)}, bf16[2,2,128,128]{3,2,1,0:T(8,128)(2,1)S(1)}, u32[]{:S(2)}, u32[]{:S(2)}) collective-permute-start(bf16[2,2,128,128]{3,2,1,0:T(8,128)(2,1)S(1)} %get-tuple-element.15), channel_id=1, source_target_pairs={{1,0},{2,1},{3,2},{5,4},{6,5},{7,6},{9,8},{10,9},{11,10},{13,12},{... | collective-permute-start | bytes 393224 | tf_op jit(solution)/shard_map/ppermute | solution.py:18
  23.1 1.3 %collective-permute-start.3 = (bf16[512,128]{1,0:T(8,128)(2,1)S(1)}, bf16[512,128]{1,0:T(8,128)(2,1)S(1)}, u32[]{:S(2)}, u32[]{:S(2)}) collective-permute-start(bf16[512,128]{1,0:T(8,128)(2,1)S(1)} %get-tuple-element.23), channel_id=1, source_target_pairs={{4,0},{8,4},{12,8},{16,12},{20,16},{24,20},{28,24},{5,1},{9,5},{13... | collective-permute-start | bytes 393224 | tf_op jit(solution)/shard_map/ppermute | solution.py:18
  24.4 6.5 %collective-permute-done.1.top_ref = bf16[32,128,128]{2,1,0:T(8,128)(2,1)S(1)} collective-permute-done((bf16[32,128,128]{2,1,0:T(8,128)(2,1)S(1)}, bf16[32,128,128]{2,1,0:T(8,128)(2,1)S(1)}, u32[]{:S(2)}, u32[]{:S(2)}) %collective-permute-start.1) | collective-permute-done | bytes 1048608 | tf_op jit(solution)/shard_map/ppermute | solution.py:18
  30.9 0.0 copy-start.2
  30.9 0.0 copy-start.4
  30.9 3.2 %shard_map.133 = (f32[32,128,128]{2,1,0:T(8,128)S(1)}, bf16[32,128,128]{2,1,0:T(8,128)(2,1)S(1)}, bf16[32,128,128]{2,1,0:T(8,128)(2,1)S(1)}) custom-call(s32[2,32]{1,0:T(2,128)S(1)} %copy-done.7, s32[2,32,128]{2,1,0:T(8,128)S(1)} %copy-done.1, bf16[2,32,256,128]{3,2,1,0:T(8,128)(2,1)S(1)} %copy-done, bf16[2,32,128]{2,1,0:T(8,128)(2,1)S(1)} %copy-done.3, ...), custom_call_target="tpu_custom_call" | custom-call | flops 1073741824 | bytes 12582912 | tf_op jit(solution)/shard_map/pallas_call | solution.py:420
  34.2 0.0 collective-permute-done.edge_ref
  34.2 2.1 %shard_map.136 = bf16[2,32,128,128]{3,2,1,0:T(8,128)(2,1)} custom-call(s32[2,32]{1,0:T(2,128)S(1)} %copy-done.5, s32[2,32,128]{2,1,0:T(8,128)S(1)} %copy-done.2, bf16[2,32,256,128]{3,2,1,0:T(8,128)(2,1)} %interp_ref.5, bf16[2,32,128]{2,1,0:T(8,128)(2,1)S(1)} %copy-done.4, ...), custom_call_target="tpu_custom_call", output_to_operand_aliasing={{}: (6, {})} | custom-call | flops 67108864 | bytes 786432 | tf_op jit(solution)/shard_map/pallas_call | solution.py:436
  36.2 3.2 %collective-permute-done.2.extra_ref.packed_ref = bf16[1552,128]{1,0:T(8,128)(2,1)S(1)} collective-permute-done((bf16[1552,128]{1,0:T(8,128)(2,1)S(1)}, bf16[1552,128]{1,0:T(8,128)(2,1)S(1)}, u32[]{:S(2)}, u32[]{:S(2)}) %collective-permute-start.2) | collective-permute-done | bytes 397344 | tf_op jit(solution)/shard_map/ppermute | solution.py:18
  39.4 1.6 %shard_map.134._ = bf16[2,32,128,128]{3,2,1,0:T(8,128)(2,1)} custom-call(f32[32,128,128]{2,1,0:T(8,128)S(1)} %get-tuple-element.19.part_ref, bf16[32,128,128]{2,1,0:T(8,128)(2,1)S(1)} %get-tuple-element.20.lower_ref, bf16[32,128,128]{2,1,0:T(8,128)(2,1)S(1)} %get-tuple-element.21.lower_turned_ref, ...), custom_call_target="tpu_custom_call", output_to_operand_aliasing={{}: (5, {})} | custom-call | flops 301989888 | bytes 4325376 | tf_op jit(solution)/shard_map/pallas_call | solution.py:460
  41.0 0.4 collective-permute-done.3.packed_ref
  41.4 1.1 %shard_map.135 = bf16[2,32,128,128]{3,2,1,0:T(8,128)(2,1)} custom-call(f32[32,128,128]{2,1,0:T(8,128)S(1)} %get-tuple-element.19.part_ref, bf16[32,128,128]{2,1,0:T(8,128)(2,1)S(1)} %get-tuple-element.20.lower_ref, bf16[32,128,128]{2,1,0:T(8,128)(2,1)S(1)} %get-tuple-element.21.lower_turned_ref, ...), custom_call_target="tpu_custom_call", output_to_operand_aliasing={{}: (5, {})} | custom-call | flops 100663296 | bytes 1441792 | tf_op jit(solution)/shard_map/pallas_call | solution.py:460
  (6 shorter events, 0.0 us)
Async XLA Ops:
  0.6 2.7 %copy-start.6 = (s32[2,32]{1,0:T(2,128)S(1)}, s32[2,32]{1,0:T(2,128)}, u32[]{:S(2)}) copy-start(s32[2,32]{1,0:T(2,128)} %rank_hbm.1) | copy-start | bytes 772
  0.6 2.7 %copy-start.5 = (s32[2,32]{1,0:T(2,128)S(1)}, s32[2,32]{1,0:T(2,128)}, u32[]{:S(2)}) copy-start(s32[2,32]{1,0:T(2,128)} %rank_ref.5) | copy-start | bytes 772
  0.7 2.7 %copy-start.7 = (s32[2,32]{1,0:T(2,128)S(1)}, s32[2,32]{1,0:T(2,128)}, u32[]{:S(2)}) copy-start(s32[2,32]{1,0:T(2,128)} %rank_ref.4) | copy-start | bytes 772
  2.0 28.9 %copy-start.1 = (s32[2,32,128]{2,1,0:T(8,128)S(1)}, s32[2,32,128]{2,1,0:T(8,128)}, u32[]{:S(2)}) copy-start(s32[2,32,128]{2,1,0:T(8,128)} %skel_ref.4) | copy-start | bytes 98308
  2.0 28.9 %copy-start.3 = (bf16[2,32,128]{2,1,0:T(8,128)(2,1)S(1)}, bf16[2,32,128]{2,1,0:T(8,128)(2,1)}, u32[]{:S(2)}) copy-start(bf16[2,32,128]{2,1,0:T(8,128)(2,1)} %coup_ref.2) | copy-start | bytes 49156
  2.0 28.9 %collective-permute-start.1 = (bf16[32,128,128]{2,1,0:T(8,128)(2,1)S(1)}, bf16[32,128,128]{2,1,0:T(8,128)(2,1)S(1)}, u32[]{:S(2)}, u32[]{:S(2)}) collective-permute-start(bf16[32,128,128]{2,1,0:T(8,128)(2,1)S(1)} %shard_map.132), channel_id=1, source_target_pairs={{4,0},{8,4},{12,8},{16,12},{20,16},{24,20},{28,24},{5,1},{9,5},{13... | collective-permute-start | bytes 3145736 | tf_op jit(solution)/shard_map/ppermute | solution.py:18
  3.4 27.5 %copy-start = (bf16[2,32,256,128]{3,2,1,0:T(8,128)(2,1)S(1)}, bf16[2,32,256,128]{3,2,1,0:T(8,128)(2,1)}, u32[]{:S(2)}) copy-start(bf16[2,32,256,128]{3,2,1,0:T(8,128)(2,1)} %interp_ref.4) | copy-start | bytes 12582916
  20.5 18.9 %collective-permute-start.2 = (bf16[1552,128]{1,0:T(8,128)(2,1)S(1)}, bf16[1552,128]{1,0:T(8,128)(2,1)S(1)}, u32[]{:S(2)}, u32[]{:S(2)}) collective-permute-start(bf16[1552,128]{1,0:T(8,128)(2,1)S(1)} %get-tuple-element.22), channel_id=1, source_target_pairs={{4,0},{8,4},{12,8},{16,12},{20,16},{24,20},{28,24},{5,1},{9,5},{13... | collective-permute-start | bytes 1191944 | tf_op jit(solution)/shard_map/ppermute | solution.py:18
  21.8 12.4 %collective-permute-start = (bf16[2,2,128,128]{3,2,1,0:T(8,128)(2,1)S(1)}, bf16[2,2,128,128]{3,2,1,0:T(8,128)(2,1)S(1)}, u32[]{:S(2)}, u32[]{:S(2)}) collective-permute-start(bf16[2,2,128,128]{3,2,1,0:T(8,128)(2,1)S(1)} %get-tuple-element.15), channel_id=1, source_target_pairs={{1,0},{2,1},{3,2},{5,4},{6,5},{7,6},{9,8},{10,9},{11,10},{13,12},{... | collective-permute-start | bytes 393224 | tf_op jit(solution)/shard_map/ppermute | solution.py:18
  23.1 18.3 %collective-permute-start.3 = (bf16[512,128]{1,0:T(8,128)(2,1)S(1)}, bf16[512,128]{1,0:T(8,128)(2,1)S(1)}, u32[]{:S(2)}, u32[]{:S(2)}) collective-permute-start(bf16[512,128]{1,0:T(8,128)(2,1)S(1)} %get-tuple-element.23), channel_id=1, source_target_pairs={{4,0},{8,4},{12,8},{16,12},{20,16},{24,20},{28,24},{5,1},{9,5},{13... | collective-permute-start | bytes 393224 | tf_op jit(solution)/shard_map/ppermute | solution.py:18
  30.9 3.3 %copy-start.2 = (s32[2,32,128]{2,1,0:T(8,128)S(1)}, s32[2,32,128]{2,1,0:T(8,128)}, u32[]{:S(2)}) copy-start(s32[2,32,128]{2,1,0:T(8,128)} %skel_ref.5) | copy-start | bytes 98308
  30.9 3.3 %copy-start.4 = (bf16[2,32,128]{2,1,0:T(8,128)(2,1)S(1)}, bf16[2,32,128]{2,1,0:T(8,128)(2,1)}, u32[]{:S(2)}) copy-start(bf16[2,32,128]{2,1,0:T(8,128)(2,1)} %coup_ref.3) | copy-start | bytes 49156

commit v18 on v17

--- a/solution.py
+++ b/solution.py
@@ -247,34 +247,52 @@
             part_ref[k] = result
 
 
+def unpack_scale(row, lane, half):
+    ahead = lane - jnp.where(row < half, row, row - half)
+    inside = (ahead >= 0) & (ahead < half)
+    one, zero, mid = F32(1.0), F32(0.0), F32(0.5)
+    first = jnp.where(ahead == 0, mid, jnp.where(inside, one, zero))
+    second = jnp.where(ahead == half, mid, jnp.where(inside, zero, one))
+    return jnp.where(row < half, first, second).astype(BF)
+
+
 def x_last_kernel(
     cells, layer, places, part_ref, lower_ref, lower_turned_ref, extra_ref, packed_ref, _, out_ref, held, sems
 ):
     slots = part_ref.shape[-1]
     half = slots // 2
-    upper, same, opposite = pack_masks(slots)
-    one, zero, mid = F32(1.0), F32(0.0), F32(0.5)
-    top_scale = jnp.where(same, mid, jnp.where(upper, one, zero))
-    low_scale = jnp.where(opposite, mid, jnp.where(upper, zero, one))
-    same_scale = jnp.where(same, one, zero)
-    opposite_scale = jnp.where(opposite, one, zero)
+    row = lax.broadcasted_iota(jnp.int32, (slots, slots), 0)
+    lane = lax.broadcasted_iota(jnp.int32, (slots, slots), 1)
+    direct = unpack_scale(row, lane, half)
+    mirrored = unpack_scale(lane, row, half)
+    apart = jnp.where(jnp.abs(row - lane) == half, F32(1.0), F32(0.0)).astype(BF)
+    left = lane < half
     extras = extra_ref[(part_ref.shape[0] // cells - 1) * cells * half :].astype(F32)
+    rolled = pltpu.roll(extras, half, 1)
+    left_row = lax.broadcasted_iota(jnp.int32, extras.shape, 1) < half
+    extra_pair = (
+        jnp.where(left_row, rolled, extras).astype(BF).astype(F32),
+        jnp.where(left_row, extras, rolled).astype(BF).astype(F32),
+    )
     pairs = -(-cells // 2)
     copies = []
     for n, c in enumerate(places):
         group = range(c * cells, (c + 1) * cells)
         schurs = []
-        for k in range(cells):
+        for k in range(0, cells, 2):
             start = (n * cells + k) * half
-            packed = packed_ref[start : start + half].astype(F32)
-            extra = extras[c * pairs + k // 2 : c * pairs + k // 2 + 1]
-            top, low = packed * top_scale, packed * low_scale
-            if k % 2 == 0:
-                top += extra * opposite_scale
+            if k + 1 < cells:
+                stacked = packed_ref[start : start + slots]
             else:
-                low += extra * same_scale
-            tri = jnp.concatenate([top, low], axis=0).astype(BF)
-            schurs.append(tri + jnp.transpose(tri))
+                stacked = jnp.concatenate([packed_ref[start : start + half]] * 2, axis=0)
+            turned = jnp.transpose(stacked)
+            swapped = jnp.concatenate([turned[:, half:], turned[:, :half]], axis=1)
+            wide = (jnp.where(left, turned, swapped), jnp.where(left, swapped, turned))
+            for member in range(min(2, cells - k)):
+                block = stacked[member * half : (member + 1) * half]
+                double = jnp.concatenate([block, block], axis=0)
+                extra = extra_pair[member][c * pairs + k // 2 : c * pairs + k // 2 + 1].astype(BF)
+                schurs.append(double * direct + wide[member] * mirrored + extra * apart)
         inner = [dot(lower_turned_ref[k], h).astype(BF) for k, h in zip(group, schurs)]
         results = [dot(i, lower_ref[k]) for k, i in zip(group, inner)]
         part_cells = max(1, cells // 2)

time: 42.9 us -> 43 us (level)
  transfers between devices with their start and end apart: 4 -> 4, of which waited for: 3 -> 3; matrix products, arithmetic and copies ran while one was open for 0% -> 0% of each run, Pallas kernels for 56% -> 57%
where the time goes in v18:
time: 43 us; the launch traced here: 42.6 us
  Pallas kernels  26.7 us (62%)
  waiting for transfers between devices  9.9 us (23%)
  starting transfers between devices  5.16 us (12%)
  between operations  0.8 us (2%)
    pallas_call x1, Pallas kernels, body(): call(functools.partial(main_kernel, cells, nx, chunks), (nx, chunks), [sm...  17.1 us
    ppermute x4, waiting for transfers between devices, passed_along(): return lax.ppermute(x, axis, pairs)  9.9 us
    ppermute x4, starting transfers between devices, passed_along(): return lax.ppermute(x, axis, pairs)  5.16 us
    pallas_call x1, Pallas kernels, body(): call(functools.partial(x_part_kernel, cells, last), (), [smem, vmem, vmem...  3.22 us
    pallas_call x2, Pallas kernels, body(): call(functools.partial(x_last_kernel, cells, last, places), (), [vmem, vm...  2.96 us
    pallas_call x1, Pallas kernels, body(): call(functools.partial(y_edge_kernel, nx, tail), (1,), [smem, pl.BlockSpe...  2.05 us
    pallas_call x1, Pallas kernels, body(): call(functools.partial(top_kernel, cells), (), [hbm, hbm, hbm], vmem, sha...  1.35 us
  transfers between devices with their start and end apart: 4, of which 3 were waited for; matrix products, arithmetic and copies ran while one was open for 0% of the time, Pallas kernels for 57%

profile of v18, /device:TPU:0, one launch (start us, length us, event | category | flops | bytes accessed | tf_op | source)
XLA Modules:
  0.0 42.6 jit_solution(14651003364175708804)
XLA Ops:
  0.7 1.3 %shard_map.132 = bf16[32,128,128]{2,1,0:T(8,128)(2,1)S(1)} custom-call(s32[2,32]{1,0:T(2,128)} %rank_hbm.1, s32[2,32,128]{2,1,0:T(8,128)} %skel_hbm.1, bf16[2,32,256,128]{3,2,1,0:T(8,128)(2,1)} %interp_hbm.1), custom_call_target="tpu_custom_call" | custom-call | bytes 2097152 | tf_op jit(solution)/shard_map/pallas_call | solution.py:356
  2.0 0.0 copy-start.1
  2.0 0.0 copy-start.3
  2.0 1.3 %collective-permute-start.1 = (bf16[32,128,128]{2,1,0:T(8,128)(2,1)S(1)}, bf16[32,128,128]{2,1,0:T(8,128)(2,1)S(1)}, u32[]{:S(2)}, u32[]{:S(2)}) collective-permute-start(bf16[32,128,128]{2,1,0:T(8,128)(2,1)S(1)} %shard_map.132), channel_id=1, source_target_pairs={{4,0},{8,4},{12,8},{16,12},{20,16},{24,20},{28,24},{5,1},{9,5},{13... | collective-permute-start | bytes 3145736 | tf_op jit(solution)/shard_map/ppermute | solution.py:18
  3.3 0.0 copy-done.6
  3.4 0.0 copy-done.5
  3.4 0.0 copy-done.7
  3.4 0.0 copy-start
  3.4 17.1 %shard_map.131 = (bf16[2,32,128,128]{3,2,1,0:T(8,128)(2,1)}, bf16[2,32,128,128]{3,2,1,0:T(8,128)(2,1)}, bf16[1552,128]{1,0:T(8,128)(2,1)S(1)}, bf16[512,128]{1,0...) custom-call(s32[2,32]{1,0:T(2,128)S(1)} %copy-done.6, ...), custom_call_target="tpu_custom_call" | custom-call | flops 5368709120 | bytes 27262976 | tf_op jit(solution)/shard_map/pallas_call | solution.py:393
  20.5 1.3 %collective-permute-start.2 = (bf16[1552,128]{1,0:T(8,128)(2,1)S(1)}, bf16[1552,128]{1,0:T(8,128)(2,1)S(1)}, u32[]{:S(2)}, u32[]{:S(2)}) collective-permute-start(bf16[1552,128]{1,0:T(8,128)(2,1)S(1)} %get-tuple-element.22), channel_id=1, source_target_pairs={{4,0},{8,4},{12,8},{16,12},{20,16},{24,20},{28,24},{5,1},{9,5},{13... | collective-permute-start | bytes 1191944 | tf_op jit(solution)/shard_map/ppermute | solution.py:18
  21.8 1.3 %collective-permute-start = (bf16[2,2,128,128]{3,2,1,0:T(8,128)(2,1)S(1)}, bf16[2,2,128,128]{3,2,1,0:T(8,128)(2,1)S(1)}, u32[]{:S(2)}, u32[]{:S(2)}) collective-permute-start(bf16[2,2,128,128]{3,2,1,0:T(8,128)(2,1)S(1)} %get-tuple-element.15), channel_id=1, source_target_pairs={{1,0},{2,1},{3,2},{5,4},{6,5},{7,6},{9,8},{10,9},{11,10},{13,12},{... | collective-permute-start | bytes 393224 | tf_op jit(solution)/shard_map/ppermute | solution.py:18
  23.1 1.3 %collective-permute-start.3 = (bf16[512,128]{1,0:T(8,128)(2,1)S(1)}, bf16[512,128]{1,0:T(8,128)(2,1)S(1)}, u32[]{:S(2)}, u32[]{:S(2)}) collective-permute-start(bf16[512,128]{1,0:T(8,128)(2,1)S(1)} %get-tuple-element.23), channel_id=1, source_target_pairs={{4,0},{8,4},{12,8},{16,12},{20,16},{24,20},{28,24},{5,1},{9,5},{13... | collective-permute-start | bytes 393224 | tf_op jit(solution)/shard_map/ppermute | solution.py:18
  24.4 6.5 %collective-permute-done.1.top_ref = bf16[32,128,128]{2,1,0:T(8,128)(2,1)S(1)} collective-permute-done((bf16[32,128,128]{2,1,0:T(8,128)(2,1)S(1)}, bf16[32,128,128]{2,1,0:T(8,128)(2,1)S(1)}, u32[]{:S(2)}, u32[]{:S(2)}) %collective-permute-start.1) | collective-permute-done | bytes 1048608 | tf_op jit(solution)/shard_map/ppermute | solution.py:18
  30.9 0.0 copy-done
  30.9 0.0 copy-start.2
  30.9 0.0 copy-start.4
  30.9 3.2 %shard_map.133 = (f32[32,128,128]{2,1,0:T(8,128)S(1)}, bf16[32,128,128]{2,1,0:T(8,128)(2,1)S(1)}, bf16[32,128,128]{2,1,0:T(8,128)(2,1)S(1)}) custom-call(s32[2,32]{1,0:T(2,128)S(1)} %copy-done.7, s32[2,32,128]{2,1,0:T(8,128)S(1)} %copy-done.1, bf16[2,32,256,128]{3,2,1,0:T(8,128)(2,1)S(1)} %copy-done, bf16[2,32,128]{2,1,0:T(8,128)(2,1)S(1)} %copy-done.3, ...), custom_call_target="tpu_custom_call" | custom-call | flops 1073741824 | bytes 12582912 | tf_op jit(solution)/shard_map/pallas_call | solution.py:438
  34.2 0.0 collective-permute-done.edge_ref
  34.2 0.0 copy-done.2
  34.2 2.1 %shard_map.136 = bf16[2,32,128,128]{3,2,1,0:T(8,128)(2,1)} custom-call(s32[2,32]{1,0:T(2,128)S(1)} %copy-done.5, s32[2,32,128]{2,1,0:T(8,128)S(1)} %copy-done.2, bf16[2,32,256,128]{3,2,1,0:T(8,128)(2,1)} %interp_ref.5, bf16[2,32,128]{2,1,0:T(8,128)(2,1)S(1)} %copy-done.4, ...), custom_call_target="tpu_custom_call", output_to_operand_aliasing={{}: (6, {})} | custom-call | flops 67108864 | bytes 786432 | tf_op jit(solution)/shard_map/pallas_call | solution.py:454
  36.2 3.2 %collective-permute-done.2.extra_ref.packed_ref = bf16[1552,128]{1,0:T(8,128)(2,1)S(1)} collective-permute-done((bf16[1552,128]{1,0:T(8,128)(2,1)S(1)}, bf16[1552,128]{1,0:T(8,128)(2,1)S(1)}, u32[]{:S(2)}, u32[]{:S(2)}) %collective-permute-start.2) | collective-permute-done | bytes 397344 | tf_op jit(solution)/shard_map/ppermute | solution.py:18
  39.4 1.8 %shard_map.134._ = bf16[2,32,128,128]{3,2,1,0:T(8,128)(2,1)} custom-call(f32[32,128,128]{2,1,0:T(8,128)S(1)} %get-tuple-element.19.part_ref, bf16[32,128,128]{2,1,0:T(8,128)(2,1)S(1)} %get-tuple-element.20.lower_ref, bf16[32,128,128]{2,1,0:T(8,128)(2,1)S(1)} %get-tuple-element.21.lower_turned_ref, ...), custom_call_target="tpu_custom_call", output_to_operand_aliasing={{}: (5, {})} | custom-call | flops 301989888 | bytes 4325376 | tf_op jit(solution)/shard_map/pallas_call | solution.py:478
  41.2 0.2 collective-permute-done.3.packed_ref
  41.4 1.2 %shard_map.135 = bf16[2,32,128,128]{3,2,1,0:T(8,128)(2,1)} custom-call(f32[32,128,128]{2,1,0:T(8,128)S(1)} %get-tuple-element.19.part_ref, bf16[32,128,128]{2,1,0:T(8,128)(2,1)S(1)} %get-tuple-element.20.lower_ref, bf16[32,128,128]{2,1,0:T(8,128)(2,1)S(1)} %get-tuple-element.21.lower_turned_ref, ...), custom_call_target="tpu_custom_call", output_to_operand_aliasing={{}: (5, {})} | custom-call | flops 100663296 | bytes 1441792 | tf_op jit(solution)/shard_map/pallas_call | solution.py:478
  (6 shorter events, 0.0 us)
Async XLA Ops:
  0.6 2.7 %copy-start.6 = (s32[2,32]{1,0:T(2,128)S(1)}, s32[2,32]{1,0:T(2,128)}, u32[]{:S(2)}) copy-start(s32[2,32]{1,0:T(2,128)} %rank_hbm.1) | copy-start | bytes 772
  0.6 2.7 %copy-start.5 = (s32[2,32]{1,0:T(2,128)S(1)}, s32[2,32]{1,0:T(2,128)}, u32[]{:S(2)}) copy-start(s32[2,32]{1,0:T(2,128)} %rank_ref.5) | copy-start | bytes 772
  0.7 2.7 %copy-start.7 = (s32[2,32]{1,0:T(2,128)S(1)}, s32[2,32]{1,0:T(2,128)}, u32[]{:S(2)}) copy-start(s32[2,32]{1,0:T(2,128)} %rank_ref.4) | copy-start | bytes 772
  2.0 28.9 %copy-start.1 = (s32[2,32,128]{2,1,0:T(8,128)S(1)}, s32[2,32,128]{2,1,0:T(8,128)}, u32[]{:S(2)}) copy-start(s32[2,32,128]{2,1,0:T(8,128)} %skel_ref.4) | copy-start | bytes 98308
  2.0 28.9 %copy-start.3 = (bf16[2,32,128]{2,1,0:T(8,128)(2,1)S(1)}, bf16[2,32,128]{2,1,0:T(8,128)(2,1)}, u32[]{:S(2)}) copy-start(bf16[2,32,128]{2,1,0:T(8,128)(2,1)} %coup_ref.2) | copy-start | bytes 49156
  2.0 28.9 %collective-permute-start.1 = (bf16[32,128,128]{2,1,0:T(8,128)(2,1)S(1)}, bf16[32,128,128]{2,1,0:T(8,128)(2,1)S(1)}, u32[]{:S(2)}, u32[]{:S(2)}) collective-permute-start(bf16[32,128,128]{2,1,0:T(8,128)(2,1)S(1)} %shard_map.132), channel_id=1, source_target_pairs={{4,0},{8,4},{12,8},{16,12},{20,16},{24,20},{28,24},{5,1},{9,5},{13... | collective-permute-start | bytes 3145736 | tf_op jit(solution)/shard_map/ppermute | solution.py:18
  3.4 27.5 %copy-start = (bf16[2,32,256,128]{3,2,1,0:T(8,128)(2,1)S(1)}, bf16[2,32,256,128]{3,2,1,0:T(8,128)(2,1)}, u32[]{:S(2)}) copy-start(bf16[2,32,256,128]{3,2,1,0:T(8,128)(2,1)} %interp_ref.4) | copy-start | bytes 12582916
  20.5 18.9 %collective-permute-start.2 = (bf16[1552,128]{1,0:T(8,128)(2,1)S(1)}, bf16[1552,128]{1,0:T(8,128)(2,1)S(1)}, u32[]{:S(2)}, u32[]{:S(2)}) collective-permute-start(bf16[1552,128]{1,0:T(8,128)(2,1)S(1)} %get-tuple-element.22), channel_id=1, source_target_pairs={{4,0},{8,4},{12,8},{16,12},{20,16},{24,20},{28,24},{5,1},{9,5},{13... | collective-permute-start | bytes 1191944 | tf_op jit(solution)/shard_map/ppermute | solution.py:18
  21.8 12.4 %collective-permute-start = (bf16[2,2,128,128]{3,2,1,0:T(8,128)(2,1)S(1)}, bf16[2,2,128,128]{3,2,1,0:T(8,128)(2,1)S(1)}, u32[]{:S(2)}, u32[]{:S(2)}) collective-permute-start(bf16[2,2,128,128]{3,2,1,0:T(8,128)(2,1)S(1)} %get-tuple-element.15), channel_id=1, source_target_pairs={{1,0},{2,1},{3,2},{5,4},{6,5},{7,6},{9,8},{10,9},{11,10},{13,12},{... | collective-permute-start | bytes 393224 | tf_op jit(solution)/shard_map/ppermute | solution.py:18
  23.1 18.3 %collective-permute-start.3 = (bf16[512,128]{1,0:T(8,128)(2,1)S(1)}, bf16[512,128]{1,0:T(8,128)(2,1)S(1)}, u32[]{:S(2)}, u32[]{:S(2)}) collective-permute-start(bf16[512,128]{1,0:T(8,128)(2,1)S(1)} %get-tuple-element.23), channel_id=1, source_target_pairs={{4,0},{8,4},{12,8},{16,12},{20,16},{24,20},{28,24},{5,1},{9,5},{13... | collective-permute-start | bytes 393224 | tf_op jit(solution)/shard_map/ppermute | solution.py:18
  30.9 3.3 %copy-start.2 = (s32[2,32,128]{2,1,0:T(8,128)S(1)}, s32[2,32,128]{2,1,0:T(8,128)}, u32[]{:S(2)}) copy-start(s32[2,32,128]{2,1,0:T(8,128)} %skel_ref.5) | copy-start | bytes 98308
  30.9 3.3 %copy-start.4 = (bf16[2,32,128]{2,1,0:T(8,128)(2,1)S(1)}, bf16[2,32,128]{2,1,0:T(8,128)(2,1)}, u32[]{:S(2)}) copy-start(bf16[2,32,128]{2,1,0:T(8,128)(2,1)} %coup_ref.3) | copy-start | bytes 49156

commit v19 on v17

--- a/solution.py
+++ b/solution.py
@@ -69,27 +69,29 @@
     return [dot_nt(i, t) for i, t in zip(inner, turned)]
 
 
-def top_kernel(cells, rank_hbm, skel_hbm, interp_hbm, out_ref, rank_ref, skel_ref, held, small_sems, sems):
+def top_kernel(rank_hbm, skel_hbm, interp_hbm, out_ref, rank_ref, skel_ref, held, small_sems, sems):
     count, half, _ = out_ref.shape
     small = [
         pltpu.make_async_copy(rank_hbm, rank_ref, small_sems.at[0]),
         pltpu.make_async_copy(skel_hbm.at[0], skel_ref, small_sems.at[1]),
     ]
+    bounds = [0, count // 2, count // 4 * 3, count // 8 * 7, count]
+    groups = [(begin, end) for begin, end in zip(bounds, bounds[1:]) if begin < end]
     copies = []
-    for c in range(count // cells):
-        group = pl.ds(c * cells, cells)
+    for n, (begin, end) in enumerate(groups):
+        group = pl.ds(begin, end - begin)
         copies.append(
             pltpu.make_async_copy(
-                interp_hbm.at[0, group, pl.ds(0, half)], held.at[group], sems.at[c]
+                interp_hbm.at[0, group, pl.ds(0, half)], held.at[group], sems.at[n]
             )
         )
-    for copy in small + copies:
+    for copy in copies + small:
         copy.start()
     for copy in small:
         copy.wait()
-    for c in range(count // cells):
-        copies[c].wait()
-        for k in range(c * cells, (c + 1) * cells):
+    for copy, (begin, end) in zip(copies, groups):
+        copy.wait()
+        for k in range(begin, end):
             out_ref[k] = marked_of(skel_ref[k : k + 1], rank_ref[0, k], held[k])
 
 
@@ -336,7 +338,7 @@
     hbm = pl.BlockSpec(memory_space=pltpu.HBM)
     vmem = pl.BlockSpec(memory_space=pltpu.VMEM)
     top = call(
-        functools.partial(top_kernel, cells),
+        top_kernel,
         (),
         [hbm, hbm, hbm],
         vmem,
@@ -349,7 +351,7 @@
             pltpu.VMEM((nj, slots), jnp.int32),
             pltpu.VMEM((nj, half, slots), BF),
             pltpu.SemaphoreType.DMA((2,)),
-            pltpu.SemaphoreType.DMA((chunks,)),
+            pltpu.SemaphoreType.DMA((4,)),
         ],
     )(in_hbm(cell_rank), in_hbm(cell_skel), in_hbm(cell_interp))
     top_in = passed_along(top, "gx", -1)

time: 42.9 us -> 42.9 us (level)
  no operation moved by 1% of the time
where the time goes in v19:
time: 42.9 us; the launch traced here: 42.6 us
  Pallas kernels  26.5 us (62%)
  waiting for transfers between devices  10.1 us (24%)
  starting transfers between devices  5.16 us (12%)
  between operations  0.8 us (2%)
    pallas_call x1, Pallas kernels, body(): call(functools.partial(main_kernel, cells, nx, chunks), (nx, chunks), [sm...  17.1 us
    ppermute x4, waiting for transfers between devices, passed_along(): return lax.ppermute(x, axis, pairs)  10.1 us
    ppermute x4, starting transfers between devices, passed_along(): return lax.ppermute(x, axis, pairs)  5.16 us
    pallas_call x1, Pallas kernels, body(): call(functools.partial(x_part_kernel, cells, last), (), [smem, vmem, vmem...  3.22 us
    pallas_call x2, Pallas kernels, body(): call(functools.partial(x_last_kernel, cells, last, places), (), [vmem, vm...  2.68 us
    pallas_call x1, Pallas kernels, body(): call(functools.partial(y_edge_kernel, nx, tail), (1,), [smem, pl.BlockSpe...  2.05 us
    pallas_call x1, Pallas kernels, body(): call(top_kernel, (), [hbm, hbm, hbm], vmem, shape((nj, half, slots), BF),...  1.43 us
  transfers between devices with their start and end apart: 4, of which 3 were waited for; matrix products, arithmetic and copies ran while one was open for 0% of the time, Pallas kernels for 56%

profile of v19, /device:TPU:0, one launch (start us, length us, event | category | flops | bytes accessed | tf_op | source)
XLA Modules:
  0.0 42.6 jit_solution(4269718281770303723)
XLA Ops:
  0.6 0.0 copy-start.6
  0.6 0.0 copy-start.5
  0.7 0.0 copy-start.7
  0.7 1.4 %shard_map.132 = bf16[32,128,128]{2,1,0:T(8,128)(2,1)S(1)} custom-call(s32[2,32]{1,0:T(2,128)} %rank_hbm.1, s32[2,32,128]{2,1,0:T(8,128)} %skel_hbm.1, bf16[2,32,256,128]{3,2,1,0:T(8,128)(2,1)} %interp_hbm.1), custom_call_target="tpu_custom_call" | custom-call | bytes 2097152 | tf_op jit(solution)/shard_map/pallas_call | solution.py:340
  2.1 0.0 copy-start.1
  2.1 0.0 copy-start.3
  2.1 1.3 %collective-permute-start.1 = (bf16[32,128,128]{2,1,0:T(8,128)(2,1)S(1)}, bf16[32,128,128]{2,1,0:T(8,128)(2,1)S(1)}, u32[]{:S(2)}, u32[]{:S(2)}) collective-permute-start(bf16[32,128,128]{2,1,0:T(8,128)(2,1)S(1)} %shard_map.132), channel_id=1, source_target_pairs={{4,0},{8,4},{12,8},{16,12},{20,16},{24,20},{28,24},{5,1},{9,5},{13... | collective-permute-start | bytes 3145736 | tf_op jit(solution)/shard_map/ppermute | solution.py:18
  3.4 0.0 copy-done.6
  3.5 0.0 copy-start
  3.5 17.1 %shard_map.131 = (bf16[2,32,128,128]{3,2,1,0:T(8,128)(2,1)}, bf16[2,32,128,128]{3,2,1,0:T(8,128)(2,1)}, bf16[1552,128]{1,0:T(8,128)(2,1)S(1)}, bf16[512,128]{1,0...) custom-call(s32[2,32]{1,0:T(2,128)S(1)} %copy-done.6, ...), custom_call_target="tpu_custom_call" | custom-call | flops 5368709120 | bytes 27262976 | tf_op jit(solution)/shard_map/pallas_call | solution.py:377
  20.6 1.3 %collective-permute-start.2 = (bf16[1552,128]{1,0:T(8,128)(2,1)S(1)}, bf16[1552,128]{1,0:T(8,128)(2,1)S(1)}, u32[]{:S(2)}, u32[]{:S(2)}) collective-permute-start(bf16[1552,128]{1,0:T(8,128)(2,1)S(1)} %get-tuple-element.22), channel_id=1, source_target_pairs={{4,0},{8,4},{12,8},{16,12},{20,16},{24,20},{28,24},{5,1},{9,5},{13... | collective-permute-start | bytes 1191944 | tf_op jit(solution)/shard_map/ppermute | solution.py:18
  21.8 1.3 %collective-permute-start = (bf16[2,2,128,128]{3,2,1,0:T(8,128)(2,1)S(1)}, bf16[2,2,128,128]{3,2,1,0:T(8,128)(2,1)S(1)}, u32[]{:S(2)}, u32[]{:S(2)}) collective-permute-start(bf16[2,2,128,128]{3,2,1,0:T(8,128)(2,1)S(1)} %get-tuple-element.15), channel_id=1, source_target_pairs={{1,0},{2,1},{3,2},{5,4},{6,5},{7,6},{9,8},{10,9},{11,10},{13,12},{... | collective-permute-start | bytes 393224 | tf_op jit(solution)/shard_map/ppermute | solution.py:18
  23.1 1.3 %collective-permute-start.3 = (bf16[512,128]{1,0:T(8,128)(2,1)S(1)}, bf16[512,128]{1,0:T(8,128)(2,1)S(1)}, u32[]{:S(2)}, u32[]{:S(2)}) collective-permute-start(bf16[512,128]{1,0:T(8,128)(2,1)S(1)} %get-tuple-element.23), channel_id=1, source_target_pairs={{4,0},{8,4},{12,8},{16,12},{20,16},{24,20},{28,24},{5,1},{9,5},{13... | collective-permute-start | bytes 393224 | tf_op jit(solution)/shard_map/ppermute | solution.py:18
  24.4 6.5 %collective-permute-done.1.top_ref = bf16[32,128,128]{2,1,0:T(8,128)(2,1)S(1)} collective-permute-done((bf16[32,128,128]{2,1,0:T(8,128)(2,1)S(1)}, bf16[32,128,128]{2,1,0:T(8,128)(2,1)S(1)}, u32[]{:S(2)}, u32[]{:S(2)}) %collective-permute-start.1) | collective-permute-done | bytes 1048608 | tf_op jit(solution)/shard_map/ppermute | solution.py:18
  31.0 0.0 copy-done.3
  31.0 0.0 copy-start.2
  31.0 0.0 copy-start.4
  31.0 3.2 %shard_map.133 = (f32[32,128,128]{2,1,0:T(8,128)S(1)}, bf16[32,128,128]{2,1,0:T(8,128)(2,1)S(1)}, bf16[32,128,128]{2,1,0:T(8,128)(2,1)S(1)}) custom-call(s32[2,32]{1,0:T(2,128)S(1)} %copy-done.7, s32[2,32,128]{2,1,0:T(8,128)S(1)} %copy-done.1, bf16[2,32,256,128]{3,2,1,0:T(8,128)(2,1)S(1)} %copy-done, bf16[2,32,128]{2,1,0:T(8,128)(2,1)S(1)} %copy-done.3, ...), custom_call_target="tpu_custom_call" | custom-call | flops 1073741824 | bytes 12582912 | tf_op jit(solution)/shard_map/pallas_call | solution.py:422
  34.2 0.0 collective-permute-done.edge_ref
  34.3 2.1 %shard_map.136 = bf16[2,32,128,128]{3,2,1,0:T(8,128)(2,1)} custom-call(s32[2,32]{1,0:T(2,128)S(1)} %copy-done.5, s32[2,32,128]{2,1,0:T(8,128)S(1)} %copy-done.2, bf16[2,32,256,128]{3,2,1,0:T(8,128)(2,1)} %interp_ref.5, bf16[2,32,128]{2,1,0:T(8,128)(2,1)S(1)} %copy-done.4, ...), custom_call_target="tpu_custom_call", output_to_operand_aliasing={{}: (6, {})} | custom-call | flops 67108864 | bytes 786432 | tf_op jit(solution)/shard_map/pallas_call | solution.py:438
  36.3 3.2 %collective-permute-done.2.extra_ref.packed_ref = bf16[1552,128]{1,0:T(8,128)(2,1)S(1)} collective-permute-done((bf16[1552,128]{1,0:T(8,128)(2,1)S(1)}, bf16[1552,128]{1,0:T(8,128)(2,1)S(1)}, u32[]{:S(2)}, u32[]{:S(2)}) %collective-permute-start.2) | collective-permute-done | bytes 397344 | tf_op jit(solution)/shard_map/ppermute | solution.py:18
  39.5 1.6 %shard_map.134._ = bf16[2,32,128,128]{3,2,1,0:T(8,128)(2,1)} custom-call(f32[32,128,128]{2,1,0:T(8,128)S(1)} %get-tuple-element.19.part_ref, bf16[32,128,128]{2,1,0:T(8,128)(2,1)S(1)} %get-tuple-element.20.lower_ref, bf16[32,128,128]{2,1,0:T(8,128)(2,1)S(1)} %get-tuple-element.21.lower_turned_ref, ...), custom_call_target="tpu_custom_call", output_to_operand_aliasing={{}: (5, {})} | custom-call | flops 301989888 | bytes 4325376 | tf_op jit(solution)/shard_map/pallas_call | solution.py:462
  41.1 0.4 collective-permute-done.3.packed_ref
  41.5 1.1 %shard_map.135 = bf16[2,32,128,128]{3,2,1,0:T(8,128)(2,1)} custom-call(f32[32,128,128]{2,1,0:T(8,128)S(1)} %get-tuple-element.19.part_ref, bf16[32,128,128]{2,1,0:T(8,128)(2,1)S(1)} %get-tuple-element.20.lower_ref, bf16[32,128,128]{2,1,0:T(8,128)(2,1)S(1)} %get-tuple-element.21.lower_turned_ref, ...), custom_call_target="tpu_custom_call", output_to_operand_aliasing={{}: (5, {})} | custom-call | flops 100663296 | bytes 1441792 | tf_op jit(solution)/shard_map/pallas_call | solution.py:462
  (6 shorter events, 0.0 us)
Async XLA Ops:
  0.6 2.8 %copy-start.6 = (s32[2,32]{1,0:T(2,128)S(1)}, s32[2,32]{1,0:T(2,128)}, u32[]{:S(2)}) copy-start(s32[2,32]{1,0:T(2,128)} %rank_hbm.1) | copy-start | bytes 772
  0.6 2.8 %copy-start.5 = (s32[2,32]{1,0:T(2,128)S(1)}, s32[2,32]{1,0:T(2,128)}, u32[]{:S(2)}) copy-start(s32[2,32]{1,0:T(2,128)} %rank_ref.5) | copy-start | bytes 772
  0.7 2.8 %copy-start.7 = (s32[2,32]{1,0:T(2,128)S(1)}, s32[2,32]{1,0:T(2,128)}, u32[]{:S(2)}) copy-start(s32[2,32]{1,0:T(2,128)} %rank_ref.4) | copy-start | bytes 772
  2.1 28.9 %copy-start.1 = (s32[2,32,128]{2,1,0:T(8,128)S(1)}, s32[2,32,128]{2,1,0:T(8,128)}, u32[]{:S(2)}) copy-start(s32[2,32,128]{2,1,0:T(8,128)} %skel_ref.4) | copy-start | bytes 98308
  2.1 28.9 %copy-start.3 = (bf16[2,32,128]{2,1,0:T(8,128)(2,1)S(1)}, bf16[2,32,128]{2,1,0:T(8,128)(2,1)}, u32[]{:S(2)}) copy-start(bf16[2,32,128]{2,1,0:T(8,128)(2,1)} %coup_ref.2) | copy-start | bytes 49156
  2.1 28.9 %collective-permute-start.1 = (bf16[32,128,128]{2,1,0:T(8,128)(2,1)S(1)}, bf16[32,128,128]{2,1,0:T(8,128)(2,1)S(1)}, u32[]{:S(2)}, u32[]{:S(2)}) collective-permute-start(bf16[32,128,128]{2,1,0:T(8,128)(2,1)S(1)} %shard_map.132), channel_id=1, source_target_pairs={{4,0},{8,4},{12,8},{16,12},{20,16},{24,20},{28,24},{5,1},{9,5},{13... | collective-permute-start | bytes 3145736 | tf_op jit(solution)/shard_map/ppermute | solution.py:18
  3.5 27.5 %copy-start = (bf16[2,32,256,128]{3,2,1,0:T(8,128)(2,1)S(1)}, bf16[2,32,256,128]{3,2,1,0:T(8,128)(2,1)}, u32[]{:S(2)}) copy-start(bf16[2,32,256,128]{3,2,1,0:T(8,128)(2,1)} %interp_ref.4) | copy-start | bytes 12582916
  20.6 18.9 %collective-permute-start.2 = (bf16[1552,128]{1,0:T(8,128)(2,1)S(1)}, bf16[1552,128]{1,0:T(8,128)(2,1)S(1)}, u32[]{:S(2)}, u32[]{:S(2)}) collective-permute-start(bf16[1552,128]{1,0:T(8,128)(2,1)S(1)} %get-tuple-element.22), channel_id=1, source_target_pairs={{4,0},{8,4},{12,8},{16,12},{20,16},{24,20},{28,24},{5,1},{9,5},{13... | collective-permute-start | bytes 1191944 | tf_op jit(solution)/shard_map/ppermute | solution.py:18
  21.8 12.4 %collective-permute-start = (bf16[2,2,128,128]{3,2,1,0:T(8,128)(2,1)S(1)}, bf16[2,2,128,128]{3,2,1,0:T(8,128)(2,1)S(1)}, u32[]{:S(2)}, u32[]{:S(2)}) collective-permute-start(bf16[2,2,128,128]{3,2,1,0:T(8,128)(2,1)S(1)} %get-tuple-element.15), channel_id=1, source_target_pairs={{1,0},{2,1},{3,2},{5,4},{6,5},{7,6},{9,8},{10,9},{11,10},{13,12},{... | collective-permute-start | bytes 393224 | tf_op jit(solution)/shard_map/ppermute | solution.py:18
  23.1 18.3 %collective-permute-start.3 = (bf16[512,128]{1,0:T(8,128)(2,1)S(1)}, bf16[512,128]{1,0:T(8,128)(2,1)S(1)}, u32[]{:S(2)}, u32[]{:S(2)}) collective-permute-start(bf16[512,128]{1,0:T(8,128)(2,1)S(1)} %get-tuple-element.23), channel_id=1, source_target_pairs={{4,0},{8,4},{12,8},{16,12},{20,16},{24,20},{28,24},{5,1},{9,5},{13... | collective-permute-start | bytes 393224 | tf_op jit(solution)/shard_map/ppermute | solution.py:18
  31.0 3.3 %copy-start.2 = (s32[2,32,128]{2,1,0:T(8,128)S(1)}, s32[2,32,128]{2,1,0:T(8,128)}, u32[]{:S(2)}) copy-start(s32[2,32,128]{2,1,0:T(8,128)} %skel_ref.5) | copy-start | bytes 98308
  31.0 3.3 %copy-start.4 = (bf16[2,32,128]{2,1,0:T(8,128)(2,1)S(1)}, bf16[2,32,128]{2,1,0:T(8,128)(2,1)}, u32[]{:S(2)}) copy-start(bf16[2,32,128]{2,1,0:T(8,128)(2,1)} %coup_ref.3) | copy-start | bytes 49156

commit v20 on v17

--- a/solution.py
+++ b/solution.py
@@ -16,6 +16,11 @@
     devices = lax.axis_size(axis)
     pairs = [(i, i + by) for i in range(devices) if 0 <= i + by < devices]
     return lax.ppermute(x, axis, pairs)
+
+
+def passed_round(x, axis):
+    devices = lax.axis_size(axis)
+    return lax.ppermute(x, axis, [(i, (i - 1) % devices) for i in range(devices)])
 
 
 def dot_nt(a, b):
@@ -221,11 +226,12 @@
 
 
 def x_part_kernel(
-    cells, layer, rank_ref, skel_ref, interp_ref, coup_ref, turned_ref, schur_ref, top_ref,
+    cells, layer, inner_ref, rank_ref, skel_ref, interp_ref, coup_ref, turned_ref, schur_ref, top_ref,
     part_ref, lower_ref, lower_turned_ref,
 ):
     count, slots, half = turned_ref.shape
     nothing = jnp.zeros((slots, slots), BF)
+    inner = jnp.where(jnp.full((1, slots), inner_ref[0]) > 0, F32(1.0), F32(0.0)).astype(BF)
     for first in range(0, count, cells):
         group = range(first, first + cells)
         skel = skel_ref[layer, first : first + cells]
@@ -234,9 +240,10 @@
         ]
         faces = [kept_cleared(t) for t in [jnp.transpose(m) for m in marked]]
         for k in group:
-            lower_turned_ref[k] = faces[k - first][:, half:]
-            lower_ref[k] = jnp.transpose(faces[k - first][:, half:])
-        tops = [kept_cleared(t) for t in [jnp.transpose(top_ref[k]) for k in group]]
+            lower = faces[k - first][:, half:] * inner
+            lower_turned_ref[k] = lower
+            lower_ref[k] = jnp.transpose(lower)
+        tops = [kept_cleared(t) * inner for t in [jnp.transpose(top_ref[k]) for k in group]]
         matrices = []
         for k, top in zip(group, tops):
             conduct = coup_ref[layer, k : k + 1]
@@ -352,7 +359,7 @@
             pltpu.SemaphoreType.DMA((chunks,)),
         ],
     )(in_hbm(cell_rank), in_hbm(cell_skel), in_hbm(cell_interp))
-    top_in = passed_along(top, "gx", -1)
+    top_in = passed_round(top, "gx")
 
 
     late_rows = cells * slots // 2
@@ -409,18 +416,19 @@
         y_face_rank, in_hbm(y_face_skel), in_hbm(y_face_interp), in_hbm(y_coupling),
     )
     edge_in = passed_along(edge, "yz", -1)
-    packed_in = passed_along(packed, "gx", -1)
-    packed_last_in = passed_along(packed_last, "gx", -1)
+    packed_in = passed_round(packed, "gx")
+    packed_last_in = passed_round(packed_last, "gx")
     face_bytes = nj * (4 * rows * slots + 4 * slots * slots) * 2
 
     last = nx - 1
     tail = nj - 1
     group = tail // cells
 
+    inner = (lax.axis_index("gx") + 1 < lax.axis_size("gx")).astype(jnp.int32).reshape(1)
     part, lower, lower_turned = call(
         functools.partial(x_part_kernel, cells, last),
         (),
-        [smem, vmem, vmem, vmem, vmem, vmem, vmem],
+        [smem, smem, vmem, vmem, vmem, vmem, vmem, vmem],
         [vmem, vmem, vmem],
         [
             shape((nj, fslots, fslots), F32),
@@ -430,7 +438,7 @@
         8 * unit // nx,
         face_bytes,
         vmem=16,
-    )(x_face_rank, x_face_skel, x_face_interp, x_coupling, last_turned, last_schur, top_in)
+    )(inner, x_face_rank, x_face_skel, x_face_interp, x_coupling, last_turned, last_schur, top_in)
 
     edge_in, part = lax.optimization_barrier((edge_in, part))
     y_out = call(

time: 42.9 us -> 46.2 us (1.077)
  waiting for transfers between devices: 10.1 us -> 2.77 us
  local copies, waits for them, and re-layouts: 0.04 us -> 4.35 us
  starting transfers between devices: 5.16 us -> 9.31 us
  Pallas kernels: 26.4 us -> 28.5 us
    ppermute x4 -> x1, waiting for transfers between devices: 10.1 us -> 0.01 us  [passed_along(): return lax.ppermute(x, axis, pairs)]
    ppermute x0 -> x3, starting transfers between devices: none -> 8.03 us  [passed_round(): lax.ppermute(x, axis, [(i, (i - 1) % devices) for i in range(devices)])]
    unnamed x16 -> x20, local copies, waits for them, and re-layouts: 0.04 us -> 4.35 us
    ppermute x4 -> x1, starting transfers between devices: 5.16 us -> 1.28 us  [passed_along(): return lax.ppermute(x, axis, pairs)]
    ppermute x0 -> x3, waiting for transfers between devices: none -> 2.77 us  [passed_round(): lax.ppermute(x, axis, [(i, (i - 1) % devices) for i in range(devices)])]
    pallas_call x1, Pallas kernels: 1.35 us -> 2.33 us  [body(): call(functools.partial(top_kernel, cells), (), [hbm, hbm, hbm], vmem, sha...]
    pallas_call x2, Pallas kernels: 2.68 us -> 3.59 us  [body(): call(functools.partial(x_last_kernel, cells, last, places), (), [vmem, vm...]
  transfers between devices with their start and end apart: 4 -> 4, of which waited for: 3 -> 1; matrix products, arithmetic and copies ran while one was open for 0% -> 0% of each run, Pallas kernels for 56% -> 53%
where the time goes in v20:
time: 46.2 us; the launch traced here: 45.7 us
  Pallas kernels  28.5 us (62%)
  starting transfers between devices  9.31 us (20%)
  local copies, waits for them, and re-layouts  4.35 us (9%)
  waiting for transfers between devices  2.77 us (6%)
  between operations  0.74 us (2%)
    pallas_call x1, Pallas kernels, body(): call(functools.partial(main_kernel, cells, nx, chunks), (nx, chunks), [sm...  17.2 us
    ppermute x3, starting transfers between devices, passed_round(): lax.ppermute(x, axis, [(i, (i - 1) % devices) for i in range(devices)])  8.03 us
    unnamed x20, local copies, waits for them, and re-layouts  4.35 us
    pallas_call x2, Pallas kernels, body(): call(functools.partial(x_last_kernel, cells, last, places), (), [vmem, vm...  3.59 us
    pallas_call x1, Pallas kernels, body(): call(functools.partial(x_part_kernel, cells, last), (), [smem, smem, vmem...  3.32 us
    ppermute x3, waiting for transfers between devices, passed_round(): lax.ppermute(x, axis, [(i, (i - 1) % devices) for i in range(devices)])  2.77 us
    pallas_call x1, Pallas kernels, body(): call(functools.partial(top_kernel, cells), (), [hbm, hbm, hbm], vmem, sha...  2.33 us
    pallas_call x1, Pallas kernels, body(): call(functools.partial(y_edge_kernel, nx, tail), (1,), [smem, pl.BlockSpe...  2.11 us
  transfers between devices with their start and end apart: 4, of which 1 were waited for; matrix products, arithmetic and copies ran while one was open for 0% of the time, Pallas kernels for 53%

profile of v20, /device:TPU:0, one launch (start us, length us, event | category | flops | bytes accessed | tf_op | source)
XLA Modules:
  0.0 45.7 jit_solution(287427426410419801)
XLA Ops:
  0.6 0.0 copy-start.9
  0.6 0.0 copy-start.8
  0.7 2.3 %shard_map.132 = bf16[32,128,128]{2,1,0:T(8,128)(2,1)} custom-call(s32[2,32]{1,0:T(2,128)} %rank_hbm.1, s32[2,32,128]{2,1,0:T(8,128)} %skel_hbm.1, bf16[2,32,256,128]{3,2,1,0:T(8,128)(2,1)} %interp_hbm.1), custom_call_target="tpu_custom_call" | custom-call | bytes 2097152 | tf_op jit(solution)/shard_map/pallas_call | solution.py:345
  3.0 6.1 %collective-permute-start.1 = (bf16[32,128,128]{2,1,0:T(8,128)(2,1)}, bf16[32,128,128]{2,1,0:T(8,128)(2,1)S(1)}, u32[]{:S(2)}, u32[]{:S(2)}) collective-permute-start(bf16[32,128,128]{2,1,0:T(8,128)(2,1)} %shard_map.132), channel_id=1, source_target_pairs={{0,28},{4,0},{8,4},{12,8},{16,12},{20,16},{24,20},{28,24},{1,29},{... | collective-permute-start | bytes 3145736 | tf_op jit(solution)/shard_map/ppermute | solution.py:23
  9.1 0.0 copy-done.8
  9.1 17.2 %shard_map.131 = (bf16[2,32,128,128]{3,2,1,0:T(8,128)(2,1)}, bf16[2,32,128,128]{3,2,1,0:T(8,128)(2,1)}, bf16[1552,128]{1,0:T(8,128)(2,1)}, bf16[512,128]{1,0:T(8...) custom-call(s32[2,32]{1,0:T(2,128)S(1)} %copy-done.9, ...), custom_call_target="tpu_custom_call" | custom-call | flops 5368709120 | bytes 27262976 | tf_op jit(solution)/shard_map/pallas_call | solution.py:382
  26.3 0.7 %copy-done.1 = bf16[2,2,128,128]{3,2,1,0:T(8,128)(2,1)} copy-done((bf16[2,2,128,128]{3,2,1,0:T(8,128)(2,1)}, bf16[2,2,128,128]{3,2,1,0:T(8,128)(2,1)S(1)}, u32[]{:S(2)}) %copy-start.1) | copy-done | bytes 131096
  26.9 0.5 %collective-permute-start.2 = (bf16[1552,128]{1,0:T(8,128)(2,1)}, bf16[1552,128]{1,0:T(8,128)(2,1)S(1)}, u32[]{:S(2)}, u32[]{:S(2)}) collective-permute-start(bf16[1552,128]{1,0:T(8,128)(2,1)} %get-tuple-element.22), channel_id=1, source_target_pairs={{0,28},{4,0},{8,4},{12,8},{16,12},{20,16},{24,20},{28,24},{1,29},{... | collective-permute-start | bytes 1191944 | tf_op jit(solution)/shard_map/ppermute | solution.py:23
  27.4 1.3 %collective-permute-start = (bf16[2,2,128,128]{3,2,1,0:T(8,128)(2,1)}, bf16[2,2,128,128]{3,2,1,0:T(8,128)(2,1)}, u32[]{:S(2)}, u32[]{:S(2)}) collective-permute-start(bf16[2,2,128,128]{3,2,1,0:T(8,128)(2,1)} %get-tuple-element.15), channel_id=1, source_target_pairs={{1,0},{2,1},{3,2},{5,4},{6,5},{7,6},{9,8},{10,9},{11,10},{13,12},{... | collective-permute-start | bytes 393224 | tf_op jit(solution)/shard_map/ppermute | solution.py:18
  28.7 1.5 %collective-permute-start.3 = (bf16[512,128]{1,0:T(8,128)(2,1)}, bf16[512,128]{1,0:T(8,128)(2,1)}, u32[]{:S(2)}, u32[]{:S(2)}) collective-permute-start(bf16[512,128]{1,0:T(8,128)(2,1)} %get-tuple-element.23), channel_id=1, source_target_pairs={{0,28},{4,0},{8,4},{12,8},{16,12},{20,16},{24,20},{28,24},{1,29},{... | collective-permute-start | bytes 393224 | tf_op jit(solution)/shard_map/ppermute | solution.py:23
  30.2 2.8 %collective-permute-done.1.top_ref = bf16[32,128,128]{2,1,0:T(8,128)(2,1)S(1)} collective-permute-done((bf16[32,128,128]{2,1,0:T(8,128)(2,1)}, bf16[32,128,128]{2,1,0:T(8,128)(2,1)S(1)}, u32[]{:S(2)}, u32[]{:S(2)}) %collective-permute-start.1) | collective-permute-done | bytes 1048608 | tf_op jit(solution)/shard_map/ppermute | solution.py:23
  32.9 2.2 %copy-done = bf16[2,32,256,128]{3,2,1,0:T(8,128)(2,1)S(1)} copy-done((bf16[2,32,256,128]{3,2,1,0:T(8,128)(2,1)S(1)}, bf16[2,32,256,128]{3,2,1,0:T(8,128)(2,1)}, u32[]{:S(2)}) %copy-start) | copy-done | bytes 4194328
  35.1 0.8 %copy-done.3 = s32[2,32,128]{2,1,0:T(8,128)S(1)} copy-done((s32[2,32,128]{2,1,0:T(8,128)S(1)}, s32[2,32,128]{2,1,0:T(8,128)}, u32[]{:S(2)}) %copy-start.3) | copy-done | bytes 32792
  35.9 0.7 %copy-done.5 = bf16[2,32,128]{2,1,0:T(8,128)(2,1)S(1)} copy-done((bf16[2,32,128]{2,1,0:T(8,128)(2,1)S(1)}, bf16[2,32,128]{2,1,0:T(8,128)(2,1)}, u32[]{:S(2)}) %copy-start.5) | copy-done | bytes 16408
  36.6 3.3 %shard_map.133 = (f32[32,128,128]{2,1,0:T(8,128)S(1)}, bf16[32,128,128]{2,1,0:T(8,128)(2,1)S(1)}, bf16[32,128,128]{2,1,0:T(8,128)(2,1)S(1)}) custom-call(s32[1]{0:T(128)} %bitcast.inner_ref, s32[2,32]{1,0:T(2,128)S(1)} %copy-done.7, s32[2,32,128]{2,1,0:T(8,128)S(1)} %copy-done.3, bf16[2,32,256,128]{3,2,1,0:T(8,128)(2,1)S(1)} %copy-done, ...), custom_call_target="tpu_custom_call" | custom-call | flops 1073741824 | bytes 12582912 | tf_op jit(solution)/shard_map/pallas_call | solution.py:428
  39.9 0.0 collective-permute-done.edge_ref
  39.9 0.0 copy-done.2
  39.9 0.0 copy-done.4
  40.0 0.0 copy-done.6
  40.0 2.1 %shard_map.136 = bf16[2,32,128,128]{3,2,1,0:T(8,128)(2,1)} custom-call(s32[2,32]{1,0:T(2,128)S(1)} %copy-done.8, s32[2,32,128]{2,1,0:T(8,128)S(1)} %copy-done.4, bf16[2,32,256,128]{3,2,1,0:T(8,128)(2,1)} %interp_ref.5, bf16[2,32,128]{2,1,0:T(8,128)(2,1)S(1)} %copy-done.6, bf16[2,2,128,128]{3,2,1,0:T(8,128)(2,1)S(1)} %copy-done.2, ...), custom_call_target="tpu_custom_call", output_to_operand_aliasing={{}: (6, {})} | custom-call | flops 67108864 | bytes 786432 | tf_op jit(solution)/shard_map/pallas_call | solution.py:444
  42.1 0.0 collective-permute-done.2.extra_ref.packed_ref
  42.1 1.6 %shard_map.134._ = bf16[2,32,128,128]{3,2,1,0:T(8,128)(2,1)} custom-call(f32[32,128,128]{2,1,0:T(8,128)S(1)} %get-tuple-element.19.part_ref, bf16[32,128,128]{2,1,0:T(8,128)(2,1)S(1)} %get-tuple-element.20.lower_ref, bf16[32,128,128]{2,1,0:T(8,128)(2,1)S(1)} %get-tuple-element.21.lower_turned_ref, ...), custom_call_target="tpu_custom_call", output_to_operand_aliasing={{}: (5, {})} | custom-call | flops 301989888 | bytes 4325376 | tf_op jit(solution)/shard_map/pallas_call | solution.py:468
  43.7 0.0 collective-permute-done.3.packed_ref
  43.7 2.0 %shard_map.135 = bf16[2,32,128,128]{3,2,1,0:T(8,128)(2,1)} custom-call(f32[32,128,128]{2,1,0:T(8,128)S(1)} %get-tuple-element.19.part_ref, bf16[32,128,128]{2,1,0:T(8,128)(2,1)S(1)} %get-tuple-element.20.lower_ref, bf16[32,128,128]{2,1,0:T(8,128)(2,1)S(1)} %get-tuple-element.21.lower_turned_ref, ...), custom_call_target="tpu_custom_call", output_to_operand_aliasing={{}: (5, {})} | custom-call | flops 100663296 | bytes 1441792 | tf_op jit(solution)/shard_map/pallas_call | solution.py:468
  (10 shorter events, 0.0 us)
Async XLA Ops:
  0.6 8.4 %copy-start.9 = (s32[2,32]{1,0:T(2,128)S(1)}, s32[2,32]{1,0:T(2,128)}, u32[]{:S(2)}) copy-start(s32[2,32]{1,0:T(2,128)} %rank_hbm.1) | copy-start | bytes 772
  0.6 8.4 %copy-start.8 = (s32[2,32]{1,0:T(2,128)S(1)}, s32[2,32]{1,0:T(2,128)}, u32[]{:S(2)}) copy-start(s32[2,32]{1,0:T(2,128)} %rank_ref.5) | copy-start | bytes 772
  0.7 8.4 %copy-start.7 = (s32[2,32]{1,0:T(2,128)S(1)}, s32[2,32]{1,0:T(2,128)}, u32[]{:S(2)}) copy-start(s32[2,32]{1,0:T(2,128)} %rank_ref.4) | copy-start | bytes 772
  3.0 29.9 %collective-permute-start.1 = (bf16[32,128,128]{2,1,0:T(8,128)(2,1)}, bf16[32,128,128]{2,1,0:T(8,128)(2,1)S(1)}, u32[]{:S(2)}, u32[]{:S(2)}) collective-permute-start(bf16[32,128,128]{2,1,0:T(8,128)(2,1)} %shard_map.132), channel_id=1, source_target_pairs={{0,28},{4,0},{8,4},{12,8},{16,12},{20,16},{24,20},{28,24},{1,29},{... | collective-permute-start | bytes 3145736 | tf_op jit(solution)/shard_map/ppermute | solution.py:23
  26.2 0.7 %copy-start.1 = (bf16[2,2,128,128]{3,2,1,0:T(8,128)(2,1)}, bf16[2,2,128,128]{3,2,1,0:T(8,128)(2,1)S(1)}, u32[]{:S(2)}) copy-start(bf16[2,2,128,128]{3,2,1,0:T(8,128)(2,1)S(1)} %get-tuple-element.25.corner_ref) | copy-start | bytes 393220
  26.9 15.2 %collective-permute-start.2 = (bf16[1552,128]{1,0:T(8,128)(2,1)}, bf16[1552,128]{1,0:T(8,128)(2,1)S(1)}, u32[]{:S(2)}, u32[]{:S(2)}) collective-permute-start(bf16[1552,128]{1,0:T(8,128)(2,1)} %get-tuple-element.22), channel_id=1, source_target_pairs={{0,28},{4,0},{8,4},{12,8},{16,12},{20,16},{24,20},{28,24},{1,29},{... | collective-permute-start | bytes 1191944 | tf_op jit(solution)/shard_map/ppermute | solution.py:23
  27.4 12.5 %collective-permute-start = (bf16[2,2,128,128]{3,2,1,0:T(8,128)(2,1)}, bf16[2,2,128,128]{3,2,1,0:T(8,128)(2,1)}, u32[]{:S(2)}, u32[]{:S(2)}) collective-permute-start(bf16[2,2,128,128]{3,2,1,0:T(8,128)(2,1)} %get-tuple-element.15), channel_id=1, source_target_pairs={{1,0},{2,1},{3,2},{5,4},{6,5},{7,6},{9,8},{10,9},{11,10},{13,12},{... | collective-permute-start | bytes 393224 | tf_op jit(solution)/shard_map/ppermute | solution.py:18
  28.7 15.0 %collective-permute-start.3 = (bf16[512,128]{1,0:T(8,128)(2,1)}, bf16[512,128]{1,0:T(8,128)(2,1)}, u32[]{:S(2)}, u32[]{:S(2)}) collective-permute-start(bf16[512,128]{1,0:T(8,128)(2,1)} %get-tuple-element.23), channel_id=1, source_target_pairs={{0,28},{4,0},{8,4},{12,8},{16,12},{20,16},{24,20},{28,24},{1,29},{... | collective-permute-start | bytes 393224 | tf_op jit(solution)/shard_map/ppermute | solution.py:23
  32.9 2.2 %copy-start = (bf16[2,32,256,128]{3,2,1,0:T(8,128)(2,1)S(1)}, bf16[2,32,256,128]{3,2,1,0:T(8,128)(2,1)}, u32[]{:S(2)}) copy-start(bf16[2,32,256,128]{3,2,1,0:T(8,128)(2,1)} %interp_ref.4) | copy-start | bytes 12582916
  35.1 0.8 %copy-start.3 = (s32[2,32,128]{2,1,0:T(8,128)S(1)}, s32[2,32,128]{2,1,0:T(8,128)}, u32[]{:S(2)}) copy-start(s32[2,32,128]{2,1,0:T(8,128)} %skel_ref.4) | copy-start | bytes 98308
  35.9 0.7 %copy-start.5 = (bf16[2,32,128]{2,1,0:T(8,128)(2,1)S(1)}, bf16[2,32,128]{2,1,0:T(8,128)(2,1)}, u32[]{:S(2)}) copy-start(bf16[2,32,128]{2,1,0:T(8,128)(2,1)} %coup_ref.2) | copy-start | bytes 49156
  36.6 3.3 %copy-start.2 = (bf16[2,2,128,128]{3,2,1,0:T(8,128)(2,1)S(1)}, bf16[2,2,128,128]{3,2,1,0:T(8,128)(2,1)}, u32[]{:S(2)}) copy-start(bf16[2,2,128,128]{3,2,1,0:T(8,128)(2,1)} %copy-done.1) | copy-start | bytes 393220
  36.6 3.3 %copy-start.4 = (s32[2,32,128]{2,1,0:T(8,128)S(1)}, s32[2,32,128]{2,1,0:T(8,128)}, u32[]{:S(2)}) copy-start(s32[2,32,128]{2,1,0:T(8,128)} %skel_ref.5) | copy-start | bytes 98308
  36.6 3.4 %copy-start.6 = (bf16[2,32,128]{2,1,0:T(8,128)(2,1)S(1)}, bf16[2,32,128]{2,1,0:T(8,128)(2,1)}, u32[]{:S(2)}) copy-start(bf16[2,32,128]{2,1,0:T(8,128)(2,1)} %coup_ref.3) | copy-start | bytes 49156

commit v21 on v20

--- a/solution.py
+++ b/solution.py
@@ -226,17 +226,32 @@
 
 
 def x_part_kernel(
-    cells, layer, inner_ref, rank_ref, skel_ref, interp_ref, coup_ref, turned_ref, schur_ref, top_ref,
-    part_ref, lower_ref, lower_turned_ref,
+    cells, layer, inner_ref, rank_ref, skel_hbm, interp_hbm, coup_hbm, turned_ref, schur_ref, top_ref,
+    part_ref, lower_ref, lower_turned_ref, skel_ref, interp_ref, coup_ref, small_sems, sems,
 ):
     count, slots, half = turned_ref.shape
+    small = [
+        pltpu.make_async_copy(skel_hbm.at[layer], skel_ref, small_sems.at[0]),
+        pltpu.make_async_copy(coup_hbm.at[layer], coup_ref, small_sems.at[1]),
+    ]
+    fetches = []
+    for n in range(count // cells):
+        places = pl.ds(n * cells, cells)
+        fetches.append(
+            pltpu.make_async_copy(interp_hbm.at[layer, places], interp_ref.at[places], sems.at[n])
+        )
+    for copy in small + fetches:
+        copy.start()
+    for copy in small:
+        copy.wait()
     nothing = jnp.zeros((slots, slots), BF)
     inner = jnp.where(jnp.full((1, slots), inner_ref[0]) > 0, F32(1.0), F32(0.0)).astype(BF)
     for first in range(0, count, cells):
         group = range(first, first + cells)
-        skel = skel_ref[layer, first : first + cells]
+        fetches[first // cells].wait()
+        skel = skel_ref[first : first + cells]
         marked = [
-            marked_of(skel[k - first : k - first + 1], rank_ref[layer, k], interp_ref[layer, k]) for k in group
+            marked_of(skel[k - first : k - first + 1], rank_ref[layer, k], interp_ref[k]) for k in group
         ]
         faces = [kept_cleared(t) for t in [jnp.transpose(m) for m in marked]]
         for k in group:
@@ -246,7 +261,7 @@
         tops = [kept_cleared(t) * inner for t in [jnp.transpose(top_ref[k]) for k in group]]
         matrices = []
         for k, top in zip(group, tops):
-            conduct = coup_ref[layer, k : k + 1]
+            conduct = coup_ref[k : k + 1]
             link = dot_nt(scaled(turned_ref[k], conduct), top).astype(BF)
             link_t = dot_nt(scaled(top, conduct), turned_ref[k]).astype(BF)
             matrices.append(face_of(schur_ref[k], link, link_t, nothing))
@@ -317,6 +332,10 @@
     return pltpu.with_memory_space_constraint(x, pltpu.HBM)
 
 
+def in_vmem(x):
+    return pltpu.with_memory_space_constraint(x, pltpu.VMEM)
+
+
 def body(
     cell_matrix,
     x_coupling,
@@ -359,7 +378,7 @@
             pltpu.SemaphoreType.DMA((chunks,)),
         ],
     )(in_hbm(cell_rank), in_hbm(cell_skel), in_hbm(cell_interp))
-    top_in = passed_round(top, "gx")
+    top_in = passed_round(in_vmem(top), "gx")
 
 
     late_rows = cells * slots // 2
@@ -390,7 +409,7 @@
         [
             down_x(fslots, fslots),
             down(fslots, fslots),
-            vmem, vmem, vmem, vmem, vmem, vmem,
+            vmem, vmem, vmem, pl.BlockSpec((nx, 2, slots, half), lambda i, c: (0, 0, 0, 0)), vmem, vmem,
         ],
         [
             shape((nx, nj, fslots, fslots), BF),
@@ -417,7 +436,7 @@
     )
     edge_in = passed_along(edge, "yz", -1)
     packed_in = passed_round(packed, "gx")
-    packed_last_in = passed_round(packed_last, "gx")
+    packed_last_in = in_vmem(passed_round(packed_last, "gx"))
     face_bytes = nj * (4 * rows * slots + 4 * slots * slots) * 2
 
     last = nx - 1
@@ -428,7 +447,7 @@
     part, lower, lower_turned = call(
         functools.partial(x_part_kernel, cells, last),
         (),
-        [smem, smem, vmem, vmem, vmem, vmem, vmem, vmem],
+        [smem, smem, hbm, hbm, hbm, vmem, vmem, vmem],
         [vmem, vmem, vmem],
         [
             shape((nj, fslots, fslots), F32),
@@ -438,7 +457,14 @@
         8 * unit // nx,
         face_bytes,
         vmem=16,
-    )(inner, x_face_rank, x_face_skel, x_face_interp, x_coupling, last_turned, last_schur, top_in)
+        scratch=[
+            pltpu.VMEM((nj, slots), jnp.int32),
+            pltpu.VMEM((nj, rows, fslots), BF),
+            pltpu.VMEM((nj, half), BF),
+            pltpu.SemaphoreType.DMA((2,)),
+            pltpu.SemaphoreType.DMA((chunks,)),
+        ],
+    )(inner, x_face_rank, in_hbm(x_face_skel), in_hbm(x_face_interp), in_hbm(x_coupling), last_turned, last_schur, top_in)
 
     edge_in, part = lax.optimization_barrier((edge_in, part))
     y_out = call(

time: 46.2 us -> 45.4 us (0.983)
  local copies, waits for them, and re-layouts: 4.35 us -> 0.67 us
  Pallas kernels: 28.5 us -> 30.7 us
  waiting for transfers between devices: 2.77 us -> 3.73 us
    unnamed x20 -> x14, local copies, waits for them, and re-layouts: 4.35 us -> 0.67 us
    pallas_call x1, Pallas kernels: 3.32 us -> 5.47 us  [body(): call(functools.partial(x_part_kernel, cells, last), (), [smem, smem, hbm,...]
    ppermute x3, waiting for transfers between devices: 2.77 us -> 3.73 us  [passed_round(): lax.ppermute(x, axis, [(i, (i - 1) % devices) for i in range(devices)])]
  transfers between devices with their start and end apart: 4 -> 4, of which waited for: 1 -> 3; matrix products, arithmetic and copies ran while one was open for 0% -> 0% of each run, Pallas kernels for 53% -> 58%
where the time goes in v21:
time: 45.4 us; the launch traced here: 45.1 us
  Pallas kernels  30.7 us (68%)
  starting transfers between devices  9.3 us (20%)
  waiting for transfers between devices  3.73 us (8%)
  between operations  0.74 us (2%)
  local copies, waits for them, and re-layouts  0.67 us (1%)
    pallas_call x1, Pallas kernels, body(): call(functools.partial(main_kernel, cells, nx, chunks), (nx, chunks), [sm...  17.2 us
    ppermute x3, starting transfers between devices, passed_round(): lax.ppermute(x, axis, [(i, (i - 1) % devices) for i in range(devices)])  8.02 us
    pallas_call x1, Pallas kernels, body(): call(functools.partial(x_part_kernel, cells, last), (), [smem, smem, hbm,...  5.47 us
    ppermute x3, waiting for transfers between devices, passed_round(): lax.ppermute(x, axis, [(i, (i - 1) % devices) for i in range(devices)])  3.73 us
    pallas_call x2, Pallas kernels, body(): call(functools.partial(x_last_kernel, cells, last, places), (), [vmem, vm...  3.58 us
    pallas_call x1, Pallas kernels, body(): call(functools.partial(top_kernel, cells), (), [hbm, hbm, hbm], vmem, sha...  2.32 us
    pallas_call x1, Pallas kernels, body(): call(functools.partial(y_edge_kernel, nx, tail), (1,), [smem, pl.BlockSpe...  2.11 us
    ppermute x1, starting transfers between devices, passed_along(): return lax.ppermute(x, axis, pairs)  1.28 us
  transfers between devices with their start and end apart: 4, of which 3 were waited for; matrix products, arithmetic and copies ran while one was open for 0% of the time, Pallas kernels for 58%

profile of v21, /device:TPU:0, one launch (start us, length us, event | category | flops | bytes accessed | tf_op | source)
XLA Modules:
  0.0 45.1 jit_solution(14719004145659623829)
XLA Ops:
  0.6 0.0 copy-start.6
  0.6 0.0 copy-start.5
  0.7 0.0 copy-start.4
  0.7 2.3 %shard_map.132 = bf16[32,128,128]{2,1,0:T(8,128)(2,1)} custom-call(s32[2,32]{1,0:T(2,128)} %rank_hbm.1, s32[2,32,128]{2,1,0:T(8,128)} %skel_hbm.2, bf16[2,32,256,128]{3,2,1,0:T(8,128)(2,1)} %interp_hbm.2), custom_call_target="tpu_custom_call" | custom-call | bytes 2097152 | tf_op jit(solution)/shard_map/pallas_call | solution.py:364
  3.0 6.1 %collective-permute-start.1 = (bf16[32,128,128]{2,1,0:T(8,128)(2,1)}, bf16[32,128,128]{2,1,0:T(8,128)(2,1)S(1)}, u32[]{:S(2)}, u32[]{:S(2)}) collective-permute-start(bf16[32,128,128]{2,1,0:T(8,128)(2,1)} %shard_map.132), channel_id=1, source_target_pairs={{0,28},{4,0},{8,4},{12,8},{16,12},{20,16},{24,20},{28,24},{1,29},{... | collective-permute-start | bytes 3145736 | tf_op jit(solution)/shard_map/ppermute | solution.py:23
  9.0 0.0 copy-done.6
  9.1 0.0 copy-done.5
  9.1 0.0 copy-done.4
  9.1 17.2 %shard_map.131 = (bf16[2,32,128,128]{3,2,1,0:T(8,128)(2,1)}, bf16[2,32,128,128]{3,2,1,0:T(8,128)(2,1)}, bf16[1552,128]{1,0:T(8,128)(2,1)}, bf16[512,128]{1,0:T(8...) custom-call(s32[2,32]{1,0:T(2,128)S(1)} %copy-done.6, ...), custom_call_target="tpu_custom_call" | custom-call | flops 5368709120 | bytes 27262976 | tf_op jit(solution)/shard_map/pallas_call | solution.py:401
  26.2 0.0 copy-start
  26.2 0.6 %copy-done = bf16[2,2,128,128]{3,2,1,0:T(8,128)(2,1)} copy-done((bf16[2,2,128,128]{3,2,1,0:T(8,128)(2,1)}, bf16[2,2,128,128]{3,2,1,0:T(8,128)(2,1)S(1)}, u32[]{:S(2)}) %copy-start) | copy-done | bytes 131096
  26.9 0.5 %collective-permute-start.2 = (bf16[1552,128]{1,0:T(8,128)(2,1)}, bf16[1552,128]{1,0:T(8,128)(2,1)S(1)}, u32[]{:S(2)}, u32[]{:S(2)}) collective-permute-start(bf16[1552,128]{1,0:T(8,128)(2,1)} %get-tuple-element.22), channel_id=1, source_target_pairs={{0,28},{4,0},{8,4},{12,8},{16,12},{20,16},{24,20},{28,24},{1,29},{... | collective-permute-start | bytes 1191944 | tf_op jit(solution)/shard_map/ppermute | solution.py:23
  27.4 1.3 %collective-permute-start = (bf16[2,2,128,128]{3,2,1,0:T(8,128)(2,1)}, bf16[2,2,128,128]{3,2,1,0:T(8,128)(2,1)}, u32[]{:S(2)}, u32[]{:S(2)}) collective-permute-start(bf16[2,2,128,128]{3,2,1,0:T(8,128)(2,1)} %get-tuple-element.15), channel_id=1, source_target_pairs={{1,0},{2,1},{3,2},{5,4},{6,5},{7,6},{9,8},{10,9},{11,10},{13,12},{... | collective-permute-start | bytes 393224 | tf_op jit(solution)/shard_map/ppermute | solution.py:18
  28.7 1.5 %collective-permute-start.3 = (bf16[512,128]{1,0:T(8,128)(2,1)}, bf16[512,128]{1,0:T(8,128)(2,1)}, u32[]{:S(2)}, u32[]{:S(2)}) collective-permute-start(bf16[512,128]{1,0:T(8,128)(2,1)} %get-tuple-element.23), channel_id=1, source_target_pairs={{0,28},{4,0},{8,4},{12,8},{16,12},{20,16},{24,20},{28,24},{1,29},{... | collective-permute-start | bytes 393224 | tf_op jit(solution)/shard_map/ppermute | solution.py:23
  30.1 2.8 %collective-permute-done.1.top_ref = bf16[32,128,128]{2,1,0:T(8,128)(2,1)S(1)} collective-permute-done((bf16[32,128,128]{2,1,0:T(8,128)(2,1)}, bf16[32,128,128]{2,1,0:T(8,128)(2,1)S(1)}, u32[]{:S(2)}, u32[]{:S(2)}) %collective-permute-start.1) | collective-permute-done | bytes 1048608 | tf_op jit(solution)/shard_map/ppermute | solution.py:23
  32.9 5.5 %shard_map.133 = (f32[32,128,128]{2,1,0:T(8,128)S(1)}, bf16[32,128,128]{2,1,0:T(8,128)(2,1)S(1)}, bf16[32,128,128]{2,1,0:T(8,128)(2,1)S(1)}) custom-call(s32[1]{0:T(128)} %bitcast.inner_ref, s32[2,32]{1,0:T(2,128)S(1)} %copy-done.4, s32[2,32,128]{2,1,0:T(8,128)} %skel_hbm.3, bf16[2,32,256,128]{3,2,1,0:T(8,128)(2,1)} %interp_hbm.3, ...), custom_call_target="tpu_custom_call" | custom-call | flops 1073741824 | bytes 12582912 | tf_op jit(solution)/shard_map/pallas_call | solution.py:447
  38.4 0.0 collective-permute-done.edge_ref
  38.4 0.0 copy-done.1
  38.4 0.0 copy-done.2
  38.5 2.1 %shard_map.136 = bf16[2,32,128,128]{3,2,1,0:T(8,128)(2,1)} custom-call(s32[2,32]{1,0:T(2,128)S(1)} %copy-done.5, s32[2,32,128]{2,1,0:T(8,128)S(1)} %copy-done.2, bf16[2,32,256,128]{3,2,1,0:T(8,128)(2,1)} %interp_ref.3, bf16[2,32,128]{2,1,0:T(8,128)(2,1)S(1)} %copy-done.3, bf16[2,2,128,128]{3,2,1,0:T(8,128)(2,1)S(1)} %copy-done.1, ...), custom_call_target="tpu_custom_call", output_to_operand_aliasing={{}: (6, {})} | custom-call | flops 67108864 | bytes 786432 | tf_op jit(solution)/shard_map/pallas_call | solution.py:470
  40.6 0.9 %collective-permute-done.2.extra_ref.packed_ref = bf16[1552,128]{1,0:T(8,128)(2,1)S(1)} collective-permute-done((bf16[1552,128]{1,0:T(8,128)(2,1)}, bf16[1552,128]{1,0:T(8,128)(2,1)S(1)}, u32[]{:S(2)}, u32[]{:S(2)}) %collective-permute-start.2) | collective-permute-done | bytes 397344 | tf_op jit(solution)/shard_map/ppermute | solution.py:23
  41.4 1.6 %shard_map.134._ = bf16[2,32,128,128]{3,2,1,0:T(8,128)(2,1)} custom-call(f32[32,128,128]{2,1,0:T(8,128)S(1)} %get-tuple-element.19.part_ref, bf16[32,128,128]{2,1,0:T(8,128)(2,1)S(1)} %get-tuple-element.20.lower_ref, bf16[32,128,128]{2,1,0:T(8,128)(2,1)S(1)} %get-tuple-element.21.lower_turned_ref, ...), custom_call_target="tpu_custom_call", output_to_operand_aliasing={{}: (5, {})} | custom-call | flops 301989888 | bytes 4325376 | tf_op jit(solution)/shard_map/pallas_call | solution.py:494
  43.0 0.1 collective-permute-done.3.packed_ref
  43.1 2.0 %shard_map.135 = bf16[2,32,128,128]{3,2,1,0:T(8,128)(2,1)} custom-call(f32[32,128,128]{2,1,0:T(8,128)S(1)} %get-tuple-element.19.part_ref, bf16[32,128,128]{2,1,0:T(8,128)(2,1)S(1)} %get-tuple-element.20.lower_ref, bf16[32,128,128]{2,1,0:T(8,128)(2,1)S(1)} %get-tuple-element.21.lower_turned_ref, ...), custom_call_target="tpu_custom_call", output_to_operand_aliasing={{}: (5, {})} | custom-call | flops 100663296 | bytes 1441792 | tf_op jit(solution)/shard_map/pallas_call | solution.py:494
  (4 shorter events, 0.0 us)
Async XLA Ops:
  0.6 8.4 %copy-start.6 = (s32[2,32]{1,0:T(2,128)S(1)}, s32[2,32]{1,0:T(2,128)}, u32[]{:S(2)}) copy-start(s32[2,32]{1,0:T(2,128)} %rank_hbm.1) | copy-start | bytes 772
  0.6 8.4 %copy-start.5 = (s32[2,32]{1,0:T(2,128)S(1)}, s32[2,32]{1,0:T(2,128)}, u32[]{:S(2)}) copy-start(s32[2,32]{1,0:T(2,128)} %rank_ref.5) | copy-start | bytes 772
  0.7 8.4 %copy-start.4 = (s32[2,32]{1,0:T(2,128)S(1)}, s32[2,32]{1,0:T(2,128)}, u32[]{:S(2)}) copy-start(s32[2,32]{1,0:T(2,128)} %rank_ref.4) | copy-start | bytes 772
  3.0 29.9 %collective-permute-start.1 = (bf16[32,128,128]{2,1,0:T(8,128)(2,1)}, bf16[32,128,128]{2,1,0:T(8,128)(2,1)S(1)}, u32[]{:S(2)}, u32[]{:S(2)}) collective-permute-start(bf16[32,128,128]{2,1,0:T(8,128)(2,1)} %shard_map.132), channel_id=1, source_target_pairs={{0,28},{4,0},{8,4},{12,8},{16,12},{20,16},{24,20},{28,24},{1,29},{... | collective-permute-start | bytes 3145736 | tf_op jit(solution)/shard_map/ppermute | solution.py:23
  26.2 0.7 %copy-start = (bf16[2,2,128,128]{3,2,1,0:T(8,128)(2,1)}, bf16[2,2,128,128]{3,2,1,0:T(8,128)(2,1)S(1)}, u32[]{:S(2)}) copy-start(bf16[2,2,128,128]{3,2,1,0:T(8,128)(2,1)S(1)} %get-tuple-element.25.corner_ref) | copy-start | bytes 393220
  26.9 14.6 %collective-permute-start.2 = (bf16[1552,128]{1,0:T(8,128)(2,1)}, bf16[1552,128]{1,0:T(8,128)(2,1)S(1)}, u32[]{:S(2)}, u32[]{:S(2)}) collective-permute-start(bf16[1552,128]{1,0:T(8,128)(2,1)} %get-tuple-element.22), channel_id=1, source_target_pairs={{0,28},{4,0},{8,4},{12,8},{16,12},{20,16},{24,20},{28,24},{1,29},{... | collective-permute-start | bytes 1191944 | tf_op jit(solution)/shard_map/ppermute | solution.py:23
  27.4 11.0 %collective-permute-start = (bf16[2,2,128,128]{3,2,1,0:T(8,128)(2,1)}, bf16[2,2,128,128]{3,2,1,0:T(8,128)(2,1)}, u32[]{:S(2)}, u32[]{:S(2)}) collective-permute-start(bf16[2,2,128,128]{3,2,1,0:T(8,128)(2,1)} %get-tuple-element.15), channel_id=1, source_target_pairs={{1,0},{2,1},{3,2},{5,4},{6,5},{7,6},{9,8},{10,9},{11,10},{13,12},{... | collective-permute-start | bytes 393224 | tf_op jit(solution)/shard_map/ppermute | solution.py:18
  28.7 14.4 %collective-permute-start.3 = (bf16[512,128]{1,0:T(8,128)(2,1)}, bf16[512,128]{1,0:T(8,128)(2,1)}, u32[]{:S(2)}, u32[]{:S(2)}) collective-permute-start(bf16[512,128]{1,0:T(8,128)(2,1)} %get-tuple-element.23), channel_id=1, source_target_pairs={{0,28},{4,0},{8,4},{12,8},{16,12},{20,16},{24,20},{28,24},{1,29},{... | collective-permute-start | bytes 393224 | tf_op jit(solution)/shard_map/ppermute | solution.py:23
  32.9 5.5 %copy-start.1 = (bf16[2,2,128,128]{3,2,1,0:T(8,128)(2,1)S(1)}, bf16[2,2,128,128]{3,2,1,0:T(8,128)(2,1)}, u32[]{:S(2)}) copy-start(bf16[2,2,128,128]{3,2,1,0:T(8,128)(2,1)} %copy-done) | copy-start | bytes 393220
  32.9 5.5 %copy-start.2 = (s32[2,32,128]{2,1,0:T(8,128)S(1)}, s32[2,32,128]{2,1,0:T(8,128)}, u32[]{:S(2)}) copy-start(s32[2,32,128]{2,1,0:T(8,128)} %skel_ref.3) | copy-start | bytes 98308
  32.9 5.5 %copy-start.3 = (bf16[2,32,128]{2,1,0:T(8,128)(2,1)S(1)}, bf16[2,32,128]{2,1,0:T(8,128)(2,1)}, u32[]{:S(2)}) copy-start(bf16[2,32,128]{2,1,0:T(8,128)(2,1)} %coup_ref.1) | copy-start | bytes 49156

commit v22 on v17

--- a/solution.py
+++ b/solution.py
@@ -248,7 +248,8 @@
 
 
 def x_last_kernel(
-    cells, layer, places, part_ref, lower_ref, lower_turned_ref, extra_ref, packed_ref, _, out_ref, held, sems
+    cells, layer, places, extra_start, part_ref, lower_ref, lower_turned_ref, extra_ref, packed_ref, _,
+    out_ref, held, sems,
 ):
     slots = part_ref.shape[-1]
     half = slots // 2
@@ -258,7 +259,7 @@
     low_scale = jnp.where(opposite, mid, jnp.where(upper, zero, one))
     same_scale = jnp.where(same, one, zero)
     opposite_scale = jnp.where(opposite, one, zero)
-    extras = extra_ref[(part_ref.shape[0] // cells - 1) * cells * half :].astype(F32)
+    extras = extra_ref[extra_start:].astype(F32)
     pairs = -(-cells // 2)
     copies = []
     for n, c in enumerate(places):
@@ -277,7 +278,7 @@
             schurs.append(tri + jnp.transpose(tri))
         inner = [dot(lower_turned_ref[k], h).astype(BF) for k, h in zip(group, schurs)]
         results = [dot(i, lower_ref[k]) for k, i in zip(group, inner)]
-        part_cells = max(1, cells // 2)
+        part_cells = cells
         for start in range(0, cells, part_cells):
             for k in range(start, start + part_cells):
                 held[n * cells + k] = (part_ref[c * cells + k] + results[k]).astype(BF)
@@ -452,23 +453,25 @@
         {6: 0},
     )(y_face_rank, y_face_skel, in_hbm(y_face_interp), y_coupling, corner, edge_in, y_out)
 
+    few = cells // 2 if cells % 4 == 0 else cells
+    late = cells // few
     for places, arrived in (
-        (range(chunks - 1), packed_in),
-        (range(chunks - 1, chunks), packed_last_in),
+        (range((chunks - 1) * late), packed_in),
+        (range((chunks - 1) * late, chunks * late), packed_last_in),
     ):
         count = len(places)
         x_out = call(
-            functools.partial(x_last_kernel, cells, last, places),
+            functools.partial(x_last_kernel, few, last, places, (chunks - 1) * late_rows),
             (),
             [vmem, vmem, vmem, vmem, vmem, hbm],
             hbm,
             shape((nx, nj, fslots, fslots), BF),
-            3 * unit // nx * count // chunks,
-            nj * slots * slots * 11 * count // chunks,
+            3 * unit // nx * count // (chunks * late),
+            nj * slots * slots * 11 * count // (chunks * late),
             {5: 0},
             scratch=[
-                pltpu.VMEM((count * cells, fslots, fslots), BF),
-                pltpu.SemaphoreType.DMA((count, 2)),
+                pltpu.VMEM((count * few, fslots, fslots), BF),
+                pltpu.SemaphoreType.DMA((count, 1)),
             ],
         )(part, lower, lower_turned, packed_in, arrived, x_out)
     return (x_out, y_out)

time: 42.9 us -> 43 us (level)
  Pallas kernels: 26.4 us -> 26.9 us
    pallas_call x2, Pallas kernels: 2.68 us -> 3.14 us  [body(): call(functools.partial(x_last_kernel, few, last, places, (chunks - 1) * l...]
  transfers between devices with their start and end apart: 4 -> 4, of which waited for: 3 -> 2; matrix products, arithmetic and copies ran while one was open for 0% -> 0% of each run, Pallas kernels for 56% -> 57%
where the time goes in v22:
time: 43 us; the launch traced here: 42.6 us
  Pallas kernels  26.9 us (63%)
  waiting for transfers between devices  9.74 us (23%)
  starting transfers between devices  5.16 us (12%)
  between operations  0.8 us (2%)
    pallas_call x1, Pallas kernels, body(): call(functools.partial(main_kernel, cells, nx, chunks), (nx, chunks), [sm...  17.1 us
    ppermute x4, waiting for transfers between devices, passed_along(): return lax.ppermute(x, axis, pairs)  9.74 us
    ppermute x4, starting transfers between devices, passed_along(): return lax.ppermute(x, axis, pairs)  5.16 us
    pallas_call x1, Pallas kernels, body(): call(functools.partial(x_part_kernel, cells, last), (), [smem, vmem, vmem...  3.22 us
    pallas_call x2, Pallas kernels, body(): call(functools.partial(x_last_kernel, few, last, places, (chunks - 1) * l...  3.14 us
    pallas_call x1, Pallas kernels, body(): call(functools.partial(y_edge_kernel, nx, tail), (1,), [smem, pl.BlockSpe...  2.05 us
    pallas_call x1, Pallas kernels, body(): call(functools.partial(top_kernel, cells), (), [hbm, hbm, hbm], vmem, sha...  1.35 us
  transfers between devices with their start and end apart: 4, of which 2 were waited for; matrix products, arithmetic and copies ran while one was open for 0% of the time, Pallas kernels for 57%

profile of v22, /device:TPU:0, one launch (start us, length us, event | category | flops | bytes accessed | tf_op | source)
XLA Modules:
  0.0 42.6 jit_solution(10684645110687514182)
XLA Ops:
  0.6 0.0 copy-start.6
  0.6 0.0 copy-start.5
  0.7 0.0 copy-start.7
  0.7 1.3 %shard_map.132 = bf16[32,128,128]{2,1,0:T(8,128)(2,1)S(1)} custom-call(s32[2,32]{1,0:T(2,128)} %rank_hbm.1, s32[2,32,128]{2,1,0:T(8,128)} %skel_hbm.1, bf16[2,32,256,128]{3,2,1,0:T(8,128)(2,1)} %interp_hbm.1), custom_call_target="tpu_custom_call" | custom-call | bytes 2097152 | tf_op jit(solution)/shard_map/pallas_call | solution.py:339
  2.0 0.0 copy-start.1
  2.0 0.0 copy-start.3
  2.0 1.3 %collective-permute-start.1 = (bf16[32,128,128]{2,1,0:T(8,128)(2,1)S(1)}, bf16[32,128,128]{2,1,0:T(8,128)(2,1)S(1)}, u32[]{:S(2)}, u32[]{:S(2)}) collective-permute-start(bf16[32,128,128]{2,1,0:T(8,128)(2,1)S(1)} %shard_map.132), channel_id=1, source_target_pairs={{4,0},{8,4},{12,8},{16,12},{20,16},{24,20},{28,24},{5,1},{9,5},{13... | collective-permute-start | bytes 3145736 | tf_op jit(solution)/shard_map/ppermute | solution.py:18
  3.3 0.0 copy-done.6
  3.4 0.0 copy-start
  3.4 17.1 %shard_map.131 = (bf16[2,32,128,128]{3,2,1,0:T(8,128)(2,1)}, bf16[2,32,128,128]{3,2,1,0:T(8,128)(2,1)}, bf16[1552,128]{1,0:T(8,128)(2,1)S(1)}, bf16[512,128]{1,0...) custom-call(s32[2,32]{1,0:T(2,128)S(1)} %copy-done.6, ...), custom_call_target="tpu_custom_call" | custom-call | flops 5368709120 | bytes 27262976 | tf_op jit(solution)/shard_map/pallas_call | solution.py:376
  20.5 1.3 %collective-permute-start.2 = (bf16[1552,128]{1,0:T(8,128)(2,1)S(1)}, bf16[1552,128]{1,0:T(8,128)(2,1)S(1)}, u32[]{:S(2)}, u32[]{:S(2)}) collective-permute-start(bf16[1552,128]{1,0:T(8,128)(2,1)S(1)} %get-tuple-element.22), channel_id=1, source_target_pairs={{4,0},{8,4},{12,8},{16,12},{20,16},{24,20},{28,24},{5,1},{9,5},{13... | collective-permute-start | bytes 1191944 | tf_op jit(solution)/shard_map/ppermute | solution.py:18
  21.8 1.3 %collective-permute-start = (bf16[2,2,128,128]{3,2,1,0:T(8,128)(2,1)S(1)}, bf16[2,2,128,128]{3,2,1,0:T(8,128)(2,1)S(1)}, u32[]{:S(2)}, u32[]{:S(2)}) collective-permute-start(bf16[2,2,128,128]{3,2,1,0:T(8,128)(2,1)S(1)} %get-tuple-element.15), channel_id=1, source_target_pairs={{1,0},{2,1},{3,2},{5,4},{6,5},{7,6},{9,8},{10,9},{11,10},{13,12},{... | collective-permute-start | bytes 393224 | tf_op jit(solution)/shard_map/ppermute | solution.py:18
  23.1 1.3 %collective-permute-start.3 = (bf16[512,128]{1,0:T(8,128)(2,1)S(1)}, bf16[512,128]{1,0:T(8,128)(2,1)S(1)}, u32[]{:S(2)}, u32[]{:S(2)}) collective-permute-start(bf16[512,128]{1,0:T(8,128)(2,1)S(1)} %get-tuple-element.23), channel_id=1, source_target_pairs={{4,0},{8,4},{12,8},{16,12},{20,16},{24,20},{28,24},{5,1},{9,5},{13... | collective-permute-start | bytes 393224 | tf_op jit(solution)/shard_map/ppermute | solution.py:18
  24.4 6.5 %collective-permute-done.1.top_ref = bf16[32,128,128]{2,1,0:T(8,128)(2,1)S(1)} collective-permute-done((bf16[32,128,128]{2,1,0:T(8,128)(2,1)S(1)}, bf16[32,128,128]{2,1,0:T(8,128)(2,1)S(1)}, u32[]{:S(2)}, u32[]{:S(2)}) %collective-permute-start.1) | collective-permute-done | bytes 1048608 | tf_op jit(solution)/shard_map/ppermute | solution.py:18
  30.9 0.0 copy-done.3
  30.9 0.0 copy-start.2
  30.9 0.0 copy-start.4
  30.9 3.2 %shard_map.133 = (f32[32,128,128]{2,1,0:T(8,128)S(1)}, bf16[32,128,128]{2,1,0:T(8,128)(2,1)S(1)}, bf16[32,128,128]{2,1,0:T(8,128)(2,1)S(1)}) custom-call(s32[2,32]{1,0:T(2,128)S(1)} %copy-done.7, s32[2,32,128]{2,1,0:T(8,128)S(1)} %copy-done.1, bf16[2,32,256,128]{3,2,1,0:T(8,128)(2,1)S(1)} %copy-done, bf16[2,32,128]{2,1,0:T(8,128)(2,1)S(1)} %copy-done.3, ...), custom_call_target="tpu_custom_call" | custom-call | flops 1073741824 | bytes 12582912 | tf_op jit(solution)/shard_map/pallas_call | solution.py:421
  34.2 0.0 collective-permute-done.edge_ref
  34.2 2.1 %shard_map.136 = bf16[2,32,128,128]{3,2,1,0:T(8,128)(2,1)} custom-call(s32[2,32]{1,0:T(2,128)S(1)} %copy-done.5, s32[2,32,128]{2,1,0:T(8,128)S(1)} %copy-done.2, bf16[2,32,256,128]{3,2,1,0:T(8,128)(2,1)} %interp_ref.5, bf16[2,32,128]{2,1,0:T(8,128)(2,1)S(1)} %copy-done.4, ...), custom_call_target="tpu_custom_call", output_to_operand_aliasing={{}: (6, {})} | custom-call | flops 67108864 | bytes 786432 | tf_op jit(solution)/shard_map/pallas_call | solution.py:437
  36.2 3.2 %collective-permute-done.2.extra_ref.packed_ref = bf16[1552,128]{1,0:T(8,128)(2,1)S(1)} collective-permute-done((bf16[1552,128]{1,0:T(8,128)(2,1)S(1)}, bf16[1552,128]{1,0:T(8,128)(2,1)S(1)}, u32[]{:S(2)}, u32[]{:S(2)}) %collective-permute-start.2) | collective-permute-done | bytes 397344 | tf_op jit(solution)/shard_map/ppermute | solution.py:18
  39.4 1.9 %shard_map.134._ = bf16[2,32,128,128]{3,2,1,0:T(8,128)(2,1)} custom-call(f32[32,128,128]{2,1,0:T(8,128)S(1)} %get-tuple-element.19.part_ref, bf16[32,128,128]{2,1,0:T(8,128)(2,1)S(1)} %get-tuple-element.20.lower_ref, bf16[32,128,128]{2,1,0:T(8,128)(2,1)S(1)} %get-tuple-element.21.lower_turned_ref, ...), custom_call_target="tpu_custom_call", output_to_operand_aliasing={{}: (5, {})} | custom-call | flops 301989888 | bytes 4325376 | tf_op jit(solution)/shard_map/pallas_call | solution.py:463
  41.3 0.0 collective-permute-done.3.packed_ref
  41.4 1.2 %shard_map.135 = bf16[2,32,128,128]{3,2,1,0:T(8,128)(2,1)} custom-call(f32[32,128,128]{2,1,0:T(8,128)S(1)} %get-tuple-element.19.part_ref, bf16[32,128,128]{2,1,0:T(8,128)(2,1)S(1)} %get-tuple-element.20.lower_ref, bf16[32,128,128]{2,1,0:T(8,128)(2,1)S(1)} %get-tuple-element.21.lower_turned_ref, ...), custom_call_target="tpu_custom_call", output_to_operand_aliasing={{}: (5, {})} | custom-call | flops 100663296 | bytes 1441792 | tf_op jit(solution)/shard_map/pallas_call | solution.py:463
  (6 shorter events, 0.0 us)
Async XLA Ops:
  0.6 2.7 %copy-start.6 = (s32[2,32]{1,0:T(2,128)S(1)}, s32[2,32]{1,0:T(2,128)}, u32[]{:S(2)}) copy-start(s32[2,32]{1,0:T(2,128)} %rank_hbm.1) | copy-start | bytes 772
  0.6 2.7 %copy-start.5 = (s32[2,32]{1,0:T(2,128)S(1)}, s32[2,32]{1,0:T(2,128)}, u32[]{:S(2)}) copy-start(s32[2,32]{1,0:T(2,128)} %rank_ref.5) | copy-start | bytes 772
  0.7 2.7 %copy-start.7 = (s32[2,32]{1,0:T(2,128)S(1)}, s32[2,32]{1,0:T(2,128)}, u32[]{:S(2)}) copy-start(s32[2,32]{1,0:T(2,128)} %rank_ref.4) | copy-start | bytes 772
  2.0 28.9 %copy-start.1 = (s32[2,32,128]{2,1,0:T(8,128)S(1)}, s32[2,32,128]{2,1,0:T(8,128)}, u32[]{:S(2)}) copy-start(s32[2,32,128]{2,1,0:T(8,128)} %skel_ref.4) | copy-start | bytes 98308
  2.0 28.9 %copy-start.3 = (bf16[2,32,128]{2,1,0:T(8,128)(2,1)S(1)}, bf16[2,32,128]{2,1,0:T(8,128)(2,1)}, u32[]{:S(2)}) copy-start(bf16[2,32,128]{2,1,0:T(8,128)(2,1)} %coup_ref.2) | copy-start | bytes 49156
  2.0 28.9 %collective-permute-start.1 = (bf16[32,128,128]{2,1,0:T(8,128)(2,1)S(1)}, bf16[32,128,128]{2,1,0:T(8,128)(2,1)S(1)}, u32[]{:S(2)}, u32[]{:S(2)}) collective-permute-start(bf16[32,128,128]{2,1,0:T(8,128)(2,1)S(1)} %shard_map.132), channel_id=1, source_target_pairs={{4,0},{8,4},{12,8},{16,12},{20,16},{24,20},{28,24},{5,1},{9,5},{13... | collective-permute-start | bytes 3145736 | tf_op jit(solution)/shard_map/ppermute | solution.py:18
  3.4 27.5 %copy-start = (bf16[2,32,256,128]{3,2,1,0:T(8,128)(2,1)S(1)}, bf16[2,32,256,128]{3,2,1,0:T(8,128)(2,1)}, u32[]{:S(2)}) copy-start(bf16[2,32,256,128]{3,2,1,0:T(8,128)(2,1)} %interp_ref.4) | copy-start | bytes 12582916
  20.5 18.9 %collective-permute-start.2 = (bf16[1552,128]{1,0:T(8,128)(2,1)S(1)}, bf16[1552,128]{1,0:T(8,128)(2,1)S(1)}, u32[]{:S(2)}, u32[]{:S(2)}) collective-permute-start(bf16[1552,128]{1,0:T(8,128)(2,1)S(1)} %get-tuple-element.22), channel_id=1, source_target_pairs={{4,0},{8,4},{12,8},{16,12},{20,16},{24,20},{28,24},{5,1},{9,5},{13... | collective-permute-start | bytes 1191944 | tf_op jit(solution)/shard_map/ppermute | solution.py:18
  21.8 12.4 %collective-permute-start = (bf16[2,2,128,128]{3,2,1,0:T(8,128)(2,1)S(1)}, bf16[2,2,128,128]{3,2,1,0:T(8,128)(2,1)S(1)}, u32[]{:S(2)}, u32[]{:S(2)}) collective-permute-start(bf16[2,2,128,128]{3,2,1,0:T(8,128)(2,1)S(1)} %get-tuple-element.15), channel_id=1, source_target_pairs={{1,0},{2,1},{3,2},{5,4},{6,5},{7,6},{9,8},{10,9},{11,10},{13,12},{... | collective-permute-start | bytes 393224 | tf_op jit(solution)/shard_map/ppermute | solution.py:18
  23.1 18.3 %collective-permute-start.3 = (bf16[512,128]{1,0:T(8,128)(2,1)S(1)}, bf16[512,128]{1,0:T(8,128)(2,1)S(1)}, u32[]{:S(2)}, u32[]{:S(2)}) collective-permute-start(bf16[512,128]{1,0:T(8,128)(2,1)S(1)} %get-tuple-element.23), channel_id=1, source_target_pairs={{4,0},{8,4},{12,8},{16,12},{20,16},{24,20},{28,24},{5,1},{9,5},{13... | collective-permute-start | bytes 393224 | tf_op jit(solution)/shard_map/ppermute | solution.py:18
  30.9 3.3 %copy-start.2 = (s32[2,32,128]{2,1,0:T(8,128)S(1)}, s32[2,32,128]{2,1,0:T(8,128)}, u32[]{:S(2)}) copy-start(s32[2,32,128]{2,1,0:T(8,128)} %skel_ref.5) | copy-start | bytes 98308
  30.9 3.3 %copy-start.4 = (bf16[2,32,128]{2,1,0:T(8,128)(2,1)S(1)}, bf16[2,32,128]{2,1,0:T(8,128)(2,1)}, u32[]{:S(2)}) copy-start(bf16[2,32,128]{2,1,0:T(8,128)(2,1)} %coup_ref.3) | copy-start | bytes 49156

commit v23 on v22

--- a/solution.py
+++ b/solution.py
@@ -248,7 +248,7 @@
 
 
 def x_last_kernel(
-    cells, layer, places, extra_start, part_ref, lower_ref, lower_turned_ref, extra_ref, packed_ref, _,
+    cells, layer, begin, extra_start, part_ref, lower_ref, lower_turned_ref, extra_ref, packed_ref, _,
     out_ref, held, sems,
 ):
     slots = part_ref.shape[-1]
@@ -260,35 +260,33 @@
     same_scale = jnp.where(same, one, zero)
     opposite_scale = jnp.where(opposite, one, zero)
     extras = extra_ref[extra_start:].astype(F32)
-    pairs = -(-cells // 2)
     copies = []
-    for n, c in enumerate(places):
-        group = range(c * cells, (c + 1) * cells)
-        schurs = []
-        for k in range(cells):
-            start = (n * cells + k) * half
-            packed = packed_ref[start : start + half].astype(F32)
-            extra = extras[c * pairs + k // 2 : c * pairs + k // 2 + 1]
-            top, low = packed * top_scale, packed * low_scale
-            if k % 2 == 0:
-                top += extra * opposite_scale
-            else:
-                low += extra * same_scale
-            tri = jnp.concatenate([top, low], axis=0).astype(BF)
-            schurs.append(tri + jnp.transpose(tri))
-        inner = [dot(lower_turned_ref[k], h).astype(BF) for k, h in zip(group, schurs)]
-        results = [dot(i, lower_ref[k]) for k, i in zip(group, inner)]
-        part_cells = cells
-        for start in range(0, cells, part_cells):
-            for k in range(start, start + part_cells):
-                held[n * cells + k] = (part_ref[c * cells + k] + results[k]).astype(BF)
-            copy = pltpu.make_async_copy(
-                held.at[pl.ds(n * cells + start, part_cells)],
-                out_ref.at[layer, pl.ds(c * cells + start, part_cells)],
-                sems.at[n, start // part_cells],
-            )
-            copy.start()
-            copies.append(copy)
+    group = range(begin, begin + cells)
+    schurs = []
+    for k in range(cells):
+        start = k * half
+        packed = packed_ref[start : start + half].astype(F32)
+        extra = extras[(begin + k) // 2 : (begin + k) // 2 + 1]
+        top, low = packed * top_scale, packed * low_scale
+        if k % 2 == 0:
+            top += extra * opposite_scale
+        else:
+            low += extra * same_scale
+        tri = jnp.concatenate([top, low], axis=0).astype(BF)
+        schurs.append(tri + jnp.transpose(tri))
+    inner = [dot(lower_turned_ref[k], h).astype(BF) for k, h in zip(group, schurs)]
+    results = [dot(i, lower_ref[k]) for k, i in zip(group, inner)]
+    part_cells = max(1, cells // 4)
+    for start in range(0, cells, part_cells):
+        for k in range(start, start + part_cells):
+            held[k] = (part_ref[begin + k] + results[k]).astype(BF)
+        copy = pltpu.make_async_copy(
+            held.at[pl.ds(start, part_cells)],
+            out_ref.at[layer, pl.ds(begin + start, part_cells)],
+            sems.at[start // part_cells],
+        )
+        copy.start()
+        copies.append(copy)
     for copy in copies:
         copy.wait()
 
@@ -453,25 +451,20 @@
         {6: 0},
     )(y_face_rank, y_face_skel, in_hbm(y_face_interp), y_coupling, corner, edge_in, y_out)
 
-    few = cells // 2 if cells % 4 == 0 else cells
-    late = cells // few
-    for places, arrived in (
-        (range((chunks - 1) * late), packed_in),
-        (range((chunks - 1) * late, chunks * late), packed_last_in),
-    ):
-        count = len(places)
+    early = (chunks - 1) * cells
+    for begin, count, arrived in ((0, early, packed_in), (early, cells, packed_last_in)):
         x_out = call(
-            functools.partial(x_last_kernel, few, last, places, (chunks - 1) * late_rows),
+            functools.partial(x_last_kernel, count, last, begin, (chunks - 1) * late_rows),
             (),
             [vmem, vmem, vmem, vmem, vmem, hbm],
             hbm,
             shape((nx, nj, fslots, fslots), BF),
-            3 * unit // nx * count // (chunks * late),
-            nj * slots * slots * 11 * count // (chunks * late),
+            3 * unit // nx * count // nj,
+            slots * slots * 11 * count,
             {5: 0},
             scratch=[
-                pltpu.VMEM((count * few, fslots, fslots), BF),
-                pltpu.SemaphoreType.DMA((count, 1)),
+                pltpu.VMEM((count, fslots, fslots), BF),
+                pltpu.SemaphoreType.DMA((8,)),
             ],
         )(part, lower, lower_turned, packed_in, arrived, x_out)
     return (x_out, y_out)

time: 43 us -> 42.9 us (level)
  Pallas kernels: 26.9 us -> 26.3 us
  waiting for transfers between devices: 9.74 us -> 10.2 us
    pallas_call x2, Pallas kernels: 3.14 us -> 2.57 us  [body(): call(functools.partial(x_last_kernel, count, last, begin, (chunks - 1) *...]
    ppermute x4, waiting for transfers between devices: 9.74 us -> 10.2 us  [passed_along(): return lax.ppermute(x, axis, pairs)]
  transfers between devices with their start and end apart: 4 -> 4, of which waited for: 2 -> 3; matrix products, arithmetic and copies ran while one was open for 0% -> 0% of each run, Pallas kernels for 57% -> 56%
where the time goes in v23:
time: 42.9 us; the launch traced here: 42.5 us
  Pallas kernels  26.3 us (61%)
  waiting for transfers between devices  10.2 us (24%)
  starting transfers between devices  5.16 us (12%)
  between operations  0.8 us (2%)
    pallas_call x1, Pallas kernels, body(): call(functools.partial(main_kernel, cells, nx, chunks), (nx, chunks), [sm...  17.1 us
    ppermute x4, waiting for transfers between devices, passed_along(): return lax.ppermute(x, axis, pairs)  10.2 us
    ppermute x4, starting transfers between devices, passed_along(): return lax.ppermute(x, axis, pairs)  5.16 us
    pallas_call x1, Pallas kernels, body(): call(functools.partial(x_part_kernel, cells, last), (), [smem, vmem, vmem...  3.22 us
    pallas_call x2, Pallas kernels, body(): call(functools.partial(x_last_kernel, count, last, begin, (chunks - 1) *...  2.57 us
    pallas_call x1, Pallas kernels, body(): call(functools.partial(y_edge_kernel, nx, tail), (1,), [smem, pl.BlockSpe...  2.05 us
    pallas_call x1, Pallas kernels, body(): call(functools.partial(top_kernel, cells), (), [hbm, hbm, hbm], vmem, sha...  1.35 us
  transfers between devices with their start and end apart: 4, of which 3 were waited for; matrix products, arithmetic and copies ran while one was open for 0% of the time, Pallas kernels for 56%

profile of v23, /device:TPU:0, one launch (start us, length us, event | category | flops | bytes accessed | tf_op | source)
XLA Modules:
  0.0 42.5 jit_solution(4648159949909304408)
XLA Ops:
  0.6 0.0 copy-start.6
  0.6 0.0 copy-start.5
  0.7 0.0 copy-start.7
  0.7 1.3 %shard_map.132 = bf16[32,128,128]{2,1,0:T(8,128)(2,1)S(1)} custom-call(s32[2,32]{1,0:T(2,128)} %rank_hbm.1, s32[2,32,128]{2,1,0:T(8,128)} %skel_hbm.1, bf16[2,32,256,128]{3,2,1,0:T(8,128)(2,1)} %interp_hbm.1), custom_call_target="tpu_custom_call" | custom-call | bytes 2097152 | tf_op jit(solution)/shard_map/pallas_call | solution.py:337
  2.0 0.0 copy-start.1
  2.0 0.0 copy-start.3
  2.0 1.3 %collective-permute-start.1 = (bf16[32,128,128]{2,1,0:T(8,128)(2,1)S(1)}, bf16[32,128,128]{2,1,0:T(8,128)(2,1)S(1)}, u32[]{:S(2)}, u32[]{:S(2)}) collective-permute-start(bf16[32,128,128]{2,1,0:T(8,128)(2,1)S(1)} %shard_map.132), channel_id=1, source_target_pairs={{4,0},{8,4},{12,8},{16,12},{20,16},{24,20},{28,24},{5,1},{9,5},{13... | collective-permute-start | bytes 3145736 | tf_op jit(solution)/shard_map/ppermute | solution.py:18
  3.3 0.0 copy-done.6
  3.4 0.0 copy-start
  3.4 17.1 %shard_map.131 = (bf16[2,32,128,128]{3,2,1,0:T(8,128)(2,1)}, bf16[2,32,128,128]{3,2,1,0:T(8,128)(2,1)}, bf16[1552,128]{1,0:T(8,128)(2,1)S(1)}, bf16[512,128]{1,0...) custom-call(s32[2,32]{1,0:T(2,128)S(1)} %copy-done.6, ...), custom_call_target="tpu_custom_call" | custom-call | flops 5368709120 | bytes 27262976 | tf_op jit(solution)/shard_map/pallas_call | solution.py:374
  20.5 1.3 %collective-permute-start.2 = (bf16[1552,128]{1,0:T(8,128)(2,1)S(1)}, bf16[1552,128]{1,0:T(8,128)(2,1)S(1)}, u32[]{:S(2)}, u32[]{:S(2)}) collective-permute-start(bf16[1552,128]{1,0:T(8,128)(2,1)S(1)} %get-tuple-element.22), channel_id=1, source_target_pairs={{4,0},{8,4},{12,8},{16,12},{20,16},{24,20},{28,24},{5,1},{9,5},{13... | collective-permute-start | bytes 1191944 | tf_op jit(solution)/shard_map/ppermute | solution.py:18
  21.8 1.3 %collective-permute-start = (bf16[2,2,128,128]{3,2,1,0:T(8,128)(2,1)S(1)}, bf16[2,2,128,128]{3,2,1,0:T(8,128)(2,1)S(1)}, u32[]{:S(2)}, u32[]{:S(2)}) collective-permute-start(bf16[2,2,128,128]{3,2,1,0:T(8,128)(2,1)S(1)} %get-tuple-element.15), channel_id=1, source_target_pairs={{1,0},{2,1},{3,2},{5,4},{6,5},{7,6},{9,8},{10,9},{11,10},{13,12},{... | collective-permute-start | bytes 393224 | tf_op jit(solution)/shard_map/ppermute | solution.py:18
  23.1 1.3 %collective-permute-start.3 = (bf16[512,128]{1,0:T(8,128)(2,1)S(1)}, bf16[512,128]{1,0:T(8,128)(2,1)S(1)}, u32[]{:S(2)}, u32[]{:S(2)}) collective-permute-start(bf16[512,128]{1,0:T(8,128)(2,1)S(1)} %get-tuple-element.23), channel_id=1, source_target_pairs={{4,0},{8,4},{12,8},{16,12},{20,16},{24,20},{28,24},{5,1},{9,5},{13... | collective-permute-start | bytes 393224 | tf_op jit(solution)/shard_map/ppermute | solution.py:18
  24.4 6.5 %collective-permute-done.1.top_ref = bf16[32,128,128]{2,1,0:T(8,128)(2,1)S(1)} collective-permute-done((bf16[32,128,128]{2,1,0:T(8,128)(2,1)S(1)}, bf16[32,128,128]{2,1,0:T(8,128)(2,1)S(1)}, u32[]{:S(2)}, u32[]{:S(2)}) %collective-permute-start.1) | collective-permute-done | bytes 1048608 | tf_op jit(solution)/shard_map/ppermute | solution.py:18
  30.9 0.0 copy-done.3
  30.9 0.0 copy-start.2
  30.9 0.0 copy-start.4
  30.9 3.2 %shard_map.133 = (f32[32,128,128]{2,1,0:T(8,128)S(1)}, bf16[32,128,128]{2,1,0:T(8,128)(2,1)S(1)}, bf16[32,128,128]{2,1,0:T(8,128)(2,1)S(1)}) custom-call(s32[2,32]{1,0:T(2,128)S(1)} %copy-done.7, s32[2,32,128]{2,1,0:T(8,128)S(1)} %copy-done.1, bf16[2,32,256,128]{3,2,1,0:T(8,128)(2,1)S(1)} %copy-done, bf16[2,32,128]{2,1,0:T(8,128)(2,1)S(1)} %copy-done.3, ...), custom_call_target="tpu_custom_call" | custom-call | flops 1073741824 | bytes 12582912 | tf_op jit(solution)/shard_map/pallas_call | solution.py:419
  34.2 0.0 collective-permute-done.edge_ref
  34.2 2.1 %shard_map.136 = bf16[2,32,128,128]{3,2,1,0:T(8,128)(2,1)} custom-call(s32[2,32]{1,0:T(2,128)S(1)} %copy-done.5, s32[2,32,128]{2,1,0:T(8,128)S(1)} %copy-done.2, bf16[2,32,256,128]{3,2,1,0:T(8,128)(2,1)} %interp_ref.5, bf16[2,32,128]{2,1,0:T(8,128)(2,1)S(1)} %copy-done.4, ...), custom_call_target="tpu_custom_call", output_to_operand_aliasing={{}: (6, {})} | custom-call | flops 67108864 | bytes 786432 | tf_op jit(solution)/shard_map/pallas_call | solution.py:435
  36.2 3.2 %collective-permute-done.2.extra_ref.packed_ref = bf16[1552,128]{1,0:T(8,128)(2,1)S(1)} collective-permute-done((bf16[1552,128]{1,0:T(8,128)(2,1)S(1)}, bf16[1552,128]{1,0:T(8,128)(2,1)S(1)}, u32[]{:S(2)}, u32[]{:S(2)}) %collective-permute-start.2) | collective-permute-done | bytes 397344 | tf_op jit(solution)/shard_map/ppermute | solution.py:18
  39.4 1.5 %shard_map.134._ = bf16[2,32,128,128]{3,2,1,0:T(8,128)(2,1)} custom-call(f32[32,128,128]{2,1,0:T(8,128)S(1)} %get-tuple-element.19.part_ref, bf16[32,128,128]{2,1,0:T(8,128)(2,1)S(1)} %get-tuple-element.20.lower_ref, bf16[32,128,128]{2,1,0:T(8,128)(2,1)S(1)} %get-tuple-element.21.lower_turned_ref, ...), custom_call_target="tpu_custom_call", output_to_operand_aliasing={{}: (5, {})} | custom-call | flops 301989888 | bytes 4325376 | tf_op jit(solution)/shard_map/pallas_call | solution.py:456
  40.9 0.5 %collective-permute-done.3.packed_ref = bf16[512,128]{1,0:T(8,128)(2,1)S(1)} collective-permute-done((bf16[512,128]{1,0:T(8,128)(2,1)S(1)}, bf16[512,128]{1,0:T(8,128)(2,1)S(1)}, u32[]{:S(2)}, u32[]{:S(2)}) %collective-permute-start.3) | collective-permute-done | bytes 131104 | tf_op jit(solution)/shard_map/ppermute | solution.py:18
  41.4 1.1 %shard_map.135 = bf16[2,32,128,128]{3,2,1,0:T(8,128)(2,1)} custom-call(f32[32,128,128]{2,1,0:T(8,128)S(1)} %get-tuple-element.19.part_ref, bf16[32,128,128]{2,1,0:T(8,128)(2,1)S(1)} %get-tuple-element.20.lower_ref, bf16[32,128,128]{2,1,0:T(8,128)(2,1)S(1)} %get-tuple-element.21.lower_turned_ref, ...), custom_call_target="tpu_custom_call", output_to_operand_aliasing={{}: (5, {})} | custom-call | flops 100663296 | bytes 1441792 | tf_op jit(solution)/shard_map/pallas_call | solution.py:456
  (6 shorter events, 0.0 us)
Async XLA Ops:
  0.6 2.7 %copy-start.6 = (s32[2,32]{1,0:T(2,128)S(1)}, s32[2,32]{1,0:T(2,128)}, u32[]{:S(2)}) copy-start(s32[2,32]{1,0:T(2,128)} %rank_hbm.1) | copy-start | bytes 772
  0.6 2.7 %copy-start.5 = (s32[2,32]{1,0:T(2,128)S(1)}, s32[2,32]{1,0:T(2,128)}, u32[]{:S(2)}) copy-start(s32[2,32]{1,0:T(2,128)} %rank_ref.5) | copy-start | bytes 772
  0.7 2.7 %copy-start.7 = (s32[2,32]{1,0:T(2,128)S(1)}, s32[2,32]{1,0:T(2,128)}, u32[]{:S(2)}) copy-start(s32[2,32]{1,0:T(2,128)} %rank_ref.4) | copy-start | bytes 772
  2.0 28.9 %copy-start.1 = (s32[2,32,128]{2,1,0:T(8,128)S(1)}, s32[2,32,128]{2,1,0:T(8,128)}, u32[]{:S(2)}) copy-start(s32[2,32,128]{2,1,0:T(8,128)} %skel_ref.4) | copy-start | bytes 98308
  2.0 28.9 %copy-start.3 = (bf16[2,32,128]{2,1,0:T(8,128)(2,1)S(1)}, bf16[2,32,128]{2,1,0:T(8,128)(2,1)}, u32[]{:S(2)}) copy-start(bf16[2,32,128]{2,1,0:T(8,128)(2,1)} %coup_ref.2) | copy-start | bytes 49156
  2.0 28.9 %collective-permute-start.1 = (bf16[32,128,128]{2,1,0:T(8,128)(2,1)S(1)}, bf16[32,128,128]{2,1,0:T(8,128)(2,1)S(1)}, u32[]{:S(2)}, u32[]{:S(2)}) collective-permute-start(bf16[32,128,128]{2,1,0:T(8,128)(2,1)S(1)} %shard_map.132), channel_id=1, source_target_pairs={{4,0},{8,4},{12,8},{16,12},{20,16},{24,20},{28,24},{5,1},{9,5},{13... | collective-permute-start | bytes 3145736 | tf_op jit(solution)/shard_map/ppermute | solution.py:18
  3.4 27.5 %copy-start = (bf16[2,32,256,128]{3,2,1,0:T(8,128)(2,1)S(1)}, bf16[2,32,256,128]{3,2,1,0:T(8,128)(2,1)}, u32[]{:S(2)}) copy-start(bf16[2,32,256,128]{3,2,1,0:T(8,128)(2,1)} %interp_ref.4) | copy-start | bytes 12582916
  20.5 18.9 %collective-permute-start.2 = (bf16[1552,128]{1,0:T(8,128)(2,1)S(1)}, bf16[1552,128]{1,0:T(8,128)(2,1)S(1)}, u32[]{:S(2)}, u32[]{:S(2)}) collective-permute-start(bf16[1552,128]{1,0:T(8,128)(2,1)S(1)} %get-tuple-element.22), channel_id=1, source_target_pairs={{4,0},{8,4},{12,8},{16,12},{20,16},{24,20},{28,24},{5,1},{9,5},{13... | collective-permute-start | bytes 1191944 | tf_op jit(solution)/shard_map/ppermute | solution.py:18
  21.8 12.4 %collective-permute-start = (bf16[2,2,128,128]{3,2,1,0:T(8,128)(2,1)S(1)}, bf16[2,2,128,128]{3,2,1,0:T(8,128)(2,1)S(1)}, u32[]{:S(2)}, u32[]{:S(2)}) collective-permute-start(bf16[2,2,128,128]{3,2,1,0:T(8,128)(2,1)S(1)} %get-tuple-element.15), channel_id=1, source_target_pairs={{1,0},{2,1},{3,2},{5,4},{6,5},{7,6},{9,8},{10,9},{11,10},{13,12},{... | collective-permute-start | bytes 393224 | tf_op jit(solution)/shard_map/ppermute | solution.py:18
  23.1 18.3 %collective-permute-start.3 = (bf16[512,128]{1,0:T(8,128)(2,1)S(1)}, bf16[512,128]{1,0:T(8,128)(2,1)S(1)}, u32[]{:S(2)}, u32[]{:S(2)}) collective-permute-start(bf16[512,128]{1,0:T(8,128)(2,1)S(1)} %get-tuple-element.23), channel_id=1, source_target_pairs={{4,0},{8,4},{12,8},{16,12},{20,16},{24,20},{28,24},{5,1},{9,5},{13... | collective-permute-start | bytes 393224 | tf_op jit(solution)/shard_map/ppermute | solution.py:18
  30.9 3.3 %copy-start.2 = (s32[2,32,128]{2,1,0:T(8,128)S(1)}, s32[2,32,128]{2,1,0:T(8,128)}, u32[]{:S(2)}) copy-start(s32[2,32,128]{2,1,0:T(8,128)} %skel_ref.5) | copy-start | bytes 98308
  30.9 3.3 %copy-start.4 = (bf16[2,32,128]{2,1,0:T(8,128)(2,1)S(1)}, bf16[2,32,128]{2,1,0:T(8,128)(2,1)}, u32[]{:S(2)}) copy-start(bf16[2,32,128]{2,1,0:T(8,128)(2,1)} %coup_ref.3) | copy-start | bytes 49156

commit v24 on v23

--- a/solution.py
+++ b/solution.py
@@ -403,9 +403,9 @@
             pltpu.VMEM((chunks, cells, slots), F32),
         ],
     )(
-        cell_rank, in_hbm(cell_skel), in_hbm(cell_interp), in_hbm(cell_matrix),
-        x_face_rank, in_hbm(x_face_skel), in_hbm(x_face_interp), in_hbm(x_coupling),
-        y_face_rank, in_hbm(y_face_skel), in_hbm(y_face_interp), in_hbm(y_coupling),
+        in_hbm(cell_rank), in_hbm(cell_skel), in_hbm(cell_interp), in_hbm(cell_matrix),
+        in_hbm(x_face_rank), in_hbm(x_face_skel), in_hbm(x_face_interp), in_hbm(x_coupling),
+        in_hbm(y_face_rank), in_hbm(y_face_skel), in_hbm(y_face_interp), in_hbm(y_coupling),
     )
     edge_in = passed_along(edge, "yz", -1)
     packed_in = passed_along(packed, "gx", -1)

time: 42.9 us -> 43 us (level)
  no operation moved by 1% of the time
where the time goes in v24:
time: 43 us; the launch traced here: 42.6 us
  Pallas kernels  26.4 us (61%)
  waiting for transfers between devices  10.1 us (23%)
  starting transfers between devices  5.3 us (12%)
  between operations  0.78 us (2%)
    pallas_call x1, Pallas kernels, body(): call(functools.partial(main_kernel, cells, nx, chunks), (nx, chunks), [sm...  17.1 us
    ppermute x4, waiting for transfers between devices, passed_along(): return lax.ppermute(x, axis, pairs)  10.1 us
    ppermute x4, starting transfers between devices, passed_along(): return lax.ppermute(x, axis, pairs)  5.3 us
    pallas_call x1, Pallas kernels, body(): call(functools.partial(x_part_kernel, cells, last), (), [smem, vmem, vmem...  3.33 us
    pallas_call x2, Pallas kernels, body(): call(functools.partial(x_last_kernel, count, last, begin, (chunks - 1) *...  2.57 us
    pallas_call x1, Pallas kernels, body(): call(functools.partial(y_edge_kernel, nx, tail), (1,), [smem, pl.BlockSpe...  2.05 us
    pallas_call x1, Pallas kernels, body(): call(functools.partial(top_kernel, cells), (), [hbm, hbm, hbm], vmem, sha...  1.34 us
  transfers between devices with their start and end apart: 4, of which 3 were waited for; matrix products, arithmetic and copies ran while one was open for 0% of the time, Pallas kernels for 56%

profile of v24, /device:TPU:0, one launch (start us, length us, event | category | flops | bytes accessed | tf_op | source)
XLA Modules:
  0.0 42.6 jit_solution(925117044091331067)
XLA Ops:
  0.6 1.3 %shard_map.132 = bf16[32,128,128]{2,1,0:T(8,128)(2,1)S(1)} custom-call(s32[2,32]{1,0:T(2,128)} %rank_hbm.1, s32[2,32,128]{2,1,0:T(8,128)} %skel_hbm.1, bf16[2,32,256,128]{3,2,1,0:T(8,128)(2,1)} %interp_hbm.1), custom_call_target="tpu_custom_call" | custom-call | bytes 2097152 | tf_op jit(solution)/shard_map/pallas_call | solution.py:337
  2.0 0.0 copy-start.1
  2.0 0.0 copy-start.3
  2.0 0.0 copy-start.6
  2.0 1.4 %collective-permute-start.1 = (bf16[32,128,128]{2,1,0:T(8,128)(2,1)S(1)}, bf16[32,128,128]{2,1,0:T(8,128)(2,1)S(1)}, u32[]{:S(2)}, u32[]{:S(2)}) collective-permute-start(bf16[32,128,128]{2,1,0:T(8,128)(2,1)S(1)} %shard_map.132), channel_id=1, source_target_pairs={{4,0},{8,4},{12,8},{16,12},{20,16},{24,20},{28,24},{5,1},{9,5},{13... | collective-permute-start | bytes 3145736 | tf_op jit(solution)/shard_map/ppermute | solution.py:18
  3.4 0.0 copy-start
  3.5 17.1 %shard_map.131 = (bf16[2,32,128,128]{3,2,1,0:T(8,128)(2,1)}, bf16[2,32,128,128]{3,2,1,0:T(8,128)(2,1)}, bf16[1552,128]{1,0:T(8,128)(2,1)S(1)}, bf16[512,128]{1,0...) custom-call(s32[2,32]{1,0:T(2,128)} %rank_hbm.1, ...), custom_call_target="tpu_custom_call" | custom-call | flops 5368709120 | bytes 27262976 | tf_op jit(solution)/shard_map/pallas_call | solution.py:374
  20.5 1.3 %collective-permute-start.2 = (bf16[1552,128]{1,0:T(8,128)(2,1)S(1)}, bf16[1552,128]{1,0:T(8,128)(2,1)S(1)}, u32[]{:S(2)}, u32[]{:S(2)}) collective-permute-start(bf16[1552,128]{1,0:T(8,128)(2,1)S(1)} %get-tuple-element.22), channel_id=1, source_target_pairs={{4,0},{8,4},{12,8},{16,12},{20,16},{24,20},{28,24},{5,1},{9,5},{13... | collective-permute-start | bytes 1191944 | tf_op jit(solution)/shard_map/ppermute | solution.py:18
  21.8 1.3 %collective-permute-start = (bf16[2,2,128,128]{3,2,1,0:T(8,128)(2,1)S(1)}, bf16[2,2,128,128]{3,2,1,0:T(8,128)(2,1)S(1)}, u32[]{:S(2)}, u32[]{:S(2)}) collective-permute-start(bf16[2,2,128,128]{3,2,1,0:T(8,128)(2,1)S(1)} %get-tuple-element.15), channel_id=1, source_target_pairs={{1,0},{2,1},{3,2},{5,4},{6,5},{7,6},{9,8},{10,9},{11,10},{13,12},{... | collective-permute-start | bytes 393224 | tf_op jit(solution)/shard_map/ppermute | solution.py:18
  23.1 1.3 %collective-permute-start.3 = (bf16[512,128]{1,0:T(8,128)(2,1)S(1)}, bf16[512,128]{1,0:T(8,128)(2,1)S(1)}, u32[]{:S(2)}, u32[]{:S(2)}) collective-permute-start(bf16[512,128]{1,0:T(8,128)(2,1)S(1)} %get-tuple-element.23), channel_id=1, source_target_pairs={{4,0},{8,4},{12,8},{16,12},{20,16},{24,20},{28,24},{5,1},{9,5},{13... | collective-permute-start | bytes 393224 | tf_op jit(solution)/shard_map/ppermute | solution.py:18
  24.4 6.6 %collective-permute-done.1.top_ref = bf16[32,128,128]{2,1,0:T(8,128)(2,1)S(1)} collective-permute-done((bf16[32,128,128]{2,1,0:T(8,128)(2,1)S(1)}, bf16[32,128,128]{2,1,0:T(8,128)(2,1)S(1)}, u32[]{:S(2)}, u32[]{:S(2)}) %collective-permute-start.1) | collective-permute-done | bytes 1048608 | tf_op jit(solution)/shard_map/ppermute | solution.py:18
  31.0 0.0 copy-start.2
  31.0 0.0 copy-start.4
  31.0 0.0 copy-start.5
  31.1 3.3 %shard_map.133 = (f32[32,128,128]{2,1,0:T(8,128)S(1)}, bf16[32,128,128]{2,1,0:T(8,128)(2,1)S(1)}, bf16[32,128,128]{2,1,0:T(8,128)(2,1)S(1)}) custom-call(s32[2,32]{1,0:T(2,128)S(1)} %copy-done.6, s32[2,32,128]{2,1,0:T(8,128)S(1)} %copy-done.1, bf16[2,32,256,128]{3,2,1,0:T(8,128)(2,1)S(1)} %copy-done, bf16[2,32,128]{2,1,0:T(8,128)(2,1)S(1)} %copy-done.3, ...), custom_call_target="tpu_custom_call" | custom-call | flops 1073741824 | bytes 12582912 | tf_op jit(solution)/shard_map/pallas_call | solution.py:419
  34.4 0.0 collective-permute-done.edge_ref
  34.4 0.0 copy-done.2
  34.4 0.0 copy-done.4
  34.4 0.0 copy-done.5
  34.4 2.1 %shard_map.136 = bf16[2,32,128,128]{3,2,1,0:T(8,128)(2,1)} custom-call(s32[2,32]{1,0:T(2,128)S(1)} %copy-done.5, s32[2,32,128]{2,1,0:T(8,128)S(1)} %copy-done.2, bf16[2,32,256,128]{3,2,1,0:T(8,128)(2,1)} %interp_ref.5, bf16[2,32,128]{2,1,0:T(8,128)(2,1)S(1)} %copy-done.4, ...), custom_call_target="tpu_custom_call", output_to_operand_aliasing={{}: (6, {})} | custom-call | flops 67108864 | bytes 786432 | tf_op jit(solution)/shard_map/pallas_call | solution.py:435
  36.5 3.0 %collective-permute-done.2.extra_ref.packed_ref = bf16[1552,128]{1,0:T(8,128)(2,1)S(1)} collective-permute-done((bf16[1552,128]{1,0:T(8,128)(2,1)S(1)}, bf16[1552,128]{1,0:T(8,128)(2,1)S(1)}, u32[]{:S(2)}, u32[]{:S(2)}) %collective-permute-start.2) | collective-permute-done | bytes 397344 | tf_op jit(solution)/shard_map/ppermute | solution.py:18
  39.5 1.5 %shard_map.134._ = bf16[2,32,128,128]{3,2,1,0:T(8,128)(2,1)} custom-call(f32[32,128,128]{2,1,0:T(8,128)S(1)} %get-tuple-element.19.part_ref, bf16[32,128,128]{2,1,0:T(8,128)(2,1)S(1)} %get-tuple-element.20.lower_ref, bf16[32,128,128]{2,1,0:T(8,128)(2,1)S(1)} %get-tuple-element.21.lower_turned_ref, ...), custom_call_target="tpu_custom_call", output_to_operand_aliasing={{}: (5, {})} | custom-call | flops 301989888 | bytes 4325376 | tf_op jit(solution)/shard_map/pallas_call | solution.py:456
  41.0 0.5 %collective-permute-done.3.packed_ref = bf16[512,128]{1,0:T(8,128)(2,1)S(1)} collective-permute-done((bf16[512,128]{1,0:T(8,128)(2,1)S(1)}, bf16[512,128]{1,0:T(8,128)(2,1)S(1)}, u32[]{:S(2)}, u32[]{:S(2)}) %collective-permute-start.3) | collective-permute-done | bytes 131104 | tf_op jit(solution)/shard_map/ppermute | solution.py:18
  41.5 1.1 %shard_map.135 = bf16[2,32,128,128]{3,2,1,0:T(8,128)(2,1)} custom-call(f32[32,128,128]{2,1,0:T(8,128)S(1)} %get-tuple-element.19.part_ref, bf16[32,128,128]{2,1,0:T(8,128)(2,1)S(1)} %get-tuple-element.20.lower_ref, bf16[32,128,128]{2,1,0:T(8,128)(2,1)S(1)} %get-tuple-element.21.lower_turned_ref, ...), custom_call_target="tpu_custom_call", output_to_operand_aliasing={{}: (5, {})} | custom-call | flops 100663296 | bytes 1441792 | tf_op jit(solution)/shard_map/pallas_call | solution.py:456
  (4 shorter events, 0.0 us)
Async XLA Ops:
  2.0 29.0 %copy-start.1 = (s32[2,32,128]{2,1,0:T(8,128)S(1)}, s32[2,32,128]{2,1,0:T(8,128)}, u32[]{:S(2)}) copy-start(s32[2,32,128]{2,1,0:T(8,128)} %skel_ref.4) | copy-start | bytes 98308
  2.0 29.0 %copy-start.3 = (bf16[2,32,128]{2,1,0:T(8,128)(2,1)S(1)}, bf16[2,32,128]{2,1,0:T(8,128)(2,1)}, u32[]{:S(2)}) copy-start(bf16[2,32,128]{2,1,0:T(8,128)(2,1)} %coup_ref.2) | copy-start | bytes 49156
  2.0 29.0 %copy-start.6 = (s32[2,32]{1,0:T(2,128)S(1)}, s32[2,32]{1,0:T(2,128)}, u32[]{:S(2)}) copy-start(s32[2,32]{1,0:T(2,128)} %rank_ref.4) | copy-start | bytes 772
  2.0 29.0 %collective-permute-start.1 = (bf16[32,128,128]{2,1,0:T(8,128)(2,1)S(1)}, bf16[32,128,128]{2,1,0:T(8,128)(2,1)S(1)}, u32[]{:S(2)}, u32[]{:S(2)}) collective-permute-start(bf16[32,128,128]{2,1,0:T(8,128)(2,1)S(1)} %shard_map.132), channel_id=1, source_target_pairs={{4,0},{8,4},{12,8},{16,12},{20,16},{24,20},{28,24},{5,1},{9,5},{13... | collective-permute-start | bytes 3145736 | tf_op jit(solution)/shard_map/ppermute | solution.py:18
  3.4 27.6 %copy-start = (bf16[2,32,256,128]{3,2,1,0:T(8,128)(2,1)S(1)}, bf16[2,32,256,128]{3,2,1,0:T(8,128)(2,1)}, u32[]{:S(2)}) copy-start(bf16[2,32,256,128]{3,2,1,0:T(8,128)(2,1)} %interp_ref.4) | copy-start | bytes 12582916
  20.5 19.0 %collective-permute-start.2 = (bf16[1552,128]{1,0:T(8,128)(2,1)S(1)}, bf16[1552,128]{1,0:T(8,128)(2,1)S(1)}, u32[]{:S(2)}, u32[]{:S(2)}) collective-permute-start(bf16[1552,128]{1,0:T(8,128)(2,1)S(1)} %get-tuple-element.22), channel_id=1, source_target_pairs={{4,0},{8,4},{12,8},{16,12},{20,16},{24,20},{28,24},{5,1},{9,5},{13... | collective-permute-start | bytes 1191944 | tf_op jit(solution)/shard_map/ppermute | solution.py:18
  21.8 12.6 %collective-permute-start = (bf16[2,2,128,128]{3,2,1,0:T(8,128)(2,1)S(1)}, bf16[2,2,128,128]{3,2,1,0:T(8,128)(2,1)S(1)}, u32[]{:S(2)}, u32[]{:S(2)}) collective-permute-start(bf16[2,2,128,128]{3,2,1,0:T(8,128)(2,1)S(1)} %get-tuple-element.15), channel_id=1, source_target_pairs={{1,0},{2,1},{3,2},{5,4},{6,5},{7,6},{9,8},{10,9},{11,10},{13,12},{... | collective-permute-start | bytes 393224 | tf_op jit(solution)/shard_map/ppermute | solution.py:18
  23.1 18.4 %collective-permute-start.3 = (bf16[512,128]{1,0:T(8,128)(2,1)S(1)}, bf16[512,128]{1,0:T(8,128)(2,1)S(1)}, u32[]{:S(2)}, u32[]{:S(2)}) collective-permute-start(bf16[512,128]{1,0:T(8,128)(2,1)S(1)} %get-tuple-element.23), channel_id=1, source_target_pairs={{4,0},{8,4},{12,8},{16,12},{20,16},{24,20},{28,24},{5,1},{9,5},{13... | collective-permute-start | bytes 393224 | tf_op jit(solution)/shard_map/ppermute | solution.py:18
  31.0 3.4 %copy-start.2 = (s32[2,32,128]{2,1,0:T(8,128)S(1)}, s32[2,32,128]{2,1,0:T(8,128)}, u32[]{:S(2)}) copy-start(s32[2,32,128]{2,1,0:T(8,128)} %skel_ref.5) | copy-start | bytes 98308
  31.0 3.4 %copy-start.4 = (bf16[2,32,128]{2,1,0:T(8,128)(2,1)S(1)}, bf16[2,32,128]{2,1,0:T(8,128)(2,1)}, u32[]{:S(2)}) copy-start(bf16[2,32,128]{2,1,0:T(8,128)(2,1)} %coup_ref.3) | copy-start | bytes 49156
  31.0 3.4 %copy-start.5 = (s32[2,32]{1,0:T(2,128)S(1)}, s32[2,32]{1,0:T(2,128)}, u32[]{:S(2)}) copy-start(s32[2,32]{1,0:T(2,128)} %rank_ref.5) | copy-start | bytes 772
